TPU v7x, 32 devices: a whole 2x2x4 slice. The times are simulated.
32 devices in a mesh: ia: 4 (over y, x), ja: 2 (over core), ka: 4 (over z).
Axes of the slice: x: 2, y: 2, z: 4, core: 2. Of those that a mesh axis runs over, the one named last changes fastest.
Arguments:
- observed: bfloat16 [4, 2, 20, 128, 32, 128], P('ia', 'ja', 'ka'), may hold values from -6 to 6
- weights: bfloat16 [4, 2, 20, 128, 32, 128], P('ia', 'ja', 'ka'), may hold values from 0 to 4, as said below
- coords: int32 [4, 2, 20, 3], P('ia', 'ja', 'ka'), may hold values from 0 to 31, as said below
- counts: int32 [4, 2, 4], P('ia', 'ja', 'ka'), may hold values from 0 to 5, as said below
- factor_rows: bfloat16 [64, 4096], P(None, ('ia', 'ja', 'ka')), may hold values from -0.75 to 0.75
- factor_cols: bfloat16 [64, 1024], P(None, ('ja', 'ka')), may hold values from -0.75 to 0.75
- factor_depth: bfloat16 [64, 512], replicated, may hold values from -0.75 to 0.75
- core_tensor: bfloat16 [64, 64, 64], replicated, may hold values from -6 to 6
Outputs:
- rows_gradient: float32 [64, 4096], P(None, ('ia', 'ja', 'ka'))
- cols_gradient: float32 [64, 1024], P(None, ('ja', 'ka'))
- depth_gradient: float32 [64, 512], P(None, 'ka')
- core_gradient: float32 [64, 64, 64], replicated
Inputs may be any that keep to these rules, and one draw needn't show every extreme that they name: counts[a, b, c] is the number of live slots of the device at index a of ia, b of ja, c of ka; the busiest devices hold 5. coords[a, b, c * 5 + s] = (p, q, t) with a * 8 <= p < (a + 1) * 8, b * 4 <= q < (b + 1) * 4, c * 4 <= t < (c + 1) * 4; the 5 slots of one device name distinct blocks. `weights`: zero at unobserved entries, positive at observed ones.
All inputs are finite; a program needn't handle non-finite values.
Results may differ from a plain program's by a relative error of at most 0.0012.
Values may be sent and summed in bfloat16 or wider, within the bound.
No kernel may reach another device: no remote copies, remote signals or barrier semaphores. Data moves between devices by JAX's collectives and lax.ppermute only.
A program may use at most 64 MiB of HBM per device.

v0:
```python
import jax
import jax.numpy as jnp
from jax import lax
from jax.sharding import PartitionSpec as P

resid_scale = 1.0 / 64.0


def block_terms(observed_block, weight_block, row_factor, col_factor, depth_factor, core_tensor):
    rank_width, block_rows = row_factor.shape
    block_cols = col_factor.shape[1]
    slab_depth = depth_factor.shape[1]
    core_flat = core_tensor.reshape(rank_width * rank_width, rank_width)
    first_cube = jnp.dot(core_flat, depth_factor, preferred_element_type=jnp.float32).astype(
        jnp.bfloat16
    )
    first_cube = first_cube.reshape(rank_width, rank_width, slab_depth)
    second_cube = jnp.einsum(
        "rsk,sj->rkj", first_cube, col_factor, preferred_element_type=jnp.float32
    ).astype(jnp.bfloat16)
    second_flat = second_cube.reshape(rank_width, slab_depth * block_cols)
    model_block = lax.dot_general(
        row_factor, second_flat, (((0,), (0,)), ((), ())), preferred_element_type=jnp.float32
    )
    weight_flat = weight_block.reshape(block_rows, slab_depth * block_cols).astype(jnp.float32)
    data_flat = observed_block.reshape(block_rows, slab_depth * block_cols).astype(jnp.float32)
    residual = (weight_flat * (model_block - data_flat) * resid_scale).astype(jnp.bfloat16)
    row_term = lax.dot_general(
        second_flat, residual, (((1,), (1,)), ((), ())), preferred_element_type=jnp.float32
    )
    first_back = jnp.dot(row_factor, residual, preferred_element_type=jnp.float32).astype(
        jnp.bfloat16
    )
    back_cube = first_back.reshape(rank_width, slab_depth, block_cols)
    col_term = jnp.einsum("rsk,rkj->sj", first_cube, back_cube, preferred_element_type=jnp.float32)
    second_back = jnp.einsum(
        "sj,rkj->rsk", col_factor, back_cube, preferred_element_type=jnp.float32
    ).astype(jnp.bfloat16)
    back_flat = second_back.reshape(rank_width * rank_width, slab_depth)
    depth_term = lax.dot_general(
        core_flat, back_flat, (((0,), (0,)), ((), ())), preferred_element_type=jnp.float32
    )
    core_term = lax.dot_general(
        back_flat, depth_factor, (((1,), (1,)), ((), ())), preferred_element_type=jnp.float32
    )
    return (row_term, col_term, depth_term, core_term.reshape(rank_width, rank_width, rank_width))


def add_columns(table, piece, start_col):
    width = piece.shape[1]
    return lax.dynamic_update_slice_in_dim(
        table, lax.dynamic_slice_in_dim(table, start_col, width, 1) + piece, start_col, 1
    )


def accumulate_blocks(
    live_count,
    data_slots,
    weight_slots,
    coord_slots,
    row_table,
    col_table,
    factor_depth,
    core_tensor,
    row_base,
    col_base,
):
    rank_width = core_tensor.shape[0]
    block_rows = data_slots.shape[1]
    slab_depth = data_slots.shape[2]
    block_cols = data_slots.shape[3]
    start_sums = (
        jnp.zeros((rank_width, row_table.shape[1]), jnp.float32),
        jnp.zeros((rank_width, col_table.shape[1]), jnp.float32),
        jnp.zeros((rank_width, factor_depth.shape[1]), jnp.float32),
        jnp.zeros((rank_width, rank_width, rank_width), jnp.float32),
    )

    def add_slot(slot_index, running):
        rows_sum, cols_sum, depth_sum, core_sum = running
        position = coord_slots[slot_index]
        row_start = (position[0] - row_base) * block_rows
        col_start = (position[1] - col_base) * block_cols
        depth_start = position[2] * slab_depth
        row_factor = lax.dynamic_slice_in_dim(row_table, row_start, block_rows, 1)
        col_factor = lax.dynamic_slice_in_dim(col_table, col_start, block_cols, 1)
        depth_factor = lax.dynamic_slice_in_dim(factor_depth, depth_start, slab_depth, 1)
        block_sums = block_terms(
            data_slots[slot_index],
            weight_slots[slot_index],
            row_factor,
            col_factor,
            depth_factor,
            core_tensor,
        )
        rows_sum = add_columns(rows_sum, block_sums[0], row_start)
        cols_sum = add_columns(cols_sum, block_sums[1], col_start)
        depth_sum = add_columns(depth_sum, block_sums[2], depth_start)
        return (rows_sum, cols_sum, depth_sum, core_sum + block_sums[3])

    return lax.fori_loop(0, live_count, add_slot, start_sums)


def on_device(
    observed, weights, coords, counts, factor_rows, factor_cols, factor_depth, core_tensor
):
    slot_count = observed.shape[2]
    data_slots = observed.reshape(observed.shape[2:])
    weight_slots = weights.reshape(weights.shape[2:])
    coord_slots = coords.reshape(slot_count, 3)
    own_count = counts.reshape(())
    row_table = lax.all_gather(factor_rows, ("ja", "ka"), axis=1, tiled=True)
    col_table = lax.all_gather(factor_cols, "ka", axis=1, tiled=True)
    row_base = lax.axis_index("ia") * (row_table.shape[1] // observed.shape[3])
    col_base = lax.axis_index("ja") * (col_table.shape[1] // observed.shape[5])
    rows_sum, cols_sum, depth_sum, core_sum = accumulate_blocks(
        own_count,
        data_slots,
        weight_slots,
        coord_slots,
        row_table,
        col_table,
        factor_depth,
        core_tensor,
        row_base,
        col_base,
    )
    rows_gradient = lax.psum_scatter(rows_sum, ("ja", "ka"), scatter_dimension=1, tiled=True)
    cols_whole = lax.psum(cols_sum, "ia")
    depth_whole = lax.psum(depth_sum, ("ia", "ja"))
    cols_gradient, depth_gradient = (
        lax.psum_scatter(cols_whole, "ka", scatter_dimension=1, tiled=True),
        lax.psum_scatter(depth_whole, "ka", scatter_dimension=1, tiled=True),
    )
    core_gradient = lax.psum(core_sum, ("ia", "ja", "ka"))
    return (rows_gradient, cols_gradient, depth_gradient, core_gradient)


def solution(mesh):
    in_specs = (
        P("ia", "ja", "ka", None, None, None),
        P("ia", "ja", "ka", None, None, None),
        P("ia", "ja", "ka", None),
        P("ia", "ja", "ka"),
        P(None, ("ia", "ja", "ka")),
        P(None, ("ja", "ka")),
        P(),
        P(),
    )
    out_specs = (P(None, ("ia", "ja", "ka")), P(None, ("ja", "ka")), P(None, "ka"), P())
    return jax.shard_map(
        on_device, mesh=mesh, in_specs=in_specs, out_specs=out_specs, check_vma=False
    )
```

profile of v0, /device:TPU:0, one launch (start us, length us, event | category | flops | bytes accessed | tf_op | source)
XLA Modules:
  0.0 306.0 jit_solution(17779499878476485826)
XLA Ops:
  8.0 0.0 copy-start
  8.0 0.0 reduce-scatter.6.cloned.1.call-start
  8.1 0.8 copy.42
  8.8 13.9 %all_gather.6 = bf16[64,512]{1,0:T(8,128)(2,1)S(1)} all-gather(bf16[64,128]{1,0:T(8,128)(2,1)} %param.15), channel_id=1, replica_groups=mesh['ia'=4,'ja'=2,'ka'=4] {'ka'}, dimensions={1}, use_global_device_ids=true | all-gather | bytes 81920 | tf_op jit(solution)/shard_map/all_gather | solution.py:113
  22.7 23.7 %all_gather.7 = bf16[64,1024]{1,0:T(8,128)(2,1)} all-gather(bf16[64,128]{1,0:T(8,128)(2,1)} %param.14), channel_id=1, replica_groups=mesh['ia'=4,'ja'=2,'ka'=4] {'ja','ka'}, dimensions={1}, use_global_device_ids=true | all-gather | bytes 147456 | tf_op jit(solution)/shard_map/all_gather | solution.py:112
  46.4 1.6 copy.16
  48.0 0.7 broadcast.6
  48.7 0.7 broadcast.6.clone
  49.4 0.8 broadcast_in_dim.6
  50.2 0.2 broadcast_in_dim.7
  50.4 0.0 copy-done
  50.4 21.4 %while.16 = (s32[]{:T(128)}, f32[64,1024]{1,0:T(8,128)}, f32[64,512]{1,0:T(8,128)}, f32[64,512]{0,1:T(8,128)}, f32[64,64,64]{2,1,0:T(8,128)S(1)}, /*index=5*/s32...) while((s32[]{:T(128)}, f32[64,1024]{1,0:T(8,128)}, ...), condition=%wide.region_1.0_spmd, body=%wide.region_0.0_spmd.sunk | while | flops 356534272 | bytes 24363528 | solution.py:101
  51.1 0.1 constant_dynamic-slice_fusion.2
  51.2 0.6 fusion.87
  53.6 1.1 fusion.88
  54.8 1.4 reshape.59
  56.1 1.5 convolution_convert_fusion.6
  57.6 2.1 dynamic-slice_convert_fusion.3
  59.7 3.4 %fusion.89 = bf16[128,4096]{1,0:T(8,128)(2,1)S(1)} fusion(f32[16,8,32,128]{3,2,1,0:T(8,128)S(1)} %bitcast.129, f32[16,8,32,128]{3,2,1,0:T(8,128)S(1)} %bitcast.130, bf16[8,8,32,128]{3,2,1,0:T(8,128)(2,1)S(1)} %bitcast.131, bf16[64,1024]{1,0:T(8,128)(2,1)} %get-tuple-element.298, s32[]{:T(128)S(6)} %select_n.25), kind=kOutput, calls=%fused_computation.3.clone.1 | convolution fusion | flops 69206016 | bytes 5783556 | tf_op jit(solution)/shard_map/while/body/dot_general | solution.py:22
  63.1 0.0 copy-start.2
  63.1 1.9 fusion.90
  65.1 1.0 convolution_convert_fusion.7
  66.1 0.0 copy-done.2
  66.1 1.7 fusion.91
  67.8 0.1 copy.56
  67.9 0.3 fusion.92
  68.2 1.7 fusion.93
  69.8 1.4 convolution_add_fusion.3
  71.9 0.0 copy-start.1
  71.9 0.0 reduce-scatter.6.cloned.1.call-update
  71.9 0.0 reduce-scatter.8.cloned.1.call-start
  71.9 1.9 copy.17
  73.9 0.0 reduce-scatter.8.cloned.1.call-update
  73.9 0.0 all-reduce.2.cloned.1.call-start
  73.9 0.0 copy-done.1
  74.0 0.5 all-reduce.2.cloned.1.call-update
  74.5 0.0 reduce-scatter.4.cloned.1.call-start
  74.5 0.7 reduce-scatter.4.cloned.1.call-update
  75.2 96.6 %reduce-scatter.6.cloned.1.call-done = f32[64,128]{1,0:T(8,128)} async-done(((f32[64,512]{1,0:T(8,128)}), f32[64,128]{1,0:T(8,128)}) %reduce-scatter.6.cloned.1.call-update) | async-done | bytes 32784 | tf_op jit(solution)/shard_map/reduce_scatter | solution.py:132
  171.8 17.6 %psum.24 = f32[64,128]{1,0:T(8,128)} all-reduce(f32[64,128]{1,0:T(8,128)} %reduce-scatter.6.cloned.1.call-done), channel_id=1, replica_groups=mesh['ia'=4,'ja'=2,'ka'=4] {'ia'}, use_global_device_ids=true, to_apply=%region_3.0 | all-reduce | flops 8192 | bytes 65536 | tf_op jit(solution)/shard_map/psum | solution.py:129
  189.4 2.7 reduce-scatter.8.cloned.1.call-done
  192.1 24.3 %psum.25 = f32[64,128]{1,0:T(8,128)} all-reduce(f32[64,128]{1,0:T(8,128)} %reduce-scatter.8.cloned.1.call-done), channel_id=1, replica_groups=mesh['ia'=4,'ja'=2,'ka'=4] {'ia','ja'}, use_global_device_ids=true, to_apply=%region_5.0 | all-reduce | flops 8192 | bytes 65536 | tf_op jit(solution)/shard_map/psum | solution.py:130
  216.3 79.4 %all-reduce.2.cloned.1.call-done = f32[64,64,64]{2,1,0:T(8,128)} async-done(((f32[64,64,64]{2,1,0:T(8,128)}), f32[64,64,64]{2,1,0:T(8,128)}) %all-reduce.2.cloned.1.call-update) | async-done | bytes 1048592 | tf_op jit(solution)/shard_map/psum | solution.py:135
  295.7 0.0 reduce-scatter.4.cloned.1.call-done
  295.7 3.2 %copy.76 = f32[64,64,64]{2,1,0:T(8,128)} copy(f32[64,64,64]{2,1,0:T(8,128)} %all-reduce.2.cloned.1.call-done) | data formatting | bytes 2097152
Async XLA Ops:
  8.0 42.4 %copy-start = (bf16[64,64,64]{2,1,0:T(8,128)(2,1)S(1)}, bf16[64,64,64]{2,1,0:T(8,128)(2,1)}, u32[]{:S(2)}) copy-start(bf16[64,64,64]{2,1,0:T(8,128)(2,1)} %param.17) | copy-start | bytes 1572868
  8.0 163.8 %reduce-scatter.6.cloned.1.call-start = ((), (), s32[]{:S(2)}) async-start(), calls=%async_computation.5 | async-start | bytes 163840 | tf_op jit(solution)/shard_map/reduce_scatter | solution.py:132
  63.1 3.0 copy-start.2
  71.9 2.1 copy-start.1
  71.9 120.2 %reduce-scatter.8.cloned.1.call-start = ((), (), s32[]{:S(2)}) async-start(), calls=%async_computation.6 | async-start | bytes 163840 | tf_op jit(solution)/shard_map/reduce_scatter | solution.py:133
  73.9 221.8 %all-reduce.2.cloned.1.call-start = ((), (), s32[]{:S(2)}) async-start(), calls=%async_computation.4 | async-start | bytes 4194304 | tf_op jit(solution)/shard_map/psum | solution.py:135
  74.5 221.2 %reduce-scatter.4.cloned.1.call-start = ((), (), s32[]{:S(2)}) async-start(), calls=%async_computation.3 | async-start | bytes 294912 | tf_op jit(solution)/shard_map/reduce_scatter | solution.py:128
Sparse Core Ops, SparseCore 0:
  72.0 99.7 reduce-scatter.5
  174.2 17.8 reduce-scatter.7
  194.9 29.8 reduce-scatter.3
Sparse Core Ops, SparseCore 1:
  81.1 214.5 all-reduce.1
where the time goes:
time: 308 us; the launch traced here: 306 us
  waiting for transfers between devices  180 us (58%)
  blocking collectives  79.4 us (26%)
  between operations  15.2 us (5%)
  matrix products  13.9 us (5%)
  local copies, waits for them, and re-layouts  11.9 us (4%)
  loops' own time  3.25 us (1%)
    reduce_scatter x1, waiting for transfers between devices, on_device(): lax.psum_scatter(cols_whole, 'ka', scatter_dimension=1, tiled=True)  96.6 us
    psum x1, waiting for transfers between devices, on_device(): core_gradient = lax.psum(core_sum, ('ia', 'ja', 'ka'))  79.4 us
    psum x1, blocking collectives, on_device(): depth_whole = lax.psum(depth_sum, ('ia', 'ja'))  24.3 us
    all_gather x1, blocking collectives, on_device(): row_table = lax.all_gather(factor_rows, ('ja', 'ka'), axis=1, tiled=True)  23.7 us
    psum x1, blocking collectives, on_device(): cols_whole = lax.psum(cols_sum, 'ia')  17.6 us
    all_gather x1, blocking collectives, on_device(): col_table = lax.all_gather(factor_cols, 'ka', axis=1, tiled=True)  13.9 us
  transfers between devices with their start and end apart: 4, of which 3 were waited for; matrix products, arithmetic and copies ran while one was open for 1% of the time, Pallas kernels for 0%

commit v1 on v0

v1 whole, which is shorter than its diff:
```python
import functools

import jax
import jax.numpy as jnp
from jax import lax
from jax.experimental import pallas as pl
from jax.experimental.pallas import tpu as pltpu
from jax.sharding import PartitionSpec as P

resid_scale = 1.0 / 64.0
f32 = jnp.float32
bf16 = jnp.bfloat16


def dot(a, b, contract=((1,), (0,))):
    return lax.dot_general(a, b, (contract, ((), ())), preferred_element_type=f32)


def prepare_kernel(
    scalars, observed, weights, factor_depth, core, data_out, weight_out, cube_out, cube_turned_out, spread, cube_wide
):
    slot = pl.program_id(0)
    rank = core.shape[0]
    _, rows, slab, cols = observed.shape
    depth_blocks = cube_out.shape[0]
    half = slab // 2

    @pl.when(slot == 0)
    def _():
        width = depth_blocks * slab
        start = pl.multiple_of(scalars[1] * width, width)
        depth = factor_depth[:, pl.ds(start, width)].astype(f32).T
        order = [
            depth[t * slab + h * half : t * slab + (h + 1) * half] for h in range(2) for t in range(depth_blocks)
        ]
        depth = jnp.concatenate(order, axis=0).astype(bf16)
        count = depth_blocks * half

        def one_rank(r1, carry):
            piece = dot(depth, core[r1], ((1,), (1,)))
            wide = jnp.concatenate([piece[:count], piece[count:]], axis=1)
            cube_wide[pl.ds(r1, count, stride=rank), :] = wide
            return carry

        lax.fori_loop(0, rank, one_rank, 0, unroll=8)
        for t in range(depth_blocks):
            block = cube_wide[t * half * rank : (t + 1) * half * rank, :]
            cube_out[t] = block.astype(bf16)
            cube_turned_out[t] = block.T.astype(bf16)

    @pl.when(slot < scalars[0])
    def _():
        for source, target in ((observed, data_out), (weights, weight_out)):
            for i in range(0, rows, 16):
                spread[i * slab : (i + 16) * slab, :] = (
                    source[0, i : i + 16].astype(f32).reshape(16 * slab, cols)
                )
            for k in range(slab):
                target[0, k] = spread[pl.ds(k, rows, stride=slab), :].astype(bf16)


def prepare(scalars, observed, weights, factor_depth, core, depth_blocks):
    slots, rows, slab, cols = observed.shape
    rank = core.shape[0]
    half = slab // 2

    def live(slot, scalars):
        return (jnp.minimum(slot, jnp.maximum(scalars[0] - 1, 0)), 0, 0, 0)

    def whole(ndim):
        return lambda slot, scalars: (0,) * ndim

    turned = (slots, slab, rows, cols)
    cube = (depth_blocks, half * rank, 2 * rank)
    cube_turned = (depth_blocks, 2 * rank, half * rank)
    return pl.pallas_call(
        prepare_kernel,
        out_shape=(
            jax.ShapeDtypeStruct(turned, bf16),
            jax.ShapeDtypeStruct(turned, bf16),
            jax.ShapeDtypeStruct(cube, bf16),
            jax.ShapeDtypeStruct(cube_turned, bf16),
        ),
        grid_spec=pltpu.PrefetchScalarGridSpec(
            num_scalar_prefetch=1,
            grid=(slots,),
            in_specs=[
                pl.BlockSpec((1, rows, slab, cols), live),
                pl.BlockSpec((1, rows, slab, cols), live),
                pl.BlockSpec(factor_depth.shape, whole(2)),
                pl.BlockSpec(core.shape, whole(3)),
            ],
            out_specs=[
                pl.BlockSpec((1, slab, rows, cols), live),
                pl.BlockSpec((1, slab, rows, cols), live),
                pl.BlockSpec(cube, whole(3)),
                pl.BlockSpec(cube_turned, whole(3)),
            ],
            scratch_shapes=[
                pltpu.VMEM((rows * slab, cols), f32),
                pltpu.VMEM((depth_blocks * half * rank, 2 * rank), f32),
            ],
        ),
        compiler_params=pltpu.CompilerParams(vmem_limit_bytes=48 * 2**20),
        cost_estimate=pl.CostEstimate(flops=10**8, bytes_accessed=16 * 2**20, transcendentals=0),
        name="prepare",
    )(scalars, observed, weights, factor_depth, core)


COUNT, KA, ROW_BASE, COL_BASE, ROW_MASK, COL_MASK, CORE_MASK, COORDS = range(8)


def terms_kernel(
    row_chunks,
    scalars,
    data,
    weight,
    cube,
    cube_turned,
    row_table,
    col_table,
    factor_depth,
    core,
    core_out,
    rows_out,
    cols_out,
    depth_out,
    wide_col,
    forward,
    backward,
    by_rank,
    second_all,
    depth_all,
    depth_turned,
    depth_sum,
):
    slot = pl.program_id(0)
    slots = pl.num_programs(0)
    _, slab, rows, cols = data.shape
    rank = core.shape[0]
    half = slab // 2
    pairs = rank // 2
    depth_blocks = cube.shape[0]

    @pl.when(slot == 0)
    def _():
        second_all[...] = jnp.zeros_like(second_all)
        depth_all[...] = jnp.zeros_like(depth_all)
        depth_sum[...] = jnp.zeros_like(depth_sum)
        rows_out[...] = jnp.zeros_like(rows_out)
        cols_out[...] = jnp.zeros_like(cols_out)
        wide_col[...] = jnp.zeros_like(wide_col)
        width = depth_blocks * slab
        start = pl.multiple_of(scalars[KA] * width, width)
        depth_turned[...] = factor_depth[:, pl.ds(start, width)].astype(f32).T

    @pl.when(slot < scalars[COUNT])
    def _():
        row_at = (scalars[COORDS + 3 * slot] - scalars[ROW_BASE]) ^ scalars[ROW_MASK]
        col_at = (scalars[COORDS + 3 * slot + 1] - scalars[COL_BASE]) ^ scalars[COL_MASK]
        depth_at = scalars[COORDS + 3 * slot + 2] - scalars[KA] * depth_blocks
        row_factor = row_table[row_at]
        row_turned = row_factor.astype(f32).T.astype(bf16)
        col_factor = col_table[col_at]
        wide_col[:rank, :cols] = col_factor
        wide_col[rank:, cols:] = col_factor
        own_depth = depth_turned[pl.ds(pl.multiple_of(depth_at * slab, slab), slab), :]
        depth_all[pl.ds(pl.multiple_of(slot * slab, slab), slab), :] = own_depth.astype(bf16)

        step = 4

        def some_pairs(at, row_sum):
            first = at * step
            for extra in range(step):
                kp = first + extra
                lines = pl.ds(pl.multiple_of(kp * rank, rank), rank)
                second = dot(cube[depth_at, lines, :], wide_col[...]).astype(bf16)
                model = dot(row_turned, second)
                parts = []
                for h in range(2):
                    seen = data[0, h * half + kp].astype(f32)
                    scale = weight[0, h * half + kp].astype(f32)
                    gap = model[:, h * cols : (h + 1) * cols] - seen
                    parts.append((scale * gap * resid_scale).astype(bf16))
                residual = jnp.concatenate(parts, axis=1)
                row_sum = row_sum + dot(second, residual, ((1,), (1,)))
                back = dot(row_factor, residual).astype(bf16)
                backward[lines, :] = back
                back = back.astype(f32)
                for h in range(2):
                    by_rank[pl.ds(h * half + kp, rank, stride=slab), :] = back[:, h * cols : (h + 1) * cols]
            return row_sum

        row_sum = lax.fori_loop(0, half // step, some_pairs, jnp.zeros((rank, rows), f32))
        rows_out[row_at] += row_sum
        wide = dot(cube_turned[depth_at], backward[...])
        cols_out[col_at] += wide[:rank, :cols] + wide[rank:, cols:]
        count = pairs * slab
        for part in range(4):
            lo, size = part * count // 4, count // 4
            ranked = jnp.concatenate(
                [by_rank[lo : lo + size, :].astype(bf16), by_rank[count + lo : count + lo + size, :].astype(bf16)],
                axis=1,
            )
            second_back = dot(ranked, wide_col[...], ((1,), (1,))).astype(bf16)
            second_all[pl.ds(part * pairs // 4, pairs // 4), pl.ds(pl.multiple_of(slot * slab, slab), slab), :] = (
                second_back.reshape(pairs // 4, slab, 2 * rank)
            )

    @pl.when(slot == slots - 1)
    def _():
        def one_chunk(at, total):
            pair = at ^ scalars[CORE_MASK]
            second = second_all[pair]
            both = jnp.concatenate([core[pair], core[pairs + pair]], axis=0)
            total = total + dot(second, both)
            piece = dot(second, depth_all[...], ((0,), (0,)))
            core_out[at] = jnp.concatenate([piece[:rank], piece[rank:]], axis=1)
            return total

        total = lax.fori_loop(0, pairs, one_chunk, jnp.zeros((second_all.shape[1], rank), f32), unroll=2)
        for s in range(second_all.shape[1] // slab):

            @pl.when(s < scalars[COUNT])
            def _():
                at = scalars[COORDS + 3 * s + 2] - scalars[KA] * depth_blocks
                lines = pl.ds(pl.multiple_of(at * slab, slab), slab)
                depth_sum[lines, :] += total[s * slab : (s + 1) * slab]

        depth_out[...] = depth_sum[...].T


def terms(scalars, data, weight, cube, cube_turned, row_table, col_table, factor_depth, core):
    slots, slab, rows, cols = data.shape
    rank = core.shape[0]
    half = slab // 2
    depth_blocks = cube.shape[0]

    def live(slot, scalars):
        return (jnp.minimum(slot, jnp.maximum(scalars[COUNT] - 1, 0)), 0, 0, 0)

    def whole(array):
        return pl.BlockSpec(array.shape, lambda slot, scalars: (0,) * len(array.shape))

    outs = (
        jax.ShapeDtypeStruct((rank // 2, rank, 2 * rank), f32),
        jax.ShapeDtypeStruct((row_table.shape[0], rank, rows), f32),
        jax.ShapeDtypeStruct((col_table.shape[0], rank, cols), f32),
        jax.ShapeDtypeStruct((rank, depth_blocks * slab), f32),
    )
    return pl.pallas_call(
        functools.partial(terms_kernel, row_table.shape[0]),
        out_shape=outs,
        grid_spec=pltpu.PrefetchScalarGridSpec(
            num_scalar_prefetch=1,
            grid=(slots,),
            in_specs=[
                pl.BlockSpec((1, slab, rows, cols), live),
                pl.BlockSpec((1, slab, rows, cols), live),
                whole(cube),
                whole(cube_turned),
                whole(row_table),
                whole(col_table),
                whole(factor_depth),
                whole(core),
            ],
            out_specs=[whole(out) for out in outs],
            scratch_shapes=[
                pltpu.VMEM((2 * rank, 2 * cols), bf16),
                pltpu.VMEM((8, 128), bf16),
                pltpu.VMEM((half * rank, 2 * cols), bf16),
                pltpu.VMEM((rank * slab, cols), f32),
                pltpu.VMEM((rank // 2, slots * slab, 2 * rank), bf16),
                pltpu.VMEM((slots * slab, rank), bf16),
                pltpu.VMEM((depth_blocks * slab, rank), f32),
                pltpu.VMEM((depth_blocks * slab, rank), f32),
            ],
        ),
        compiler_params=pltpu.CompilerParams(vmem_limit_bytes=48 * 2**20),
        cost_estimate=pl.CostEstimate(flops=10**9, bytes_accessed=16 * 2**20, transcendentals=0),
        name="terms",
    )(scalars, data, weight, cube, cube_turned, row_table, col_table, factor_depth, core)


def unpack_kernel(scalars, own, other, out):
    rank = out.shape[1]
    mine = pl.program_id(0)
    high = pl.program_id(1)
    count = out.shape[0]
    low = scalars[0] & (count - 1)

    for source, which in ((own, 0), (other, 1)):
        for h in range(2):

            @pl.when(jnp.logical_and(mine == which, high == h))
            def _():
                def one(at, carry):
                    out[at ^ low] = source[at][:, h * rank : (h + 1) * rank]
                    return carry

                lax.fori_loop(0, count, one, 0, unroll=4)


def unpack(mask, own, other):
    count, rank, _ = own.shape
    parts = 2

    def place(mine, high, scalars):
        return (high * parts + ((scalars[0] // count) ^ mine), 0, 0)

    def all_of(mine, high, scalars):
        return (0, 0, 0)

    return pl.pallas_call(
        unpack_kernel,
        out_shape=jax.ShapeDtypeStruct((rank, rank, rank), f32),
        grid_spec=pltpu.PrefetchScalarGridSpec(
            num_scalar_prefetch=1,
            grid=(parts, 2),
            in_specs=[pl.BlockSpec(own.shape, all_of), pl.BlockSpec(other.shape, all_of)],
            out_specs=pl.BlockSpec((count, rank, rank), place),
        ),
        compiler_params=pltpu.CompilerParams(vmem_limit_bytes=32 * 2**20),
        name="unpack",
    )(mask, own, other)


def power_of_two(n):
    return n & (n - 1) == 0


def swap(value, axis, size, mask):
    return lax.ppermute(value, axis, [(at, at ^ mask) for at in range(size)])


def on_device(sizes, observed, weights, coords, counts, factor_rows, factor_cols, factor_depth, core_tensor):
    n_ia, n_ja, n_ka = sizes["ia"], sizes["ja"], sizes["ka"]
    devices = n_ia * n_ja * n_ka
    rank = core_tensor.shape[0]
    _, _, slots, rows, slab, cols = observed.shape
    data = observed.reshape(observed.shape[2:])
    weight = weights.reshape(weights.shape[2:])
    own_coords = coords.reshape(slots * 3)
    own_count = counts.reshape(())
    row_chunks = factor_rows.shape[1] * n_ja * n_ka // rows
    col_chunks = factor_cols.shape[1] * n_ka // cols
    depth_blocks = factor_depth.shape[1] // n_ka // slab
    ia, ja, ka = lax.axis_index("ia"), lax.axis_index("ja"), lax.axis_index("ka")
    by_swaps = (
        n_ja == 2
        and power_of_two(n_ia)
        and power_of_two(n_ka)
        and rank // 2 == devices
        and factor_rows.shape[1] == rows
        and factor_cols.shape[1] == cols
    )

    data, weight, cube, cube_turned = prepare(
        jnp.stack([own_count, ka]).astype(jnp.int32), data, weight, factor_depth, core_tensor, depth_blocks
    )

    if by_swaps:
        both = jnp.stack([factor_rows, factor_cols])
        from_ka = [both] + [swap(both, "ka", n_ka, mask) for mask in range(1, n_ka)]
        own_rows = jnp.stack([piece[0] for piece in from_ka])
        row_table = jnp.concatenate([own_rows, swap(own_rows, "ja", n_ja, 1)])
        col_table = jnp.stack([piece[1] for piece in from_ka])
        masks = [ja * n_ka + ka, ka, (ja * n_ia + ia) * n_ka + ka]
    else:
        row_table = lax.all_gather(factor_rows, ("ja", "ka"), axis=1, tiled=True)
        row_table = row_table.reshape(rank, row_chunks, rows).transpose(1, 0, 2)
        col_table = lax.all_gather(factor_cols, "ka", axis=1, tiled=True)
        col_table = col_table.reshape(rank, col_chunks, cols).transpose(1, 0, 2)
        masks = [0, 0, 0]

    scalars = jnp.stack([own_count, ka, ia * row_chunks, ja * col_chunks, *masks]).astype(jnp.int32)
    core_sum, rows_sum, cols_sum, depth_sum = terms(
        jnp.concatenate([scalars, own_coords]),
        data,
        weight,
        cube,
        cube_turned,
        row_table,
        col_table,
        factor_depth,
        core_tensor,
    )

    if not by_swaps:
        rows_whole = rows_sum.transpose(1, 0, 2).reshape(rank, row_chunks * rows)
        cols_whole = cols_sum.transpose(1, 0, 2).reshape(rank, col_chunks * cols)
        core_whole = core_sum.reshape(rank // 2, rank, 2, rank).transpose(2, 0, 1, 3).reshape(rank, rank, rank)
        return (
            lax.psum_scatter(rows_whole, ("ja", "ka"), scatter_dimension=1, tiled=True),
            lax.psum_scatter(lax.psum(cols_whole, "ia"), "ka", scatter_dimension=1, tiled=True),
            lax.psum(depth_sum, ("ia", "ja")),
            lax.psum(core_whole, ("ia", "ja", "ka")),
        )

    half = devices // 2
    keep = jnp.concatenate([core_sum[:half], rows_sum[:n_ka], depth_sum[None]])
    send = jnp.concatenate([core_sum[half:], rows_sum[n_ka:], depth_sum[None]])
    total = keep + swap(send, "ja", n_ja, 1)
    core_half, rows_half, depth_half = total[:half], total[half : half + n_ka], total[half + n_ka :]
    core_quarter = core_half[:n_ka]
    depth_total = depth_half[0]
    for mask in range(1, n_ia):
        piece = jnp.concatenate([core_half[mask * n_ka : (mask + 1) * n_ka], depth_half])
        got = swap(piece, "ia", n_ia, mask)
        core_quarter = core_quarter + got[:n_ka]
        depth_total = depth_total + got[n_ka]
    own = jnp.stack([core_quarter[0], rows_half[0], cols_sum[0]])
    for mask in range(1, n_ka):
        own = own + swap(jnp.stack([core_quarter[mask], rows_half[mask], cols_sum[mask]]), "ka", n_ka, mask)
    core_own, rows_total, cols_own = own[0], own[1], own[2]
    pieces = [core_own] + [swap(core_own, "ka", n_ka, mask) for mask in range(1, n_ka)]
    pack = jnp.stack(pieces + [cols_own])
    cols_total = cols_own
    gathered = [pack[:n_ka]]
    for mask in range(1, n_ia):
        got = swap(pack, "ia", n_ia, mask)
        gathered.append(got[:n_ka])
        cols_total = cols_total + got[n_ka]
    mine = jnp.concatenate(gathered)
    other = swap(mine, "ja", n_ja, 1)
    core_total = unpack(jnp.stack([masks[2]]).astype(jnp.int32), mine, other)
    return (rows_total, cols_total, depth_total, core_total)


def solution(mesh):
    in_specs = (
        P("ia", "ja", "ka", None, None, None),
        P("ia", "ja", "ka", None, None, None),
        P("ia", "ja", "ka", None),
        P("ia", "ja", "ka"),
        P(None, ("ia", "ja", "ka")),
        P(None, ("ja", "ka")),
        P(),
        P(),
    )
    out_specs = (P(None, ("ia", "ja", "ka")), P(None, ("ja", "ka")), P(None, "ka"), P())
    return jax.shard_map(
        functools.partial(on_device, dict(mesh.shape)),
        mesh=mesh,
        in_specs=in_specs,
        out_specs=out_specs,
        check_vma=False,
    )
```

time: 308 us -> 128 us (0.42)
  waiting for transfers between devices: 180 us -> 30 us
  blocking collectives: 79.4 us -> 0 us
  starting transfers between devices: 0.16 us -> 61.5 us
  Pallas kernels: 0 us -> 27.8 us
  matrix products: 13.9 us -> 0 us
  between operations: 15.2 us -> 1.51 us
  local copies, waits for them, and re-layouts: 11.9 us -> 4.64 us
  loops' own time: 3.25 us -> 0 us
    reduce_scatter x3 -> x0, waiting for transfers between devices: 99.3 us -> none  [the longest x1 96.6 us: on_device(): lax.psum_scatter(cols_whole, 'ka', scatter_dimension=1, tiled=True)]
    psum x1 -> x0, waiting for transfers between devices: 79.4 us -> none  [on_device(): core_gradient = lax.psum(core_sum, ('ia', 'ja', 'ka'))]
    ppermute x0 -> x18, starting transfers between devices: none -> 61.5 us  [swap(): return lax.ppermute(value, axis, [(at, at ^ mask) for at in range(size)])]
    psum x2 -> x0, blocking collectives: 41.8 us -> none  [the longest x1 24.3 us: on_device(): depth_whole = lax.psum(depth_sum, ('ia', 'ja'))]
    all_gather x2 -> x0, blocking collectives: 37.6 us -> none  [the longest x1 23.7 us: on_device(): row_table = lax.all_gather(factor_rows, ('ja', 'ka'), axis=1, tiled=True)]
    ppermute x0 -> x18, waiting for transfers between devices: none -> 30 us  [swap(): return lax.ppermute(value, axis, [(at, at ^ mask) for at in range(size)])]
    pallas_call x0 -> x3, Pallas kernels: none -> 27.8 us  [the longest x1 14.1 us: terms(): pl.pallas_call(functools.partial(terms_kernel, row_table.shape[0]), out_s...]
    dot_general x9 -> x0, matrix products: 13.9 us -> none  [the longest x1 3.39 us: block_terms(): lax.dot_general(row_factor, second_flat, (((0,), (0,)), ((), ())), prefer...]
  transfers between devices with their start and end apart: 4 -> 18, of which waited for: 3 -> 10; matrix products, arithmetic and copies ran while one was open for 1% -> 2% of each run, Pallas kernels for 0% -> 9%
where the time goes in v1:
time: 128 us
  starting transfers between devices  61.5 us (48%)
  waiting for transfers between devices  30 us (23%)
  Pallas kernels  27.8 us (22%)
  local copies, waits for them, and re-layouts  4.64 us (4%)
  other arithmetic  2.38 us (2%)
  between operations  1.51 us (1%)
    ppermute x18, starting transfers between devices, swap(): return lax.ppermute(value, axis, [(at, at ^ mask) for at in range(size)])  61.5 us
    ppermute x18, waiting for transfers between devices, swap(): return lax.ppermute(value, axis, [(at, at ^ mask) for at in range(size)])  30 us
    pallas_call x1, Pallas kernels, terms(): pl.pallas_call(functools.partial(terms_kernel, row_table.shape[0]), out_s...  14.1 us
    pallas_call x1, Pallas kernels, prepare(): pl.pallas_call(prepare_kernel, out_shape=(jax.ShapeDtypeStruct(turned, bf...  11.2 us
    unnamed x20, local copies, waits for them, and re-layouts  4.23 us
  transfers between devices with their start and end apart: 18, of which 10 were waited for; matrix products, arithmetic and copies ran while one was open for 2% of the time, Pallas kernels for 9%

profile of v1, /device:TPU:0, one launch (start us, length us, event | category | flops | bytes accessed | tf_op | source)
XLA Modules:
  0.0 127.8 jit_solution(16498135998674132708)
XLA Ops:
  0.6 0.7 pad_maximum_fusion.10
  1.4 5.0 %collective-permute-start.2 = (bf16[2,64,128]{2,1,0:T(8,128)(2,1)S(1)}, bf16[2,64,128]{2,1,0:T(8,128)(2,1)S(1)}, u32[]{:S(2)}, u32[]{:S(2)}) collective-permute-start(bf16[2,64,128]{2,1,0:T(8,128)(2,1)S(1)} %pad_maximum_fusion.10), channel_id=1, source_target_pairs={{0,3},{1,2},{2,1},{3,0},{4,7},{5,6},{6,5},{7,4},{8,11},{9,10},{10,... | collective-permute-start | bytes 98312 | tf_op jit(solution)/shard_map/ppermute | solution.py:333
  6.4 0.0 collective-permute-start.1
  6.4 0.6 collective-permute-start
  7.0 0.7 constant_dynamic-update-slice_fusion.4
  8.4 0.1 pad_add_fusion.scalars
  8.5 0.8 copy.13
  9.3 0.1 reshape.23
  9.3 0.1 concatenate.27.scalars
  9.4 1.2 copy-done
  10.7 0.8 copy-done.2
  11.5 11.2 %prepare.1 = (bf16[5,32,128,128]{3,2,1,0:T(8,128)(2,1)}, bf16[5,32,128,128]{3,2,1,0:T(8,128)(2,1)}, bf16[4,1024,128]{2,1,0:T(8,128)(2,1)S(1)}, bf16[4,128,1024]{2,1,0:T(8,128)(2,1)S(1)}) custom-call(s32[2]{0:T(128)S(1)} %pad_add_fusion.scalars, bf16[5,128,32,128]{3,2,1,0:T(8,128)(2,1)} %bitcast.33, bf16[5,128,32,128]{3,2,1,0:T(8,128)(2,1)} %bitcast.34, ...), custom_call_target="tpu_custom_call" | custom-call | flops 100000000 | bytes 16777216 | tf_op jit(solution)/shard_map/prepare/pallas_call | solution.py:76
  22.7 0.0 collective-permute-done
  22.8 2.8 %collective-permute-start.3 = (bf16[4,64,128]{2,1,0:T(8,128)(2,1)S(1)}, bf16[4,64,128]{2,1,0:T(8,128)(2,1)S(1)}, u32[]{:S(2)}, u32[]{:S(2)}) collective-permute-start(bf16[4,64,128]{2,1,0:T(8,128)(2,1)S(1)} %pad_maximum_fusion.8), channel_id=1, source_target_pairs={{0,4},{4,0},{1,5},{5,1},{2,6},{6,2},{3,7},{7,3},{8,12},{12,8},{9,1... | collective-permute-start | bytes 196616 | tf_op jit(solution)/shard_map/ppermute | solution.py:333
  25.7 0.9 collective-permute-done.3
  26.6 14.1 %terms.1 = (f32[32,64,128]{2,1,0:T(8,128)S(1)}, f32[8,64,128]{2,1,0:T(8,128)S(1)}, f32[4,64,128]{2,1,0:T(8,128)S(1)}, f32[64,128]{1,0:T(8,128)S(1)}) custom-call(s32[22]{0:T(128)S(1)} %concatenate.27.scalars, bf16[5,32,128,128]{3,2,1,0:T(8,128)(2,1)} %get-tuple-element.12.data, bf16[5,32,128,128]{3,2,1,0:T(8,128)(2,1)} %get-tuple-element.13.weight, ...), custom_call_target="tpu_custom_call" | custom-call | flops 1000000000 | bytes 16777216 | tf_op jit(solution)/shard_map/terms/pallas_call | solution.py:251
  40.7 0.1 fusion.5
  40.8 0.1 pad_maximum_fusion
  40.9 6.9 %collective-permute-start.4 = (f32[21,64,128]{2,1,0:T(8,128)S(1)}, f32[21,64,128]{2,1,0:T(8,128)S(1)}, u32[]{:S(2)}, u32[]{:S(2)}) collective-permute-start(f32[21,64,128]{2,1,0:T(8,128)S(1)} %pad_maximum_fusion), channel_id=1, source_target_pairs={{0,4},{4,0},{1,5},{5,1},{2,6},{6,2},{3,7},{7,3},{8,12},{12,8},{9,1... | collective-permute-start | bytes 2064392 | tf_op jit(solution)/shard_map/ppermute | solution.py:333
  47.8 1.8 %collective-permute-done.4 = f32[21,64,128]{2,1,0:T(8,128)S(1)} collective-permute-done((f32[21,64,128]{2,1,0:T(8,128)S(1)}, f32[21,64,128]{2,1,0:T(8,128)S(1)}, u32[]{:S(2)}, u32[]{:S(2)}) %collective-permute-start.4) | collective-permute-done | bytes 688160 | tf_op jit(solution)/shard_map/ppermute | solution.py:333
  49.6 0.1 fusion
  49.7 2.8 %collective-permute-start.5 = (f32[5,64,128]{2,1,0:T(8,128)S(1)}, f32[5,64,128]{2,1,0:T(8,128)S(1)}, u32[]{:S(2)}, u32[]{:S(2)}) collective-permute-start(f32[5,64,128]{2,1,0:T(8,128)S(1)} %get-tuple-element.50), channel_id=1, source_target_pairs={{0,8},{8,0},{16,24},{24,16},{1,9},{9,1},{17,25},{25,17},{2,10},{10... | collective-permute-start | bytes 491528 | tf_op jit(solution)/shard_map/ppermute | solution.py:333
  52.6 1.5 %collective-permute-start.7 = (f32[5,64,128]{2,1,0:T(8,128)S(1)}, f32[5,64,128]{2,1,0:T(8,128)S(1)}, u32[]{:S(2)}, u32[]{:S(2)}) collective-permute-start(f32[5,64,128]{2,1,0:T(8,128)S(1)} %get-tuple-element.51), channel_id=1, source_target_pairs={{0,24},{8,16},{16,8},{24,0},{1,25},{9,17},{17,9},{25,1},{2,26},{10... | collective-permute-start | bytes 491528 | tf_op jit(solution)/shard_map/ppermute | solution.py:333
  54.0 0.1 collective-permute-start.6
  54.1 3.4 %collective-permute-done.5 = f32[5,64,128]{2,1,0:T(8,128)S(1)} collective-permute-done((f32[5,64,128]{2,1,0:T(8,128)S(1)}, f32[5,64,128]{2,1,0:T(8,128)S(1)}, u32[]{:S(2)}, u32[]{:S(2)}) %collective-permute-start.5) | collective-permute-done | bytes 163872 | tf_op jit(solution)/shard_map/ppermute | solution.py:333
  57.5 4.3 %collective-permute-done.7 = f32[5,64,128]{2,1,0:T(8,128)S(1)} collective-permute-done((f32[5,64,128]{2,1,0:T(8,128)S(1)}, f32[5,64,128]{2,1,0:T(8,128)S(1)}, u32[]{:S(2)}, u32[]{:S(2)}) %collective-permute-start.7) | collective-permute-done | bytes 163872 | tf_op jit(solution)/shard_map/ppermute | solution.py:333
  61.9 1.4 %collective-permute-done.6 = f32[5,64,128]{2,1,0:T(8,128)S(1)} collective-permute-done((f32[5,64,128]{2,1,0:T(8,128)S(1)}, f32[5,64,128]{2,1,0:T(8,128)S(1)}, u32[]{:S(2)}, u32[]{:S(2)}) %collective-permute-start.6) | collective-permute-done | bytes 163872 | tf_op jit(solution)/shard_map/ppermute | solution.py:333
  63.3 0.6 fusion.3
  63.9 0.4 collective-permute-start.8
  64.4 33.6 %collective-permute-start.9 = (f32[3,64,128]{2,1,0:T(8,128)S(1)}, f32[3,64,128]{2,1,0:T(8,128)S(1)}, u32[]{:S(2)}, u32[]{:S(2)}) collective-permute-start(f32[3,64,128]{2,1,0:T(8,128)S(1)} %pad_maximum_fusion.6), channel_id=1, source_target_pairs={{0,2},{1,3},{2,0},{3,1},{4,6},{5,7},{6,4},{7,5},{8,10},{9,11},{10,... | collective-permute-start | bytes 294920 | tf_op jit(solution)/shard_map/ppermute | solution.py:333
  98.0 0.1 collective-permute-start.10
  98.0 0.0 collective-permute-done.8
  98.0 6.8 %collective-permute-done.9 = f32[3,64,128]{2,1,0:T(8,128)S(1)} collective-permute-done((f32[3,64,128]{2,1,0:T(8,128)S(1)}, f32[3,64,128]{2,1,0:T(8,128)S(1)}, u32[]{:S(2)}, u32[]{:S(2)}) %collective-permute-start.9) | collective-permute-done | bytes 98336 | tf_op jit(solution)/shard_map/ppermute | solution.py:333
  104.9 0.0 collective-permute-done.10
  104.9 0.6 constant_dynamic-update-slice_fusion.13
  105.5 1.6 %collective-permute-start.11 = (f32[64,128]{1,0:T(8,128)S(1)}, f32[64,128]{1,0:T(8,128)S(1)}, u32[]{:S(2)}, u32[]{:S(2)}) collective-permute-start(f32[64,128]{1,0:T(8,128)S(1)} %get-tuple-element.42), channel_id=1, source_target_pairs={{0,1},{1,0},{2,3},{3,2},{4,5},{5,4},{6,7},{7,6},{8,9},{9,8},{10,11... | collective-permute-start | bytes 98312 | tf_op jit(solution)/shard_map/ppermute | solution.py:333
  107.2 2.4 %collective-permute-start.13 = (f32[64,128]{1,0:T(8,128)S(1)}, f32[64,128]{1,0:T(8,128)S(1)}, u32[]{:S(2)}, u32[]{:S(2)}) collective-permute-start(f32[64,128]{1,0:T(8,128)S(1)} %get-tuple-element.42), channel_id=1, source_target_pairs={{0,3},{1,2},{2,1},{3,0},{4,7},{5,6},{6,5},{7,4},{8,11},{9,10},{10,... | collective-permute-start | bytes 98312 | tf_op jit(solution)/shard_map/ppermute | solution.py:333
  109.5 0.0 collective-permute-start.12
  109.6 4.8 %collective-permute-done.12 = f32[64,128]{1,0:T(8,128)S(1)} collective-permute-done((f32[64,128]{1,0:T(8,128)S(1)}, f32[64,128]{1,0:T(8,128)S(1)}, u32[]{:S(2)}, u32[]{:S(2)}) %collective-permute-start.12) | collective-permute-done | bytes 32800 | tf_op jit(solution)/shard_map/ppermute | solution.py:333
  114.4 0.6 collective-permute-start.14
  115.0 1.4 %collective-permute-start.16 = (f32[5,64,128]{2,1,0:T(8,128)S(1)}, f32[5,64,128]{2,1,0:T(8,128)S(1)}, u32[]{:S(2)}, u32[]{:S(2)}) collective-permute-start(f32[5,64,128]{2,1,0:T(8,128)S(1)} %constant_dynamic-update-slice_fusion.5), channel_id=1, source_target_pairs={{0,24},{8,16},{16,8},{24,0},{1,25},{9,17},{17,9},{25,1},{2,26},{10... | collective-permute-start | bytes 491528 | tf_op jit(solution)/shard_map/ppermute | solution.py:333
  116.4 1.5 %collective-permute-start.15 = (f32[5,64,128]{2,1,0:T(8,128)S(1)}, f32[5,64,128]{2,1,0:T(8,128)S(1)}, u32[]{:S(2)}, u32[]{:S(2)}) collective-permute-start(f32[5,64,128]{2,1,0:T(8,128)S(1)} %constant_dynamic-update-slice_fusion.5), channel_id=1, source_target_pairs={{0,16},{8,24},{16,0},{24,8},{1,17},{9,25},{17,1},{25,9},{2,18},{10... | collective-permute-start | bytes 491528 | tf_op jit(solution)/shard_map/ppermute | solution.py:333
  117.9 1.8 %collective-permute-done.14 = f32[5,64,128]{2,1,0:T(8,128)S(1)} collective-permute-done((f32[5,64,128]{2,1,0:T(8,128)S(1)}, f32[5,64,128]{2,1,0:T(8,128)S(1)}, u32[]{:S(2)}, u32[]{:S(2)}) %collective-permute-start.14) | collective-permute-done | bytes 163872 | tf_op jit(solution)/shard_map/ppermute | solution.py:333
  119.8 3.4 %collective-permute-done.15 = f32[5,64,128]{2,1,0:T(8,128)S(1)} collective-permute-done((f32[5,64,128]{2,1,0:T(8,128)S(1)}, f32[5,64,128]{2,1,0:T(8,128)S(1)}, u32[]{:S(2)}, u32[]{:S(2)}) %collective-permute-start.15) | collective-permute-done | bytes 163872 | tf_op jit(solution)/shard_map/ppermute | solution.py:333
  123.3 0.1 collective-permute-start.17
  123.4 0.6 fusion.4
  124.0 1.3 collective-permute-done.17.other
  125.3 2.5 %unpack.1 = f32[64,64,64]{2,1,0:T(8,128)} custom-call(s32[1]{0:T(128)} %bitcast.5.scalars, f32[16,64,128]{2,1,0:T(8,128)S(1)} %slice_dynamic-update-slice_fusion.own, f32[16,64,128]{2,1,0:T(8,128)S(1)} %collective-permute-done.17.other), custom_call_target="tpu_custom_call" | custom-call | tf_op jit(solution)/shard_map/unpack/pallas_call | solution.py:314
  (38 shorter events, 0.4 us)
Async XLA Ops:
  1.4 21.4 %collective-permute-start.2 = (bf16[2,64,128]{2,1,0:T(8,128)(2,1)S(1)}, bf16[2,64,128]{2,1,0:T(8,128)(2,1)S(1)}, u32[]{:S(2)}, u32[]{:S(2)}) collective-permute-start(bf16[2,64,128]{2,1,0:T(8,128)(2,1)S(1)} %pad_maximum_fusion.10), channel_id=1, source_target_pairs={{0,3},{1,2},{2,1},{3,0},{4,7},{5,6},{6,5},{7,4},{8,11},{9,10},{10,... | collective-permute-start | bytes 98312 | tf_op jit(solution)/shard_map/ppermute | solution.py:333
  6.4 16.3 %collective-permute-start.1 = (bf16[2,64,128]{2,1,0:T(8,128)(2,1)S(1)}, bf16[2,64,128]{2,1,0:T(8,128)(2,1)S(1)}, u32[]{:S(2)}, u32[]{:S(2)}) collective-permute-start(bf16[2,64,128]{2,1,0:T(8,128)(2,1)S(1)} %pad_maximum_fusion.10), channel_id=1, source_target_pairs={{0,2},{1,3},{2,0},{3,1},{4,6},{5,7},{6,4},{7,5},{8,10},{9,11},{10,... | collective-permute-start | bytes 98312 | tf_op jit(solution)/shard_map/ppermute | solution.py:333
  6.4 16.3 %collective-permute-start = (bf16[2,64,128]{2,1,0:T(8,128)(2,1)S(1)}, bf16[2,64,128]{2,1,0:T(8,128)(2,1)S(1)}, u32[]{:S(2)}, u32[]{:S(2)}) collective-permute-start(bf16[2,64,128]{2,1,0:T(8,128)(2,1)S(1)} %pad_maximum_fusion.10), channel_id=1, source_target_pairs={{0,1},{1,0},{2,3},{3,2},{4,5},{5,4},{6,7},{7,6},{8,9},{9,8},{10,11... | collective-permute-start | bytes 98312 | tf_op jit(solution)/shard_map/ppermute | solution.py:333
  9.4 1.2 copy-start
  10.7 0.8 copy-start.2
  11.5 11.3 %copy-start.4 = (bf16[64,128]{1,0:T(8,128)(2,1)S(1)}, bf16[64,128]{1,0:T(8,128)(2,1)}, u32[]{:S(2)}) copy-start(bf16[64,128]{1,0:T(8,128)(2,1)} %param.12) | copy-start | bytes 49156
  11.5 14.1 %copy-start.5 = (bf16[64,128]{1,0:T(8,128)(2,1)S(1)}, bf16[64,128]{1,0:T(8,128)(2,1)}, u32[]{:S(2)}) copy-start(bf16[64,128]{1,0:T(8,128)(2,1)} %param.13) | copy-start | bytes 49156
  11.5 15.1 %copy-start.1 = (bf16[64,64,64]{2,1,0:T(8,128)(2,1)S(1)}, bf16[64,64,64]{2,1,0:T(8,128)(2,1)}, u32[]{:S(2)}) copy-start(bf16[64,64,64]{2,1,0:T(8,128)(2,1)} %core.3) | copy-start | bytes 1572868
  11.5 15.1 %copy-start.3 = (bf16[64,512]{1,0:T(8,128)(2,1)S(1)}, bf16[64,512]{1,0:T(8,128)(2,1)}, u32[]{:S(2)}) copy-start(bf16[64,512]{1,0:T(8,128)(2,1)} %factor_depth.3) | copy-start | bytes 196612
  22.8 3.7 %collective-permute-start.3 = (bf16[4,64,128]{2,1,0:T(8,128)(2,1)S(1)}, bf16[4,64,128]{2,1,0:T(8,128)(2,1)S(1)}, u32[]{:S(2)}, u32[]{:S(2)}) collective-permute-start(bf16[4,64,128]{2,1,0:T(8,128)(2,1)S(1)} %pad_maximum_fusion.8), channel_id=1, source_target_pairs={{0,4},{4,0},{1,5},{5,1},{2,6},{6,2},{3,7},{7,3},{8,12},{12,8},{9,1... | collective-permute-start | bytes 196616 | tf_op jit(solution)/shard_map/ppermute | solution.py:333
  40.9 8.6 %collective-permute-start.4 = (f32[21,64,128]{2,1,0:T(8,128)S(1)}, f32[21,64,128]{2,1,0:T(8,128)S(1)}, u32[]{:S(2)}, u32[]{:S(2)}) collective-permute-start(f32[21,64,128]{2,1,0:T(8,128)S(1)} %pad_maximum_fusion), channel_id=1, source_target_pairs={{0,4},{4,0},{1,5},{5,1},{2,6},{6,2},{3,7},{7,3},{8,12},{12,8},{9,1... | collective-permute-start | bytes 2064392 | tf_op jit(solution)/shard_map/ppermute | solution.py:333
  49.7 7.8 %collective-permute-start.5 = (f32[5,64,128]{2,1,0:T(8,128)S(1)}, f32[5,64,128]{2,1,0:T(8,128)S(1)}, u32[]{:S(2)}, u32[]{:S(2)}) collective-permute-start(f32[5,64,128]{2,1,0:T(8,128)S(1)} %get-tuple-element.50), channel_id=1, source_target_pairs={{0,8},{8,0},{16,24},{24,16},{1,9},{9,1},{17,25},{25,17},{2,10},{10... | collective-permute-start | bytes 491528 | tf_op jit(solution)/shard_map/ppermute | solution.py:333
  52.6 9.3 %collective-permute-start.7 = (f32[5,64,128]{2,1,0:T(8,128)S(1)}, f32[5,64,128]{2,1,0:T(8,128)S(1)}, u32[]{:S(2)}, u32[]{:S(2)}) collective-permute-start(f32[5,64,128]{2,1,0:T(8,128)S(1)} %get-tuple-element.51), channel_id=1, source_target_pairs={{0,24},{8,16},{16,8},{24,0},{1,25},{9,17},{17,9},{25,1},{2,26},{10... | collective-permute-start | bytes 491528 | tf_op jit(solution)/shard_map/ppermute | solution.py:333
  54.0 9.2 %collective-permute-start.6 = (f32[5,64,128]{2,1,0:T(8,128)S(1)}, f32[5,64,128]{2,1,0:T(8,128)S(1)}, u32[]{:S(2)}, u32[]{:S(2)}) collective-permute-start(f32[5,64,128]{2,1,0:T(8,128)S(1)} %get-tuple-element.52), channel_id=1, source_target_pairs={{0,16},{8,24},{16,0},{24,8},{1,17},{9,25},{17,1},{25,9},{2,18},{10... | collective-permute-start | bytes 491528 | tf_op jit(solution)/shard_map/ppermute | solution.py:333
  63.9 34.1 %collective-permute-start.8 = (f32[3,64,128]{2,1,0:T(8,128)S(1)}, f32[3,64,128]{2,1,0:T(8,128)S(1)}, u32[]{:S(2)}, u32[]{:S(2)}) collective-permute-start(f32[3,64,128]{2,1,0:T(8,128)S(1)} %pad_maximum_fusion.5), channel_id=1, source_target_pairs={{0,1},{1,0},{2,3},{3,2},{4,5},{5,4},{6,7},{7,6},{8,9},{9,8},{10,11... | collective-permute-start | bytes 294920 | tf_op jit(solution)/shard_map/ppermute | solution.py:333
  64.4 40.5 %collective-permute-start.9 = (f32[3,64,128]{2,1,0:T(8,128)S(1)}, f32[3,64,128]{2,1,0:T(8,128)S(1)}, u32[]{:S(2)}, u32[]{:S(2)}) collective-permute-start(f32[3,64,128]{2,1,0:T(8,128)S(1)} %pad_maximum_fusion.6), channel_id=1, source_target_pairs={{0,2},{1,3},{2,0},{3,1},{4,6},{5,7},{6,4},{7,5},{8,10},{9,11},{10,... | collective-permute-start | bytes 294920 | tf_op jit(solution)/shard_map/ppermute | solution.py:333
  98.0 6.9 %collective-permute-start.10 = (f32[3,64,128]{2,1,0:T(8,128)S(1)}, f32[3,64,128]{2,1,0:T(8,128)S(1)}, u32[]{:S(2)}, u32[]{:S(2)}) collective-permute-start(f32[3,64,128]{2,1,0:T(8,128)S(1)} %pad_maximum_fusion.7), channel_id=1, source_target_pairs={{0,3},{1,2},{2,1},{3,0},{4,7},{5,6},{6,5},{7,4},{8,11},{9,10},{10,... | collective-permute-start | bytes 294920 | tf_op jit(solution)/shard_map/ppermute | solution.py:333
  105.5 4.0 %collective-permute-start.11 = (f32[64,128]{1,0:T(8,128)S(1)}, f32[64,128]{1,0:T(8,128)S(1)}, u32[]{:S(2)}, u32[]{:S(2)}) collective-permute-start(f32[64,128]{1,0:T(8,128)S(1)} %get-tuple-element.42), channel_id=1, source_target_pairs={{0,1},{1,0},{2,3},{3,2},{4,5},{5,4},{6,7},{7,6},{8,9},{9,8},{10,11... | collective-permute-start | bytes 98312 | tf_op jit(solution)/shard_map/ppermute | solution.py:333
  107.2 7.2 %collective-permute-start.13 = (f32[64,128]{1,0:T(8,128)S(1)}, f32[64,128]{1,0:T(8,128)S(1)}, u32[]{:S(2)}, u32[]{:S(2)}) collective-permute-start(f32[64,128]{1,0:T(8,128)S(1)} %get-tuple-element.42), channel_id=1, source_target_pairs={{0,3},{1,2},{2,1},{3,0},{4,7},{5,6},{6,5},{7,4},{8,11},{9,10},{10,... | collective-permute-start | bytes 98312 | tf_op jit(solution)/shard_map/ppermute | solution.py:333
  109.5 4.8 %collective-permute-start.12 = (f32[64,128]{1,0:T(8,128)S(1)}, f32[64,128]{1,0:T(8,128)S(1)}, u32[]{:S(2)}, u32[]{:S(2)}) collective-permute-start(f32[64,128]{1,0:T(8,128)S(1)} %get-tuple-element.42), channel_id=1, source_target_pairs={{0,2},{1,3},{2,0},{3,1},{4,6},{5,7},{6,4},{7,5},{8,10},{9,11},{10,... | collective-permute-start | bytes 98312 | tf_op jit(solution)/shard_map/ppermute | solution.py:333
  114.4 5.4 %collective-permute-start.14 = (f32[5,64,128]{2,1,0:T(8,128)S(1)}, f32[5,64,128]{2,1,0:T(8,128)S(1)}, u32[]{:S(2)}, u32[]{:S(2)}) collective-permute-start(f32[5,64,128]{2,1,0:T(8,128)S(1)} %constant_dynamic-update-slice_fusion.5), channel_id=1, source_target_pairs={{0,8},{8,0},{16,24},{24,16},{1,9},{9,1},{17,25},{25,17},{2,10},{10... | collective-permute-start | bytes 491528 | tf_op jit(solution)/shard_map/ppermute | solution.py:333
  115.0 8.2 %collective-permute-start.16 = (f32[5,64,128]{2,1,0:T(8,128)S(1)}, f32[5,64,128]{2,1,0:T(8,128)S(1)}, u32[]{:S(2)}, u32[]{:S(2)}) collective-permute-start(f32[5,64,128]{2,1,0:T(8,128)S(1)} %constant_dynamic-update-slice_fusion.5), channel_id=1, source_target_pairs={{0,24},{8,16},{16,8},{24,0},{1,25},{9,17},{17,9},{25,1},{2,26},{10... | collective-permute-start | bytes 491528 | tf_op jit(solution)/shard_map/ppermute | solution.py:333
  116.4 6.8 %collective-permute-start.15 = (f32[5,64,128]{2,1,0:T(8,128)S(1)}, f32[5,64,128]{2,1,0:T(8,128)S(1)}, u32[]{:S(2)}, u32[]{:S(2)}) collective-permute-start(f32[5,64,128]{2,1,0:T(8,128)S(1)} %constant_dynamic-update-slice_fusion.5), channel_id=1, source_target_pairs={{0,16},{8,24},{16,0},{24,8},{1,17},{9,25},{17,1},{25,9},{2,18},{10... | collective-permute-start | bytes 491528 | tf_op jit(solution)/shard_map/ppermute | solution.py:333
  123.3 2.0 %collective-permute-start.17 = (f32[16,64,128]{2,1,0:T(8,128)S(1)}, f32[16,64,128]{2,1,0:T(8,128)S(1)}, u32[]{:S(2)}, u32[]{:S(2)}) collective-permute-start(f32[16,64,128]{2,1,0:T(8,128)S(1)} %slice_dynamic-update-slice_fusion.own), channel_id=1, source_target_pairs={{0,4},{4,0},{1,5},{5,1},{2,6},{6,2},{3,7},{7,3},{8,12},{12,8},{9,1... | collective-permute-start | bytes 1572872 | tf_op jit(solution)/shard_map/ppermute | solution.py:333

commit v2 on v1

v2 whole, which is shorter than its diff:
```python
import functools

import jax
import jax.numpy as jnp
from jax import lax
from jax.experimental import pallas as pl
from jax.experimental.pallas import tpu as pltpu
from jax.sharding import PartitionSpec as P

resid_scale = 1.0 / 64.0
f32 = jnp.float32
bf16 = jnp.bfloat16


def dot(a, b, contract=((1,), (0,))):
    return lax.dot_general(a, b, (contract, ((), ())), preferred_element_type=f32)


def cube_kernel(depth_blocks, slab, factor_depth, core, cube_out, cube_turned_out, cube_wide):
    rank = core.shape[0]
    half = slab // 2
    width = depth_blocks * slab
    start = pl.multiple_of(lax.axis_index("ka") * width, width)
    depth = factor_depth[:, pl.ds(start, width)].astype(f32).T
    order = [depth[t * slab + h * half : t * slab + (h + 1) * half] for h in range(2) for t in range(depth_blocks)]
    depth = jnp.concatenate(order, axis=0).astype(bf16)
    count = depth_blocks * half

    def one_rank(r1, carry):
        piece = dot(depth, core[r1], ((1,), (1,)))
        wide = jnp.concatenate([piece[:count], piece[count:]], axis=1)
        cube_wide[pl.ds(r1, count, stride=rank + 1), :] = wide
        return carry

    lax.fori_loop(0, rank, one_rank, 0, unroll=16)
    for t in range(depth_blocks):
        for kp in range(half):
            at = (t * half + kp) * (rank + 1)
            block = cube_wide[at : at + rank, :]
            cube_out[t, kp * rank : (kp + 1) * rank, :] = block.astype(bf16)
        cube_turned_out[t] = cube_out[t].astype(f32).T.astype(bf16)


def first_cubes(factor_depth, core, depth_blocks, slab):
    rank = core.shape[0]
    half = slab // 2
    return pl.pallas_call(
        functools.partial(cube_kernel, depth_blocks, slab),
        out_shape=(
            jax.ShapeDtypeStruct((depth_blocks, half * rank, 2 * rank), bf16),
            jax.ShapeDtypeStruct((depth_blocks, 2 * rank, half * rank), bf16),
        ),
        in_specs=[pl.BlockSpec(memory_space=pltpu.VMEM)] * 2,
        out_specs=[pl.BlockSpec(memory_space=pltpu.VMEM)] * 2,
        scratch_shapes=[pltpu.VMEM((depth_blocks * half * (rank + 1), 2 * rank), f32)],
        compiler_params=pltpu.CompilerParams(vmem_limit_bytes=24 * 2**20),
        cost_estimate=pl.CostEstimate(flops=10**9, bytes_accessed=4 * 2**20, transcendentals=0),
        name="first_cubes",
    )(factor_depth, core)


def masks_of(relative, sizes):
    ia, ja, ka = lax.axis_index("ia"), lax.axis_index("ja"), lax.axis_index("ka")
    if not relative:
        return 0, 0, 0
    return ja * sizes["ka"] + ka, ka, (ja * sizes["ia"] + ia) * sizes["ka"] + ka


def terms_kernel(
    relative,
    sizes,
    counts,
    coords,
    data,
    weight,
    cube,
    cube_turned,
    row_table,
    col_table,
    factor_depth,
    core,
    core_out,
    rows_out,
    cols_out,
    depth_out,
    wide_col,
    backward,
    by_rank,
    second_all,
    depth_all,
    depth_turned,
    depth_sum,
    spread_data,
    spread_weight,
):
    slot = pl.program_id(0)
    slots = pl.num_programs(0)
    _, rows, slab, cols = data.shape
    rank = core.shape[0]
    half = slab // 2
    pairs = rank // 2
    depth_blocks = cube.shape[0]
    count = counts[0, 0, 0]
    row_mask, col_mask, core_mask = masks_of(relative, sizes)
    row_base = lax.axis_index("ia") * row_table.shape[0]
    col_base = lax.axis_index("ja") * col_table.shape[0]
    depth_base = lax.axis_index("ka") * depth_blocks

    @pl.when(slot == 0)
    def _():
        second_all[...] = jnp.zeros_like(second_all)
        depth_all[...] = jnp.zeros_like(depth_all)
        depth_sum[...] = jnp.zeros_like(depth_sum)
        rows_out[...] = jnp.zeros_like(rows_out)
        cols_out[...] = jnp.zeros_like(cols_out)
        wide_col[...] = jnp.zeros_like(wide_col)
        width = depth_blocks * slab
        start = pl.multiple_of(lax.axis_index("ka") * width, width)
        depth_turned[...] = factor_depth[:, pl.ds(start, width)].astype(f32).T

    @pl.when(slot < count)
    def _():
        row_at = (coords[0, 0, slot, 0] - row_base) ^ row_mask
        col_at = (coords[0, 0, slot, 1] - col_base) ^ col_mask
        depth_at = coords[0, 0, slot, 2] - depth_base
        row_factor = row_table[row_at]
        row_turned = row_factor.astype(f32).T.astype(bf16)
        col_factor = col_table[col_at]
        wide_col[:rank, :cols] = col_factor
        wide_col[rank:, cols:] = col_factor
        own_depth = depth_turned[pl.ds(pl.multiple_of(depth_at * slab, slab), slab), :]
        depth_all[pl.ds(pl.multiple_of(slot * slab, slab), slab), :] = own_depth.astype(bf16)

        step = 4
        groups = half // step
        wide_factor = wide_col[...]
        for source, target in ((data, spread_data), (weight, spread_weight)):
            for i in range(rows):
                target[i * (slab + 1) : i * (slab + 1) + slab, :] = source[0, i].astype(f32)

        def second_of(g):
            lines = cube[depth_at, g * step * rank : (g + 1) * step * rank, :]
            block = dot(lines, wide_factor).astype(bf16)
            return jnp.concatenate([block[kp * rank : (kp + 1) * rank] for kp in range(step)], axis=1)

        def residual_of(g, model):
            parts = []
            for kp in range(step):
                for h in range(2):
                    lines = pl.ds(h * half + g * step + kp, rows, stride=slab + 1)
                    seen, scale = spread_data[lines, :], spread_weight[lines, :]
                    at = (kp * 2 + h) * cols
                    gap = model[:, at : at + cols] - seen
                    parts.append((scale * gap * resid_scale).astype(bf16))
            return jnp.concatenate(parts, axis=1)

        def keep_back(g, back):
            back = back.astype(bf16)
            for kp in range(step):
                pair = back[:, kp * 2 * cols : (kp + 1) * 2 * cols]
                at = (g * step + kp) * rank
                backward[at : at + rank, :] = pair
                wider = pair.astype(f32)
                for h in range(2):
                    lines = pl.ds(h * half + g * step + kp, rank, stride=slab + 1)
                    by_rank[lines, :] = wider[:, h * cols : (h + 1) * cols]

        row_sum = jnp.zeros((rank, rows), f32)
        seconds = [second_of(g) for g in range(groups)]
        models = [None] * groups
        models[0] = dot(row_turned, seconds[0])
        for g in range(groups):
            if g + 1 < groups:
                models[g + 1] = dot(row_turned, seconds[g + 1])
            residual = residual_of(g, models[g])
            keep_back(g, dot(row_factor, residual))
            row_sum = row_sum + dot(seconds[g], residual, ((1,), (1,)))
        rows_out[row_at] += row_sum
        wide = dot(cube_turned[depth_at], backward[...])
        cols_out[col_at] += wide[:rank, :cols] + wide[rank:, cols:]
        lines = pl.ds(pl.multiple_of(slot * slab, slab), slab)
        for first in range(0, pairs, 8):
            ranked = []
            for pair in range(first, first + 8):
                spots = [at * (slab + 1) for at in (pair, pairs + pair)]
                ranked.append(jnp.concatenate([by_rank[at : at + slab, :].astype(bf16) for at in spots], axis=1))
            ranked = jnp.concatenate(ranked, axis=0)
            second_back = dot(ranked, wide_col[...], ((1,), (1,))).astype(bf16)
            second_all[first : first + 8, lines, :] = second_back.reshape(8, slab, 2 * rank)

    @pl.when(slot == slots - 1)
    def _():
        def one_chunk(at, total):
            pair = at ^ core_mask
            second = second_all[pair]
            both = jnp.concatenate([core[pair], core[pairs + pair]], axis=0)
            total = total + dot(second, both)
            piece = dot(second, depth_all[...], ((0,), (0,)))
            core_out[at] = jnp.concatenate([piece[:rank], piece[rank:]], axis=1)
            return total

        total = lax.fori_loop(0, pairs, one_chunk, jnp.zeros((second_all.shape[1], rank), f32), unroll=16)
        for s in range(second_all.shape[1] // slab):

            @pl.when(s < count)
            def _():
                at = coords[0, 0, s, 2] - depth_base
                lines = pl.ds(pl.multiple_of(at * slab, slab), slab)
                depth_sum[lines, :] += total[s * slab : (s + 1) * slab]

        depth_out[...] = depth_sum[...].T


def terms(relative, sizes, counts, coords, data, weight, cube, cube_turned, row_table, col_table, factor_depth, core):
    slots, rows, slab, cols = data.shape
    rank = core.shape[0]
    half = slab // 2
    depth_blocks = cube.shape[0]

    def live(slot, counts, coords):
        return (jnp.minimum(slot, jnp.maximum(counts[0, 0, 0] - 1, 0)), 0, 0, 0)

    def whole(array):
        return pl.BlockSpec(array.shape, lambda slot, counts, coords: (0,) * len(array.shape))

    outs = (
        jax.ShapeDtypeStruct((rank // 2, rank, 2 * rank), f32),
        jax.ShapeDtypeStruct((row_table.shape[0], rank, rows), f32),
        jax.ShapeDtypeStruct((col_table.shape[0], rank, cols), f32),
        jax.ShapeDtypeStruct((rank, depth_blocks * slab), f32),
    )
    return pl.pallas_call(
        functools.partial(terms_kernel, relative, sizes),
        out_shape=outs,
        grid_spec=pltpu.PrefetchScalarGridSpec(
            num_scalar_prefetch=2,
            grid=(slots,),
            in_specs=[
                pl.BlockSpec((1, rows, slab, cols), live),
                pl.BlockSpec((1, rows, slab, cols), live),
                whole(cube),
                whole(cube_turned),
                whole(row_table),
                whole(col_table),
                whole(factor_depth),
                whole(core),
            ],
            out_specs=[whole(out) for out in outs],
            scratch_shapes=[
                pltpu.VMEM((2 * rank, 2 * cols), bf16),
                pltpu.VMEM((half * rank, 2 * cols), bf16),
                pltpu.VMEM((rank * (slab + 1), cols), f32),
                pltpu.VMEM((rank // 2, slots * slab, 2 * rank), bf16),
                pltpu.VMEM((slots * slab, rank), bf16),
                pltpu.VMEM((depth_blocks * slab, rank), f32),
                pltpu.VMEM((depth_blocks * slab, rank), f32),
                pltpu.VMEM((rows * (slab + 1), cols), f32),
                pltpu.VMEM((rows * (slab + 1), cols), f32),
            ],
        ),
        compiler_params=pltpu.CompilerParams(vmem_limit_bytes=48 * 2**20),
        cost_estimate=pl.CostEstimate(flops=10**9, bytes_accessed=16 * 2**20, transcendentals=0),
        name="terms",
    )(counts, coords, data, weight, cube, cube_turned, row_table, col_table, factor_depth, core)


def unpack_kernel(scalars, own, other, out):
    rank = out.shape[1]
    mine = pl.program_id(0)
    high = pl.program_id(1)
    count = out.shape[0]
    low = scalars[0] & (count - 1)

    for source, which in ((own, 0), (other, 1)):
        for h in range(2):

            @pl.when(jnp.logical_and(mine == which, high == h))
            def _():
                def one(at, carry):
                    out[at ^ low] = source[at][:, h * rank : (h + 1) * rank]
                    return carry

                lax.fori_loop(0, count, one, 0, unroll=4)


def unpack(mask, own, other):
    count, rank, _ = own.shape
    parts = 2

    def place(mine, high, scalars):
        return (high * parts + ((scalars[0] // count) ^ mine), 0, 0)

    def all_of(mine, high, scalars):
        return (0, 0, 0)

    return pl.pallas_call(
        unpack_kernel,
        out_shape=jax.ShapeDtypeStruct((rank, rank, rank), f32),
        grid_spec=pltpu.PrefetchScalarGridSpec(
            num_scalar_prefetch=1,
            grid=(parts, 2),
            in_specs=[pl.BlockSpec(own.shape, all_of), pl.BlockSpec(other.shape, all_of)],
            out_specs=pl.BlockSpec((count, rank, rank), place),
        ),
        compiler_params=pltpu.CompilerParams(vmem_limit_bytes=32 * 2**20),
        name="unpack",
    )(mask, own, other)


def power_of_two(n):
    return n & (n - 1) == 0


def swap(value, axis, size, mask):
    return lax.ppermute(value, axis, [(at, at ^ mask) for at in range(size)])


def on_device(sizes, observed, weights, coords, counts, factor_rows, factor_cols, factor_depth, core_tensor):
    n_ia, n_ja, n_ka = sizes["ia"], sizes["ja"], sizes["ka"]
    devices = n_ia * n_ja * n_ka
    rank = core_tensor.shape[0]
    _, _, slots, rows, slab, cols = observed.shape
    data = observed.reshape(observed.shape[2:])
    weight = weights.reshape(weights.shape[2:])
    row_chunks = factor_rows.shape[1] * n_ja * n_ka // rows
    col_chunks = factor_cols.shape[1] * n_ka // cols
    depth_blocks = factor_depth.shape[1] // n_ka // slab
    ia, ja, ka = lax.axis_index("ia"), lax.axis_index("ja"), lax.axis_index("ka")
    by_swaps = (
        n_ja == 2
        and power_of_two(n_ia)
        and power_of_two(n_ka)
        and rank // 2 == devices
        and factor_rows.shape[1] == rows
        and factor_cols.shape[1] == cols
    )

    cube, cube_turned = first_cubes(factor_depth, core_tensor, depth_blocks, slab)

    if by_swaps:
        both = jnp.stack([factor_rows, factor_cols])
        from_ka = [both] + [swap(both, "ka", n_ka, mask) for mask in range(1, n_ka)]
        own_rows = jnp.stack([piece[0] for piece in from_ka])
        row_table = jnp.concatenate([own_rows, swap(own_rows, "ja", n_ja, 1)])
        col_table = jnp.stack([piece[1] for piece in from_ka])
    else:
        row_table = lax.all_gather(factor_rows, ("ja", "ka"), axis=1, tiled=True)
        row_table = row_table.reshape(rank, row_chunks, rows).transpose(1, 0, 2)
        col_table = lax.all_gather(factor_cols, "ka", axis=1, tiled=True)
        col_table = col_table.reshape(rank, col_chunks, cols).transpose(1, 0, 2)

    core_sum, rows_sum, cols_sum, depth_sum = terms(
        by_swaps,
        sizes,
        counts,
        coords,
        data,
        weight,
        cube,
        cube_turned,
        row_table,
        col_table,
        factor_depth,
        core_tensor,
    )

    if not by_swaps:
        rows_whole = rows_sum.transpose(1, 0, 2).reshape(rank, row_chunks * rows)
        cols_whole = cols_sum.transpose(1, 0, 2).reshape(rank, col_chunks * cols)
        core_whole = core_sum.reshape(rank // 2, rank, 2, rank).transpose(2, 0, 1, 3).reshape(rank, rank, rank)
        return (
            lax.psum_scatter(rows_whole, ("ja", "ka"), scatter_dimension=1, tiled=True),
            lax.psum_scatter(lax.psum(cols_whole, "ia"), "ka", scatter_dimension=1, tiled=True),
            lax.psum(depth_sum, ("ia", "ja")),
            lax.psum(core_whole, ("ia", "ja", "ka")),
        )

    half = devices // 2
    keep = jnp.concatenate([core_sum[:half], rows_sum[:n_ka], depth_sum[None]])
    send = jnp.concatenate([core_sum[half:], rows_sum[n_ka:], depth_sum[None]])
    total = keep + swap(send, "ja", n_ja, 1)
    core_half, rows_half, depth_half = total[:half], total[half : half + n_ka], total[half + n_ka :]
    core_quarter = core_half[:n_ka]
    depth_total = depth_half[0]
    for mask in range(1, n_ia):
        piece = jnp.concatenate([core_half[mask * n_ka : (mask + 1) * n_ka], depth_half])
        got = swap(piece, "ia", n_ia, mask)
        core_quarter = core_quarter + got[:n_ka]
        depth_total = depth_total + got[n_ka]
    own = jnp.stack([core_quarter[0], rows_half[0], cols_sum[0]])
    for mask in range(1, n_ka):
        own = own + swap(jnp.stack([core_quarter[mask], rows_half[mask], cols_sum[mask]]), "ka", n_ka, mask)
    core_own, rows_total, cols_own = own[0], own[1], own[2]
    pieces = [core_own] + [swap(core_own, "ka", n_ka, mask) for mask in range(1, n_ka)]
    pack = jnp.stack(pieces + [cols_own])
    cols_total = cols_own
    gathered = [pack[:n_ka]]
    for mask in range(1, n_ia):
        got = swap(pack, "ia", n_ia, mask)
        gathered.append(got[:n_ka])
        cols_total = cols_total + got[n_ka]
    mine = jnp.concatenate(gathered)
    other = swap(mine, "ja", n_ja, 1)
    mask = (ja * n_ia + ia) * n_ka + ka
    core_total = unpack(jnp.stack([mask]).astype(jnp.int32), mine, other)
    return (rows_total, cols_total, depth_total, core_total)


def solution(mesh):
    in_specs = (
        P("ia", "ja", "ka", None, None, None),
        P("ia", "ja", "ka", None, None, None),
        P("ia", "ja", "ka", None),
        P("ia", "ja", "ka"),
        P(None, ("ia", "ja", "ka")),
        P(None, ("ja", "ka")),
        P(),
        P(),
    )
    out_specs = (P(None, ("ia", "ja", "ka")), P(None, ("ja", "ka")), P(None, "ka"), P())
    return jax.shard_map(
        functools.partial(on_device, dict(mesh.shape)),
        mesh=mesh,
        in_specs=in_specs,
        out_specs=out_specs,
        check_vma=False,
    )
```

time: 128 us -> 78.8 us (0.62)
  starting transfers between devices: 61.5 us -> 26.6 us
  Pallas kernels: 27.8 us -> 11.9 us
  waiting for transfers between devices: 30 us -> 27.9 us
  local copies, waits for them, and re-layouts: 4.64 us -> 6.51 us
  other arithmetic: 2.38 us -> 3.77 us
    ppermute x18, starting transfers between devices: 61.5 us -> 26.6 us  [swap(): return lax.ppermute(value, axis, [(at, at ^ mask) for at in range(size)])]
    pallas_call x2, Pallas kernels: 25.3 us -> 9.38 us  [the longest x1 7.48 us: terms(): pl.pallas_call(functools.partial(terms_kernel, relative, sizes), out_shap...]
    unnamed x20 -> x16, local copies, waits for them, and re-layouts: 4.23 us -> 6.27 us
    ppermute x18, waiting for transfers between devices: 30 us -> 27.9 us  [swap(): return lax.ppermute(value, axis, [(at, at ^ mask) for at in range(size)])]
  transfers between devices with their start and end apart: 18 -> 18, of which waited for: 10 -> 11; matrix products, arithmetic and copies ran while one was open for 2% -> 4% of each run, Pallas kernels for 9% -> 2%
where the time goes in v2:
time: 78.8 us; the launch traced here: 78.1 us
  waiting for transfers between devices  27.9 us (35%)
  starting transfers between devices  26.6 us (34%)
  Pallas kernels  11.9 us (15%)
  local copies, waits for them, and re-layouts  6.51 us (8%)
  other arithmetic  3.77 us (5%)
  between operations  1.5 us (2%)
    ppermute x18, waiting for transfers between devices, swap(): return lax.ppermute(value, axis, [(at, at ^ mask) for at in range(size)])  27.9 us
    ppermute x18, starting transfers between devices, swap(): return lax.ppermute(value, axis, [(at, at ^ mask) for at in range(size)])  26.6 us
    pallas_call x1, Pallas kernels, terms(): pl.pallas_call(functools.partial(terms_kernel, relative, sizes), out_shap...  7.48 us
    unnamed x16, local copies, waits for them, and re-layouts  6.27 us
    pallas_call x1, Pallas kernels, unpack(): pl.pallas_call(unpack_kernel, out_shape=jax.ShapeDtypeStruct((rank, rank,...  2.51 us
    pallas_call x1, Pallas kernels, first_cubes(): pl.pallas_call(functools.partial(cube_kernel, depth_blocks, slab), out_sh...  1.9 us
  transfers between devices with their start and end apart: 18, of which 11 were waited for; matrix products, arithmetic and copies ran while one was open for 4% of the time, Pallas kernels for 2%

profile of v2, /device:TPU:0, one launch (start us, length us, event | category | flops | bytes accessed | tf_op | source)
XLA Modules:
  0.0 78.1 jit_solution(8145409325743533652)
XLA Ops:
  0.6 0.7 pad_maximum_fusion.10
  1.4 5.0 %collective-permute-start.2 = (bf16[2,64,128]{2,1,0:T(8,128)(2,1)S(1)}, bf16[2,64,128]{2,1,0:T(8,128)(2,1)S(1)}, u32[]{:S(2)}, u32[]{:S(2)}) collective-permute-start(bf16[2,64,128]{2,1,0:T(8,128)(2,1)S(1)} %pad_maximum_fusion.10), channel_id=1, source_target_pairs={{0,3},{1,2},{2,1},{3,0},{4,7},{5,6},{6,5},{7,4},{8,11},{9,10},{10,... | collective-permute-start | bytes 98312 | tf_op jit(solution)/shard_map/ppermute | solution.py:315
  6.4 0.0 collective-permute-start.1
  6.4 0.6 collective-permute-start
  7.0 0.7 constant_dynamic-update-slice_fusion.4
  7.8 1.2 %copy-done = bf16[64,64,64]{2,1,0:T(8,128)(2,1)S(1)} copy-done((bf16[64,64,64]{2,1,0:T(8,128)(2,1)S(1)}, bf16[64,64,64]{2,1,0:T(8,128)(2,1)}, u32[]{:S(2)}) %copy-start) | copy-done | bytes 524312
  9.0 0.8 %copy-done.2 = bf16[64,512]{1,0:T(8,128)(2,1)S(1)} copy-done((bf16[64,512]{1,0:T(8,128)(2,1)S(1)}, bf16[64,512]{1,0:T(8,128)(2,1)}, u32[]{:S(2)}) %copy-start.2) | copy-done | bytes 65560
  9.8 1.9 %first_cubes.1 = (bf16[4,1024,128]{2,1,0:T(8,128)(2,1)S(1)}, bf16[4,128,1024]{2,1,0:T(8,128)(2,1)S(1)}) custom-call(bf16[64,512]{1,0:T(8,128)(2,1)S(1)} %copy-done.2, bf16[64,64,64]{2,1,0:T(8,128)(2,1)S(1)} %copy-done), custom_call_target="tpu_custom_call" | custom-call | flops 1000000000 | bytes 4194304 | tf_op jit(solution)/shard_map/first_cubes/pallas_call | solution.py:47
  12.4 0.8 copy.12.coords
  13.2 0.7 pad_maximum_fusion.8
  14.0 0.1 collective-permute-start.3
  14.0 0.7 pad_maximum_fusion.9.col_table
  14.8 0.5 collective-permute-done.3
  15.3 0.0 copy-start.1
  15.3 1.2 %copy-done.1 = bf16[64,64,64]{2,1,0:T(8,128)(2,1)S(1)} copy-done((bf16[64,64,64]{2,1,0:T(8,128)(2,1)S(1)}, bf16[64,64,64]{2,1,0:T(8,128)(2,1)}, u32[]{:S(2)}) %copy-start.1) | copy-done | bytes 524312
  16.5 0.8 %copy-done.3 = bf16[64,512]{1,0:T(8,128)(2,1)S(1)} copy-done((bf16[64,512]{1,0:T(8,128)(2,1)S(1)}, bf16[64,512]{1,0:T(8,128)(2,1)}, u32[]{:S(2)}) %copy-start.3) | copy-done | bytes 65560
  17.4 7.5 %terms.1 = (f32[32,64,128]{2,1,0:T(8,128)S(1)}, f32[8,64,128]{2,1,0:T(8,128)S(1)}, f32[4,64,128]{2,1,0:T(8,128)S(1)}, f32[64,128]{1,0:T(8,128)S(1)}) custom-call(s32[1,1,1]{2,1,0:T(1,128)S(6)} %copy.27.counts, s32[1,1,5,3]{3,2,1,0:T(8,128)S(1)} %copy.12.coords, bf16[5,128,32,128]{3,2,1,0:T(8,128)(2,1)} %bitcast.26, bf16[5,128,32,128]{3,2,1,0:T(8,128)(2,1)} %bitcast.27, ...), custom_call_target="tpu_custom_call" | custom-call | flops 1000000000 | bytes 16777216 | tf_op jit(solution)/shard_map/terms/pallas_call | solution.py:232
  24.9 0.1 fusion.5
  25.0 0.1 pad_maximum_fusion
  25.1 0.2 collective-permute-start.4
  25.3 2.0 %collective-permute-done.4 = f32[21,64,128]{2,1,0:T(8,128)S(1)} collective-permute-done((f32[21,64,128]{2,1,0:T(8,128)S(1)}, f32[21,64,128]{2,1,0:T(8,128)S(1)}, u32[]{:S(2)}, u32[]{:S(2)}) %collective-permute-start.4) | collective-permute-done | bytes 688160 | tf_op jit(solution)/shard_map/ppermute | solution.py:315
  27.3 0.1 fusion
  27.5 1.0 %collective-permute-start.7 = (f32[5,64,128]{2,1,0:T(8,128)S(1)}, f32[5,64,128]{2,1,0:T(8,128)S(1)}, u32[]{:S(2)}, u32[]{:S(2)}) collective-permute-start(f32[5,64,128]{2,1,0:T(8,128)S(1)} %get-tuple-element.47), channel_id=1, source_target_pairs={{0,24},{8,16},{16,8},{24,0},{1,25},{9,17},{17,9},{25,1},{2,26},{10... | collective-permute-start | bytes 491528 | tf_op jit(solution)/shard_map/ppermute | solution.py:315
  28.5 7.0 %collective-permute-start.6 = (f32[5,64,128]{2,1,0:T(8,128)S(1)}, f32[5,64,128]{2,1,0:T(8,128)S(1)}, u32[]{:S(2)}, u32[]{:S(2)}) collective-permute-start(f32[5,64,128]{2,1,0:T(8,128)S(1)} %get-tuple-element.48), channel_id=1, source_target_pairs={{0,16},{8,24},{16,0},{24,8},{1,17},{9,25},{17,1},{25,9},{2,18},{10... | collective-permute-start | bytes 491528 | tf_op jit(solution)/shard_map/ppermute | solution.py:315
  35.5 5.7 %collective-permute-done.6 = f32[5,64,128]{2,1,0:T(8,128)S(1)} collective-permute-done((f32[5,64,128]{2,1,0:T(8,128)S(1)}, f32[5,64,128]{2,1,0:T(8,128)S(1)}, u32[]{:S(2)}, u32[]{:S(2)}) %collective-permute-start.6) | collective-permute-done | bytes 163872 | tf_op jit(solution)/shard_map/ppermute | solution.py:315
  41.3 1.0 %collective-permute-done.5 = f32[5,64,128]{2,1,0:T(8,128)S(1)} collective-permute-done((f32[5,64,128]{2,1,0:T(8,128)S(1)}, f32[5,64,128]{2,1,0:T(8,128)S(1)}, u32[]{:S(2)}, u32[]{:S(2)}) %collective-permute-start.5) | collective-permute-done | bytes 163872 | tf_op jit(solution)/shard_map/ppermute | solution.py:315
  42.3 0.6 fusion.3
  43.0 0.1 collective-permute-start.10
  43.1 2.2 %collective-permute-start.9 = (f32[3,64,128]{2,1,0:T(8,128)S(1)}, f32[3,64,128]{2,1,0:T(8,128)S(1)}, u32[]{:S(2)}, u32[]{:S(2)}) collective-permute-start(f32[3,64,128]{2,1,0:T(8,128)S(1)} %pad_maximum_fusion.6), channel_id=1, source_target_pairs={{0,2},{1,3},{2,0},{3,1},{4,6},{5,7},{6,4},{7,5},{8,10},{9,11},{10,... | collective-permute-start | bytes 294920 | tf_op jit(solution)/shard_map/ppermute | solution.py:315
  45.3 2.3 %collective-permute-start.8 = (f32[3,64,128]{2,1,0:T(8,128)S(1)}, f32[3,64,128]{2,1,0:T(8,128)S(1)}, u32[]{:S(2)}, u32[]{:S(2)}) collective-permute-start(f32[3,64,128]{2,1,0:T(8,128)S(1)} %pad_maximum_fusion.5), channel_id=1, source_target_pairs={{0,1},{1,0},{2,3},{3,2},{4,5},{5,4},{6,7},{7,6},{8,9},{9,8},{10,11... | collective-permute-start | bytes 294920 | tf_op jit(solution)/shard_map/ppermute | solution.py:315
  47.6 3.0 %collective-permute-done.10 = f32[3,64,128]{2,1,0:T(8,128)S(1)} collective-permute-done((f32[3,64,128]{2,1,0:T(8,128)S(1)}, f32[3,64,128]{2,1,0:T(8,128)S(1)}, u32[]{:S(2)}, u32[]{:S(2)}) %collective-permute-start.10) | collective-permute-done | bytes 98336 | tf_op jit(solution)/shard_map/ppermute | solution.py:315
  50.5 3.4 %collective-permute-done.9 = f32[3,64,128]{2,1,0:T(8,128)S(1)} collective-permute-done((f32[3,64,128]{2,1,0:T(8,128)S(1)}, f32[3,64,128]{2,1,0:T(8,128)S(1)}, u32[]{:S(2)}, u32[]{:S(2)}) %collective-permute-start.9) | collective-permute-done | bytes 98336 | tf_op jit(solution)/shard_map/ppermute | solution.py:315
  54.0 0.0 collective-permute-done.8
  54.0 0.6 constant_dynamic-update-slice_fusion.13
  54.6 2.5 %collective-permute-start.12 = (f32[64,128]{1,0:T(8,128)S(1)}, f32[64,128]{1,0:T(8,128)S(1)}, u32[]{:S(2)}, u32[]{:S(2)}) collective-permute-start(f32[64,128]{1,0:T(8,128)S(1)} %get-tuple-element.38), channel_id=1, source_target_pairs={{0,2},{1,3},{2,0},{3,1},{4,6},{5,7},{6,4},{7,5},{8,10},{9,11},{10,... | collective-permute-start | bytes 98312 | tf_op jit(solution)/shard_map/ppermute | solution.py:315
  57.2 1.8 %collective-permute-start.13 = (f32[64,128]{1,0:T(8,128)S(1)}, f32[64,128]{1,0:T(8,128)S(1)}, u32[]{:S(2)}, u32[]{:S(2)}) collective-permute-start(f32[64,128]{1,0:T(8,128)S(1)} %get-tuple-element.38), channel_id=1, source_target_pairs={{0,3},{1,2},{2,1},{3,0},{4,7},{5,6},{6,5},{7,4},{8,11},{9,10},{10,... | collective-permute-start | bytes 98312 | tf_op jit(solution)/shard_map/ppermute | solution.py:315
  59.0 0.6 collective-permute-done.12
  59.7 3.2 %collective-permute-done.13 = f32[64,128]{1,0:T(8,128)S(1)} collective-permute-done((f32[64,128]{1,0:T(8,128)S(1)}, f32[64,128]{1,0:T(8,128)S(1)}, u32[]{:S(2)}, u32[]{:S(2)}) %collective-permute-start.13) | collective-permute-done | bytes 32800 | tf_op jit(solution)/shard_map/ppermute | solution.py:315
  62.9 1.6 %collective-permute-start.14 = (f32[5,64,128]{2,1,0:T(8,128)S(1)}, f32[5,64,128]{2,1,0:T(8,128)S(1)}, u32[]{:S(2)}, u32[]{:S(2)}) collective-permute-start(f32[5,64,128]{2,1,0:T(8,128)S(1)} %constant_dynamic-update-slice_fusion.5), channel_id=1, source_target_pairs={{0,8},{8,0},{16,24},{24,16},{1,9},{9,1},{17,25},{25,17},{2,10},{10... | collective-permute-start | bytes 491528 | tf_op jit(solution)/shard_map/ppermute | solution.py:315
  64.5 1.6 %collective-permute-start.16 = (f32[5,64,128]{2,1,0:T(8,128)S(1)}, f32[5,64,128]{2,1,0:T(8,128)S(1)}, u32[]{:S(2)}, u32[]{:S(2)}) collective-permute-start(f32[5,64,128]{2,1,0:T(8,128)S(1)} %constant_dynamic-update-slice_fusion.5), channel_id=1, source_target_pairs={{0,24},{8,16},{16,8},{24,0},{1,25},{9,17},{17,9},{25,1},{2,26},{10... | collective-permute-start | bytes 491528 | tf_op jit(solution)/shard_map/ppermute | solution.py:315
  66.1 0.4 collective-permute-start.15
  66.5 3.0 %collective-permute-done.14 = f32[5,64,128]{2,1,0:T(8,128)S(1)} collective-permute-done((f32[5,64,128]{2,1,0:T(8,128)S(1)}, f32[5,64,128]{2,1,0:T(8,128)S(1)}, u32[]{:S(2)}, u32[]{:S(2)}) %collective-permute-start.14) | collective-permute-done | bytes 163872 | tf_op jit(solution)/shard_map/ppermute | solution.py:315
  69.5 4.1 %collective-permute-done.15 = f32[5,64,128]{2,1,0:T(8,128)S(1)} collective-permute-done((f32[5,64,128]{2,1,0:T(8,128)S(1)}, f32[5,64,128]{2,1,0:T(8,128)S(1)}, u32[]{:S(2)}, u32[]{:S(2)}) %collective-permute-start.15) | collective-permute-done | bytes 163872 | tf_op jit(solution)/shard_map/ppermute | solution.py:315
  73.6 0.0 collective-permute-done.16
  73.7 0.1 collective-permute-start.17
  73.8 0.6 fusion.4
  74.4 1.3 %collective-permute-done.17.other = f32[16,64,128]{2,1,0:T(8,128)S(1)} collective-permute-done((f32[16,64,128]{2,1,0:T(8,128)S(1)}, f32[16,64,128]{2,1,0:T(8,128)S(1)}, u32[]{:S(2)}, u32[]{:S(2)}) %collective-permute-start.17) | collective-permute-done | bytes 524320 | tf_op jit(solution)/shard_map/ppermute | solution.py:315
  75.6 2.5 %unpack.1 = f32[64,64,64]{2,1,0:T(8,128)} custom-call(s32[1]{0:T(128)} %bitcast.12.scalars, f32[16,64,128]{2,1,0:T(8,128)S(1)} %slice_dynamic-update-slice_fusion.own, f32[16,64,128]{2,1,0:T(8,128)S(1)} %collective-permute-done.17.other), custom_call_target="tpu_custom_call" | custom-call | tf_op jit(solution)/shard_map/unpack/pallas_call | solution.py:296
  (31 shorter events, 0.3 us)
Async XLA Ops:
  1.4 11.8 %collective-permute-start.2 = (bf16[2,64,128]{2,1,0:T(8,128)(2,1)S(1)}, bf16[2,64,128]{2,1,0:T(8,128)(2,1)S(1)}, u32[]{:S(2)}, u32[]{:S(2)}) collective-permute-start(bf16[2,64,128]{2,1,0:T(8,128)(2,1)S(1)} %pad_maximum_fusion.10), channel_id=1, source_target_pairs={{0,3},{1,2},{2,1},{3,0},{4,7},{5,6},{6,5},{7,4},{8,11},{9,10},{10,... | collective-permute-start | bytes 98312 | tf_op jit(solution)/shard_map/ppermute | solution.py:315
  6.4 6.8 %collective-permute-start.1 = (bf16[2,64,128]{2,1,0:T(8,128)(2,1)S(1)}, bf16[2,64,128]{2,1,0:T(8,128)(2,1)S(1)}, u32[]{:S(2)}, u32[]{:S(2)}) collective-permute-start(bf16[2,64,128]{2,1,0:T(8,128)(2,1)S(1)} %pad_maximum_fusion.10), channel_id=1, source_target_pairs={{0,2},{1,3},{2,0},{3,1},{4,6},{5,7},{6,4},{7,5},{8,10},{9,11},{10,... | collective-permute-start | bytes 98312 | tf_op jit(solution)/shard_map/ppermute | solution.py:315
  6.4 6.7 %collective-permute-start = (bf16[2,64,128]{2,1,0:T(8,128)(2,1)S(1)}, bf16[2,64,128]{2,1,0:T(8,128)(2,1)S(1)}, u32[]{:S(2)}, u32[]{:S(2)}) collective-permute-start(bf16[2,64,128]{2,1,0:T(8,128)(2,1)S(1)} %pad_maximum_fusion.10), channel_id=1, source_target_pairs={{0,1},{1,0},{2,3},{3,2},{4,5},{5,4},{6,7},{7,6},{8,9},{9,8},{10,11... | collective-permute-start | bytes 98312 | tf_op jit(solution)/shard_map/ppermute | solution.py:315
  7.8 1.2 %copy-start = (bf16[64,64,64]{2,1,0:T(8,128)(2,1)S(1)}, bf16[64,64,64]{2,1,0:T(8,128)(2,1)}, u32[]{:S(2)}) copy-start(bf16[64,64,64]{2,1,0:T(8,128)(2,1)} %core.3) | copy-start | bytes 1572868
  9.0 0.8 %copy-start.2 = (bf16[64,512]{1,0:T(8,128)(2,1)S(1)}, bf16[64,512]{1,0:T(8,128)(2,1)}, u32[]{:S(2)}) copy-start(bf16[64,512]{1,0:T(8,128)(2,1)} %factor_depth.3) | copy-start | bytes 196612
  14.0 1.3 %collective-permute-start.3 = (bf16[4,64,128]{2,1,0:T(8,128)(2,1)S(1)}, bf16[4,64,128]{2,1,0:T(8,128)(2,1)S(1)}, u32[]{:S(2)}, u32[]{:S(2)}) collective-permute-start(bf16[4,64,128]{2,1,0:T(8,128)(2,1)S(1)} %pad_maximum_fusion.8), channel_id=1, source_target_pairs={{0,4},{4,0},{1,5},{5,1},{2,6},{6,2},{3,7},{7,3},{8,12},{12,8},{9,1... | collective-permute-start | bytes 196616 | tf_op jit(solution)/shard_map/ppermute | solution.py:315
  15.3 1.2 %copy-start.1 = (bf16[64,64,64]{2,1,0:T(8,128)(2,1)S(1)}, bf16[64,64,64]{2,1,0:T(8,128)(2,1)}, u32[]{:S(2)}) copy-start(bf16[64,64,64]{2,1,0:T(8,128)(2,1)} %core.3) | copy-start | bytes 1572868
  16.5 0.8 %copy-start.3 = (bf16[64,512]{1,0:T(8,128)(2,1)S(1)}, bf16[64,512]{1,0:T(8,128)(2,1)}, u32[]{:S(2)}) copy-start(bf16[64,512]{1,0:T(8,128)(2,1)} %factor_depth.3) | copy-start | bytes 196612
  25.1 2.2 %collective-permute-start.4 = (f32[21,64,128]{2,1,0:T(8,128)S(1)}, f32[21,64,128]{2,1,0:T(8,128)S(1)}, u32[]{:S(2)}, u32[]{:S(2)}) collective-permute-start(f32[21,64,128]{2,1,0:T(8,128)S(1)} %pad_maximum_fusion), channel_id=1, source_target_pairs={{0,4},{4,0},{1,5},{5,1},{2,6},{6,2},{3,7},{7,3},{8,12},{12,8},{9,1... | collective-permute-start | bytes 2064392 | tf_op jit(solution)/shard_map/ppermute | solution.py:315
  27.5 8.0 %collective-permute-start.7 = (f32[5,64,128]{2,1,0:T(8,128)S(1)}, f32[5,64,128]{2,1,0:T(8,128)S(1)}, u32[]{:S(2)}, u32[]{:S(2)}) collective-permute-start(f32[5,64,128]{2,1,0:T(8,128)S(1)} %get-tuple-element.47), channel_id=1, source_target_pairs={{0,24},{8,16},{16,8},{24,0},{1,25},{9,17},{17,9},{25,1},{2,26},{10... | collective-permute-start | bytes 491528 | tf_op jit(solution)/shard_map/ppermute | solution.py:315
  28.5 12.8 %collective-permute-start.6 = (f32[5,64,128]{2,1,0:T(8,128)S(1)}, f32[5,64,128]{2,1,0:T(8,128)S(1)}, u32[]{:S(2)}, u32[]{:S(2)}) collective-permute-start(f32[5,64,128]{2,1,0:T(8,128)S(1)} %get-tuple-element.48), channel_id=1, source_target_pairs={{0,16},{8,24},{16,0},{24,8},{1,17},{9,25},{17,1},{25,9},{2,18},{10... | collective-permute-start | bytes 491528 | tf_op jit(solution)/shard_map/ppermute | solution.py:315
  35.5 6.8 %collective-permute-start.5 = (f32[5,64,128]{2,1,0:T(8,128)S(1)}, f32[5,64,128]{2,1,0:T(8,128)S(1)}, u32[]{:S(2)}, u32[]{:S(2)}) collective-permute-start(f32[5,64,128]{2,1,0:T(8,128)S(1)} %get-tuple-element.46), channel_id=1, source_target_pairs={{0,8},{8,0},{16,24},{24,16},{1,9},{9,1},{17,25},{25,17},{2,10},{10... | collective-permute-start | bytes 491528 | tf_op jit(solution)/shard_map/ppermute | solution.py:315
  43.0 7.5 %collective-permute-start.10 = (f32[3,64,128]{2,1,0:T(8,128)S(1)}, f32[3,64,128]{2,1,0:T(8,128)S(1)}, u32[]{:S(2)}, u32[]{:S(2)}) collective-permute-start(f32[3,64,128]{2,1,0:T(8,128)S(1)} %pad_maximum_fusion.7), channel_id=1, source_target_pairs={{0,3},{1,2},{2,1},{3,0},{4,7},{5,6},{6,5},{7,4},{8,11},{9,10},{10,... | collective-permute-start | bytes 294920 | tf_op jit(solution)/shard_map/ppermute | solution.py:315
  43.1 10.9 %collective-permute-start.9 = (f32[3,64,128]{2,1,0:T(8,128)S(1)}, f32[3,64,128]{2,1,0:T(8,128)S(1)}, u32[]{:S(2)}, u32[]{:S(2)}) collective-permute-start(f32[3,64,128]{2,1,0:T(8,128)S(1)} %pad_maximum_fusion.6), channel_id=1, source_target_pairs={{0,2},{1,3},{2,0},{3,1},{4,6},{5,7},{6,4},{7,5},{8,10},{9,11},{10,... | collective-permute-start | bytes 294920 | tf_op jit(solution)/shard_map/ppermute | solution.py:315
  45.3 8.7 %collective-permute-start.8 = (f32[3,64,128]{2,1,0:T(8,128)S(1)}, f32[3,64,128]{2,1,0:T(8,128)S(1)}, u32[]{:S(2)}, u32[]{:S(2)}) collective-permute-start(f32[3,64,128]{2,1,0:T(8,128)S(1)} %pad_maximum_fusion.5), channel_id=1, source_target_pairs={{0,1},{1,0},{2,3},{3,2},{4,5},{5,4},{6,7},{7,6},{8,9},{9,8},{10,11... | collective-permute-start | bytes 294920 | tf_op jit(solution)/shard_map/ppermute | solution.py:315
  54.6 4.4 %collective-permute-start.11 = (f32[64,128]{1,0:T(8,128)S(1)}, f32[64,128]{1,0:T(8,128)S(1)}, u32[]{:S(2)}, u32[]{:S(2)}) collective-permute-start(f32[64,128]{1,0:T(8,128)S(1)} %get-tuple-element.38), channel_id=1, source_target_pairs={{0,1},{1,0},{2,3},{3,2},{4,5},{5,4},{6,7},{7,6},{8,9},{9,8},{10,11... | collective-permute-start | bytes 98312 | tf_op jit(solution)/shard_map/ppermute | solution.py:315
  54.6 5.0 %collective-permute-start.12 = (f32[64,128]{1,0:T(8,128)S(1)}, f32[64,128]{1,0:T(8,128)S(1)}, u32[]{:S(2)}, u32[]{:S(2)}) collective-permute-start(f32[64,128]{1,0:T(8,128)S(1)} %get-tuple-element.38), channel_id=1, source_target_pairs={{0,2},{1,3},{2,0},{3,1},{4,6},{5,7},{6,4},{7,5},{8,10},{9,11},{10,... | collective-permute-start | bytes 98312 | tf_op jit(solution)/shard_map/ppermute | solution.py:315
  57.2 5.7 %collective-permute-start.13 = (f32[64,128]{1,0:T(8,128)S(1)}, f32[64,128]{1,0:T(8,128)S(1)}, u32[]{:S(2)}, u32[]{:S(2)}) collective-permute-start(f32[64,128]{1,0:T(8,128)S(1)} %get-tuple-element.38), channel_id=1, source_target_pairs={{0,3},{1,2},{2,1},{3,0},{4,7},{5,6},{6,5},{7,4},{8,11},{9,10},{10,... | collective-permute-start | bytes 98312 | tf_op jit(solution)/shard_map/ppermute | solution.py:315
  62.9 6.6 %collective-permute-start.14 = (f32[5,64,128]{2,1,0:T(8,128)S(1)}, f32[5,64,128]{2,1,0:T(8,128)S(1)}, u32[]{:S(2)}, u32[]{:S(2)}) collective-permute-start(f32[5,64,128]{2,1,0:T(8,128)S(1)} %constant_dynamic-update-slice_fusion.5), channel_id=1, source_target_pairs={{0,8},{8,0},{16,24},{24,16},{1,9},{9,1},{17,25},{25,17},{2,10},{10... | collective-permute-start | bytes 491528 | tf_op jit(solution)/shard_map/ppermute | solution.py:315
  64.5 9.1 %collective-permute-start.16 = (f32[5,64,128]{2,1,0:T(8,128)S(1)}, f32[5,64,128]{2,1,0:T(8,128)S(1)}, u32[]{:S(2)}, u32[]{:S(2)}) collective-permute-start(f32[5,64,128]{2,1,0:T(8,128)S(1)} %constant_dynamic-update-slice_fusion.5), channel_id=1, source_target_pairs={{0,24},{8,16},{16,8},{24,0},{1,25},{9,17},{17,9},{25,1},{2,26},{10... | collective-permute-start | bytes 491528 | tf_op jit(solution)/shard_map/ppermute | solution.py:315
  66.1 7.5 %collective-permute-start.15 = (f32[5,64,128]{2,1,0:T(8,128)S(1)}, f32[5,64,128]{2,1,0:T(8,128)S(1)}, u32[]{:S(2)}, u32[]{:S(2)}) collective-permute-start(f32[5,64,128]{2,1,0:T(8,128)S(1)} %constant_dynamic-update-slice_fusion.5), channel_id=1, source_target_pairs={{0,16},{8,24},{16,0},{24,8},{1,17},{9,25},{17,1},{25,9},{2,18},{10... | collective-permute-start | bytes 491528 | tf_op jit(solution)/shard_map/ppermute | solution.py:315
  73.7 2.0 %collective-permute-start.17 = (f32[16,64,128]{2,1,0:T(8,128)S(1)}, f32[16,64,128]{2,1,0:T(8,128)S(1)}, u32[]{:S(2)}, u32[]{:S(2)}) collective-permute-start(f32[16,64,128]{2,1,0:T(8,128)S(1)} %slice_dynamic-update-slice_fusion.own), channel_id=1, source_target_pairs={{0,4},{4,0},{1,5},{5,1},{2,6},{6,2},{3,7},{7,3},{8,12},{12,8},{9,1... | collective-permute-start | bytes 1572872 | tf_op jit(solution)/shard_map/ppermute | solution.py:315

commit v3 on v2

--- a/solution.py
+++ b/solution.py
@@ -10,6 +10,7 @@
 resid_scale = 1.0 / 64.0
 f32 = jnp.float32
 bf16 = jnp.bfloat16
+wire = jnp.float16
 
 
 def dot(a, b, contract=((1,), (0,))):
@@ -264,47 +265,179 @@
     )(counts, coords, data, weight, cube, cube_turned, row_table, col_table, factor_depth, core)
 
 
-def unpack_kernel(scalars, own, other, out):
-    rank = out.shape[1]
-    mine = pl.program_id(0)
-    high = pl.program_id(1)
-    count = out.shape[0]
-    low = scalars[0] & (count - 1)
-
-    for source, which in ((own, 0), (other, 1)):
+mark_rows = 16
+top_exponent = 14.0
+
+
+def vmem_call(kernel, out_shape, *operands, name):
+    return pl.pallas_call(
+        kernel,
+        out_shape=out_shape,
+        in_specs=[pl.BlockSpec(memory_space=pltpu.VMEM)] * len(operands),
+        out_specs=jax.tree.map(lambda _: pl.BlockSpec(memory_space=pltpu.VMEM), out_shape),
+        compiler_params=pltpu.CompilerParams(vmem_limit_bytes=24 * 2**20),
+        name=name,
+    )(*operands)
+
+
+def power_of(exponent):
+    whole = jnp.abs(exponent).astype(jnp.int32)
+    value = jnp.ones_like(exponent)
+    for bit in range(7):
+        factor = jnp.where(exponent < 0, f32(2.0 ** -(2**bit)), f32(2.0 ** (2**bit)))
+        value = value * jnp.where((whole >> bit) & 1 == 1, factor, f32(1.0))
+    return value
+
+
+def exponent_of(value):
+    lanes = value.shape[-1]
+    largest = jnp.max(jnp.max(jnp.abs(value.reshape(-1, 8, lanes)), axis=0), axis=0, keepdims=True)
+    largest = jnp.max(largest, axis=1, keepdims=True)
+    largest = jnp.broadcast_to(jnp.maximum(largest, f32(1e-30)), (8, lanes))
+    return jnp.ceil(jnp.log(largest) * f32(1.4426950408889634)) - f32(top_exponent)
+
+
+def rounded(value):
+    stretched = value * f32(8193.0)
+    return stretched - (stretched - value)
+
+
+def scaled(value):
+    exponent = exponent_of(value)
+    return rounded(value * power_of(-exponent)[:1]), exponent
+
+
+def fill_message(out, *parts):
+    at = 0
+    marks = []
+    for part in parts:
+        lanes = part.shape[-1]
+        flat, exponent = scaled(part.reshape(-1, lanes))
+        out[at : at + flat.shape[0], :] = flat
+        at += flat.shape[0]
+        marks.append(jnp.concatenate([exponent] * (mark_rows // 8), axis=0))
+    for mark in marks:
+        out[at : at + mark_rows, :] = mark
+        at += mark_rows
+
+
+def message_part(message, start, rows, part, parts):
+    mark = message.shape[0] - (parts - part) * mark_rows
+    return message[start : start + rows, :] * power_of(message[mark : mark + 8, :])[:1]
+
+
+def tree_sum(values):
+    values = list(values)
+    while len(values) > 1:
+        values = [values[at] + values[at + 1] for at in range(0, len(values), 2)]
+    return values[0]
+
+
+def after_cores_kernel(n_ia, n_ka, keep, got, cols_sum, own_core, own_depth, *outs):
+    messages, columns = outs[: n_ia - 1], outs[n_ia - 1 :]
+    half = n_ia * n_ka
+    depth = keep[half + n_ka] + got[half + n_ka]
+    flat, exponent = scaled(depth)
+    own_depth[...] = flat * power_of(exponent)[:1]
+    own_core[...] = keep[:n_ka] + got[:n_ka]
+    for mask in range(1, n_ia):
+        lines = slice(mask * n_ka, (mask + 1) * n_ka)
+        fill_message(messages[mask - 1], keep[lines] + got[lines], depth)
+    for mask in range(n_ka):
+        columns[mask][0] = keep[half + mask] + got[half + mask]
+        columns[mask][1] = cols_sum[mask]
+
+
+def after_cores(n_ia, n_ka, keep, got, cols_sum):
+    _, rank, lanes = keep.shape
+    message = jax.ShapeDtypeStruct(((n_ka + 1) * rank + 2 * mark_rows, lanes), f32)
+    outs = [jax.ShapeDtypeStruct((n_ka, rank, lanes), f32), jax.ShapeDtypeStruct((rank, lanes), f32)]
+    outs += [message] * (n_ia - 1) + [jax.ShapeDtypeStruct((2, rank, lanes), f32)] * n_ka
+    outs = vmem_call(
+        functools.partial(after_cores_kernel, n_ia, n_ka), tuple(outs), keep, got, cols_sum, name="after_cores"
+    )
+    return outs[0], outs[1], outs[2 : 1 + n_ia], outs[1 + n_ia :]
+
+
+def after_rows_kernel(own_core, own_depth, *refs):
+    *messages, out, depth_out = refs
+    count, rank, lanes = own_core.shape
+    core = own_core[...].reshape(count * rank, lanes)
+    depths = [own_depth[...]]
+    for message in messages:
+        core = core + message_part(message, 0, count * rank, 0, 2)
+        depths.append(message_part(message, count * rank, rank, 1, 2))
+    depth_out[...] = tree_sum(depths)
+    fill_message(out, core)
+
+
+def after_rows(own_core, own_depth, messages):
+    count, rank, lanes = own_core.shape
+    outs = (
+        jax.ShapeDtypeStruct((count * rank + mark_rows, lanes), f32),
+        jax.ShapeDtypeStruct((rank, lanes), f32),
+    )
+    return vmem_call(after_rows_kernel, outs, own_core, own_depth, *messages, name="after_rows")
+
+
+def after_depths_kernel(n_ka, *refs):
+    messages, columns, out, rows_out = refs[:n_ka], refs[n_ka : 2 * n_ka], refs[-2], refs[-1]
+    _, rank, lanes = columns[0].shape
+    cores = []
+    for mask, message in enumerate(messages):
+        part = message_part(message, 0, n_ka * rank, 0, 1)
+        cores.append(jnp.concatenate([part[(at ^ mask) * rank : ((at ^ mask) + 1) * rank] for at in range(n_ka)]))
+    core = tree_sum(cores)
+    rows_out[...] = tree_sum(column[0] for column in columns)
+    fill_message(out, core, tree_sum(column[1] for column in columns))
+
+
+def after_depths(messages, columns):
+    n_ka = len(messages)
+    _, rank, lanes = columns[0].shape
+    outs = (
+        jax.ShapeDtypeStruct(((n_ka + 1) * rank + 2 * mark_rows, lanes), f32),
+        jax.ShapeDtypeStruct((rank, lanes), f32),
+    )
+    return vmem_call(
+        functools.partial(after_depths_kernel, n_ka), outs, *messages, *columns, name="after_depths"
+    )
+
+
+def unpack_kernel(sizes, rank, *refs):
+    n_ia, n_ka = sizes["ia"], sizes["ka"]
+    messages = refs[: 2 * n_ia]
+    core_out, cols_out, whole, sems = refs[2 * n_ia :]
+    pairs = rank // 2
+    own = masks_of(True, sizes)[2]
+    copies = []
+    for at in range(2 * n_ia):
+        first = pl.multiple_of(((own // n_ka) ^ at) * n_ka, n_ka)
+        for mask in range(n_ka):
+            piece = message_part(messages[at], mask * rank, rank, 0, 2)
+            pair = first + (lax.rem(own, n_ka) ^ mask)
+            whole[pair] = piece[:, :rank]
+            whole[pairs + pair] = piece[:, rank:]
         for h in range(2):
-
-            @pl.when(jnp.logical_and(mine == which, high == h))
-            def _():
-                def one(at, carry):
-                    out[at ^ low] = source[at][:, h * rank : (h + 1) * rank]
-                    return carry
-
-                lax.fori_loop(0, count, one, 0, unroll=4)
-
-
-def unpack(mask, own, other):
-    count, rank, _ = own.shape
-    parts = 2
-
-    def place(mine, high, scalars):
-        return (high * parts + ((scalars[0] // count) ^ mine), 0, 0)
-
-    def all_of(mine, high, scalars):
-        return (0, 0, 0)
-
+            lines = pl.ds(h * pairs + first, n_ka)
+            copies.append(pltpu.make_async_copy(whole.at[lines], core_out.at[lines], sems.at[2 * at + h]))
+            copies[-1].start()
+    cols_out[...] = tree_sum(message_part(message, n_ka * rank, rank, 1, 2) for message in messages[:n_ia])
+    for copy in copies:
+        copy.wait()
+
+
+def unpack(sizes, rank, messages):
+    lanes = messages[0].shape[1]
     return pl.pallas_call(
-        unpack_kernel,
-        out_shape=jax.ShapeDtypeStruct((rank, rank, rank), f32),
-        grid_spec=pltpu.PrefetchScalarGridSpec(
-            num_scalar_prefetch=1,
-            grid=(parts, 2),
-            in_specs=[pl.BlockSpec(own.shape, all_of), pl.BlockSpec(other.shape, all_of)],
-            out_specs=pl.BlockSpec((count, rank, rank), place),
-        ),
-        compiler_params=pltpu.CompilerParams(vmem_limit_bytes=32 * 2**20),
+        functools.partial(unpack_kernel, sizes, rank),
+        out_shape=(jax.ShapeDtypeStruct((rank, rank, rank), f32), jax.ShapeDtypeStruct((rank, lanes), f32)),
+        in_specs=[pl.BlockSpec(memory_space=pltpu.VMEM)] * len(messages),
+        out_specs=(pl.BlockSpec(memory_space=pl.ANY), pl.BlockSpec(memory_space=pltpu.VMEM)),
+        scratch_shapes=[pltpu.VMEM((rank, rank, rank), f32), pltpu.SemaphoreType.DMA((2 * len(messages),))],
+        compiler_params=pltpu.CompilerParams(vmem_limit_bytes=24 * 2**20),
         name="unpack",
-    )(mask, own, other)
+    )(*messages)
 
 
 def power_of_two(n):
@@ -378,31 +511,18 @@
     half = devices // 2
     keep = jnp.concatenate([core_sum[:half], rows_sum[:n_ka], depth_sum[None]])
     send = jnp.concatenate([core_sum[half:], rows_sum[n_ka:], depth_sum[None]])
-    total = keep + swap(send, "ja", n_ja, 1)
-    core_half, rows_half, depth_half = total[:half], total[half : half + n_ka], total[half + n_ka :]
-    core_quarter = core_half[:n_ka]
-    depth_total = depth_half[0]
-    for mask in range(1, n_ia):
-        piece = jnp.concatenate([core_half[mask * n_ka : (mask + 1) * n_ka], depth_half])
-        got = swap(piece, "ia", n_ia, mask)
-        core_quarter = core_quarter + got[:n_ka]
-        depth_total = depth_total + got[n_ka]
-    own = jnp.stack([core_quarter[0], rows_half[0], cols_sum[0]])
-    for mask in range(1, n_ka):
-        own = own + swap(jnp.stack([core_quarter[mask], rows_half[mask], cols_sum[mask]]), "ka", n_ka, mask)
-    core_own, rows_total, cols_own = own[0], own[1], own[2]
-    pieces = [core_own] + [swap(core_own, "ka", n_ka, mask) for mask in range(1, n_ka)]
-    pack = jnp.stack(pieces + [cols_own])
-    cols_total = cols_own
-    gathered = [pack[:n_ka]]
-    for mask in range(1, n_ia):
-        got = swap(pack, "ia", n_ia, mask)
-        gathered.append(got[:n_ka])
-        cols_total = cols_total + got[n_ka]
-    mine = jnp.concatenate(gathered)
-    other = swap(mine, "ja", n_ja, 1)
-    mask = (ja * n_ia + ia) * n_ka + ka
-    core_total = unpack(jnp.stack([mask]).astype(jnp.int32), mine, other)
+    got = swap(send, "ja", n_ja, 1)
+    own_core, own_depth, messages, columns = after_cores(n_ia, n_ka, keep, got, cols_sum)
+    messages = [swap(message.astype(wire), "ia", n_ia, at + 1).astype(f32) for at, message in enumerate(messages)]
+    columns = [columns[0]] + [swap(columns[mask], "ka", n_ka, mask) for mask in range(1, n_ka)]
+    message, depth_total = after_rows(own_core, own_depth, messages)
+    sent = message.astype(wire)
+    messages = [message] + [swap(sent, "ka", n_ka, mask).astype(f32) for mask in range(1, n_ka)]
+    message, rows_total = after_depths(messages, columns)
+    sent = message.astype(wire)
+    sent = [sent] + [swap(sent, "ia", n_ia, mask) for mask in range(1, n_ia)]
+    sent = sent + [swap(each, "ja", n_ja, 1) for each in sent]
+    core_total, cols_total = unpack(sizes, rank, [each.astype(f32) for each in sent])
     return (rows_total, cols_total, depth_total, core_total)
 
 

time: 78.8 us -> 66.9 us (0.85)
  waiting for transfers between devices: 27.9 us -> 15 us
  starting transfers between devices: 26.6 us -> 30.5 us
  other arithmetic: 3.77 us -> 2.61 us
    ppermute x18 -> x21, waiting for transfers between devices: 27.9 us -> 15 us  [swap(): return lax.ppermute(value, axis, [(at, at ^ mask) for at in range(size)])]
    ppermute x18 -> x21, starting transfers between devices: 26.6 us -> 30.5 us  [swap(): return lax.ppermute(value, axis, [(at, at ^ mask) for at in range(size)])]
    pallas_call x1, Pallas kernels: 7.48 us -> 5.8 us  [terms(): pl.pallas_call(functools.partial(terms_kernel, relative, sizes), out_shap...]
    add x5 -> x0, other arithmetic: 1.43 us -> none  [the longest x1 0.65 us: on_device(): depth_total = depth_total + got[n_ka]]
    pallas_call x1 -> x4, Pallas kernels: 2.51 us -> 3.8 us  [the longest x1 2.17 us: unpack(): pl.pallas_call(functools.partial(unpack_kernel, sizes, rank), out_shape=(...]
    unnamed x16 -> x10, local copies, waits for them, and re-layouts: 6.27 us -> 5.61 us
  transfers between devices with their start and end apart: 18 -> 21, of which waited for: 11 -> 14; matrix products, arithmetic and copies ran while one was open for 4% -> 4% of each run, Pallas kernels for 2% -> 3%
where the time goes in v3:
time: 66.9 us
  starting transfers between devices  30.5 us (46%)
  waiting for transfers between devices  15 us (22%)
  Pallas kernels  11.5 us (17%)
  local copies, waits for them, and re-layouts  5.79 us (9%)
  other arithmetic  2.61 us (4%)
  between operations  1.52 us (2%)
    ppermute x21, starting transfers between devices, swap(): return lax.ppermute(value, axis, [(at, at ^ mask) for at in range(size)])  30.5 us
    ppermute x21, waiting for transfers between devices, swap(): return lax.ppermute(value, axis, [(at, at ^ mask) for at in range(size)])  15 us
    pallas_call x1, Pallas kernels, terms(): pl.pallas_call(functools.partial(terms_kernel, relative, sizes), out_shap...  5.8 us
    unnamed x10, local copies, waits for them, and re-layouts  5.61 us
    pallas_call x1, Pallas kernels, unpack(): pl.pallas_call(functools.partial(unpack_kernel, sizes, rank), out_shape=(...  2.17 us
    pallas_call x1, Pallas kernels, first_cubes(): pl.pallas_call(functools.partial(cube_kernel, depth_blocks, slab), out_sh...  1.9 us
    pallas_call x3, Pallas kernels, vmem_call(): pl.pallas_call(kernel, out_shape=out_shape, in_specs=[pl.BlockSpec(memory...  1.63 us
  transfers between devices with their start and end apart: 21, of which 14 were waited for; matrix products, arithmetic and copies ran while one was open for 4% of the time, Pallas kernels for 3%

profile of v3, /device:TPU:0, one launch (start us, length us, event | category | flops | bytes accessed | tf_op | source)
XLA Modules:
  0.0 66.9 jit_solution(10354378699362476493)
XLA Ops:
  0.6 0.7 %pad_maximum_fusion.4 = bf16[2,64,128]{2,1,0:T(8,128)(2,1)S(1)} fusion(bf16[1,64,128]{2,1,0:T(8,128)(2,1)} %bitcast.11, bf16[1,64,128]{2,1,0:T(8,128)(2,1)} %bitcast.9), kind=kLoop, calls=%fused_computation.4 | loop fusion | flops 16384 | bytes 65536 | tf_op jit(solution)/shard_map/stack | solution.py:474
  1.4 5.0 %collective-permute-start.2 = (bf16[2,64,128]{2,1,0:T(8,128)(2,1)S(1)}, bf16[2,64,128]{2,1,0:T(8,128)(2,1)S(1)}, u32[]{:S(2)}, u32[]{:S(2)}) collective-permute-start(bf16[2,64,128]{2,1,0:T(8,128)(2,1)S(1)} %pad_maximum_fusion.4), channel_id=1, source_target_pairs={{0,3},{1,2},{2,1},{3,0},{4,7},{5,6},{6,5},{7,4},{8,11},{9,10},{10,... | collective-permute-start | bytes 98312 | tf_op jit(solution)/shard_map/ppermute | solution.py:448
  6.4 0.6 collective-permute-start
  7.0 0.7 %constant_dynamic-update-slice_fusion.4 = bf16[8,64,128]{2,1,0:T(8,128)(2,1)S(1)} fusion(bf16[64,128]{1,0:T(8,128)(2,1)} %param.12), kind=kLoop, calls=%fused_computation.9 | loop fusion | bytes 32768
  7.8 1.2 %copy-done = bf16[64,64,64]{2,1,0:T(8,128)(2,1)S(1)} copy-done((bf16[64,64,64]{2,1,0:T(8,128)(2,1)S(1)}, bf16[64,64,64]{2,1,0:T(8,128)(2,1)}, u32[]{:S(2)}) %copy-start) | copy-done | bytes 524312
  9.0 0.8 %copy-done.2 = bf16[64,512]{1,0:T(8,128)(2,1)S(1)} copy-done((bf16[64,512]{1,0:T(8,128)(2,1)S(1)}, bf16[64,512]{1,0:T(8,128)(2,1)}, u32[]{:S(2)}) %copy-start.2) | copy-done | bytes 65560
  9.8 1.9 %first_cubes.1 = (bf16[4,1024,128]{2,1,0:T(8,128)(2,1)S(1)}, bf16[4,128,1024]{2,1,0:T(8,128)(2,1)S(1)}) custom-call(bf16[64,512]{1,0:T(8,128)(2,1)S(1)} %copy-done.2, bf16[64,64,64]{2,1,0:T(8,128)(2,1)S(1)} %copy-done), custom_call_target="tpu_custom_call" | custom-call | flops 1000000000 | bytes 4194304 | tf_op jit(solution)/shard_map/first_cubes/pallas_call | solution.py:48
  12.4 0.8 %copy.12.coords = s32[1,1,5,3]{3,2,1,0:T(8,128)S(1)} copy(s32[1,1,5,3]{2,1,3,0:T(1,128)} %param.10) | data formatting | bytes 120 | tf_op args[2]
  13.2 0.7 %pad_maximum_fusion.2 = bf16[4,64,128]{2,1,0:T(8,128)(2,1)S(1)} fusion(bf16[1,64,128]{2,1,0:T(8,128)(2,1)S(1)} %get-tuple-element.62, bf16[1,64,128]{2,1,0:T(8,128)(2,1)S(1)} %get-tuple-element.59, bf16[1,64,128]{2,1,0:T(8,128)(2,1)S(1)} %get-tuple-element.56, bf16[1,64,128]{2,1,0:T(8,128)(2,1)} %bitcast.10), kind=kLoop, calls=%fused_computation.2 | loop fusion | flops 98304 | bytes 131072 | tf_op jit(solution)/shard_map/stack | solution.py:476
  14.0 0.1 collective-permute-start.3
  14.0 0.7 %pad_maximum_fusion.3.col_table = bf16[4,64,128]{2,1,0:T(8,128)(2,1)S(1)} fusion(bf16[1,64,128]{2,1,0:T(8,128)(2,1)S(1)} %get-tuple-element.60, bf16[1,64,128]{2,1,0:T(8,128)(2,1)S(1)} %get-tuple-element.57, bf16[1,64,128]{2,1,0:T(8,128)(2,1)S(1)} %get-tuple-element.54, bf16[1,64,128]{2,1,0:T(8,128)(2,1)} %bitcast.12), kind=kLoop, calls=%fused_computation.3 | loop fusion | flops 98304 | bytes 131072 | tf_op jit(solution)/shard_map/stack | solution.py:478
  14.8 0.5 collective-permute-done.3
  15.3 0.0 copy-start.1
  15.3 1.2 %copy-done.1 = bf16[64,64,64]{2,1,0:T(8,128)(2,1)S(1)} copy-done((bf16[64,64,64]{2,1,0:T(8,128)(2,1)S(1)}, bf16[64,64,64]{2,1,0:T(8,128)(2,1)}, u32[]{:S(2)}) %copy-start.1) | copy-done | bytes 524312
  16.5 0.8 %copy-done.3 = bf16[64,512]{1,0:T(8,128)(2,1)S(1)} copy-done((bf16[64,512]{1,0:T(8,128)(2,1)S(1)}, bf16[64,512]{1,0:T(8,128)(2,1)}, u32[]{:S(2)}) %copy-start.3) | copy-done | bytes 65560
  17.4 5.8 %terms.1 = (f32[32,64,128]{2,1,0:T(8,128)S(1)}, f32[8,64,128]{2,1,0:T(8,128)S(1)}, f32[4,64,128]{2,1,0:T(8,128)S(1)}, f32[64,128]{1,0:T(8,128)S(1)}) custom-call(s32[1,1,1]{2,1,0:T(1,128)S(6)} %copy.17.counts, s32[1,1,5,3]{3,2,1,0:T(8,128)S(1)} %copy.12.coords, bf16[5,128,32,128]{3,2,1,0:T(8,128)(2,1)} %bitcast.7, bf16[5,128,32,128]{3,2,1,0:T(8,128)(2,1)} %bitcast.8, ...), custom_call_target="tpu_custom_call" | custom-call | flops 1000000000 | bytes 16777216 | tf_op jit(solution)/shard_map/terms/pallas_call | solution.py:233
  23.2 0.1 fusion.1
  23.3 0.1 pad_maximum_fusion
  23.5 0.1 collective-permute-start.4
  23.5 2.1 %collective-permute-done.4.got = f32[21,64,128]{2,1,0:T(8,128)S(1)} collective-permute-done((f32[21,64,128]{2,1,0:T(8,128)S(1)}, f32[21,64,128]{2,1,0:T(8,128)S(1)}, u32[]{:S(2)}, u32[]{:S(2)}) %collective-permute-start.4) | collective-permute-done | bytes 688160 | tf_op jit(solution)/shard_map/ppermute | solution.py:448
  25.7 0.2 after_cores.1
  26.0 2.7 %collective-permute-start.7 = (f16[352,128]{1,0:T(8,128)(2,1)S(1)}, f16[352,128]{1,0:T(8,128)(2,1)S(1)}, u32[]{:S(2)}, u32[]{:S(2)}) collective-permute-start(f16[352,128]{1,0:T(8,128)(2,1)S(1)} %convert_element_type.61), channel_id=1, source_target_pairs={{0,24},{8,16},{16,8},{24,0},{1,25},{9,17},{17,9},{25,1},{2,26},{10... | collective-permute-start | bytes 270344 | tf_op jit(solution)/shard_map/ppermute | solution.py:448
  28.6 0.5 collective-permute-start.6
  29.2 0.4 collective-permute-start.5
  29.6 2.1 %collective-permute-done.7 = f16[352,128]{1,0:T(8,128)(2,1)S(1)} collective-permute-done((f16[352,128]{1,0:T(8,128)(2,1)S(1)}, f16[352,128]{1,0:T(8,128)(2,1)S(1)}, u32[]{:S(2)}, u32[]{:S(2)}) %collective-permute-start.7) | collective-permute-done | bytes 90144 | tf_op jit(solution)/shard_map/ppermute | solution.py:448
  31.7 1.8 %collective-permute-done.6 = f16[352,128]{1,0:T(8,128)(2,1)S(1)} collective-permute-done((f16[352,128]{1,0:T(8,128)(2,1)S(1)}, f16[352,128]{1,0:T(8,128)(2,1)S(1)}, u32[]{:S(2)}, u32[]{:S(2)}) %collective-permute-start.6) | collective-permute-done | bytes 90144 | tf_op jit(solution)/shard_map/ppermute | solution.py:448
  33.6 0.2 collective-permute-done.5
  33.8 0.7 %after_rows.1 = (f32[272,128]{1,0:T(8,128)S(1)}, f32[64,128]{1,0:T(8,128)}) custom-call(f32[4,64,128]{2,1,0:T(8,128)S(1)} %get-tuple-element.31.own_core, f32[64,128]{1,0:T(8,128)S(1)} %get-tuple-element.32.own_depth, f32[352,128]{1,0:T(8,128)S(1)} %convert_element_type.58.refs_0_, f32[352,128]{1,0:T(8,128)S(1)} %convert_element_type.60.refs_1_, ...), custom_call_target="tpu_custom_call" | custom-call | tf_op jit(solution)/shard_map/after_rows/pallas_call | solution.py:273
  34.5 10.4 %collective-permute-start.10 = (f16[272,128]{1,0:T(8,128)(2,1)S(1)}, f16[272,128]{1,0:T(8,128)(2,1)S(1)}, u32[]{:S(2)}, u32[]{:S(2)}) collective-permute-start(f16[272,128]{1,0:T(8,128)(2,1)S(1)} %convert_element_type.63), channel_id=1, source_target_pairs={{0,3},{1,2},{2,1},{3,0},{4,7},{5,6},{6,5},{7,4},{8,11},{9,10},{10,... | collective-permute-start | bytes 208904 | tf_op jit(solution)/shard_map/ppermute | solution.py:448
  44.9 0.6 collective-permute-start.8
  45.5 1.4 %collective-permute-start.11 = (f32[2,64,128]{2,1,0:T(8,128)S(1)}, f32[2,64,128]{2,1,0:T(8,128)S(1)}, u32[]{:S(2)}, u32[]{:S(2)}) collective-permute-start(f32[2,64,128]{2,1,0:T(8,128)S(1)} %get-tuple-element.38), channel_id=1, source_target_pairs={{0,1},{1,0},{2,3},{3,2},{4,5},{5,4},{6,7},{7,6},{8,9},{9,8},{10,11... | collective-permute-start | bytes 196616 | tf_op jit(solution)/shard_map/ppermute | solution.py:448
  46.9 2.9 %collective-permute-start.12 = (f32[2,64,128]{2,1,0:T(8,128)S(1)}, f32[2,64,128]{2,1,0:T(8,128)S(1)}, u32[]{:S(2)}, u32[]{:S(2)}) collective-permute-start(f32[2,64,128]{2,1,0:T(8,128)S(1)} %get-tuple-element.39), channel_id=1, source_target_pairs={{0,2},{1,3},{2,0},{3,1},{4,6},{5,7},{6,4},{7,5},{8,10},{9,11},{10,... | collective-permute-start | bytes 196616 | tf_op jit(solution)/shard_map/ppermute | solution.py:448
  49.8 1.9 %collective-permute-start.13 = (f32[2,64,128]{2,1,0:T(8,128)S(1)}, f32[2,64,128]{2,1,0:T(8,128)S(1)}, u32[]{:S(2)}, u32[]{:S(2)}) collective-permute-start(f32[2,64,128]{2,1,0:T(8,128)S(1)} %get-tuple-element.40), channel_id=1, source_target_pairs={{0,3},{1,2},{2,1},{3,0},{4,7},{5,6},{6,5},{7,4},{8,11},{9,10},{10,... | collective-permute-start | bytes 196616 | tf_op jit(solution)/shard_map/ppermute | solution.py:448
  51.8 0.2 collective-permute-done.8
  52.0 1.5 %collective-permute-done.11.refs_5_ = f32[2,64,128]{2,1,0:T(8,128)S(1)} collective-permute-done((f32[2,64,128]{2,1,0:T(8,128)S(1)}, f32[2,64,128]{2,1,0:T(8,128)S(1)}, u32[]{:S(2)}, u32[]{:S(2)}) %collective-permute-start.11) | collective-permute-done | bytes 65568 | tf_op jit(solution)/shard_map/ppermute | solution.py:448
  53.5 1.0 %collective-permute-done.12.refs_6_ = f32[2,64,128]{2,1,0:T(8,128)S(1)} collective-permute-done((f32[2,64,128]{2,1,0:T(8,128)S(1)}, f32[2,64,128]{2,1,0:T(8,128)S(1)}, u32[]{:S(2)}, u32[]{:S(2)}) %collective-permute-start.12) | collective-permute-done | bytes 65568 | tf_op jit(solution)/shard_map/ppermute | solution.py:448
  54.6 1.4 %collective-permute-done.13.refs_7_ = f32[2,64,128]{2,1,0:T(8,128)S(1)} collective-permute-done((f32[2,64,128]{2,1,0:T(8,128)S(1)}, f32[2,64,128]{2,1,0:T(8,128)S(1)}, u32[]{:S(2)}, u32[]{:S(2)}) %collective-permute-start.13) | collective-permute-done | bytes 65568 | tf_op jit(solution)/shard_map/ppermute | solution.py:448
  56.0 0.7 %after_depths.1 = (f32[352,128]{1,0:T(8,128)S(1)}, f32[64,128]{1,0:T(8,128)}) custom-call(f32[272,128]{1,0:T(8,128)S(1)} %get-tuple-element.36.refs_0_, f32[272,128]{1,0:T(8,128)S(1)} %convert_element_type.64.refs_1_, f32[272,128]{1,0:T(8,128)S(1)} %convert_element_type.65.refs_2_, f32[272,128]{1,0:T(8,128)S(1)} %convert_element_type.66.refs_3_, ...), custom_call_target="tpu_custom_call" | custom-call | tf_op jit(solution)/shard_map/after_depths/pallas_call | solution.py:273
  56.7 1.6 %collective-permute-start.16 = (f16[352,128]{1,0:T(8,128)(2,1)S(1)}, f16[352,128]{1,0:T(8,128)(2,1)S(1)}, u32[]{:S(2)}, u32[]{:S(2)}) collective-permute-start(f16[352,128]{1,0:T(8,128)(2,1)S(1)} %get-tuple-element.47), channel_id=1, source_target_pairs={{0,24},{8,16},{16,8},{24,0},{1,25},{9,17},{17,9},{25,1},{2,26},{10... | collective-permute-start | bytes 270344 | tf_op jit(solution)/shard_map/ppermute | solution.py:448
  58.3 0.6 collective-permute-start.15
  58.9 1.3 %collective-permute-start.14 = (f16[352,128]{1,0:T(8,128)(2,1)S(1)}, f16[352,128]{1,0:T(8,128)(2,1)S(1)}, u32[]{:S(2)}, u32[]{:S(2)}) collective-permute-start(f16[352,128]{1,0:T(8,128)(2,1)S(1)} %get-tuple-element.47), channel_id=1, source_target_pairs={{0,8},{8,0},{16,24},{24,16},{1,9},{9,1},{17,25},{25,17},{2,10},{10... | collective-permute-start | bytes 270344 | tf_op jit(solution)/shard_map/ppermute | solution.py:448
  60.3 2.0 %collective-permute-done.16 = f16[352,128]{1,0:T(8,128)(2,1)S(1)} collective-permute-done((f16[352,128]{1,0:T(8,128)(2,1)S(1)}, f16[352,128]{1,0:T(8,128)(2,1)S(1)}, u32[]{:S(2)}, u32[]{:S(2)}) %collective-permute-start.16) | collective-permute-done | bytes 90144 | tf_op jit(solution)/shard_map/ppermute | solution.py:448
  62.2 0.9 %collective-permute-done.15 = f16[352,128]{1,0:T(8,128)(2,1)S(1)} collective-permute-done((f16[352,128]{1,0:T(8,128)(2,1)S(1)}, f16[352,128]{1,0:T(8,128)(2,1)S(1)}, u32[]{:S(2)}, u32[]{:S(2)}) %collective-permute-start.15) | collective-permute-done | bytes 90144 | tf_op jit(solution)/shard_map/ppermute | solution.py:448
  63.2 0.3 collective-permute-done.14
  63.4 0.2 collective-permute-start.18
  63.8 0.6 collective-permute-done.19
  64.5 0.3 collective-permute-done.18
  64.8 2.2 %unpack.1 = (f32[64,64,64]{2,1,0:T(8,128)}, f32[64,128]{1,0:T(8,128)}) custom-call(f32[352,128]{1,0:T(8,128)S(1)} %get-tuple-element.46.refs_0_, f32[352,128]{1,0:T(8,128)S(1)} %convert_element_type.69.refs_1_, f32[352,128]{1,0:T(8,128)S(1)} %convert_element_type.70.refs_2_, f32[352,128]{1,0:T(8,128)S(1)} %convert_element_type.71.refs_3_, ...), custom_call_target="tpu_custom_call" | custom-call | tf_op jit(solution)/shard_map/unpack/pallas_call | solution.py:432
  (38 shorter events, 0.4 us)
Async XLA Ops:
  1.4 11.8 %collective-permute-start.2 = (bf16[2,64,128]{2,1,0:T(8,128)(2,1)S(1)}, bf16[2,64,128]{2,1,0:T(8,128)(2,1)S(1)}, u32[]{:S(2)}, u32[]{:S(2)}) collective-permute-start(bf16[2,64,128]{2,1,0:T(8,128)(2,1)S(1)} %pad_maximum_fusion.4), channel_id=1, source_target_pairs={{0,3},{1,2},{2,1},{3,0},{4,7},{5,6},{6,5},{7,4},{8,11},{9,10},{10,... | collective-permute-start | bytes 98312 | tf_op jit(solution)/shard_map/ppermute | solution.py:448
  6.4 6.8 %collective-permute-start.1 = (bf16[2,64,128]{2,1,0:T(8,128)(2,1)S(1)}, bf16[2,64,128]{2,1,0:T(8,128)(2,1)S(1)}, u32[]{:S(2)}, u32[]{:S(2)}) collective-permute-start(bf16[2,64,128]{2,1,0:T(8,128)(2,1)S(1)} %pad_maximum_fusion.4), channel_id=1, source_target_pairs={{0,2},{1,3},{2,0},{3,1},{4,6},{5,7},{6,4},{7,5},{8,10},{9,11},{10,... | collective-permute-start | bytes 98312 | tf_op jit(solution)/shard_map/ppermute | solution.py:448
  6.4 6.7 %collective-permute-start = (bf16[2,64,128]{2,1,0:T(8,128)(2,1)S(1)}, bf16[2,64,128]{2,1,0:T(8,128)(2,1)S(1)}, u32[]{:S(2)}, u32[]{:S(2)}) collective-permute-start(bf16[2,64,128]{2,1,0:T(8,128)(2,1)S(1)} %pad_maximum_fusion.4), channel_id=1, source_target_pairs={{0,1},{1,0},{2,3},{3,2},{4,5},{5,4},{6,7},{7,6},{8,9},{9,8},{10,11... | collective-permute-start | bytes 98312 | tf_op jit(solution)/shard_map/ppermute | solution.py:448
  7.8 1.2 %copy-start = (bf16[64,64,64]{2,1,0:T(8,128)(2,1)S(1)}, bf16[64,64,64]{2,1,0:T(8,128)(2,1)}, u32[]{:S(2)}) copy-start(bf16[64,64,64]{2,1,0:T(8,128)(2,1)} %core.3) | copy-start | bytes 1572868
  9.0 0.8 %copy-start.2 = (bf16[64,512]{1,0:T(8,128)(2,1)S(1)}, bf16[64,512]{1,0:T(8,128)(2,1)}, u32[]{:S(2)}) copy-start(bf16[64,512]{1,0:T(8,128)(2,1)} %factor_depth.3) | copy-start | bytes 196612
  14.0 1.3 %collective-permute-start.3 = (bf16[4,64,128]{2,1,0:T(8,128)(2,1)S(1)}, bf16[4,64,128]{2,1,0:T(8,128)(2,1)S(1)}, u32[]{:S(2)}, u32[]{:S(2)}) collective-permute-start(bf16[4,64,128]{2,1,0:T(8,128)(2,1)S(1)} %pad_maximum_fusion.2), channel_id=1, source_target_pairs={{0,4},{4,0},{1,5},{5,1},{2,6},{6,2},{3,7},{7,3},{8,12},{12,8},{9,1... | collective-permute-start | bytes 196616 | tf_op jit(solution)/shard_map/ppermute | solution.py:448
  15.3 1.2 %copy-start.1 = (bf16[64,64,64]{2,1,0:T(8,128)(2,1)S(1)}, bf16[64,64,64]{2,1,0:T(8,128)(2,1)}, u32[]{:S(2)}) copy-start(bf16[64,64,64]{2,1,0:T(8,128)(2,1)} %core.3) | copy-start | bytes 1572868
  16.5 0.8 %copy-start.3 = (bf16[64,512]{1,0:T(8,128)(2,1)S(1)}, bf16[64,512]{1,0:T(8,128)(2,1)}, u32[]{:S(2)}) copy-start(bf16[64,512]{1,0:T(8,128)(2,1)} %factor_depth.3) | copy-start | bytes 196612
  23.5 2.2 %collective-permute-start.4 = (f32[21,64,128]{2,1,0:T(8,128)S(1)}, f32[21,64,128]{2,1,0:T(8,128)S(1)}, u32[]{:S(2)}, u32[]{:S(2)}) collective-permute-start(f32[21,64,128]{2,1,0:T(8,128)S(1)} %get-tuple-element.52), channel_id=1, source_target_pairs={{0,4},{4,0},{1,5},{5,1},{2,6},{6,2},{3,7},{7,3},{8,12},{12,8},{9,1... | collective-permute-start | bytes 2064392 | tf_op jit(solution)/shard_map/ppermute | solution.py:448
  26.0 5.7 %collective-permute-start.7 = (f16[352,128]{1,0:T(8,128)(2,1)S(1)}, f16[352,128]{1,0:T(8,128)(2,1)S(1)}, u32[]{:S(2)}, u32[]{:S(2)}) collective-permute-start(f16[352,128]{1,0:T(8,128)(2,1)S(1)} %convert_element_type.61), channel_id=1, source_target_pairs={{0,24},{8,16},{16,8},{24,0},{1,25},{9,17},{17,9},{25,1},{2,26},{10... | collective-permute-start | bytes 270344 | tf_op jit(solution)/shard_map/ppermute | solution.py:448
  28.6 4.9 %collective-permute-start.6 = (f16[352,128]{1,0:T(8,128)(2,1)S(1)}, f16[352,128]{1,0:T(8,128)(2,1)S(1)}, u32[]{:S(2)}, u32[]{:S(2)}) collective-permute-start(f16[352,128]{1,0:T(8,128)(2,1)S(1)} %convert_element_type.59), channel_id=1, source_target_pairs={{0,16},{8,24},{16,0},{24,8},{1,17},{9,25},{17,1},{25,9},{2,18},{10... | collective-permute-start | bytes 270344 | tf_op jit(solution)/shard_map/ppermute | solution.py:448
  29.2 4.6 %collective-permute-start.5 = (f16[352,128]{1,0:T(8,128)(2,1)S(1)}, f16[352,128]{1,0:T(8,128)(2,1)S(1)}, u32[]{:S(2)}, u32[]{:S(2)}) collective-permute-start(f16[352,128]{1,0:T(8,128)(2,1)S(1)} %convert_element_type.57), channel_id=1, source_target_pairs={{0,8},{8,0},{16,24},{24,16},{1,9},{9,1},{17,25},{25,17},{2,10},{10... | collective-permute-start | bytes 270344 | tf_op jit(solution)/shard_map/ppermute | solution.py:448
  34.5 15.3 %collective-permute-start.10 = (f16[272,128]{1,0:T(8,128)(2,1)S(1)}, f16[272,128]{1,0:T(8,128)(2,1)S(1)}, u32[]{:S(2)}, u32[]{:S(2)}) collective-permute-start(f16[272,128]{1,0:T(8,128)(2,1)S(1)} %convert_element_type.63), channel_id=1, source_target_pairs={{0,3},{1,2},{2,1},{3,0},{4,7},{5,6},{6,5},{7,4},{8,11},{9,10},{10,... | collective-permute-start | bytes 208904 | tf_op jit(solution)/shard_map/ppermute | solution.py:448
  44.9 6.9 %collective-permute-start.9 = (f16[272,128]{1,0:T(8,128)(2,1)S(1)}, f16[272,128]{1,0:T(8,128)(2,1)S(1)}, u32[]{:S(2)}, u32[]{:S(2)}) collective-permute-start(f16[272,128]{1,0:T(8,128)(2,1)S(1)} %convert_element_type.63), channel_id=1, source_target_pairs={{0,2},{1,3},{2,0},{3,1},{4,6},{5,7},{6,4},{7,5},{8,10},{9,11},{10,... | collective-permute-start | bytes 208904 | tf_op jit(solution)/shard_map/ppermute | solution.py:448
  44.9 7.1 %collective-permute-start.8 = (f16[272,128]{1,0:T(8,128)(2,1)S(1)}, f16[272,128]{1,0:T(8,128)(2,1)S(1)}, u32[]{:S(2)}, u32[]{:S(2)}) collective-permute-start(f16[272,128]{1,0:T(8,128)(2,1)S(1)} %convert_element_type.63), channel_id=1, source_target_pairs={{0,1},{1,0},{2,3},{3,2},{4,5},{5,4},{6,7},{7,6},{8,9},{9,8},{10,11... | collective-permute-start | bytes 208904 | tf_op jit(solution)/shard_map/ppermute | solution.py:448
  45.5 8.0 %collective-permute-start.11 = (f32[2,64,128]{2,1,0:T(8,128)S(1)}, f32[2,64,128]{2,1,0:T(8,128)S(1)}, u32[]{:S(2)}, u32[]{:S(2)}) collective-permute-start(f32[2,64,128]{2,1,0:T(8,128)S(1)} %get-tuple-element.38), channel_id=1, source_target_pairs={{0,1},{1,0},{2,3},{3,2},{4,5},{5,4},{6,7},{7,6},{8,9},{9,8},{10,11... | collective-permute-start | bytes 196616 | tf_op jit(solution)/shard_map/ppermute | solution.py:448
  46.9 7.7 %collective-permute-start.12 = (f32[2,64,128]{2,1,0:T(8,128)S(1)}, f32[2,64,128]{2,1,0:T(8,128)S(1)}, u32[]{:S(2)}, u32[]{:S(2)}) collective-permute-start(f32[2,64,128]{2,1,0:T(8,128)S(1)} %get-tuple-element.39), channel_id=1, source_target_pairs={{0,2},{1,3},{2,0},{3,1},{4,6},{5,7},{6,4},{7,5},{8,10},{9,11},{10,... | collective-permute-start | bytes 196616 | tf_op jit(solution)/shard_map/ppermute | solution.py:448
  49.8 6.2 %collective-permute-start.13 = (f32[2,64,128]{2,1,0:T(8,128)S(1)}, f32[2,64,128]{2,1,0:T(8,128)S(1)}, u32[]{:S(2)}, u32[]{:S(2)}) collective-permute-start(f32[2,64,128]{2,1,0:T(8,128)S(1)} %get-tuple-element.40), channel_id=1, source_target_pairs={{0,3},{1,2},{2,1},{3,0},{4,7},{5,6},{6,5},{7,4},{8,11},{9,10},{10,... | collective-permute-start | bytes 196616 | tf_op jit(solution)/shard_map/ppermute | solution.py:448
  56.7 5.5 %collective-permute-start.16 = (f16[352,128]{1,0:T(8,128)(2,1)S(1)}, f16[352,128]{1,0:T(8,128)(2,1)S(1)}, u32[]{:S(2)}, u32[]{:S(2)}) collective-permute-start(f16[352,128]{1,0:T(8,128)(2,1)S(1)} %get-tuple-element.47), channel_id=1, source_target_pairs={{0,24},{8,16},{16,8},{24,0},{1,25},{9,17},{17,9},{25,1},{2,26},{10... | collective-permute-start | bytes 270344 | tf_op jit(solution)/shard_map/ppermute | solution.py:448
  58.3 4.9 %collective-permute-start.15 = (f16[352,128]{1,0:T(8,128)(2,1)S(1)}, f16[352,128]{1,0:T(8,128)(2,1)S(1)}, u32[]{:S(2)}, u32[]{:S(2)}) collective-permute-start(f16[352,128]{1,0:T(8,128)(2,1)S(1)} %get-tuple-element.47), channel_id=1, source_target_pairs={{0,16},{8,24},{16,0},{24,8},{1,17},{9,25},{17,1},{25,9},{2,18},{10... | collective-permute-start | bytes 270344 | tf_op jit(solution)/shard_map/ppermute | solution.py:448
  58.9 4.5 %collective-permute-start.14 = (f16[352,128]{1,0:T(8,128)(2,1)S(1)}, f16[352,128]{1,0:T(8,128)(2,1)S(1)}, u32[]{:S(2)}, u32[]{:S(2)}) collective-permute-start(f16[352,128]{1,0:T(8,128)(2,1)S(1)} %get-tuple-element.47), channel_id=1, source_target_pairs={{0,8},{8,0},{16,24},{24,16},{1,9},{9,1},{17,25},{25,17},{2,10},{10... | collective-permute-start | bytes 270344 | tf_op jit(solution)/shard_map/ppermute | solution.py:448
  60.3 3.5 %collective-permute-start.17 = (f16[352,128]{1,0:T(8,128)(2,1)S(1)}, f16[352,128]{1,0:T(8,128)(2,1)S(1)}, u32[]{:S(2)}, u32[]{:S(2)}) collective-permute-start(f16[352,128]{1,0:T(8,128)(2,1)S(1)} %get-tuple-element.47), channel_id=1, source_target_pairs={{0,4},{4,0},{1,5},{5,1},{2,6},{6,2},{3,7},{7,3},{8,12},{12,8},{9,1... | collective-permute-start | bytes 270344 | tf_op jit(solution)/shard_map/ppermute | solution.py:448
  62.2 1.5 %collective-permute-start.20 = (f16[352,128]{1,0:T(8,128)(2,1)S(1)}, f16[352,128]{1,0:T(8,128)(2,1)S(1)}, u32[]{:S(2)}, u32[]{:S(2)}) collective-permute-start(f16[352,128]{1,0:T(8,128)(2,1)S(1)} %collective-permute-done.16), channel_id=1, source_target_pairs={{0,4},{4,0},{1,5},{5,1},{2,6},{6,2},{3,7},{7,3},{8,12},{12,8},{9,1... | collective-permute-start | bytes 270344 | tf_op jit(solution)/shard_map/ppermute | solution.py:448
  63.2 1.3 %collective-permute-start.19 = (f16[352,128]{1,0:T(8,128)(2,1)S(1)}, f16[352,128]{1,0:T(8,128)(2,1)S(1)}, u32[]{:S(2)}, u32[]{:S(2)}) collective-permute-start(f16[352,128]{1,0:T(8,128)(2,1)S(1)} %collective-permute-done.15), channel_id=1, source_target_pairs={{0,4},{4,0},{1,5},{5,1},{2,6},{6,2},{3,7},{7,3},{8,12},{12,8},{9,1... | collective-permute-start | bytes 270344 | tf_op jit(solution)/shard_map/ppermute | solution.py:448
  63.4 1.3 %collective-permute-start.18 = (f16[352,128]{1,0:T(8,128)(2,1)S(1)}, f16[352,128]{1,0:T(8,128)(2,1)S(1)}, u32[]{:S(2)}, u32[]{:S(2)}) collective-permute-start(f16[352,128]{1,0:T(8,128)(2,1)S(1)} %collective-permute-done.14), channel_id=1, source_target_pairs={{0,4},{4,0},{1,5},{5,1},{2,6},{6,2},{3,7},{7,3},{8,12},{12,8},{9,1... | collective-permute-start | bytes 270344 | tf_op jit(solution)/shard_map/ppermute | solution.py:448

commit v4 on v3

--- a/solution.py
+++ b/solution.py
@@ -17,23 +17,47 @@
     return lax.dot_general(a, b, (contract, ((), ())), preferred_element_type=f32)
 
 
-def cube_kernel(depth_blocks, slab, factor_depth, core, cube_out, cube_turned_out, cube_wide):
+def cube_kernel(
+    depth_blocks,
+    slab,
+    after,
+    factor_depth,
+    core,
+    cube_out,
+    cube_turned_out,
+    core_out,
+    depth_out,
+    depth_here,
+    core_here,
+    cube_wide,
+    sems,
+):
     rank = core.shape[0]
     half = slab // 2
+    pairs = rank // 2
     width = depth_blocks * slab
     start = pl.multiple_of(lax.axis_index("ka") * width, width)
-    depth = factor_depth[:, pl.ds(start, width)].astype(f32).T
+    core_copy = pltpu.make_async_copy(core, core_here, sems.at[0])
+    core_copy.start()
+    depth_copy = pltpu.make_async_copy(factor_depth.at[:, pl.ds(start, width)], depth_here, sems.at[1])
+    depth_copy.start()
+    depth_copy.wait()
+    depth = depth_here[...].astype(f32).T
+    depth_out[...] = depth.astype(bf16)
     order = [depth[t * slab + h * half : t * slab + (h + 1) * half] for h in range(2) for t in range(depth_blocks)]
     depth = jnp.concatenate(order, axis=0).astype(bf16)
     count = depth_blocks * half
+    core_copy.wait()
 
     def one_rank(r1, carry):
-        piece = dot(depth, core[r1], ((1,), (1,)))
+        piece = dot(depth, core_here[r1], ((1,), (1,)))
         wide = jnp.concatenate([piece[:count], piece[count:]], axis=1)
         cube_wide[pl.ds(r1, count, stride=rank + 1), :] = wide
         return carry
 
     lax.fori_loop(0, rank, one_rank, 0, unroll=16)
+    for pair in range(pairs):
+        core_out[pair] = jnp.concatenate([core_here[pair], core_here[pairs + pair]], axis=0)
     for t in range(depth_blocks):
         for kp in range(half):
             at = (t * half + kp) * (rank + 1)
@@ -42,22 +66,30 @@
         cube_turned_out[t] = cube_out[t].astype(f32).T.astype(bf16)
 
 
-def first_cubes(factor_depth, core, depth_blocks, slab):
+def first_cubes(after, factor_depth, core, depth_blocks, slab):
     rank = core.shape[0]
     half = slab // 2
+    width = depth_blocks * slab
     return pl.pallas_call(
         functools.partial(cube_kernel, depth_blocks, slab),
         out_shape=(
             jax.ShapeDtypeStruct((depth_blocks, half * rank, 2 * rank), bf16),
             jax.ShapeDtypeStruct((depth_blocks, 2 * rank, half * rank), bf16),
+            jax.ShapeDtypeStruct((rank // 2, 2 * rank, rank), bf16),
+            jax.ShapeDtypeStruct((width, rank), bf16),
         ),
-        in_specs=[pl.BlockSpec(memory_space=pltpu.VMEM)] * 2,
-        out_specs=[pl.BlockSpec(memory_space=pltpu.VMEM)] * 2,
-        scratch_shapes=[pltpu.VMEM((depth_blocks * half * (rank + 1), 2 * rank), f32)],
+        in_specs=[pl.BlockSpec(memory_space=pl.ANY)] + [pl.BlockSpec(memory_space=pltpu.HBM)] * 2,
+        out_specs=[pl.BlockSpec(memory_space=pltpu.VMEM)] * 4,
+        scratch_shapes=[
+            pltpu.VMEM((rank, width), bf16),
+            pltpu.VMEM(core.shape, bf16),
+            pltpu.VMEM((depth_blocks * half * (rank + 1), 2 * rank), f32),
+            pltpu.SemaphoreType.DMA((2,)),
+        ],
         compiler_params=pltpu.CompilerParams(vmem_limit_bytes=24 * 2**20),
         cost_estimate=pl.CostEstimate(flops=10**9, bytes_accessed=4 * 2**20, transcendentals=0),
         name="first_cubes",
-    )(factor_depth, core)
+    )(after, factor_depth, core)
 
 
 def masks_of(relative, sizes):
@@ -67,39 +99,32 @@
     return ja * sizes["ka"] + ka, ka, (ja * sizes["ia"] + ia) * sizes["ka"] + ka
 
 
-def terms_kernel(
-    relative,
-    sizes,
-    counts,
-    coords,
-    data,
-    weight,
-    cube,
-    cube_turned,
-    row_table,
-    col_table,
-    factor_depth,
-    core,
-    core_out,
-    rows_out,
-    cols_out,
-    depth_out,
-    wide_col,
-    backward,
-    by_rank,
-    second_all,
-    depth_all,
-    depth_turned,
-    depth_sum,
-    spread_data,
-    spread_weight,
-):
+def terms_kernel(relative, sizes, row_spots, col_spots, counts, coords, data, weight, cube, cube_turned, *refs):
+    pieces = refs[: 1 + max(at for at, _ in row_spots + col_spots)]
+    (
+        core,
+        depth_turned,
+        core_out,
+        rows_out,
+        cols_out,
+        depth_out,
+        row_table,
+        col_table,
+        wide_col,
+        backward,
+        by_rank,
+        second_all,
+        depth_all,
+        depth_sum,
+        spread_data,
+        spread_weight,
+    ) = refs[len(pieces) :]
     slot = pl.program_id(0)
     slots = pl.num_programs(0)
     _, rows, slab, cols = data.shape
-    rank = core.shape[0]
+    pairs = core.shape[0]
+    rank = 2 * pairs
     half = slab // 2
-    pairs = rank // 2
     depth_blocks = cube.shape[0]
     count = counts[0, 0, 0]
     row_mask, col_mask, core_mask = masks_of(relative, sizes)
@@ -115,9 +140,9 @@
         rows_out[...] = jnp.zeros_like(rows_out)
         cols_out[...] = jnp.zeros_like(cols_out)
         wide_col[...] = jnp.zeros_like(wide_col)
-        width = depth_blocks * slab
-        start = pl.multiple_of(lax.axis_index("ka") * width, width)
-        depth_turned[...] = factor_depth[:, pl.ds(start, width)].astype(f32).T
+        for spots, table in ((row_spots, row_table), (col_spots, col_table)):
+            for at, (piece, line) in enumerate(spots):
+                table[at] = pieces[piece][line]
 
     @pl.when(slot < count)
     def _():
@@ -130,7 +155,7 @@
         wide_col[:rank, :cols] = col_factor
         wide_col[rank:, cols:] = col_factor
         own_depth = depth_turned[pl.ds(pl.multiple_of(depth_at * slab, slab), slab), :]
-        depth_all[pl.ds(pl.multiple_of(slot * slab, slab), slab), :] = own_depth.astype(bf16)
+        depth_all[pl.ds(pl.multiple_of(slot * slab, slab), slab), :] = own_depth
 
         step = 4
         groups = half // step
@@ -194,8 +219,7 @@
         def one_chunk(at, total):
             pair = at ^ core_mask
             second = second_all[pair]
-            both = jnp.concatenate([core[pair], core[pairs + pair]], axis=0)
-            total = total + dot(second, both)
+            total = total + dot(second, core[pair])
             piece = dot(second, depth_all[...], ((0,), (0,)))
             core_out[at] = jnp.concatenate([piece[:rank], piece[rank:]], axis=1)
             return total
@@ -212,9 +236,9 @@
         depth_out[...] = depth_sum[...].T
 
 
-def terms(relative, sizes, counts, coords, data, weight, cube, cube_turned, row_table, col_table, factor_depth, core):
+def terms(relative, sizes, row_spots, col_spots, counts, coords, data, weight, cube, cube_turned, pieces, core, depth):
     slots, rows, slab, cols = data.shape
-    rank = core.shape[0]
+    rank = core.shape[2]
     half = slab // 2
     depth_blocks = cube.shape[0]
 
@@ -226,12 +250,12 @@
 
     outs = (
         jax.ShapeDtypeStruct((rank // 2, rank, 2 * rank), f32),
-        jax.ShapeDtypeStruct((row_table.shape[0], rank, rows), f32),
-        jax.ShapeDtypeStruct((col_table.shape[0], rank, cols), f32),
+        jax.ShapeDtypeStruct((len(row_spots), rank, rows), f32),
+        jax.ShapeDtypeStruct((len(col_spots), rank, cols), f32),
         jax.ShapeDtypeStruct((rank, depth_blocks * slab), f32),
     )
     return pl.pallas_call(
-        functools.partial(terms_kernel, relative, sizes),
+        functools.partial(terms_kernel, relative, sizes, row_spots, col_spots),
         out_shape=outs,
         grid_spec=pltpu.PrefetchScalarGridSpec(
             num_scalar_prefetch=2,
@@ -241,19 +265,19 @@
                 pl.BlockSpec((1, rows, slab, cols), live),
                 whole(cube),
                 whole(cube_turned),
-                whole(row_table),
-                whole(col_table),
-                whole(factor_depth),
+                *[whole(piece) for piece in pieces],
                 whole(core),
+                whole(depth),
             ],
             out_specs=[whole(out) for out in outs],
             scratch_shapes=[
+                pltpu.VMEM((len(row_spots), rank, rows), bf16),
+                pltpu.VMEM((len(col_spots), rank, cols), bf16),
                 pltpu.VMEM((2 * rank, 2 * cols), bf16),
                 pltpu.VMEM((half * rank, 2 * cols), bf16),
                 pltpu.VMEM((rank * (slab + 1), cols), f32),
                 pltpu.VMEM((rank // 2, slots * slab, 2 * rank), bf16),
                 pltpu.VMEM((slots * slab, rank), bf16),
-                pltpu.VMEM((depth_blocks * slab, rank), f32),
                 pltpu.VMEM((depth_blocks * slab, rank), f32),
                 pltpu.VMEM((rows * (slab + 1), cols), f32),
                 pltpu.VMEM((rows * (slab + 1), cols), f32),
@@ -262,7 +286,7 @@
         compiler_params=pltpu.CompilerParams(vmem_limit_bytes=48 * 2**20),
         cost_estimate=pl.CostEstimate(flops=10**9, bytes_accessed=16 * 2**20, transcendentals=0),
         name="terms",
-    )(counts, coords, data, weight, cube, cube_turned, row_table, col_table, factor_depth, core)
+    )(counts, coords, data, weight, cube, cube_turned, *pieces, core, depth)
 
 
 mark_rows = 16
@@ -309,21 +333,25 @@
 
 def fill_message(out, *parts):
     at = 0
-    marks = []
-    for part in parts:
+    mark = None
+    for which, part in enumerate(parts):
         lanes = part.shape[-1]
         flat, exponent = scaled(part.reshape(-1, lanes))
         out[at : at + flat.shape[0], :] = flat
         at += flat.shape[0]
-        marks.append(jnp.concatenate([exponent] * (mark_rows // 8), axis=0))
-    for mark in marks:
-        out[at : at + mark_rows, :] = mark
-        at += mark_rows
-
-
-def message_part(message, start, rows, part, parts):
-    mark = message.shape[0] - (parts - part) * mark_rows
-    return message[start : start + rows, :] * power_of(message[mark : mark + 8, :])[:1]
+        exponent = jnp.broadcast_to(exponent[:1], (mark_rows, lanes))
+        line = lax.broadcasted_iota(jnp.int32, exponent.shape, 0)
+        mark = exponent if mark is None else jnp.where(line >= which, exponent, mark)
+    out[at : at + mark_rows, :] = mark
+
+
+def message_part(message, start, rows, part):
+    mark = message.shape[0] - mark_rows + part
+    return message[start : start + rows, :] * power_of(message[mark : mark + 1, :])
+
+
+def message_shape(chunks, rank, lanes):
+    return jax.ShapeDtypeStruct((chunks * rank + mark_rows, lanes), f32)
 
 
 def tree_sum(values):
@@ -333,111 +361,119 @@
     return values[0]
 
 
-def after_cores_kernel(n_ia, n_ka, keep, got, cols_sum, own_core, own_depth, *outs):
-    messages, columns = outs[: n_ia - 1], outs[n_ia - 1 :]
+def after_cores_kernel(n_ia, n_ka, keep, got, own_core, own_depth, own_rows, *messages):
     half = n_ia * n_ka
     depth = keep[half + n_ka] + got[half + n_ka]
     flat, exponent = scaled(depth)
     own_depth[...] = flat * power_of(exponent)[:1]
     own_core[...] = keep[:n_ka] + got[:n_ka]
+    own_rows[...] = keep[half : half + n_ka] + got[half : half + n_ka]
     for mask in range(1, n_ia):
         lines = slice(mask * n_ka, (mask + 1) * n_ka)
         fill_message(messages[mask - 1], keep[lines] + got[lines], depth)
-    for mask in range(n_ka):
-        columns[mask][0] = keep[half + mask] + got[half + mask]
-        columns[mask][1] = cols_sum[mask]
-
-
-def after_cores(n_ia, n_ka, keep, got, cols_sum):
+
+
+def after_cores(n_ia, n_ka, keep, got):
     _, rank, lanes = keep.shape
-    message = jax.ShapeDtypeStruct(((n_ka + 1) * rank + 2 * mark_rows, lanes), f32)
-    outs = [jax.ShapeDtypeStruct((n_ka, rank, lanes), f32), jax.ShapeDtypeStruct((rank, lanes), f32)]
-    outs += [message] * (n_ia - 1) + [jax.ShapeDtypeStruct((2, rank, lanes), f32)] * n_ka
-    outs = vmem_call(
-        functools.partial(after_cores_kernel, n_ia, n_ka), tuple(outs), keep, got, cols_sum, name="after_cores"
-    )
-    return outs[0], outs[1], outs[2 : 1 + n_ia], outs[1 + n_ia :]
-
-
-def after_rows_kernel(own_core, own_depth, *refs):
-    *messages, out, depth_out = refs
+    outs = [jax.ShapeDtypeStruct(shape, f32) for shape in ((n_ka, rank, lanes), (rank, lanes), (n_ka, rank, lanes))]
+    outs += [message_shape(n_ka + 1, rank, lanes)] * (n_ia - 1)
+    outs = vmem_call(functools.partial(after_cores_kernel, n_ia, n_ka), tuple(outs), keep, got, name="after_cores")
+    return outs[0], outs[1], outs[2], outs[3:]
+
+
+def after_rows_kernel(n_ia, n_ka, own_core, own_depth, own_rows, cols_sum, *refs):
+    messages, depth_out, outs = refs[: n_ia - 1], refs[n_ia - 1], refs[n_ia:]
     count, rank, lanes = own_core.shape
     core = own_core[...].reshape(count * rank, lanes)
     depths = [own_depth[...]]
     for message in messages:
-        core = core + message_part(message, 0, count * rank, 0, 2)
-        depths.append(message_part(message, count * rank, rank, 1, 2))
+        core = core + message_part(message, 0, count * rank, 0)
+        depths.append(message_part(message, count * rank, rank, 1))
     depth_out[...] = tree_sum(depths)
-    fill_message(out, core)
-
-
-def after_rows(own_core, own_depth, messages):
+    for mask in range(n_ka):
+        fill_message(outs[mask], core, own_rows[mask], cols_sum[mask])
+
+
+def after_rows(n_ia, n_ka, own_core, own_depth, own_rows, cols_sum, messages):
     count, rank, lanes = own_core.shape
-    outs = (
-        jax.ShapeDtypeStruct((count * rank + mark_rows, lanes), f32),
-        jax.ShapeDtypeStruct((rank, lanes), f32),
+    outs = (jax.ShapeDtypeStruct((rank, lanes), f32),) + (message_shape(count + 2, rank, lanes),) * n_ka
+    outs = vmem_call(
+        functools.partial(after_rows_kernel, n_ia, n_ka),
+        outs,
+        own_core,
+        own_depth,
+        own_rows,
+        cols_sum,
+        *messages,
+        name="after_rows",
     )
-    return vmem_call(after_rows_kernel, outs, own_core, own_depth, *messages, name="after_rows")
-
-
-def after_depths_kernel(n_ka, *refs):
-    messages, columns, out, rows_out = refs[:n_ka], refs[n_ka : 2 * n_ka], refs[-2], refs[-1]
-    _, rank, lanes = columns[0].shape
+    return outs[0], outs[1:]
+
+
+def after_depths_kernel(n_ka, rank, *refs):
+    messages, out, rows_out = refs[:n_ka], refs[-2], refs[-1]
     cores = []
     for mask, message in enumerate(messages):
-        part = message_part(message, 0, n_ka * rank, 0, 1)
+        part = message_part(message, 0, n_ka * rank, 0)
         cores.append(jnp.concatenate([part[(at ^ mask) * rank : ((at ^ mask) + 1) * rank] for at in range(n_ka)]))
-    core = tree_sum(cores)
-    rows_out[...] = tree_sum(column[0] for column in columns)
-    fill_message(out, core, tree_sum(column[1] for column in columns))
-
-
-def after_depths(messages, columns):
-    n_ka = len(messages)
-    _, rank, lanes = columns[0].shape
-    outs = (
-        jax.ShapeDtypeStruct(((n_ka + 1) * rank + 2 * mark_rows, lanes), f32),
-        jax.ShapeDtypeStruct((rank, lanes), f32),
-    )
-    return vmem_call(
-        functools.partial(after_depths_kernel, n_ka), outs, *messages, *columns, name="after_depths"
-    )
-
-
-def unpack_kernel(sizes, rank, *refs):
+    rows_out[...] = tree_sum(message_part(message, n_ka * rank, rank, 1) for message in messages)
+    cols = tree_sum(message_part(message, (n_ka + 1) * rank, rank, 2) for message in messages)
+    fill_message(out, tree_sum(cores), cols)
+
+
+def after_depths(n_ka, rank, messages):
+    lanes = messages[0].shape[1]
+    outs = (message_shape(n_ka + 1, rank, lanes), jax.ShapeDtypeStruct((rank, lanes), f32))
+    return vmem_call(functools.partial(after_depths_kernel, n_ka, rank), outs, *messages, name="after_depths")
+
+
+def unpack_kernel(sizes, rank, first_message, *refs):
     n_ia, n_ka = sizes["ia"], sizes["ka"]
-    messages = refs[: 2 * n_ia]
-    core_out, cols_out, whole, sems = refs[2 * n_ia :]
+    messages = refs[:n_ia]
+    core_out, *cols_out, whole, sems = refs[n_ia if first_message == 0 else n_ia + 1 :]
     pairs = rank // 2
     own = masks_of(True, sizes)[2]
     copies = []
-    for at in range(2 * n_ia):
-        first = pl.multiple_of(((own // n_ka) ^ at) * n_ka, n_ka)
+    for at in range(n_ia):
+        first = pl.multiple_of(((own // n_ka) ^ (first_message + at)) * n_ka, n_ka)
         for mask in range(n_ka):
-            piece = message_part(messages[at], mask * rank, rank, 0, 2)
-            pair = first + (lax.rem(own, n_ka) ^ mask)
-            whole[pair] = piece[:, :rank]
-            whole[pairs + pair] = piece[:, rank:]
+            piece = message_part(messages[at], mask * rank, rank, 0)
+            line = lax.rem(own, n_ka) ^ mask
+            whole[at, 0, line] = piece[:, :rank]
+            whole[at, 1, line] = piece[:, rank:]
         for h in range(2):
             lines = pl.ds(h * pairs + first, n_ka)
-            copies.append(pltpu.make_async_copy(whole.at[lines], core_out.at[lines], sems.at[2 * at + h]))
+            copies.append(pltpu.make_async_copy(whole.at[at, h], core_out.at[lines], sems.at[2 * at + h]))
             copies[-1].start()
-    cols_out[...] = tree_sum(message_part(message, n_ka * rank, rank, 1, 2) for message in messages[:n_ia])
+    for out in cols_out:
+        out[...] = tree_sum(message_part(message, n_ka * rank, rank, 1) for message in messages)
     for copy in copies:
         copy.wait()
 
 
-def unpack(sizes, rank, messages):
+def unpack(sizes, rank, messages, core=None):
     lanes = messages[0].shape[1]
+    near = core is None
+    out_shape = [jax.ShapeDtypeStruct((rank, rank, rank), f32)]
+    out_specs = [pl.BlockSpec(memory_space=pltpu.HBM)]
+    if near:
+        out_shape.append(jax.ShapeDtypeStruct((rank, lanes), f32))
+        out_specs.append(pl.BlockSpec(memory_space=pltpu.VMEM))
     return pl.pallas_call(
-        functools.partial(unpack_kernel, sizes, rank),
-        out_shape=(jax.ShapeDtypeStruct((rank, rank, rank), f32), jax.ShapeDtypeStruct((rank, lanes), f32)),
-        in_specs=[pl.BlockSpec(memory_space=pltpu.VMEM)] * len(messages),
-        out_specs=(pl.BlockSpec(memory_space=pl.ANY), pl.BlockSpec(memory_space=pltpu.VMEM)),
-        scratch_shapes=[pltpu.VMEM((rank, rank, rank), f32), pltpu.SemaphoreType.DMA((2 * len(messages),))],
+        functools.partial(unpack_kernel, sizes, rank, 0 if near else sizes["ia"]),
+        out_shape=tuple(out_shape),
+        in_specs=[pl.BlockSpec(memory_space=pltpu.VMEM)] * len(messages)
+        + ([] if near else [pl.BlockSpec(memory_space=pltpu.HBM)]),
+        out_specs=tuple(out_specs),
+        scratch_shapes=[
+            pltpu.VMEM((len(messages), 2, sizes["ka"], rank, rank), f32),
+            pltpu.SemaphoreType.DMA((2 * len(messages),)),
+        ],
+        input_output_aliases={} if near else {len(messages): 0},
         compiler_params=pltpu.CompilerParams(vmem_limit_bytes=24 * 2**20),
-        name="unpack",
-    )(*messages)
+        cost_estimate=pl.CostEstimate(flops=10**6, bytes_accessed=4 * 2**20, transcendentals=0),
+        name="unpack_near" if near else "unpack_far",
+    )(*messages, *([] if near else [core]))
 
 
 def power_of_two(n):
@@ -468,33 +504,35 @@
         and factor_cols.shape[1] == cols
     )
 
-    cube, cube_turned = first_cubes(factor_depth, core_tensor, depth_blocks, slab)
-
     if by_swaps:
-        both = jnp.stack([factor_rows, factor_cols])
-        from_ka = [both] + [swap(both, "ka", n_ka, mask) for mask in range(1, n_ka)]
-        own_rows = jnp.stack([piece[0] for piece in from_ka])
-        row_table = jnp.concatenate([own_rows, swap(own_rows, "ja", n_ja, 1)])
-        col_table = jnp.stack([piece[1] for piece in from_ka])
+        own = jnp.stack([factor_rows, swap(factor_rows, "ja", n_ja, 1), factor_cols])
+        pieces = [own] + [swap(own, "ka", n_ka, mask) for mask in range(1, n_ka)]
+        row_spots = [(mask, line) for line in range(n_ja) for mask in range(n_ka)]
+        col_spots = [(mask, n_ja) for mask in range(n_ka)]
     else:
         row_table = lax.all_gather(factor_rows, ("ja", "ka"), axis=1, tiled=True)
         row_table = row_table.reshape(rank, row_chunks, rows).transpose(1, 0, 2)
         col_table = lax.all_gather(factor_cols, "ka", axis=1, tiled=True)
         col_table = col_table.reshape(rank, col_chunks, cols).transpose(1, 0, 2)
-
+        pieces = [row_table, col_table]
+        row_spots = [(0, line) for line in range(row_chunks)]
+        col_spots = [(1, line) for line in range(col_chunks)]
+
+    cube, cube_turned, core_pairs, own_depth = first_cubes(pieces[0], factor_depth, core_tensor, depth_blocks, slab)
     core_sum, rows_sum, cols_sum, depth_sum = terms(
         by_swaps,
         sizes,
+        row_spots,
+        col_spots,
         counts,
         coords,
         data,
         weight,
         cube,
         cube_turned,
-        row_table,
-        col_table,
-        factor_depth,
-        core_tensor,
+        pieces,
+        core_pairs,
+        own_depth,
     )
 
     if not by_swaps:
@@ -512,17 +550,18 @@
     keep = jnp.concatenate([core_sum[:half], rows_sum[:n_ka], depth_sum[None]])
     send = jnp.concatenate([core_sum[half:], rows_sum[n_ka:], depth_sum[None]])
     got = swap(send, "ja", n_ja, 1)
-    own_core, own_depth, messages, columns = after_cores(n_ia, n_ka, keep, got, cols_sum)
+    own_core, own_depth, own_rows, messages = after_cores(n_ia, n_ka, keep, got)
     messages = [swap(message.astype(wire), "ia", n_ia, at + 1).astype(f32) for at, message in enumerate(messages)]
-    columns = [columns[0]] + [swap(columns[mask], "ka", n_ka, mask) for mask in range(1, n_ka)]
-    message, depth_total = after_rows(own_core, own_depth, messages)
-    sent = message.astype(wire)
-    messages = [message] + [swap(sent, "ka", n_ka, mask).astype(f32) for mask in range(1, n_ka)]
-    message, rows_total = after_depths(messages, columns)
+    depth_total, messages = after_rows(n_ia, n_ka, own_core, own_depth, own_rows, cols_sum, messages)
+    messages = [messages[0]] + [
+        swap(messages[mask].astype(wire), "ka", n_ka, mask).astype(f32) for mask in range(1, n_ka)
+    ]
+    message, rows_total = after_depths(n_ka, rank, messages)
     sent = message.astype(wire)
     sent = [sent] + [swap(sent, "ia", n_ia, mask) for mask in range(1, n_ia)]
-    sent = sent + [swap(each, "ja", n_ja, 1) for each in sent]
-    core_total, cols_total = unpack(sizes, rank, [each.astype(f32) for each in sent])
+    other = [swap(each, "ja", n_ja, 1) for each in sent]
+    core_near, cols_total = unpack(sizes, rank, [each.astype(f32) for each in sent])
+    (core_total,) = unpack(sizes, rank, [each.astype(f32) for each in other], core_near)
     return (rows_total, cols_total, depth_total, core_total)
 
 

time: 66.9 us -> 59.5 us (0.89)
  starting transfers between devices: 30.5 us -> 23.3 us
  local copies, waits for them, and re-layouts: 5.79 us -> 2.92 us
  waiting for transfers between devices: 15 us -> 17.1 us
  other arithmetic: 2.61 us -> 1.2 us
  Pallas kernels: 11.5 us -> 12.8 us
    ppermute x21 -> x18, starting transfers between devices: 30.5 us -> 23.3 us  [swap(): return lax.ppermute(value, axis, [(at, at ^ mask) for at in range(size)])]
    unnamed x10 -> x5, local copies, waits for them, and re-layouts: 5.61 us -> 2.83 us
    ppermute x21 -> x18, waiting for transfers between devices: 15 us -> 17.1 us  [swap(): return lax.ppermute(value, axis, [(at, at ^ mask) for at in range(size)])]
    another operation x3 -> x1, other arithmetic: 2.2 us -> 0.74 us  [on_device(): jnp.stack([factor_rows, swap(factor_rows, 'ja', n_ja, 1), factor_cols])]
    pallas_call x2 -> x3, Pallas kernels: 7.97 us -> 8.72 us  [the longest x1 5.8 us: terms(): pl.pallas_call(functools.partial(terms_kernel, relative, sizes, row_spots...]
  transfers between devices with their start and end apart: 21 -> 18, of which waited for: 14 -> 10; matrix products, arithmetic and copies ran while one was open for 4% -> 2% of each run, Pallas kernels for 3% -> 7%
where the time goes in v4:
time: 59.5 us; the launch traced here: 58.9 us
  starting transfers between devices  23.3 us (39%)
  waiting for transfers between devices  17.1 us (29%)
  Pallas kernels  12.8 us (22%)
  local copies, waits for them, and re-layouts  2.92 us (5%)
  between operations  1.53 us (3%)
  other arithmetic  1.2 us (2%)
    ppermute x18, starting transfers between devices, swap(): return lax.ppermute(value, axis, [(at, at ^ mask) for at in range(size)])  23.3 us
    ppermute x18, waiting for transfers between devices, swap(): return lax.ppermute(value, axis, [(at, at ^ mask) for at in range(size)])  17.1 us
    pallas_call x1, Pallas kernels, terms(): pl.pallas_call(functools.partial(terms_kernel, relative, sizes, row_spots...  5.8 us
    pallas_call x2, Pallas kernels, unpack(): pl.pallas_call(functools.partial(unpack_kernel, sizes, rank, 0 if near el...  2.92 us
    unnamed x5, local copies, waits for them, and re-layouts  2.83 us
    pallas_call x1, Pallas kernels, first_cubes(): pl.pallas_call(functools.partial(cube_kernel, depth_blocks, slab), out_sh...  2.11 us
    pallas_call x3, Pallas kernels, vmem_call(): pl.pallas_call(kernel, out_shape=out_shape, in_specs=[pl.BlockSpec(memory...  1.97 us
  transfers between devices with their start and end apart: 18, of which 10 were waited for; matrix products, arithmetic and copies ran while one was open for 2% of the time, Pallas kernels for 7%

profile of v4, /device:TPU:0, one launch (start us, length us, event | category | flops | bytes accessed | tf_op | source)
XLA Modules:
  0.0 58.9 jit_solution(7927145675582085353)
XLA Ops:
  0.6 0.5 collective-permute-start
  1.8 0.8 %copy.13.coords = s32[1,1,5,3]{3,2,1,0:T(8,128)S(1)} copy(s32[1,1,5,3]{2,1,3,0:T(1,128)} %param.10) | data formatting | bytes 120 | tf_op args[2]
  2.6 0.0 collective-permute-done
  2.6 0.7 %pad_maximum_fusion.2.after.refs_0_ = bf16[3,64,128]{2,1,0:T(8,128)(2,1)S(1)} fusion(bf16[1,64,128]{2,1,0:T(8,128)(2,1)} %bitcast.9, bf16[1,64,128]{2,1,0:T(8,128)(2,1)S(1)} %bitcast.11, bf16[1,64,128]{2,1,0:T(8,128)(2,1)} %bitcast.10), kind=kLoop, calls=%fused_computation.2 | loop fusion | flops 49152 | bytes 98304 | tf_op jit(solution)/shard_map/stack | solution.py:508
  3.3 4.7 %collective-permute-start.3 = (bf16[3,64,128]{2,1,0:T(8,128)(2,1)S(1)}, bf16[3,64,128]{2,1,0:T(8,128)(2,1)S(1)}, u32[]{:S(2)}, u32[]{:S(2)}) collective-permute-start(bf16[3,64,128]{2,1,0:T(8,128)(2,1)S(1)} %pad_maximum_fusion.2.after.refs_0_), channel_id=1, source_target_pairs={{0,3},{1,2},{2,1},{3,0},{4,7},{5,6},{6,5},{7,4},{8,11},{9,10},{10,... | collective-permute-start | bytes 147464 | tf_op jit(solution)/shard_map/ppermute | solution.py:484
  8.0 0.0 collective-permute-start.2
  8.0 0.6 %collective-permute-start.1 = (bf16[3,64,128]{2,1,0:T(8,128)(2,1)S(1)}, bf16[3,64,128]{2,1,0:T(8,128)(2,1)S(1)}, u32[]{:S(2)}, u32[]{:S(2)}) collective-permute-start(bf16[3,64,128]{2,1,0:T(8,128)(2,1)S(1)} %pad_maximum_fusion.2.after.refs_0_), channel_id=1, source_target_pairs={{0,1},{1,0},{2,3},{3,2},{4,5},{5,4},{6,7},{7,6},{8,9},{9,8},{10,11... | collective-permute-start | bytes 147464 | tf_op jit(solution)/shard_map/ppermute | solution.py:484
  8.6 1.2 %copy-done = bf16[64,64,64]{2,1,0:T(8,128)(2,1)S(1)} copy-done((bf16[64,64,64]{2,1,0:T(8,128)(2,1)S(1)}, bf16[64,64,64]{2,1,0:T(8,128)(2,1)}, u32[]{:S(2)}) %copy-start) | copy-done | bytes 524312
  9.8 0.8 %copy-done.1 = bf16[64,512]{1,0:T(8,128)(2,1)S(1)} copy-done((bf16[64,512]{1,0:T(8,128)(2,1)S(1)}, bf16[64,512]{1,0:T(8,128)(2,1)}, u32[]{:S(2)}) %copy-start.1) | copy-done | bytes 65560
  10.7 2.1 %first_cubes.1 = (bf16[4,1024,128]{2,1,0:T(8,128)(2,1)S(1)}, bf16[4,128,1024]{2,1,0:T(8,128)(2,1)S(1)}, bf16[32,128,64]{2,1,0:T(8,128)(2,1)S(1)}, bf16[128,64]{1,0:T(8,128)(2,1)S(1)}) custom-call(bf16[3,64,128]{2,1,0:T(8,128)(2,1)S(1)} %pad_maximum_fusion.2.after.refs_0_, bf16[64,512]{1,0:T(8,128)(2,1)S(1)} %copy-done.1, bf16[64,64,64]{2,1,0:T(8,128)(2,1)S(1)} %copy-done), custom_call_target="tpu_custom_call" | custom-call | flops 1000000000 | bytes 4194304 | tf_op jit(solution)/shard_map/first_cubes/pallas_call | solution.py:73
  12.8 0.0 collective-permute-done.3.refs_3_
  12.8 0.3 collective-permute-done.2.refs_2_
  13.1 0.0 collective-permute-done.1.refs_1_
  13.1 5.8 %terms.1 = (f32[32,64,128]{2,1,0:T(8,128)S(1)}, f32[8,64,128]{2,1,0:T(8,128)S(1)}, f32[4,64,128]{2,1,0:T(8,128)S(1)}, f32[64,128]{1,0:T(8,128)S(1)}) custom-call(s32[1,1,1]{2,1,0:T(1,128)S(6)} %copy.15.counts, s32[1,1,5,3]{3,2,1,0:T(8,128)S(1)} %copy.13.coords, bf16[5,128,32,128]{3,2,1,0:T(8,128)(2,1)} %bitcast.7, bf16[5,128,32,128]{3,2,1,0:T(8,128)(2,1)} %bitcast.8, ...), custom_call_target="tpu_custom_call" | custom-call | flops 1000000000 | bytes 16777216 | tf_op jit(solution)/shard_map/terms/pallas_call | solution.py:257
  18.9 0.1 fusion.1
  19.0 0.1 pad_maximum_fusion
  19.2 0.1 collective-permute-start.4
  19.3 2.1 %collective-permute-done.4.got = f32[21,64,128]{2,1,0:T(8,128)S(1)} collective-permute-done((f32[21,64,128]{2,1,0:T(8,128)S(1)}, f32[21,64,128]{2,1,0:T(8,128)S(1)}, u32[]{:S(2)}, u32[]{:S(2)}) %collective-permute-start.4) | collective-permute-done | bytes 688160 | tf_op jit(solution)/shard_map/ppermute | solution.py:484
  21.4 0.3 after_cores.1
  21.7 4.2 %collective-permute-start.7 = (f16[336,128]{1,0:T(8,128)(2,1)S(1)}, f16[336,128]{1,0:T(8,128)(2,1)S(1)}, u32[]{:S(2)}, u32[]{:S(2)}) collective-permute-start(f16[336,128]{1,0:T(8,128)(2,1)S(1)} %convert_element_type.67), channel_id=1, source_target_pairs={{0,24},{8,16},{16,8},{24,0},{1,25},{9,17},{17,9},{25,1},{2,26},{10... | collective-permute-start | bytes 258056 | tf_op jit(solution)/shard_map/ppermute | solution.py:484
  25.9 0.5 collective-permute-start.6
  26.5 0.2 collective-permute-start.5
  26.7 2.2 %collective-permute-done.7 = f16[336,128]{1,0:T(8,128)(2,1)S(1)} collective-permute-done((f16[336,128]{1,0:T(8,128)(2,1)S(1)}, f16[336,128]{1,0:T(8,128)(2,1)S(1)}, u32[]{:S(2)}, u32[]{:S(2)}) %collective-permute-start.7) | collective-permute-done | bytes 86048 | tf_op jit(solution)/shard_map/ppermute | solution.py:484
  28.9 1.7 %collective-permute-done.6 = f16[336,128]{1,0:T(8,128)(2,1)S(1)} collective-permute-done((f16[336,128]{1,0:T(8,128)(2,1)S(1)}, f16[336,128]{1,0:T(8,128)(2,1)S(1)}, u32[]{:S(2)}, u32[]{:S(2)}) %collective-permute-start.6) | collective-permute-done | bytes 86048 | tf_op jit(solution)/shard_map/ppermute | solution.py:484
  30.6 0.4 collective-permute-done.5
  31.0 0.9 %after_rows.1 = (f32[64,128]{1,0:T(8,128)}, f32[400,128]{1,0:T(8,128)S(1)}, f32[400,128]{1,0:T(8,128)S(1)}, f32[400,128]{1,0:T(8,128)S(1)}, f32[400,128]{1,0:T(8,128)S(1)}) custom-call(f32[4,64,128]{2,1,0:T(8,128)S(1)} %get-tuple-element.34.own_core, f32[64,128]{1,0:T(8,128)S(1)} %get-tuple-element.35.own_depth, ...), custom_call_target="tpu_custom_call" | custom-call | tf_op jit(solution)/shard_map/after_rows/pallas_call | solution.py:297
  32.0 7.9 %collective-permute-start.10 = (f16[400,128]{1,0:T(8,128)(2,1)S(1)}, f16[400,128]{1,0:T(8,128)(2,1)S(1)}, u32[]{:S(2)}, u32[]{:S(2)}) collective-permute-start(f16[400,128]{1,0:T(8,128)(2,1)S(1)} %convert_element_type.73), channel_id=1, source_target_pairs={{0,3},{1,2},{2,1},{3,0},{4,7},{5,6},{6,5},{7,4},{8,11},{9,10},{10,... | collective-permute-start | bytes 307208 | tf_op jit(solution)/shard_map/ppermute | solution.py:484
  39.8 0.0 collective-permute-start.9
  39.9 0.7 %collective-permute-start.8 = (f16[400,128]{1,0:T(8,128)(2,1)S(1)}, f16[400,128]{1,0:T(8,128)(2,1)S(1)}, u32[]{:S(2)}, u32[]{:S(2)}) collective-permute-start(f16[400,128]{1,0:T(8,128)(2,1)S(1)} %convert_element_type.69), channel_id=1, source_target_pairs={{0,1},{1,0},{2,3},{3,2},{4,5},{5,4},{6,7},{7,6},{8,9},{9,8},{10,11... | collective-permute-start | bytes 307208 | tf_op jit(solution)/shard_map/ppermute | solution.py:484
  40.6 2.5 %collective-permute-done.10 = f16[400,128]{1,0:T(8,128)(2,1)S(1)} collective-permute-done((f16[400,128]{1,0:T(8,128)(2,1)S(1)}, f16[400,128]{1,0:T(8,128)(2,1)S(1)}, u32[]{:S(2)}, u32[]{:S(2)}) %collective-permute-start.10) | collective-permute-done | bytes 102432 | tf_op jit(solution)/shard_map/ppermute | solution.py:484
  43.1 4.4 %collective-permute-done.9 = f16[400,128]{1,0:T(8,128)(2,1)S(1)} collective-permute-done((f16[400,128]{1,0:T(8,128)(2,1)S(1)}, f16[400,128]{1,0:T(8,128)(2,1)S(1)}, u32[]{:S(2)}, u32[]{:S(2)}) %collective-permute-start.9) | collective-permute-done | bytes 102432 | tf_op jit(solution)/shard_map/ppermute | solution.py:484
  47.5 0.0 collective-permute-done.8
  47.5 0.8 %after_depths.1 = (f32[336,128]{1,0:T(8,128)S(1)}, f32[64,128]{1,0:T(8,128)}) custom-call(f32[400,128]{1,0:T(8,128)S(1)} %get-tuple-element.41.refs_0_, f32[400,128]{1,0:T(8,128)S(1)} %convert_element_type.70.refs_1_, f32[400,128]{1,0:T(8,128)S(1)} %convert_element_type.72.refs_2_, f32[400,128]{1,0:T(8,128)S(1)} %convert_element_type.74.refs_3_), custom_call_target="tpu_custom_call" | custom-call | tf_op jit(solution)/shard_map/after_depths/pallas_call | solution.py:297
  48.3 2.3 %collective-permute-start.13 = (f16[336,128]{1,0:T(8,128)(2,1)S(1)}, f16[336,128]{1,0:T(8,128)(2,1)S(1)}, u32[]{:S(2)}, u32[]{:S(2)}) collective-permute-start(f16[336,128]{1,0:T(8,128)(2,1)S(1)} %get-tuple-element.51), channel_id=1, source_target_pairs={{0,24},{8,16},{16,8},{24,0},{1,25},{9,17},{17,9},{25,1},{2,26},{10... | collective-permute-start | bytes 258056 | tf_op jit(solution)/shard_map/ppermute | solution.py:484
  50.6 0.3 collective-permute-start.12
  50.9 1.0 %collective-permute-start.11 = (f16[336,128]{1,0:T(8,128)(2,1)S(1)}, f16[336,128]{1,0:T(8,128)(2,1)S(1)}, u32[]{:S(2)}, u32[]{:S(2)}) collective-permute-start(f16[336,128]{1,0:T(8,128)(2,1)S(1)} %get-tuple-element.51), channel_id=1, source_target_pairs={{0,8},{8,0},{16,24},{24,16},{1,9},{9,1},{17,25},{25,17},{2,10},{10... | collective-permute-start | bytes 258056 | tf_op jit(solution)/shard_map/ppermute | solution.py:484
  51.9 0.0 collective-permute-start.14
  51.9 2.5 %collective-permute-done.13 = f16[336,128]{1,0:T(8,128)(2,1)S(1)} collective-permute-done((f16[336,128]{1,0:T(8,128)(2,1)S(1)}, f16[336,128]{1,0:T(8,128)(2,1)S(1)}, u32[]{:S(2)}, u32[]{:S(2)}) %collective-permute-start.13) | collective-permute-done | bytes 86048 | tf_op jit(solution)/shard_map/ppermute | solution.py:484
  54.4 0.0 collective-permute-start.17
  54.4 0.8 %collective-permute-done.12 = f16[336,128]{1,0:T(8,128)(2,1)S(1)} collective-permute-done((f16[336,128]{1,0:T(8,128)(2,1)S(1)}, f16[336,128]{1,0:T(8,128)(2,1)S(1)}, u32[]{:S(2)}, u32[]{:S(2)}) %collective-permute-start.12) | collective-permute-done | bytes 86048 | tf_op jit(solution)/shard_map/ppermute | solution.py:484
  55.2 0.0 collective-permute-start.16
  55.2 0.2 collective-permute-done.11
  55.4 0.3 collective-permute-start.15
  55.8 0.0 collective-permute-done.14
  55.8 1.8 %unpack_near.1 = (f32[64,64,64]{2,1,0:T(8,128)}, f32[64,128]{1,0:T(8,128)}) custom-call(f32[336,128]{1,0:T(8,128)S(1)} %get-tuple-element.50.refs_0_, f32[336,128]{1,0:T(8,128)S(1)} %convert_element_type.77.refs_1_, f32[336,128]{1,0:T(8,128)S(1)} %convert_element_type.78.refs_2_, f32[336,128]{1,0:T(8,128)S(1)} %convert_element_type.79.refs_3_), custom_call_target="tpu_custom_call" | custom-call | flops 1000000 | bytes 4194304 | tf_op jit(solution)/shard_map/unpack_near/pallas_call | solution.py:462
  57.6 0.0 collective-permute-done.17
  57.7 0.0 collective-permute-done.16
  57.7 1.1 %unpack_far.1 = f32[64,64,64]{2,1,0:T(8,128)} custom-call(f32[336,128]{1,0:T(8,128)S(1)} %convert_element_type.80.refs_0_, f32[336,128]{1,0:T(8,128)S(1)} %convert_element_type.81.refs_1_, f32[336,128]{1,0:T(8,128)S(1)} %convert_element_type.82.refs_2_, f32[336,128]{1,0:T(8,128)S(1)} %convert_element_type.83.refs_3_, ...), custom_call_target="tpu_custom_call", output_to_operand_aliasing={{}: (4, {})} | custom-call | flops 1000000 | bytes 4194304 | tf_op jit(solution)/shard_map/unpack_far/pallas_call | solution.py:462
  (24 shorter events, 0.3 us)
Async XLA Ops:
  0.6 1.9 %collective-permute-start = (bf16[64,128]{1,0:T(8,128)(2,1)}, bf16[64,128]{1,0:T(8,128)(2,1)S(1)}, u32[]{:S(2)}, u32[]{:S(2)}) collective-permute-start(bf16[64,128]{1,0:T(8,128)(2,1)} %param.12), channel_id=1, source_target_pairs={{0,4},{4,0},{1,5},{5,1},{2,6},{6,2},{3,7},{7,3},{8,12},{12,8},{9,1... | collective-permute-start | bytes 49160 | tf_op jit(solution)/shard_map/ppermute | solution.py:484
  3.3 9.5 %collective-permute-start.3 = (bf16[3,64,128]{2,1,0:T(8,128)(2,1)S(1)}, bf16[3,64,128]{2,1,0:T(8,128)(2,1)S(1)}, u32[]{:S(2)}, u32[]{:S(2)}) collective-permute-start(bf16[3,64,128]{2,1,0:T(8,128)(2,1)S(1)} %pad_maximum_fusion.2.after.refs_0_), channel_id=1, source_target_pairs={{0,3},{1,2},{2,1},{3,0},{4,7},{5,6},{6,5},{7,4},{8,11},{9,10},{10,... | collective-permute-start | bytes 147464 | tf_op jit(solution)/shard_map/ppermute | solution.py:484
  8.0 5.1 %collective-permute-start.2 = (bf16[3,64,128]{2,1,0:T(8,128)(2,1)S(1)}, bf16[3,64,128]{2,1,0:T(8,128)(2,1)S(1)}, u32[]{:S(2)}, u32[]{:S(2)}) collective-permute-start(bf16[3,64,128]{2,1,0:T(8,128)(2,1)S(1)} %pad_maximum_fusion.2.after.refs_0_), channel_id=1, source_target_pairs={{0,2},{1,3},{2,0},{3,1},{4,6},{5,7},{6,4},{7,5},{8,10},{9,11},{10,... | collective-permute-start | bytes 147464 | tf_op jit(solution)/shard_map/ppermute | solution.py:484
  8.0 5.1 %collective-permute-start.1 = (bf16[3,64,128]{2,1,0:T(8,128)(2,1)S(1)}, bf16[3,64,128]{2,1,0:T(8,128)(2,1)S(1)}, u32[]{:S(2)}, u32[]{:S(2)}) collective-permute-start(bf16[3,64,128]{2,1,0:T(8,128)(2,1)S(1)} %pad_maximum_fusion.2.after.refs_0_), channel_id=1, source_target_pairs={{0,1},{1,0},{2,3},{3,2},{4,5},{5,4},{6,7},{7,6},{8,9},{9,8},{10,11... | collective-permute-start | bytes 147464 | tf_op jit(solution)/shard_map/ppermute | solution.py:484
  8.6 1.2 %copy-start = (bf16[64,64,64]{2,1,0:T(8,128)(2,1)S(1)}, bf16[64,64,64]{2,1,0:T(8,128)(2,1)}, u32[]{:S(2)}) copy-start(bf16[64,64,64]{2,1,0:T(8,128)(2,1)} %core.1) | copy-start | bytes 1572868
  9.8 0.8 %copy-start.1 = (bf16[64,512]{1,0:T(8,128)(2,1)S(1)}, bf16[64,512]{1,0:T(8,128)(2,1)}, u32[]{:S(2)}) copy-start(bf16[64,512]{1,0:T(8,128)(2,1)} %factor_depth.1) | copy-start | bytes 196612
  19.2 2.2 %collective-permute-start.4 = (f32[21,64,128]{2,1,0:T(8,128)S(1)}, f32[21,64,128]{2,1,0:T(8,128)S(1)}, u32[]{:S(2)}, u32[]{:S(2)}) collective-permute-start(f32[21,64,128]{2,1,0:T(8,128)S(1)} %get-tuple-element.56), channel_id=1, source_target_pairs={{0,4},{4,0},{1,5},{5,1},{2,6},{6,2},{3,7},{7,3},{8,12},{12,8},{9,1... | collective-permute-start | bytes 2064392 | tf_op jit(solution)/shard_map/ppermute | solution.py:484
  21.7 7.1 %collective-permute-start.7 = (f16[336,128]{1,0:T(8,128)(2,1)S(1)}, f16[336,128]{1,0:T(8,128)(2,1)S(1)}, u32[]{:S(2)}, u32[]{:S(2)}) collective-permute-start(f16[336,128]{1,0:T(8,128)(2,1)S(1)} %convert_element_type.67), channel_id=1, source_target_pairs={{0,24},{8,16},{16,8},{24,0},{1,25},{9,17},{17,9},{25,1},{2,26},{10... | collective-permute-start | bytes 258056 | tf_op jit(solution)/shard_map/ppermute | solution.py:484
  25.9 4.7 %collective-permute-start.6 = (f16[336,128]{1,0:T(8,128)(2,1)S(1)}, f16[336,128]{1,0:T(8,128)(2,1)S(1)}, u32[]{:S(2)}, u32[]{:S(2)}) collective-permute-start(f16[336,128]{1,0:T(8,128)(2,1)S(1)} %convert_element_type.65), channel_id=1, source_target_pairs={{0,16},{8,24},{16,0},{24,8},{1,17},{9,25},{17,1},{25,9},{2,18},{10... | collective-permute-start | bytes 258056 | tf_op jit(solution)/shard_map/ppermute | solution.py:484
  26.5 4.6 %collective-permute-start.5 = (f16[336,128]{1,0:T(8,128)(2,1)S(1)}, f16[336,128]{1,0:T(8,128)(2,1)S(1)}, u32[]{:S(2)}, u32[]{:S(2)}) collective-permute-start(f16[336,128]{1,0:T(8,128)(2,1)S(1)} %convert_element_type.63), channel_id=1, source_target_pairs={{0,8},{8,0},{16,24},{24,16},{1,9},{9,1},{17,25},{25,17},{2,10},{10... | collective-permute-start | bytes 258056 | tf_op jit(solution)/shard_map/ppermute | solution.py:484
  32.0 11.1 %collective-permute-start.10 = (f16[400,128]{1,0:T(8,128)(2,1)S(1)}, f16[400,128]{1,0:T(8,128)(2,1)S(1)}, u32[]{:S(2)}, u32[]{:S(2)}) collective-permute-start(f16[400,128]{1,0:T(8,128)(2,1)S(1)} %convert_element_type.73), channel_id=1, source_target_pairs={{0,3},{1,2},{2,1},{3,0},{4,7},{5,6},{6,5},{7,4},{8,11},{9,10},{10,... | collective-permute-start | bytes 307208 | tf_op jit(solution)/shard_map/ppermute | solution.py:484
  39.8 7.6 %collective-permute-start.9 = (f16[400,128]{1,0:T(8,128)(2,1)S(1)}, f16[400,128]{1,0:T(8,128)(2,1)S(1)}, u32[]{:S(2)}, u32[]{:S(2)}) collective-permute-start(f16[400,128]{1,0:T(8,128)(2,1)S(1)} %convert_element_type.71), channel_id=1, source_target_pairs={{0,2},{1,3},{2,0},{3,1},{4,6},{5,7},{6,4},{7,5},{8,10},{9,11},{10,... | collective-permute-start | bytes 307208 | tf_op jit(solution)/shard_map/ppermute | solution.py:484
  39.9 7.6 %collective-permute-start.8 = (f16[400,128]{1,0:T(8,128)(2,1)S(1)}, f16[400,128]{1,0:T(8,128)(2,1)S(1)}, u32[]{:S(2)}, u32[]{:S(2)}) collective-permute-start(f16[400,128]{1,0:T(8,128)(2,1)S(1)} %convert_element_type.69), channel_id=1, source_target_pairs={{0,1},{1,0},{2,3},{3,2},{4,5},{5,4},{6,7},{7,6},{8,9},{9,8},{10,11... | collective-permute-start | bytes 307208 | tf_op jit(solution)/shard_map/ppermute | solution.py:484
  48.3 6.1 %collective-permute-start.13 = (f16[336,128]{1,0:T(8,128)(2,1)S(1)}, f16[336,128]{1,0:T(8,128)(2,1)S(1)}, u32[]{:S(2)}, u32[]{:S(2)}) collective-permute-start(f16[336,128]{1,0:T(8,128)(2,1)S(1)} %get-tuple-element.51), channel_id=1, source_target_pairs={{0,24},{8,16},{16,8},{24,0},{1,25},{9,17},{17,9},{25,1},{2,26},{10... | collective-permute-start | bytes 258056 | tf_op jit(solution)/shard_map/ppermute | solution.py:484
  50.6 4.6 %collective-permute-start.12 = (f16[336,128]{1,0:T(8,128)(2,1)S(1)}, f16[336,128]{1,0:T(8,128)(2,1)S(1)}, u32[]{:S(2)}, u32[]{:S(2)}) collective-permute-start(f16[336,128]{1,0:T(8,128)(2,1)S(1)} %get-tuple-element.51), channel_id=1, source_target_pairs={{0,16},{8,24},{16,0},{24,8},{1,17},{9,25},{17,1},{25,9},{2,18},{10... | collective-permute-start | bytes 258056 | tf_op jit(solution)/shard_map/ppermute | solution.py:484
  50.9 4.5 %collective-permute-start.11 = (f16[336,128]{1,0:T(8,128)(2,1)S(1)}, f16[336,128]{1,0:T(8,128)(2,1)S(1)}, u32[]{:S(2)}, u32[]{:S(2)}) collective-permute-start(f16[336,128]{1,0:T(8,128)(2,1)S(1)} %get-tuple-element.51), channel_id=1, source_target_pairs={{0,8},{8,0},{16,24},{24,16},{1,9},{9,1},{17,25},{25,17},{2,10},{10... | collective-permute-start | bytes 258056 | tf_op jit(solution)/shard_map/ppermute | solution.py:484
  51.9 3.9 %collective-permute-start.14 = (f16[336,128]{1,0:T(8,128)(2,1)S(1)}, f16[336,128]{1,0:T(8,128)(2,1)S(1)}, u32[]{:S(2)}, u32[]{:S(2)}) collective-permute-start(f16[336,128]{1,0:T(8,128)(2,1)S(1)} %get-tuple-element.51), channel_id=1, source_target_pairs={{0,4},{4,0},{1,5},{5,1},{2,6},{6,2},{3,7},{7,3},{8,12},{12,8},{9,1... | collective-permute-start | bytes 258056 | tf_op jit(solution)/shard_map/ppermute | solution.py:484
  54.4 3.2 %collective-permute-start.17 = (f16[336,128]{1,0:T(8,128)(2,1)S(1)}, f16[336,128]{1,0:T(8,128)(2,1)S(1)}, u32[]{:S(2)}, u32[]{:S(2)}) collective-permute-start(f16[336,128]{1,0:T(8,128)(2,1)S(1)} %collective-permute-done.13), channel_id=1, source_target_pairs={{0,4},{4,0},{1,5},{5,1},{2,6},{6,2},{3,7},{7,3},{8,12},{12,8},{9,1... | collective-permute-start | bytes 258056 | tf_op jit(solution)/shard_map/ppermute | solution.py:484
  55.2 2.4 %collective-permute-start.16 = (f16[336,128]{1,0:T(8,128)(2,1)S(1)}, f16[336,128]{1,0:T(8,128)(2,1)S(1)}, u32[]{:S(2)}, u32[]{:S(2)}) collective-permute-start(f16[336,128]{1,0:T(8,128)(2,1)S(1)} %collective-permute-done.12), channel_id=1, source_target_pairs={{0,4},{4,0},{1,5},{5,1},{2,6},{6,2},{3,7},{7,3},{8,12},{12,8},{9,1... | collective-permute-start | bytes 258056 | tf_op jit(solution)/shard_map/ppermute | solution.py:484
  55.4 2.3 %collective-permute-start.15 = (f16[336,128]{1,0:T(8,128)(2,1)S(1)}, f16[336,128]{1,0:T(8,128)(2,1)S(1)}, u32[]{:S(2)}, u32[]{:S(2)}) collective-permute-start(f16[336,128]{1,0:T(8,128)(2,1)S(1)} %collective-permute-done.11), channel_id=1, source_target_pairs={{0,4},{4,0},{1,5},{5,1},{2,6},{6,2},{3,7},{7,3},{8,12},{12,8},{9,1... | collective-permute-start | bytes 258056 | tf_op jit(solution)/shard_map/ppermute | solution.py:484

commit v5 on v4

--- a/solution.py
+++ b/solution.py
@@ -17,18 +17,28 @@
     return lax.dot_general(a, b, (contract, ((), ())), preferred_element_type=f32)
 
 
+def spread_out(source, target):
+    rows, slab, _ = source.shape
+    for i in range(rows):
+        target[i * (slab + 1) : i * (slab + 1) + slab, :] = source[i].astype(f32)
+
+
 def cube_kernel(
     depth_blocks,
     slab,
     after,
     factor_depth,
     core,
+    data,
+    weight,
     cube_out,
     cube_turned_out,
     core_out,
     depth_out,
+    spread,
     depth_here,
     core_here,
+    fetched,
     cube_wide,
     sems,
 ):
@@ -37,10 +47,15 @@
     pairs = rank // 2
     width = depth_blocks * slab
     start = pl.multiple_of(lax.axis_index("ka") * width, width)
+    copies = [
+        pltpu.make_async_copy(source.at[0], fetched.at[at], sems.at[2 + at]) for at, source in enumerate((data, weight))
+    ]
     core_copy = pltpu.make_async_copy(core, core_here, sems.at[0])
     core_copy.start()
     depth_copy = pltpu.make_async_copy(factor_depth.at[:, pl.ds(start, width)], depth_here, sems.at[1])
     depth_copy.start()
+    for copy in copies:
+        copy.start()
     depth_copy.wait()
     depth = depth_here[...].astype(f32).T
     depth_out[...] = depth.astype(bf16)
@@ -64,10 +79,14 @@
             block = cube_wide[at : at + rank, :]
             cube_out[t, kp * rank : (kp + 1) * rank, :] = block.astype(bf16)
         cube_turned_out[t] = cube_out[t].astype(f32).T.astype(bf16)
-
-
-def first_cubes(after, factor_depth, core, depth_blocks, slab):
+    for at, copy in enumerate(copies):
+        copy.wait()
+        spread_out(fetched.at[at], spread.at[at])
+
+
+def first_cubes(after, factor_depth, core, data, weight, depth_blocks):
     rank = core.shape[0]
+    _, rows, slab, cols = data.shape
     half = slab // 2
     width = depth_blocks * slab
     return pl.pallas_call(
@@ -77,19 +96,21 @@
             jax.ShapeDtypeStruct((depth_blocks, 2 * rank, half * rank), bf16),
             jax.ShapeDtypeStruct((rank // 2, 2 * rank, rank), bf16),
             jax.ShapeDtypeStruct((width, rank), bf16),
+            jax.ShapeDtypeStruct((2, rows * (slab + 1), cols), f32),
         ),
-        in_specs=[pl.BlockSpec(memory_space=pl.ANY)] + [pl.BlockSpec(memory_space=pltpu.HBM)] * 2,
-        out_specs=[pl.BlockSpec(memory_space=pltpu.VMEM)] * 4,
+        in_specs=[pl.BlockSpec(memory_space=pl.ANY)] + [pl.BlockSpec(memory_space=pltpu.HBM)] * 4,
+        out_specs=[pl.BlockSpec(memory_space=pltpu.VMEM)] * 5,
         scratch_shapes=[
             pltpu.VMEM((rank, width), bf16),
             pltpu.VMEM(core.shape, bf16),
+            pltpu.VMEM((2, rows, slab, cols), bf16),
             pltpu.VMEM((depth_blocks * half * (rank + 1), 2 * rank), f32),
-            pltpu.SemaphoreType.DMA((2,)),
+            pltpu.SemaphoreType.DMA((4,)),
         ],
-        compiler_params=pltpu.CompilerParams(vmem_limit_bytes=24 * 2**20),
+        compiler_params=pltpu.CompilerParams(vmem_limit_bytes=40 * 2**20),
         cost_estimate=pl.CostEstimate(flops=10**9, bytes_accessed=4 * 2**20, transcendentals=0),
         name="first_cubes",
-    )(after, factor_depth, core)
+    )(after, factor_depth, core, data, weight)
 
 
 def masks_of(relative, sizes):
@@ -104,10 +125,12 @@
     (
         core,
         depth_turned,
+        _,
         core_out,
         rows_out,
         cols_out,
         depth_out,
+        spread,
         row_table,
         col_table,
         wide_col,
@@ -116,12 +139,10 @@
         second_all,
         depth_all,
         depth_sum,
-        spread_data,
-        spread_weight,
+        fetched,
+        sems,
     ) = refs[len(pieces) :]
-    slot = pl.program_id(0)
-    slots = pl.num_programs(0)
-    _, rows, slab, cols = data.shape
+    slots, rows, slab, cols = data.shape
     pairs = core.shape[0]
     rank = 2 * pairs
     half = slab // 2
@@ -132,20 +153,42 @@
     col_base = lax.axis_index("ja") * col_table.shape[0]
     depth_base = lax.axis_index("ka") * depth_blocks
 
-    @pl.when(slot == 0)
-    def _():
-        second_all[...] = jnp.zeros_like(second_all)
-        depth_all[...] = jnp.zeros_like(depth_all)
-        depth_sum[...] = jnp.zeros_like(depth_sum)
-        rows_out[...] = jnp.zeros_like(rows_out)
-        cols_out[...] = jnp.zeros_like(cols_out)
-        wide_col[...] = jnp.zeros_like(wide_col)
-        for spots, table in ((row_spots, row_table), (col_spots, col_table)):
-            for at, (piece, line) in enumerate(spots):
-                table[at] = pieces[piece][line]
-
-    @pl.when(slot < count)
-    def _():
+    def fetches(slot):
+        side = lax.rem(slot, 2)
+        return [
+            pltpu.make_async_copy(source.at[slot], fetched.at[side, which], sems.at[side, which])
+            for which, source in enumerate((data, weight))
+        ]
+
+    def fetch(slot):
+        @pl.when(slot < count)
+        def _():
+            for copy in fetches(slot):
+                copy.start()
+
+    def arrive(slot):
+        for copy in fetches(slot):
+            copy.wait()
+
+    second_all[...] = jnp.zeros_like(second_all)
+    depth_all[...] = jnp.zeros_like(depth_all)
+    depth_sum[...] = jnp.zeros_like(depth_sum)
+    rows_out[...] = jnp.zeros_like(rows_out)
+    cols_out[...] = jnp.zeros_like(cols_out)
+    wide_col[...] = jnp.zeros_like(wide_col)
+    for spots, table in ((row_spots, row_table), (col_spots, col_table)):
+        for at, (piece, line) in enumerate(spots):
+            table[at] = pieces[piece][line]
+
+    def one_slot(slot, carry):
+        fetch(slot + 1)
+
+        @pl.when(slot > 0)
+        def _():
+            arrive(slot)
+            for which in range(2):
+                spread_out(fetched.at[lax.rem(slot, 2), which], spread.at[which])
+
         row_at = (coords[0, 0, slot, 0] - row_base) ^ row_mask
         col_at = (coords[0, 0, slot, 1] - col_base) ^ col_mask
         depth_at = coords[0, 0, slot, 2] - depth_base
@@ -160,10 +203,6 @@
         step = 4
         groups = half // step
         wide_factor = wide_col[...]
-        for source, target in ((data, spread_data), (weight, spread_weight)):
-            for i in range(rows):
-                target[i * (slab + 1) : i * (slab + 1) + slab, :] = source[0, i].astype(f32)
-
         def second_of(g):
             lines = cube[depth_at, g * step * rank : (g + 1) * step * rank, :]
             block = dot(lines, wide_factor).astype(bf16)
@@ -174,7 +213,7 @@
             for kp in range(step):
                 for h in range(2):
                     lines = pl.ds(h * half + g * step + kp, rows, stride=slab + 1)
-                    seen, scale = spread_data[lines, :], spread_weight[lines, :]
+                    seen, scale = spread[0, lines, :], spread[1, lines, :]
                     at = (kp * 2 + h) * cols
                     gap = model[:, at : at + cols] - seen
                     parts.append((scale * gap * resid_scale).astype(bf16))
@@ -214,62 +253,52 @@
             second_back = dot(ranked, wide_col[...], ((1,), (1,))).astype(bf16)
             second_all[first : first + 8, lines, :] = second_back.reshape(8, slab, 2 * rank)
 
-    @pl.when(slot == slots - 1)
-    def _():
-        def one_chunk(at, total):
-            pair = at ^ core_mask
-            second = second_all[pair]
-            total = total + dot(second, core[pair])
-            piece = dot(second, depth_all[...], ((0,), (0,)))
-            core_out[at] = jnp.concatenate([piece[:rank], piece[rank:]], axis=1)
-            return total
-
-        total = lax.fori_loop(0, pairs, one_chunk, jnp.zeros((second_all.shape[1], rank), f32), unroll=16)
-        for s in range(second_all.shape[1] // slab):
-
-            @pl.when(s < count)
-            def _():
-                at = coords[0, 0, s, 2] - depth_base
-                lines = pl.ds(pl.multiple_of(at * slab, slab), slab)
-                depth_sum[lines, :] += total[s * slab : (s + 1) * slab]
-
-        depth_out[...] = depth_sum[...].T
-
-
-def terms(relative, sizes, row_spots, col_spots, counts, coords, data, weight, cube, cube_turned, pieces, core, depth):
+        return carry
+
+    lax.fori_loop(0, count, one_slot, 0)
+
+    def one_chunk(at, total):
+        pair = at ^ core_mask
+        second = second_all[pair]
+        total = total + dot(second, core[pair])
+        piece = dot(second, depth_all[...], ((0,), (0,)))
+        core_out[at] = jnp.concatenate([piece[:rank], piece[rank:]], axis=1)
+        return total
+
+    total = lax.fori_loop(0, pairs, one_chunk, jnp.zeros((second_all.shape[1], rank), f32), unroll=16)
+    for s in range(slots):
+
+        @pl.when(s < count)
+        def _():
+            at = coords[0, 0, s, 2] - depth_base
+            lines = pl.ds(pl.multiple_of(at * slab, slab), slab)
+            depth_sum[lines, :] += total[s * slab : (s + 1) * slab]
+
+    depth_out[...] = depth_sum[...].T
+
+
+def terms(relative, sizes, row_spots, col_spots, counts, coords, data, weight, cube, cube_turned, pieces, core, depth, spread):
     slots, rows, slab, cols = data.shape
     rank = core.shape[2]
     half = slab // 2
     depth_blocks = cube.shape[0]
-
-    def live(slot, counts, coords):
-        return (jnp.minimum(slot, jnp.maximum(counts[0, 0, 0] - 1, 0)), 0, 0, 0)
-
-    def whole(array):
-        return pl.BlockSpec(array.shape, lambda slot, counts, coords: (0,) * len(array.shape))
 
     outs = (
         jax.ShapeDtypeStruct((rank // 2, rank, 2 * rank), f32),
         jax.ShapeDtypeStruct((len(row_spots), rank, rows), f32),
         jax.ShapeDtypeStruct((len(col_spots), rank, cols), f32),
         jax.ShapeDtypeStruct((rank, depth_blocks * slab), f32),
+        jax.ShapeDtypeStruct(spread.shape, f32),
     )
     return pl.pallas_call(
         functools.partial(terms_kernel, relative, sizes, row_spots, col_spots),
         out_shape=outs,
         grid_spec=pltpu.PrefetchScalarGridSpec(
             num_scalar_prefetch=2,
-            grid=(slots,),
-            in_specs=[
-                pl.BlockSpec((1, rows, slab, cols), live),
-                pl.BlockSpec((1, rows, slab, cols), live),
-                whole(cube),
-                whole(cube_turned),
-                *[whole(piece) for piece in pieces],
-                whole(core),
-                whole(depth),
-            ],
-            out_specs=[whole(out) for out in outs],
+            grid=(),
+            in_specs=[pl.BlockSpec(memory_space=pl.ANY)] * 2
+            + [pl.BlockSpec(memory_space=pltpu.VMEM)] * (5 + len(pieces)),
+            out_specs=[pl.BlockSpec(memory_space=pltpu.VMEM)] * 5,
             scratch_shapes=[
                 pltpu.VMEM((len(row_spots), rank, rows), bf16),
                 pltpu.VMEM((len(col_spots), rank, cols), bf16),
@@ -279,14 +308,15 @@
                 pltpu.VMEM((rank // 2, slots * slab, 2 * rank), bf16),
                 pltpu.VMEM((slots * slab, rank), bf16),
                 pltpu.VMEM((depth_blocks * slab, rank), f32),
-                pltpu.VMEM((rows * (slab + 1), cols), f32),
-                pltpu.VMEM((rows * (slab + 1), cols), f32),
+                pltpu.VMEM((2, 2, rows, slab, cols), bf16),
+                pltpu.SemaphoreType.DMA((2, 2)),
             ],
         ),
-        compiler_params=pltpu.CompilerParams(vmem_limit_bytes=48 * 2**20),
+        input_output_aliases={8 + len(pieces): 4},
+        compiler_params=pltpu.CompilerParams(vmem_limit_bytes=40 * 2**20),
         cost_estimate=pl.CostEstimate(flops=10**9, bytes_accessed=16 * 2**20, transcendentals=0),
         name="terms",
-    )(counts, coords, data, weight, cube, cube_turned, *pieces, core, depth)
+    )(counts, coords, data, weight, cube, cube_turned, *pieces, core, depth, spread)
 
 
 mark_rows = 16
@@ -489,8 +519,10 @@
     devices = n_ia * n_ja * n_ka
     rank = core_tensor.shape[0]
     _, _, slots, rows, slab, cols = observed.shape
-    data = observed.reshape(observed.shape[2:])
-    weight = weights.reshape(weights.shape[2:])
+    data = pltpu.with_memory_space_constraint(observed.reshape(observed.shape[2:]), pltpu.HBM)
+    weight = pltpu.with_memory_space_constraint(weights.reshape(weights.shape[2:]), pltpu.HBM)
+    core_here = pltpu.with_memory_space_constraint(core_tensor, pltpu.HBM)
+    depth_here = pltpu.with_memory_space_constraint(factor_depth, pltpu.HBM)
     row_chunks = factor_rows.shape[1] * n_ja * n_ka // rows
     col_chunks = factor_cols.shape[1] * n_ka // cols
     depth_blocks = factor_depth.shape[1] // n_ka // slab
@@ -518,8 +550,10 @@
         row_spots = [(0, line) for line in range(row_chunks)]
         col_spots = [(1, line) for line in range(col_chunks)]
 
-    cube, cube_turned, core_pairs, own_depth = first_cubes(pieces[0], factor_depth, core_tensor, depth_blocks, slab)
-    core_sum, rows_sum, cols_sum, depth_sum = terms(
+    cube, cube_turned, core_pairs, own_depth, spread = first_cubes(
+        pieces[0], depth_here, core_here, data, weight, depth_blocks
+    )
+    core_sum, rows_sum, cols_sum, depth_sum, _ = terms(
         by_swaps,
         sizes,
         row_spots,
@@ -533,6 +567,7 @@
         pieces,
         core_pairs,
         own_depth,
+        spread,
     )
 
     if not by_swaps:

time: 59.5 us -> 56.7 us (0.953); the launches traced: 58.9 us -> 57.5 us
  Pallas kernels: 12.8 us -> 18.8 us
  starting transfers between devices: 23.3 us -> 17.6 us
  local copies, waits for them, and re-layouts: 2.92 us -> 0.86 us
    ppermute x18, starting transfers between devices: 23.3 us -> 17.6 us  [swap(): return lax.ppermute(value, axis, [(at, at ^ mask) for at in range(size)])]
    pallas_call x1, Pallas kernels: 5.8 us -> 10.4 us  [terms(): pl.pallas_call(functools.partial(terms_kernel, relative, sizes, row_spots...]
    unnamed x5 -> x1, local copies, waits for them, and re-layouts: 2.83 us -> 0.77 us
    pallas_call x1, Pallas kernels: 2.11 us -> 3.44 us  [first_cubes(): pl.pallas_call(functools.partial(cube_kernel, depth_blocks, slab), out_sh...]
  transfers between devices with their start and end apart: 18 -> 18, of which waited for: 10 -> 10; matrix products, arithmetic and copies ran while one was open for 2% -> 2% of each run, Pallas kernels for 7% -> 9%
where the time goes in v5:
time: 56.7 us; the launch traced here: 57.5 us
  Pallas kernels  18.8 us (33%)
  starting transfers between devices  17.6 us (31%)
  waiting for transfers between devices  17.6 us (31%)
  between operations  1.54 us (3%)
  other arithmetic  1.2 us (2%)
  local copies, waits for them, and re-layouts  0.86 us (2%)
    ppermute x18, waiting for transfers between devices, swap(): return lax.ppermute(value, axis, [(at, at ^ mask) for at in range(size)])  17.6 us
    ppermute x18, starting transfers between devices, swap(): return lax.ppermute(value, axis, [(at, at ^ mask) for at in range(size)])  17.6 us
    pallas_call x1, Pallas kernels, terms(): pl.pallas_call(functools.partial(terms_kernel, relative, sizes, row_spots...  10.4 us
    pallas_call x1, Pallas kernels, first_cubes(): pl.pallas_call(functools.partial(cube_kernel, depth_blocks, slab), out_sh...  3.44 us
    pallas_call x2, Pallas kernels, unpack(): pl.pallas_call(functools.partial(unpack_kernel, sizes, rank, 0 if near el...  2.92 us
    pallas_call x3, Pallas kernels, vmem_call(): pl.pallas_call(kernel, out_shape=out_shape, in_specs=[pl.BlockSpec(memory...  1.97 us
  transfers between devices with their start and end apart: 18, of which 10 were waited for; matrix products, arithmetic and copies ran while one was open for 2% of the time, Pallas kernels for 9%

profile of v5, /device:TPU:0, one launch (start us, length us, event | category | flops | bytes accessed | tf_op | source)
XLA Modules:
  0.0 57.5 jit_solution(13186358883309923867)
XLA Ops:
  0.6 0.5 collective-permute-start
  1.8 0.8 %copy.14.coords = s32[1,1,5,3]{3,2,1,0:T(8,128)S(1)} copy(s32[1,1,5,3]{2,1,3,0:T(1,128)} %param.10) | data formatting | bytes 120 | tf_op args[2]
  2.6 0.0 collective-permute-done
  2.6 0.7 %pad_maximum_fusion.2.after.refs_0_ = bf16[3,64,128]{2,1,0:T(8,128)(2,1)S(1)} fusion(bf16[1,64,128]{2,1,0:T(8,128)(2,1)} %bitcast.11, bf16[1,64,128]{2,1,0:T(8,128)(2,1)S(1)} %bitcast.13, bf16[1,64,128]{2,1,0:T(8,128)(2,1)} %bitcast.12), kind=kLoop, calls=%fused_computation.2 | loop fusion | flops 49152 | bytes 98304 | tf_op jit(solution)/shard_map/stack | solution.py:540
  3.3 4.7 %collective-permute-start.3 = (bf16[3,64,128]{2,1,0:T(8,128)(2,1)S(1)}, bf16[3,64,128]{2,1,0:T(8,128)(2,1)S(1)}, u32[]{:S(2)}, u32[]{:S(2)}) collective-permute-start(bf16[3,64,128]{2,1,0:T(8,128)(2,1)S(1)} %pad_maximum_fusion.2.after.refs_0_), channel_id=1, source_target_pairs={{0,3},{1,2},{2,1},{3,0},{4,7},{5,6},{6,5},{7,4},{8,11},{9,10},{10,... | collective-permute-start | bytes 147464 | tf_op jit(solution)/shard_map/ppermute | solution.py:514
  8.0 0.0 collective-permute-start.2
  8.0 0.6 %collective-permute-start.1 = (bf16[3,64,128]{2,1,0:T(8,128)(2,1)S(1)}, bf16[3,64,128]{2,1,0:T(8,128)(2,1)S(1)}, u32[]{:S(2)}, u32[]{:S(2)}) collective-permute-start(bf16[3,64,128]{2,1,0:T(8,128)(2,1)S(1)} %pad_maximum_fusion.2.after.refs_0_), channel_id=1, source_target_pairs={{0,1},{1,0},{2,3},{3,2},{4,5},{5,4},{6,7},{7,6},{8,9},{9,8},{10,11... | collective-permute-start | bytes 147464 | tf_op jit(solution)/shard_map/ppermute | solution.py:514
  8.6 3.4 %first_cubes.1 = (bf16[4,1024,128]{2,1,0:T(8,128)(2,1)S(1)}, bf16[4,128,1024]{2,1,0:T(8,128)(2,1)S(1)}, bf16[32,128,64]{2,1,0:T(8,128)(2,1)S(1)}, bf16[128,64]{1,0:T(8,128)(2,1)S(1)}, f32[2,4224,128]{2,1,0:T(8,128)S(1)}) custom-call(bf16[3,64,128]{2,1,0:T(8,128)(2,1)S(1)} %pad_maximum_fusion.2.after.refs_0_, bf16[64,512]{1,0:T(8,128)(2,1)} %factor_depth.1, ...), custom_call_target="tpu_custom_call" | custom-call | flops 1000000000 | bytes 4194304 | tf_op jit(solution)/shard_map/first_cubes/pallas_call | solution.py:92
  12.1 0.0 collective-permute-done.3.refs_3_
  12.1 1.0 %collective-permute-done.2.refs_2_ = bf16[3,64,128]{2,1,0:T(8,128)(2,1)S(1)} collective-permute-done((bf16[3,64,128]{2,1,0:T(8,128)(2,1)S(1)}, bf16[3,64,128]{2,1,0:T(8,128)(2,1)S(1)}, u32[]{:S(2)}, u32[]{:S(2)}) %collective-permute-start.2) | collective-permute-done | bytes 49184 | tf_op jit(solution)/shard_map/ppermute | solution.py:514
  13.1 0.0 collective-permute-done.1.refs_1_
  13.1 10.4 %terms.1 = (f32[32,64,128]{2,1,0:T(8,128)S(1)}, f32[8,64,128]{2,1,0:T(8,128)S(1)}, f32[4,64,128]{2,1,0:T(8,128)S(1)}, f32[64,128]{1,0:T(8,128)S(1)}, f32[2,4224,128]{2,1,0:T(8,128)S(1)}) custom-call(s32[1,1,1]{2,1,0:T(1,128)S(6)} %copy.17.counts, s32[1,1,5,3]{3,2,1,0:T(8,128)S(1)} %copy.14.coords, ...), custom_call_target="tpu_custom_call", output_to_operand_aliasing={{4}: (12, {})} | custom-call | flops 1000000000 | bytes 16777216 | tf_op jit(solution)/shard_map/terms/pallas_call | solution.py:293
  23.6 0.1 fusion.1
  23.7 0.1 pad_maximum_fusion
  23.8 0.1 collective-permute-start.4
  23.9 2.1 %collective-permute-done.4.got = f32[21,64,128]{2,1,0:T(8,128)S(1)} collective-permute-done((f32[21,64,128]{2,1,0:T(8,128)S(1)}, f32[21,64,128]{2,1,0:T(8,128)S(1)}, u32[]{:S(2)}, u32[]{:S(2)}) %collective-permute-start.4) | collective-permute-done | bytes 688160 | tf_op jit(solution)/shard_map/ppermute | solution.py:514
  26.0 0.3 after_cores.1
  26.4 0.1 collective-permute-start.7
  26.4 2.9 %collective-permute-start.6 = (f16[336,128]{1,0:T(8,128)(2,1)S(1)}, f16[336,128]{1,0:T(8,128)(2,1)S(1)}, u32[]{:S(2)}, u32[]{:S(2)}) collective-permute-start(f16[336,128]{1,0:T(8,128)(2,1)S(1)} %convert_element_type.65), channel_id=1, source_target_pairs={{0,16},{8,24},{16,0},{24,8},{1,17},{9,25},{17,1},{25,9},{2,18},{10... | collective-permute-start | bytes 258056 | tf_op jit(solution)/shard_map/ppermute | solution.py:514
  29.4 0.6 %collective-permute-start.5 = (f16[336,128]{1,0:T(8,128)(2,1)S(1)}, f16[336,128]{1,0:T(8,128)(2,1)S(1)}, u32[]{:S(2)}, u32[]{:S(2)}) collective-permute-start(f16[336,128]{1,0:T(8,128)(2,1)S(1)} %convert_element_type.63), channel_id=1, source_target_pairs={{0,8},{8,0},{16,24},{24,16},{1,9},{9,1},{17,25},{25,17},{2,10},{10... | collective-permute-start | bytes 258056 | tf_op jit(solution)/shard_map/ppermute | solution.py:514
  30.0 2.5 %collective-permute-done.7 = f16[336,128]{1,0:T(8,128)(2,1)S(1)} collective-permute-done((f16[336,128]{1,0:T(8,128)(2,1)S(1)}, f16[336,128]{1,0:T(8,128)(2,1)S(1)}, u32[]{:S(2)}, u32[]{:S(2)}) %collective-permute-start.7) | collective-permute-done | bytes 86048 | tf_op jit(solution)/shard_map/ppermute | solution.py:514
  32.5 1.2 %collective-permute-done.6 = f16[336,128]{1,0:T(8,128)(2,1)S(1)} collective-permute-done((f16[336,128]{1,0:T(8,128)(2,1)S(1)}, f16[336,128]{1,0:T(8,128)(2,1)S(1)}, u32[]{:S(2)}, u32[]{:S(2)}) %collective-permute-start.6) | collective-permute-done | bytes 86048 | tf_op jit(solution)/shard_map/ppermute | solution.py:514
  33.8 0.2 collective-permute-done.5
  34.0 0.9 %after_rows.1 = (f32[64,128]{1,0:T(8,128)}, f32[400,128]{1,0:T(8,128)S(1)}, f32[400,128]{1,0:T(8,128)S(1)}, f32[400,128]{1,0:T(8,128)S(1)}, f32[400,128]{1,0:T(8,128)S(1)}) custom-call(f32[4,64,128]{2,1,0:T(8,128)S(1)} %get-tuple-element.36.own_core, f32[64,128]{1,0:T(8,128)S(1)} %get-tuple-element.37.own_depth, ...), custom_call_target="tpu_custom_call" | custom-call | tf_op jit(solution)/shard_map/after_rows/pallas_call | solution.py:327
  34.9 0.1 collective-permute-start.10
  35.0 2.6 %collective-permute-start.9 = (f16[400,128]{1,0:T(8,128)(2,1)S(1)}, f16[400,128]{1,0:T(8,128)(2,1)S(1)}, u32[]{:S(2)}, u32[]{:S(2)}) collective-permute-start(f16[400,128]{1,0:T(8,128)(2,1)S(1)} %convert_element_type.71), channel_id=1, source_target_pairs={{0,2},{1,3},{2,0},{3,1},{4,6},{5,7},{6,4},{7,5},{8,10},{9,11},{10,... | collective-permute-start | bytes 307208 | tf_op jit(solution)/shard_map/ppermute | solution.py:514
  37.6 1.8 %collective-permute-start.8 = (f16[400,128]{1,0:T(8,128)(2,1)S(1)}, f16[400,128]{1,0:T(8,128)(2,1)S(1)}, u32[]{:S(2)}, u32[]{:S(2)}) collective-permute-start(f16[400,128]{1,0:T(8,128)(2,1)S(1)} %convert_element_type.69), channel_id=1, source_target_pairs={{0,1},{1,0},{2,3},{3,2},{4,5},{5,4},{6,7},{7,6},{8,9},{9,8},{10,11... | collective-permute-start | bytes 307208 | tf_op jit(solution)/shard_map/ppermute | solution.py:514
  39.4 3.1 %collective-permute-done.10 = f16[400,128]{1,0:T(8,128)(2,1)S(1)} collective-permute-done((f16[400,128]{1,0:T(8,128)(2,1)S(1)}, f16[400,128]{1,0:T(8,128)(2,1)S(1)}, u32[]{:S(2)}, u32[]{:S(2)}) %collective-permute-start.10) | collective-permute-done | bytes 102432 | tf_op jit(solution)/shard_map/ppermute | solution.py:514
  42.6 3.5 %collective-permute-done.9 = f16[400,128]{1,0:T(8,128)(2,1)S(1)} collective-permute-done((f16[400,128]{1,0:T(8,128)(2,1)S(1)}, f16[400,128]{1,0:T(8,128)(2,1)S(1)}, u32[]{:S(2)}, u32[]{:S(2)}) %collective-permute-start.9) | collective-permute-done | bytes 102432 | tf_op jit(solution)/shard_map/ppermute | solution.py:514
  46.1 0.0 collective-permute-done.8
  46.1 0.8 %after_depths.1 = (f32[336,128]{1,0:T(8,128)S(1)}, f32[64,128]{1,0:T(8,128)}) custom-call(f32[400,128]{1,0:T(8,128)S(1)} %get-tuple-element.43.refs_0_, f32[400,128]{1,0:T(8,128)S(1)} %convert_element_type.70.refs_1_, f32[400,128]{1,0:T(8,128)S(1)} %convert_element_type.72.refs_2_, f32[400,128]{1,0:T(8,128)S(1)} %convert_element_type.74.refs_3_), custom_call_target="tpu_custom_call" | custom-call | tf_op jit(solution)/shard_map/after_depths/pallas_call | solution.py:327
  47.0 1.6 %collective-permute-start.13 = (f16[336,128]{1,0:T(8,128)(2,1)S(1)}, f16[336,128]{1,0:T(8,128)(2,1)S(1)}, u32[]{:S(2)}, u32[]{:S(2)}) collective-permute-start(f16[336,128]{1,0:T(8,128)(2,1)S(1)} %get-tuple-element.53), channel_id=1, source_target_pairs={{0,24},{8,16},{16,8},{24,0},{1,25},{9,17},{17,9},{25,1},{2,26},{10... | collective-permute-start | bytes 258056 | tf_op jit(solution)/shard_map/ppermute | solution.py:514
  48.6 1.2 %collective-permute-start.12 = (f16[336,128]{1,0:T(8,128)(2,1)S(1)}, f16[336,128]{1,0:T(8,128)(2,1)S(1)}, u32[]{:S(2)}, u32[]{:S(2)}) collective-permute-start(f16[336,128]{1,0:T(8,128)(2,1)S(1)} %get-tuple-element.53), channel_id=1, source_target_pairs={{0,16},{8,24},{16,0},{24,8},{1,17},{9,25},{17,1},{25,9},{2,18},{10... | collective-permute-start | bytes 258056 | tf_op jit(solution)/shard_map/ppermute | solution.py:514
  49.8 0.7 %collective-permute-start.11 = (f16[336,128]{1,0:T(8,128)(2,1)S(1)}, f16[336,128]{1,0:T(8,128)(2,1)S(1)}, u32[]{:S(2)}, u32[]{:S(2)}) collective-permute-start(f16[336,128]{1,0:T(8,128)(2,1)S(1)} %get-tuple-element.53), channel_id=1, source_target_pairs={{0,8},{8,0},{16,24},{24,16},{1,9},{9,1},{17,25},{25,17},{2,10},{10... | collective-permute-start | bytes 258056 | tf_op jit(solution)/shard_map/ppermute | solution.py:514
  50.5 0.0 collective-permute-start.14
  50.5 2.5 %collective-permute-done.13 = f16[336,128]{1,0:T(8,128)(2,1)S(1)} collective-permute-done((f16[336,128]{1,0:T(8,128)(2,1)S(1)}, f16[336,128]{1,0:T(8,128)(2,1)S(1)}, u32[]{:S(2)}, u32[]{:S(2)}) %collective-permute-start.13) | collective-permute-done | bytes 86048 | tf_op jit(solution)/shard_map/ppermute | solution.py:514
  53.0 0.0 collective-permute-start.17
  53.0 0.5 collective-permute-done.12
  53.5 0.0 collective-permute-start.16
  53.5 0.9 %collective-permute-done.11 = f16[336,128]{1,0:T(8,128)(2,1)S(1)} collective-permute-done((f16[336,128]{1,0:T(8,128)(2,1)S(1)}, f16[336,128]{1,0:T(8,128)(2,1)S(1)}, u32[]{:S(2)}, u32[]{:S(2)}) %collective-permute-start.11) | collective-permute-done | bytes 86048 | tf_op jit(solution)/shard_map/ppermute | solution.py:514
  54.4 0.0 collective-permute-start.15
  54.5 0.0 collective-permute-done.14
  54.5 1.8 %unpack_near.1 = (f32[64,64,64]{2,1,0:T(8,128)}, f32[64,128]{1,0:T(8,128)}) custom-call(f32[336,128]{1,0:T(8,128)S(1)} %get-tuple-element.52.refs_0_, f32[336,128]{1,0:T(8,128)S(1)} %convert_element_type.77.refs_1_, f32[336,128]{1,0:T(8,128)S(1)} %convert_element_type.78.refs_2_, f32[336,128]{1,0:T(8,128)S(1)} %convert_element_type.79.refs_3_), custom_call_target="tpu_custom_call" | custom-call | flops 1000000 | bytes 4194304 | tf_op jit(solution)/shard_map/unpack_near/pallas_call | solution.py:492
  56.3 0.0 collective-permute-done.17
  56.3 0.0 collective-permute-done.16
  56.4 0.0 collective-permute-done.15
  56.4 1.1 %unpack_far.1 = f32[64,64,64]{2,1,0:T(8,128)} custom-call(f32[336,128]{1,0:T(8,128)S(1)} %convert_element_type.80.refs_0_, f32[336,128]{1,0:T(8,128)S(1)} %convert_element_type.81.refs_1_, f32[336,128]{1,0:T(8,128)S(1)} %convert_element_type.82.refs_2_, f32[336,128]{1,0:T(8,128)S(1)} %convert_element_type.83.refs_3_, ...), custom_call_target="tpu_custom_call", output_to_operand_aliasing={{}: (4, {})} | custom-call | flops 1000000 | bytes 4194304 | tf_op jit(solution)/shard_map/unpack_far/pallas_call | solution.py:492
  (21 shorter events, 0.3 us)
Async XLA Ops:
  0.6 1.9 %collective-permute-start = (bf16[64,128]{1,0:T(8,128)(2,1)}, bf16[64,128]{1,0:T(8,128)(2,1)S(1)}, u32[]{:S(2)}, u32[]{:S(2)}) collective-permute-start(bf16[64,128]{1,0:T(8,128)(2,1)} %param.12), channel_id=1, source_target_pairs={{0,4},{4,0},{1,5},{5,1},{2,6},{6,2},{3,7},{7,3},{8,12},{12,8},{9,1... | collective-permute-start | bytes 49160 | tf_op jit(solution)/shard_map/ppermute | solution.py:514
  3.3 8.7 %collective-permute-start.3 = (bf16[3,64,128]{2,1,0:T(8,128)(2,1)S(1)}, bf16[3,64,128]{2,1,0:T(8,128)(2,1)S(1)}, u32[]{:S(2)}, u32[]{:S(2)}) collective-permute-start(bf16[3,64,128]{2,1,0:T(8,128)(2,1)S(1)} %pad_maximum_fusion.2.after.refs_0_), channel_id=1, source_target_pairs={{0,3},{1,2},{2,1},{3,0},{4,7},{5,6},{6,5},{7,4},{8,11},{9,10},{10,... | collective-permute-start | bytes 147464 | tf_op jit(solution)/shard_map/ppermute | solution.py:514
  8.0 5.1 %collective-permute-start.2 = (bf16[3,64,128]{2,1,0:T(8,128)(2,1)S(1)}, bf16[3,64,128]{2,1,0:T(8,128)(2,1)S(1)}, u32[]{:S(2)}, u32[]{:S(2)}) collective-permute-start(bf16[3,64,128]{2,1,0:T(8,128)(2,1)S(1)} %pad_maximum_fusion.2.after.refs_0_), channel_id=1, source_target_pairs={{0,2},{1,3},{2,0},{3,1},{4,6},{5,7},{6,4},{7,5},{8,10},{9,11},{10,... | collective-permute-start | bytes 147464 | tf_op jit(solution)/shard_map/ppermute | solution.py:514
  8.0 5.1 %collective-permute-start.1 = (bf16[3,64,128]{2,1,0:T(8,128)(2,1)S(1)}, bf16[3,64,128]{2,1,0:T(8,128)(2,1)S(1)}, u32[]{:S(2)}, u32[]{:S(2)}) collective-permute-start(bf16[3,64,128]{2,1,0:T(8,128)(2,1)S(1)} %pad_maximum_fusion.2.after.refs_0_), channel_id=1, source_target_pairs={{0,1},{1,0},{2,3},{3,2},{4,5},{5,4},{6,7},{7,6},{8,9},{9,8},{10,11... | collective-permute-start | bytes 147464 | tf_op jit(solution)/shard_map/ppermute | solution.py:514
  23.8 2.2 %collective-permute-start.4 = (f32[21,64,128]{2,1,0:T(8,128)S(1)}, f32[21,64,128]{2,1,0:T(8,128)S(1)}, u32[]{:S(2)}, u32[]{:S(2)}) collective-permute-start(f32[21,64,128]{2,1,0:T(8,128)S(1)} %get-tuple-element.58), channel_id=1, source_target_pairs={{0,4},{4,0},{1,5},{5,1},{2,6},{6,2},{3,7},{7,3},{8,12},{12,8},{9,1... | collective-permute-start | bytes 2064392 | tf_op jit(solution)/shard_map/ppermute | solution.py:514
  26.4 6.2 %collective-permute-start.7 = (f16[336,128]{1,0:T(8,128)(2,1)S(1)}, f16[336,128]{1,0:T(8,128)(2,1)S(1)}, u32[]{:S(2)}, u32[]{:S(2)}) collective-permute-start(f16[336,128]{1,0:T(8,128)(2,1)S(1)} %convert_element_type.67), channel_id=1, source_target_pairs={{0,24},{8,16},{16,8},{24,0},{1,25},{9,17},{17,9},{25,1},{2,26},{10... | collective-permute-start | bytes 258056 | tf_op jit(solution)/shard_map/ppermute | solution.py:514
  26.4 7.3 %collective-permute-start.6 = (f16[336,128]{1,0:T(8,128)(2,1)S(1)}, f16[336,128]{1,0:T(8,128)(2,1)S(1)}, u32[]{:S(2)}, u32[]{:S(2)}) collective-permute-start(f16[336,128]{1,0:T(8,128)(2,1)S(1)} %convert_element_type.65), channel_id=1, source_target_pairs={{0,16},{8,24},{16,0},{24,8},{1,17},{9,25},{17,1},{25,9},{2,18},{10... | collective-permute-start | bytes 258056 | tf_op jit(solution)/shard_map/ppermute | solution.py:514
  29.4 4.6 %collective-permute-start.5 = (f16[336,128]{1,0:T(8,128)(2,1)S(1)}, f16[336,128]{1,0:T(8,128)(2,1)S(1)}, u32[]{:S(2)}, u32[]{:S(2)}) collective-permute-start(f16[336,128]{1,0:T(8,128)(2,1)S(1)} %convert_element_type.63), channel_id=1, source_target_pairs={{0,8},{8,0},{16,24},{24,16},{1,9},{9,1},{17,25},{25,17},{2,10},{10... | collective-permute-start | bytes 258056 | tf_op jit(solution)/shard_map/ppermute | solution.py:514
  34.9 7.7 %collective-permute-start.10 = (f16[400,128]{1,0:T(8,128)(2,1)S(1)}, f16[400,128]{1,0:T(8,128)(2,1)S(1)}, u32[]{:S(2)}, u32[]{:S(2)}) collective-permute-start(f16[400,128]{1,0:T(8,128)(2,1)S(1)} %convert_element_type.73), channel_id=1, source_target_pairs={{0,3},{1,2},{2,1},{3,0},{4,7},{5,6},{6,5},{7,4},{8,11},{9,10},{10,... | collective-permute-start | bytes 307208 | tf_op jit(solution)/shard_map/ppermute | solution.py:514
  35.0 11.1 %collective-permute-start.9 = (f16[400,128]{1,0:T(8,128)(2,1)S(1)}, f16[400,128]{1,0:T(8,128)(2,1)S(1)}, u32[]{:S(2)}, u32[]{:S(2)}) collective-permute-start(f16[400,128]{1,0:T(8,128)(2,1)S(1)} %convert_element_type.71), channel_id=1, source_target_pairs={{0,2},{1,3},{2,0},{3,1},{4,6},{5,7},{6,4},{7,5},{8,10},{9,11},{10,... | collective-permute-start | bytes 307208 | tf_op jit(solution)/shard_map/ppermute | solution.py:514
  37.6 8.5 %collective-permute-start.8 = (f16[400,128]{1,0:T(8,128)(2,1)S(1)}, f16[400,128]{1,0:T(8,128)(2,1)S(1)}, u32[]{:S(2)}, u32[]{:S(2)}) collective-permute-start(f16[400,128]{1,0:T(8,128)(2,1)S(1)} %convert_element_type.69), channel_id=1, source_target_pairs={{0,1},{1,0},{2,3},{3,2},{4,5},{5,4},{6,7},{7,6},{8,9},{9,8},{10,11... | collective-permute-start | bytes 307208 | tf_op jit(solution)/shard_map/ppermute | solution.py:514
  47.0 6.0 %collective-permute-start.13 = (f16[336,128]{1,0:T(8,128)(2,1)S(1)}, f16[336,128]{1,0:T(8,128)(2,1)S(1)}, u32[]{:S(2)}, u32[]{:S(2)}) collective-permute-start(f16[336,128]{1,0:T(8,128)(2,1)S(1)} %get-tuple-element.53), channel_id=1, source_target_pairs={{0,24},{8,16},{16,8},{24,0},{1,25},{9,17},{17,9},{25,1},{2,26},{10... | collective-permute-start | bytes 258056 | tf_op jit(solution)/shard_map/ppermute | solution.py:514
  48.6 4.9 %collective-permute-start.12 = (f16[336,128]{1,0:T(8,128)(2,1)S(1)}, f16[336,128]{1,0:T(8,128)(2,1)S(1)}, u32[]{:S(2)}, u32[]{:S(2)}) collective-permute-start(f16[336,128]{1,0:T(8,128)(2,1)S(1)} %get-tuple-element.53), channel_id=1, source_target_pairs={{0,16},{8,24},{16,0},{24,8},{1,17},{9,25},{17,1},{25,9},{2,18},{10... | collective-permute-start | bytes 258056 | tf_op jit(solution)/shard_map/ppermute | solution.py:514
  49.8 4.6 %collective-permute-start.11 = (f16[336,128]{1,0:T(8,128)(2,1)S(1)}, f16[336,128]{1,0:T(8,128)(2,1)S(1)}, u32[]{:S(2)}, u32[]{:S(2)}) collective-permute-start(f16[336,128]{1,0:T(8,128)(2,1)S(1)} %get-tuple-element.53), channel_id=1, source_target_pairs={{0,8},{8,0},{16,24},{24,16},{1,9},{9,1},{17,25},{25,17},{2,10},{10... | collective-permute-start | bytes 258056 | tf_op jit(solution)/shard_map/ppermute | solution.py:514
  50.5 4.0 %collective-permute-start.14 = (f16[336,128]{1,0:T(8,128)(2,1)S(1)}, f16[336,128]{1,0:T(8,128)(2,1)S(1)}, u32[]{:S(2)}, u32[]{:S(2)}) collective-permute-start(f16[336,128]{1,0:T(8,128)(2,1)S(1)} %get-tuple-element.53), channel_id=1, source_target_pairs={{0,4},{4,0},{1,5},{5,1},{2,6},{6,2},{3,7},{7,3},{8,12},{12,8},{9,1... | collective-permute-start | bytes 258056 | tf_op jit(solution)/shard_map/ppermute | solution.py:514
  53.0 3.3 %collective-permute-start.17 = (f16[336,128]{1,0:T(8,128)(2,1)S(1)}, f16[336,128]{1,0:T(8,128)(2,1)S(1)}, u32[]{:S(2)}, u32[]{:S(2)}) collective-permute-start(f16[336,128]{1,0:T(8,128)(2,1)S(1)} %collective-permute-done.13), channel_id=1, source_target_pairs={{0,4},{4,0},{1,5},{5,1},{2,6},{6,2},{3,7},{7,3},{8,12},{12,8},{9,1... | collective-permute-start | bytes 258056 | tf_op jit(solution)/shard_map/ppermute | solution.py:514
  53.5 2.8 %collective-permute-start.16 = (f16[336,128]{1,0:T(8,128)(2,1)S(1)}, f16[336,128]{1,0:T(8,128)(2,1)S(1)}, u32[]{:S(2)}, u32[]{:S(2)}) collective-permute-start(f16[336,128]{1,0:T(8,128)(2,1)S(1)} %collective-permute-done.12), channel_id=1, source_target_pairs={{0,4},{4,0},{1,5},{5,1},{2,6},{6,2},{3,7},{7,3},{8,12},{12,8},{9,1... | collective-permute-start | bytes 258056 | tf_op jit(solution)/shard_map/ppermute | solution.py:514
  54.4 1.9 %collective-permute-start.15 = (f16[336,128]{1,0:T(8,128)(2,1)S(1)}, f16[336,128]{1,0:T(8,128)(2,1)S(1)}, u32[]{:S(2)}, u32[]{:S(2)}) collective-permute-start(f16[336,128]{1,0:T(8,128)(2,1)S(1)} %collective-permute-done.11), channel_id=1, source_target_pairs={{0,4},{4,0},{1,5},{5,1},{2,6},{6,2},{3,7},{7,3},{8,12},{12,8},{9,1... | collective-permute-start | bytes 258056 | tf_op jit(solution)/shard_map/ppermute | solution.py:514

commit v6 on v5

--- a/solution.py
+++ b/solution.py
@@ -29,16 +29,13 @@
     after,
     factor_depth,
     core,
-    data,
-    weight,
+    coords,
     cube_out,
-    cube_turned_out,
     core_out,
     depth_out,
-    spread,
+    coords_out,
     depth_here,
     core_here,
-    fetched,
     cube_wide,
     sems,
 ):
@@ -47,14 +44,10 @@
     pairs = rank // 2
     width = depth_blocks * slab
     start = pl.multiple_of(lax.axis_index("ka") * width, width)
-    copies = [
-        pltpu.make_async_copy(source.at[0], fetched.at[at], sems.at[2 + at]) for at, source in enumerate((data, weight))
-    ]
     core_copy = pltpu.make_async_copy(core, core_here, sems.at[0])
-    core_copy.start()
     depth_copy = pltpu.make_async_copy(factor_depth.at[:, pl.ds(start, width)], depth_here, sems.at[1])
-    depth_copy.start()
-    for copy in copies:
+    coords_copy = pltpu.make_async_copy(coords, coords_out, sems.at[2])
+    for copy in (depth_copy, core_copy, coords_copy):
         copy.start()
     depth_copy.wait()
     depth = depth_here[...].astype(f32).T
@@ -78,39 +71,69 @@
             at = (t * half + kp) * (rank + 1)
             block = cube_wide[at : at + rank, :]
             cube_out[t, kp * rank : (kp + 1) * rank, :] = block.astype(bf16)
-        cube_turned_out[t] = cube_out[t].astype(f32).T.astype(bf16)
-    for at, copy in enumerate(copies):
-        copy.wait()
-        spread_out(fetched.at[at], spread.at[at])
-
-
-def first_cubes(after, factor_depth, core, data, weight, depth_blocks):
+    coords_copy.wait()
+
+
+def first_cubes(after, factor_depth, core, coords, depth_blocks, slab):
     rank = core.shape[0]
-    _, rows, slab, cols = data.shape
     half = slab // 2
     width = depth_blocks * slab
     return pl.pallas_call(
         functools.partial(cube_kernel, depth_blocks, slab),
         out_shape=(
             jax.ShapeDtypeStruct((depth_blocks, half * rank, 2 * rank), bf16),
-            jax.ShapeDtypeStruct((depth_blocks, 2 * rank, half * rank), bf16),
             jax.ShapeDtypeStruct((rank // 2, 2 * rank, rank), bf16),
             jax.ShapeDtypeStruct((width, rank), bf16),
-            jax.ShapeDtypeStruct((2, rows * (slab + 1), cols), f32),
+            jax.ShapeDtypeStruct(coords.shape, coords.dtype),
         ),
-        in_specs=[pl.BlockSpec(memory_space=pl.ANY)] + [pl.BlockSpec(memory_space=pltpu.HBM)] * 4,
-        out_specs=[pl.BlockSpec(memory_space=pltpu.VMEM)] * 5,
+        in_specs=[pl.BlockSpec(memory_space=pl.ANY)] + [pl.BlockSpec(memory_space=pltpu.HBM)] * 3,
+        out_specs=[pl.BlockSpec(memory_space=pltpu.VMEM)] * 3 + [pl.BlockSpec(memory_space=pltpu.SMEM)],
         scratch_shapes=[
             pltpu.VMEM((rank, width), bf16),
             pltpu.VMEM(core.shape, bf16),
-            pltpu.VMEM((2, rows, slab, cols), bf16),
             pltpu.VMEM((depth_blocks * half * (rank + 1), 2 * rank), f32),
-            pltpu.SemaphoreType.DMA((4,)),
+            pltpu.SemaphoreType.DMA((3,)),
         ],
-        compiler_params=pltpu.CompilerParams(vmem_limit_bytes=40 * 2**20),
+        compiler_params=pltpu.CompilerParams(vmem_limit_bytes=24 * 2**20),
         cost_estimate=pl.CostEstimate(flops=10**9, bytes_accessed=4 * 2**20, transcendentals=0),
         name="first_cubes",
-    )(after, factor_depth, core, data, weight)
+    )(after, factor_depth, core, coords)
+
+
+def first_slot_kernel(after, cube, data, weight, turned, spread, fetched, sems):
+    copies = [
+        pltpu.make_async_copy(source.at[0], fetched.at[at], sems.at[at]) for at, source in enumerate((data, weight))
+    ]
+    for copy in copies:
+        copy.start()
+    for t in range(cube.shape[0]):
+        turned[t] = cube[t].astype(f32).T.astype(bf16)
+    for at, copy in enumerate(copies):
+        copy.wait()
+        spread_out(fetched.at[at], spread.at[at])
+
+
+def first_slot(after, cube, data, weight):
+    _, rows, slab, cols = data.shape
+    blocks, height, width = cube.shape
+    return pl.pallas_call(
+        first_slot_kernel,
+        out_shape=(
+            jax.ShapeDtypeStruct((blocks, width, height), bf16),
+            jax.ShapeDtypeStruct((2, rows * (slab + 1), cols), f32),
+        ),
+        in_specs=[
+            pl.BlockSpec(memory_space=pl.ANY),
+            pl.BlockSpec(memory_space=pltpu.VMEM),
+            pl.BlockSpec(memory_space=pltpu.HBM),
+            pl.BlockSpec(memory_space=pltpu.HBM),
+        ],
+        out_specs=[pl.BlockSpec(memory_space=pltpu.VMEM)] * 2,
+        scratch_shapes=[pltpu.VMEM((2, rows, slab, cols), bf16), pltpu.SemaphoreType.DMA((2,))],
+        compiler_params=pltpu.CompilerParams(vmem_limit_bytes=32 * 2**20),
+        cost_estimate=pl.CostEstimate(flops=10**9, bytes_accessed=4 * 2**20, transcendentals=0),
+        name="first_slot",
+    )(after, cube, data, weight)
 
 
 def masks_of(relative, sizes):
@@ -170,8 +193,14 @@
         for copy in fetches(slot):
             copy.wait()
 
-    second_all[...] = jnp.zeros_like(second_all)
-    depth_all[...] = jnp.zeros_like(depth_all)
+    for s in range(slots):
+
+        @pl.when(s >= count)
+        def _():
+            lines = slice(s * slab, (s + 1) * slab)
+            second_all[:, lines, :] = jnp.zeros((pairs, slab, 2 * rank), bf16)
+            depth_all[lines, :] = jnp.zeros((slab, rank), bf16)
+
     depth_sum[...] = jnp.zeros_like(depth_sum)
     rows_out[...] = jnp.zeros_like(rows_out)
     cols_out[...] = jnp.zeros_like(cols_out)
@@ -189,9 +218,9 @@
             for which in range(2):
                 spread_out(fetched.at[lax.rem(slot, 2), which], spread.at[which])
 
-        row_at = (coords[0, 0, slot, 0] - row_base) ^ row_mask
-        col_at = (coords[0, 0, slot, 1] - col_base) ^ col_mask
-        depth_at = coords[0, 0, slot, 2] - depth_base
+        row_at = (coords[0, 0, 0, slot] - row_base) ^ row_mask
+        col_at = (coords[0, 1, 0, slot] - col_base) ^ col_mask
+        depth_at = coords[0, 2, 0, slot] - depth_base
         row_factor = row_table[row_at]
         row_turned = row_factor.astype(f32).T.astype(bf16)
         col_factor = col_table[col_at]
@@ -200,7 +229,7 @@
         own_depth = depth_turned[pl.ds(pl.multiple_of(depth_at * slab, slab), slab), :]
         depth_all[pl.ds(pl.multiple_of(slot * slab, slab), slab), :] = own_depth
 
-        step = 4
+        step = 8
         groups = half // step
         wide_factor = wide_col[...]
         def second_of(g):
@@ -230,7 +259,7 @@
                     lines = pl.ds(h * half + g * step + kp, rank, stride=slab + 1)
                     by_rank[lines, :] = wider[:, h * cols : (h + 1) * cols]
 
-        row_sum = jnp.zeros((rank, rows), f32)
+        row_sum = jnp.zeros((rows, rank), f32)
         seconds = [second_of(g) for g in range(groups)]
         models = [None] * groups
         models[0] = dot(row_turned, seconds[0])
@@ -239,8 +268,8 @@
                 models[g + 1] = dot(row_turned, seconds[g + 1])
             residual = residual_of(g, models[g])
             keep_back(g, dot(row_factor, residual))
-            row_sum = row_sum + dot(seconds[g], residual, ((1,), (1,)))
-        rows_out[row_at] += row_sum
+            row_sum = row_sum + dot(residual, seconds[g], ((1,), (1,)))
+        rows_out[row_at] += row_sum.T
         wide = dot(cube_turned[depth_at], backward[...])
         cols_out[col_at] += wide[:rank, :cols] + wide[rank:, cols:]
         lines = pl.ds(pl.multiple_of(slot * slab, slab), slab)
@@ -265,12 +294,12 @@
         core_out[at] = jnp.concatenate([piece[:rank], piece[rank:]], axis=1)
         return total
 
-    total = lax.fori_loop(0, pairs, one_chunk, jnp.zeros((second_all.shape[1], rank), f32), unroll=16)
+    total = lax.fori_loop(0, pairs, one_chunk, jnp.zeros((second_all.shape[1], rank), f32), unroll=32)
     for s in range(slots):
 
         @pl.when(s < count)
         def _():
-            at = coords[0, 0, s, 2] - depth_base
+            at = coords[0, 2, 0, s] - depth_base
             lines = pl.ds(pl.multiple_of(at * slab, slab), slab)
             depth_sum[lines, :] += total[s * slab : (s + 1) * slab]
 
@@ -294,9 +323,10 @@
         functools.partial(terms_kernel, relative, sizes, row_spots, col_spots),
         out_shape=outs,
         grid_spec=pltpu.PrefetchScalarGridSpec(
-            num_scalar_prefetch=2,
+            num_scalar_prefetch=0,
             grid=(),
-            in_specs=[pl.BlockSpec(memory_space=pl.ANY)] * 2
+            in_specs=[pl.BlockSpec(memory_space=pltpu.SMEM)] * 2
+            + [pl.BlockSpec(memory_space=pltpu.HBM)] * 2
             + [pl.BlockSpec(memory_space=pltpu.VMEM)] * (5 + len(pieces)),
             out_specs=[pl.BlockSpec(memory_space=pltpu.VMEM)] * 5,
             scratch_shapes=[
@@ -364,12 +394,10 @@
 def fill_message(out, *parts):
     at = 0
     mark = None
-    for which, part in enumerate(parts):
-        lanes = part.shape[-1]
-        flat, exponent = scaled(part.reshape(-1, lanes))
+    for which, (flat, exponent) in enumerate(parts):
         out[at : at + flat.shape[0], :] = flat
         at += flat.shape[0]
-        exponent = jnp.broadcast_to(exponent[:1], (mark_rows, lanes))
+        exponent = jnp.broadcast_to(exponent[:1], (mark_rows, flat.shape[1]))
         line = lax.broadcasted_iota(jnp.int32, exponent.shape, 0)
         mark = exponent if mark is None else jnp.where(line >= which, exponent, mark)
     out[at : at + mark_rows, :] = mark
@@ -400,7 +428,8 @@
     own_rows[...] = keep[half : half + n_ka] + got[half : half + n_ka]
     for mask in range(1, n_ia):
         lines = slice(mask * n_ka, (mask + 1) * n_ka)
-        fill_message(messages[mask - 1], keep[lines] + got[lines], depth)
+        core = (keep[lines] + got[lines]).reshape(-1, depth.shape[1])
+        fill_message(messages[mask - 1], scaled(core), (flat, exponent))
 
 
 def after_cores(n_ia, n_ka, keep, got):
@@ -420,8 +449,9 @@
         core = core + message_part(message, 0, count * rank, 0)
         depths.append(message_part(message, count * rank, rank, 1))
     depth_out[...] = tree_sum(depths)
+    flat, exponent = scaled(core)
     for mask in range(n_ka):
-        fill_message(outs[mask], core, own_rows[mask], cols_sum[mask])
+        fill_message(outs[mask], (flat, exponent), scaled(own_rows[mask]), scaled(cols_sum[mask]))
 
 
 def after_rows(n_ia, n_ka, own_core, own_depth, own_rows, cols_sum, messages):
@@ -448,7 +478,7 @@
         cores.append(jnp.concatenate([part[(at ^ mask) * rank : ((at ^ mask) + 1) * rank] for at in range(n_ka)]))
     rows_out[...] = tree_sum(message_part(message, n_ka * rank, rank, 1) for message in messages)
     cols = tree_sum(message_part(message, (n_ka + 1) * rank, rank, 2) for message in messages)
-    fill_message(out, tree_sum(cores), cols)
+    fill_message(out, scaled(tree_sum(cores)), scaled(cols))
 
 
 def after_depths(n_ka, rank, messages):
@@ -537,10 +567,12 @@
     )
 
     if by_swaps:
-        own = jnp.stack([factor_rows, swap(factor_rows, "ja", n_ja, 1), factor_cols])
-        pieces = [own] + [swap(own, "ka", n_ka, mask) for mask in range(1, n_ka)]
-        row_spots = [(mask, line) for line in range(n_ja) for mask in range(n_ka)]
-        col_spots = [(mask, n_ja) for mask in range(n_ka)]
+        own = jnp.stack([factor_rows, factor_cols])
+        near = [own] + [swap(own, "ka", n_ka, mask) for mask in range(1, n_ka)]
+        near_rows = jnp.stack([piece[0] for piece in near])
+        pieces = near + [swap(near_rows, "ja", n_ja, 1)]
+        row_spots = [(mask, 0) for mask in range(n_ka)] + [(n_ka, mask) for mask in range(n_ka)]
+        col_spots = [(mask, 1) for mask in range(n_ka)]
     else:
         row_table = lax.all_gather(factor_rows, ("ja", "ka"), axis=1, tiled=True)
         row_table = row_table.reshape(rank, row_chunks, rows).transpose(1, 0, 2)
@@ -548,11 +580,18 @@
         col_table = col_table.reshape(rank, col_chunks, cols).transpose(1, 0, 2)
         pieces = [row_table, col_table]
         row_spots = [(0, line) for line in range(row_chunks)]
+        own, near_rows = row_table, row_table
         col_spots = [(1, line) for line in range(col_chunks)]
 
-    cube, cube_turned, core_pairs, own_depth, spread = first_cubes(
-        pieces[0], depth_here, core_here, data, weight, depth_blocks
+    cube, core_pairs, own_depth, coords = first_cubes(
+        own,
+        depth_here,
+        core_here,
+        pltpu.with_memory_space_constraint(coords.transpose(0, 3, 1, 2), pltpu.HBM),
+        depth_blocks,
+        slab,
     )
+    cube_turned, spread = first_slot(near_rows, cube, data, weight)
     core_sum, rows_sum, cols_sum, depth_sum, _ = terms(
         by_swaps,
         sizes,

time: 56.7 us -> 58.8 us (1.037); the launches traced: 57.5 us -> 58.2 us
  starting transfers between devices: 17.6 us -> 21.4 us
  Pallas kernels: 18.8 us -> 15.4 us
  local copies, waits for them, and re-layouts: 0.86 us -> 0.13 us
  other arithmetic: 1.2 us -> 1.92 us
    pallas_call x1, Pallas kernels: 10.4 us -> 5.26 us  [terms(): pl.pallas_call(functools.partial(terms_kernel, relative, sizes, row_spots...]
    ppermute x18, starting transfers between devices: 17.6 us -> 21.4 us  [swap(): return lax.ppermute(value, axis, [(at, at ^ mask) for at in range(size)])]
    pallas_call x0 -> x1, Pallas kernels: none -> 1.7 us  [first_slot(): pl.pallas_call(first_slot_kernel, out_shape=(jax.ShapeDtypeStruct((blocks...]
    unnamed x1 -> x0, local copies, waits for them, and re-layouts: 0.77 us -> none
    another operation x1 -> x2, other arithmetic: 0.74 us -> 1.47 us  [the longest x1 0.74 us: on_device(): own = jnp.stack([factor_rows, factor_cols])]
  transfers between devices with their start and end apart: 18 -> 18, of which waited for: 10 -> 9; matrix products, arithmetic and copies ran while one was open for 2% -> 0% of each run, Pallas kernels for 9% -> 12%
where the time goes in v6:
time: 58.8 us; the launch traced here: 58.2 us
  starting transfers between devices  21.4 us (36%)
  waiting for transfers between devices  17.7 us (30%)
  Pallas kernels  15.4 us (26%)
  other arithmetic  1.92 us (3%)
  between operations  1.58 us (3%)
    ppermute x18, starting transfers between devices, swap(): return lax.ppermute(value, axis, [(at, at ^ mask) for at in range(size)])  21.4 us
    ppermute x18, waiting for transfers between devices, swap(): return lax.ppermute(value, axis, [(at, at ^ mask) for at in range(size)])  17.7 us
    pallas_call x1, Pallas kernels, terms(): pl.pallas_call(functools.partial(terms_kernel, relative, sizes, row_spots...  5.26 us
    pallas_call x1, Pallas kernels, first_cubes(): pl.pallas_call(functools.partial(cube_kernel, depth_blocks, slab), out_sh...  3.59 us
    pallas_call x2, Pallas kernels, unpack(): pl.pallas_call(functools.partial(unpack_kernel, sizes, rank, 0 if near el...  2.92 us
    pallas_call x3, Pallas kernels, vmem_call(): pl.pallas_call(kernel, out_shape=out_shape, in_specs=[pl.BlockSpec(memory...  1.97 us
    pallas_call x1, Pallas kernels, first_slot(): pl.pallas_call(first_slot_kernel, out_shape=(jax.ShapeDtypeStruct((blocks...  1.7 us
  transfers between devices with their start and end apart: 18, of which 9 were waited for; matrix products, arithmetic and copies ran while one was open for 0% of the time, Pallas kernels for 12%

profile of v6, /device:TPU:0, one launch (start us, length us, event | category | flops | bytes accessed | tf_op | source)
XLA Modules:
  0.0 58.2 jit_solution(5219871698657807248)
XLA Ops:
  0.6 0.7 %pad_maximum_fusion.3.after.refs_0_ = bf16[2,64,128]{2,1,0:T(8,128)(2,1)S(1)} fusion(bf16[1,64,128]{2,1,0:T(8,128)(2,1)} %bitcast.13, bf16[1,64,128]{2,1,0:T(8,128)(2,1)} %bitcast.11), kind=kLoop, calls=%fused_computation.3 | loop fusion | flops 16384 | bytes 65536 | tf_op jit(solution)/shard_map/stack | solution.py:570
  1.4 5.0 %collective-permute-start.2 = (bf16[2,64,128]{2,1,0:T(8,128)(2,1)S(1)}, bf16[2,64,128]{2,1,0:T(8,128)(2,1)S(1)}, u32[]{:S(2)}, u32[]{:S(2)}) collective-permute-start(bf16[2,64,128]{2,1,0:T(8,128)(2,1)S(1)} %pad_maximum_fusion.3.after.refs_0_), channel_id=1, source_target_pairs={{0,3},{1,2},{2,1},{3,0},{4,7},{5,6},{6,5},{7,4},{8,11},{9,10},{10,... | collective-permute-start | bytes 98312 | tf_op jit(solution)/shard_map/ppermute | solution.py:544
  6.4 0.0 collective-permute-start.1
  6.4 0.6 %collective-permute-start = (bf16[2,64,128]{2,1,0:T(8,128)(2,1)S(1)}, bf16[2,64,128]{2,1,0:T(8,128)(2,1)S(1)}, u32[]{:S(2)}, u32[]{:S(2)}) collective-permute-start(bf16[2,64,128]{2,1,0:T(8,128)(2,1)S(1)} %pad_maximum_fusion.3.after.refs_0_), channel_id=1, source_target_pairs={{0,1},{1,0},{2,3},{3,2},{4,5},{5,4},{6,7},{7,6},{8,9},{9,8},{10,11... | collective-permute-start | bytes 98312 | tf_op jit(solution)/shard_map/ppermute | solution.py:544
  7.0 3.6 %first_cubes.1 = (bf16[4,1024,128]{2,1,0:T(8,128)(2,1)S(1)}, bf16[32,128,64]{2,1,0:T(8,128)(2,1)S(1)}, bf16[128,64]{1,0:T(8,128)(2,1)S(1)}, s32[1,3,1,5]{3,2,1,0:T(1,128)S(1)}) custom-call(bf16[2,64,128]{2,1,0:T(8,128)(2,1)S(1)} %pad_maximum_fusion.3.after.refs_0_, bf16[64,512]{1,0:T(8,128)(2,1)} %factor_depth.1, bf16[64,64,64]{2,1,0:T(8,128)(2,1)} %core.1, ...), custom_call_target="tpu_custom_call" | custom-call | flops 1000000000 | bytes 4194304 | tf_op jit(solution)/shard_map/first_cubes/pallas_call | solution.py:81
  11.3 0.0 collective-permute-done.2.refs_3_
  11.3 0.0 collective-permute-done.1.refs_2_
  11.3 0.0 collective-permute-done.refs_1_
  11.4 0.7 %pad_maximum_fusion.2.after = bf16[4,64,128]{2,1,0:T(8,128)(2,1)S(1)} fusion(bf16[1,64,128]{2,1,0:T(8,128)(2,1)S(1)} %slice.30, bf16[1,64,128]{2,1,0:T(8,128)(2,1)S(1)} %slice.29, bf16[1,64,128]{2,1,0:T(8,128)(2,1)S(1)} %slice.28, bf16[1,64,128]{2,1,0:T(8,128)(2,1)} %bitcast.12), kind=kLoop, calls=%fused_computation.2 | loop fusion | flops 98304 | bytes 131072 | tf_op jit(solution)/shard_map/stack | solution.py:572
  12.1 0.1 collective-permute-start.3
  12.2 1.7 %first_slot.1 = (bf16[4,128,1024]{2,1,0:T(8,128)(2,1)S(1)}, f32[2,4224,128]{2,1,0:T(8,128)S(1)}) custom-call(bf16[4,64,128]{2,1,0:T(8,128)(2,1)S(1)} %pad_maximum_fusion.2.after, bf16[4,1024,128]{2,1,0:T(8,128)(2,1)S(1)} %get-tuple-element.30.cube, bf16[5,128,32,128]{3,2,1,0:T(8,128)(2,1)} %bitcast.7, bf16[5,128,32,128]{3,2,1,0:T(8,128)(2,1)} %bitcast.9), custom_call_target="tpu_custom_call" | custom-call | flops 1000000000 | bytes 4194304 | tf_op jit(solution)/shard_map/first_slot/pallas_call | solution.py:119
  13.9 0.0 collective-permute-done.3.refs_4_
  13.9 5.3 %terms.1 = (f32[32,64,128]{2,1,0:T(8,128)S(1)}, f32[8,64,128]{2,1,0:T(8,128)S(1)}, f32[4,64,128]{2,1,0:T(8,128)S(1)}, f32[64,128]{1,0:T(8,128)S(1)}, f32[2,4224,128]{2,1,0:T(8,128)S(1)}) custom-call(s32[1,1,1]{2,1,0:T(1,128)S(6)} %copy.16.counts, s32[1,3,1,5]{3,2,1,0:T(1,128)S(1)} %get-tuple-element.29.coords, ...), custom_call_target="tpu_custom_call", output_to_operand_aliasing={{4}: (13, {})} | custom-call | flops 1000000000 | bytes 16777216 | tf_op jit(solution)/shard_map/terms/pallas_call | solution.py:322
  19.1 0.1 fusion.1
  19.3 0.1 pad_maximum_fusion
  19.4 0.1 collective-permute-start.4
  19.5 2.1 %collective-permute-done.4.got = f32[21,64,128]{2,1,0:T(8,128)S(1)} collective-permute-done((f32[21,64,128]{2,1,0:T(8,128)S(1)}, f32[21,64,128]{2,1,0:T(8,128)S(1)}, u32[]{:S(2)}, u32[]{:S(2)}) %collective-permute-start.4) | collective-permute-done | bytes 688160 | tf_op jit(solution)/shard_map/ppermute | solution.py:544
  21.6 0.3 after_cores.1
  22.0 1.0 %collective-permute-start.7 = (f16[336,128]{1,0:T(8,128)(2,1)S(1)}, f16[336,128]{1,0:T(8,128)(2,1)S(1)}, u32[]{:S(2)}, u32[]{:S(2)}) collective-permute-start(f16[336,128]{1,0:T(8,128)(2,1)S(1)} %convert_element_type.67), channel_id=1, source_target_pairs={{0,24},{8,16},{16,8},{24,0},{1,25},{9,17},{17,9},{25,1},{2,26},{10... | collective-permute-start | bytes 258056 | tf_op jit(solution)/shard_map/ppermute | solution.py:544
  23.0 2.3 %collective-permute-start.6 = (f16[336,128]{1,0:T(8,128)(2,1)S(1)}, f16[336,128]{1,0:T(8,128)(2,1)S(1)}, u32[]{:S(2)}, u32[]{:S(2)}) collective-permute-start(f16[336,128]{1,0:T(8,128)(2,1)S(1)} %convert_element_type.65), channel_id=1, source_target_pairs={{0,16},{8,24},{16,0},{24,8},{1,17},{9,25},{17,1},{25,9},{2,18},{10... | collective-permute-start | bytes 258056 | tf_op jit(solution)/shard_map/ppermute | solution.py:544
  25.3 0.3 collective-permute-start.5
  25.6 2.0 %collective-permute-done.7 = f16[336,128]{1,0:T(8,128)(2,1)S(1)} collective-permute-done((f16[336,128]{1,0:T(8,128)(2,1)S(1)}, f16[336,128]{1,0:T(8,128)(2,1)S(1)}, u32[]{:S(2)}, u32[]{:S(2)}) %collective-permute-start.7) | collective-permute-done | bytes 86048 | tf_op jit(solution)/shard_map/ppermute | solution.py:544
  27.6 1.7 %collective-permute-done.6 = f16[336,128]{1,0:T(8,128)(2,1)S(1)} collective-permute-done((f16[336,128]{1,0:T(8,128)(2,1)S(1)}, f16[336,128]{1,0:T(8,128)(2,1)S(1)}, u32[]{:S(2)}, u32[]{:S(2)}) %collective-permute-start.6) | collective-permute-done | bytes 86048 | tf_op jit(solution)/shard_map/ppermute | solution.py:544
  29.4 0.6 collective-permute-done.5
  29.9 0.9 %after_rows.1 = (f32[64,128]{1,0:T(8,128)}, f32[400,128]{1,0:T(8,128)S(1)}, f32[400,128]{1,0:T(8,128)S(1)}, f32[400,128]{1,0:T(8,128)S(1)}, f32[400,128]{1,0:T(8,128)S(1)}) custom-call(f32[4,64,128]{2,1,0:T(8,128)S(1)} %get-tuple-element.38.own_core, f32[64,128]{1,0:T(8,128)S(1)} %get-tuple-element.39.own_depth, ...), custom_call_target="tpu_custom_call" | custom-call | tf_op jit(solution)/shard_map/after_rows/pallas_call | solution.py:357
  30.9 7.7 %collective-permute-start.10 = (f16[400,128]{1,0:T(8,128)(2,1)S(1)}, f16[400,128]{1,0:T(8,128)(2,1)S(1)}, u32[]{:S(2)}, u32[]{:S(2)}) collective-permute-start(f16[400,128]{1,0:T(8,128)(2,1)S(1)} %convert_element_type.73), channel_id=1, source_target_pairs={{0,3},{1,2},{2,1},{3,0},{4,7},{5,6},{6,5},{7,4},{8,11},{9,10},{10,... | collective-permute-start | bytes 307208 | tf_op jit(solution)/shard_map/ppermute | solution.py:544
  38.6 0.0 collective-permute-start.9
  38.6 0.7 %collective-permute-start.8 = (f16[400,128]{1,0:T(8,128)(2,1)S(1)}, f16[400,128]{1,0:T(8,128)(2,1)S(1)}, u32[]{:S(2)}, u32[]{:S(2)}) collective-permute-start(f16[400,128]{1,0:T(8,128)(2,1)S(1)} %convert_element_type.69), channel_id=1, source_target_pairs={{0,1},{1,0},{2,3},{3,2},{4,5},{5,4},{6,7},{7,6},{8,9},{9,8},{10,11... | collective-permute-start | bytes 307208 | tf_op jit(solution)/shard_map/ppermute | solution.py:544
  39.3 2.7 %collective-permute-done.10 = f16[400,128]{1,0:T(8,128)(2,1)S(1)} collective-permute-done((f16[400,128]{1,0:T(8,128)(2,1)S(1)}, f16[400,128]{1,0:T(8,128)(2,1)S(1)}, u32[]{:S(2)}, u32[]{:S(2)}) %collective-permute-start.10) | collective-permute-done | bytes 102432 | tf_op jit(solution)/shard_map/ppermute | solution.py:544
  42.0 5.0 %collective-permute-done.9 = f16[400,128]{1,0:T(8,128)(2,1)S(1)} collective-permute-done((f16[400,128]{1,0:T(8,128)(2,1)S(1)}, f16[400,128]{1,0:T(8,128)(2,1)S(1)}, u32[]{:S(2)}, u32[]{:S(2)}) %collective-permute-start.9) | collective-permute-done | bytes 102432 | tf_op jit(solution)/shard_map/ppermute | solution.py:544
  47.0 0.0 collective-permute-done.8
  47.0 0.8 %after_depths.1 = (f32[336,128]{1,0:T(8,128)S(1)}, f32[64,128]{1,0:T(8,128)}) custom-call(f32[400,128]{1,0:T(8,128)S(1)} %get-tuple-element.45.refs_0_, f32[400,128]{1,0:T(8,128)S(1)} %convert_element_type.70.refs_1_, f32[400,128]{1,0:T(8,128)S(1)} %convert_element_type.72.refs_2_, f32[400,128]{1,0:T(8,128)S(1)} %convert_element_type.74.refs_3_), custom_call_target="tpu_custom_call" | custom-call | tf_op jit(solution)/shard_map/after_depths/pallas_call | solution.py:357
  47.9 1.7 %collective-permute-start.13 = (f16[336,128]{1,0:T(8,128)(2,1)S(1)}, f16[336,128]{1,0:T(8,128)(2,1)S(1)}, u32[]{:S(2)}, u32[]{:S(2)}) collective-permute-start(f16[336,128]{1,0:T(8,128)(2,1)S(1)} %get-tuple-element.55), channel_id=1, source_target_pairs={{0,24},{8,16},{16,8},{24,0},{1,25},{9,17},{17,9},{25,1},{2,26},{10... | collective-permute-start | bytes 258056 | tf_op jit(solution)/shard_map/ppermute | solution.py:544
  49.5 1.1 %collective-permute-start.12 = (f16[336,128]{1,0:T(8,128)(2,1)S(1)}, f16[336,128]{1,0:T(8,128)(2,1)S(1)}, u32[]{:S(2)}, u32[]{:S(2)}) collective-permute-start(f16[336,128]{1,0:T(8,128)(2,1)S(1)} %get-tuple-element.55), channel_id=1, source_target_pairs={{0,16},{8,24},{16,0},{24,8},{1,17},{9,25},{17,1},{25,9},{2,18},{10... | collective-permute-start | bytes 258056 | tf_op jit(solution)/shard_map/ppermute | solution.py:544
  50.6 0.8 %collective-permute-start.11 = (f16[336,128]{1,0:T(8,128)(2,1)S(1)}, f16[336,128]{1,0:T(8,128)(2,1)S(1)}, u32[]{:S(2)}, u32[]{:S(2)}) collective-permute-start(f16[336,128]{1,0:T(8,128)(2,1)S(1)} %get-tuple-element.55), channel_id=1, source_target_pairs={{0,8},{8,0},{16,24},{24,16},{1,9},{9,1},{17,25},{25,17},{2,10},{10... | collective-permute-start | bytes 258056 | tf_op jit(solution)/shard_map/ppermute | solution.py:544
  51.4 0.0 collective-permute-start.14
  51.4 2.6 %collective-permute-done.13 = f16[336,128]{1,0:T(8,128)(2,1)S(1)} collective-permute-done((f16[336,128]{1,0:T(8,128)(2,1)S(1)}, f16[336,128]{1,0:T(8,128)(2,1)S(1)}, u32[]{:S(2)}, u32[]{:S(2)}) %collective-permute-start.13) | collective-permute-done | bytes 86048 | tf_op jit(solution)/shard_map/ppermute | solution.py:544
  54.0 0.0 collective-permute-start.17
  54.0 0.4 collective-permute-done.12
  54.5 0.1 collective-permute-start.16
  54.5 0.5 collective-permute-done.11
  55.1 0.0 collective-permute-start.15
  55.1 0.0 collective-permute-done.14
  55.2 1.8 %unpack_near.1 = (f32[64,64,64]{2,1,0:T(8,128)}, f32[64,128]{1,0:T(8,128)}) custom-call(f32[336,128]{1,0:T(8,128)S(1)} %get-tuple-element.54.refs_0_, f32[336,128]{1,0:T(8,128)S(1)} %convert_element_type.77.refs_1_, f32[336,128]{1,0:T(8,128)S(1)} %convert_element_type.78.refs_2_, f32[336,128]{1,0:T(8,128)S(1)} %convert_element_type.79.refs_3_), custom_call_target="tpu_custom_call" | custom-call | flops 1000000 | bytes 4194304 | tf_op jit(solution)/shard_map/unpack_near/pallas_call | solution.py:522
  56.9 0.0 collective-permute-done.17
  57.0 0.0 collective-permute-done.16
  57.0 0.0 collective-permute-done.15
  57.0 1.1 %unpack_far.1 = f32[64,64,64]{2,1,0:T(8,128)} custom-call(f32[336,128]{1,0:T(8,128)S(1)} %convert_element_type.80.refs_0_, f32[336,128]{1,0:T(8,128)S(1)} %convert_element_type.81.refs_1_, f32[336,128]{1,0:T(8,128)S(1)} %convert_element_type.82.refs_2_, f32[336,128]{1,0:T(8,128)S(1)} %convert_element_type.83.refs_3_, ...), custom_call_target="tpu_custom_call", output_to_operand_aliasing={{}: (4, {})} | custom-call | flops 1000000 | bytes 4194304 | tf_op jit(solution)/shard_map/unpack_far/pallas_call | solution.py:522
  (24 shorter events, 0.3 us)
Async XLA Ops:
  1.4 9.9 %collective-permute-start.2 = (bf16[2,64,128]{2,1,0:T(8,128)(2,1)S(1)}, bf16[2,64,128]{2,1,0:T(8,128)(2,1)S(1)}, u32[]{:S(2)}, u32[]{:S(2)}) collective-permute-start(bf16[2,64,128]{2,1,0:T(8,128)(2,1)S(1)} %pad_maximum_fusion.3.after.refs_0_), channel_id=1, source_target_pairs={{0,3},{1,2},{2,1},{3,0},{4,7},{5,6},{6,5},{7,4},{8,11},{9,10},{10,... | collective-permute-start | bytes 98312 | tf_op jit(solution)/shard_map/ppermute | solution.py:544
  6.4 4.9 %collective-permute-start.1 = (bf16[2,64,128]{2,1,0:T(8,128)(2,1)S(1)}, bf16[2,64,128]{2,1,0:T(8,128)(2,1)S(1)}, u32[]{:S(2)}, u32[]{:S(2)}) collective-permute-start(bf16[2,64,128]{2,1,0:T(8,128)(2,1)S(1)} %pad_maximum_fusion.3.after.refs_0_), channel_id=1, source_target_pairs={{0,2},{1,3},{2,0},{3,1},{4,6},{5,7},{6,4},{7,5},{8,10},{9,11},{10,... | collective-permute-start | bytes 98312 | tf_op jit(solution)/shard_map/ppermute | solution.py:544
  6.4 4.9 %collective-permute-start = (bf16[2,64,128]{2,1,0:T(8,128)(2,1)S(1)}, bf16[2,64,128]{2,1,0:T(8,128)(2,1)S(1)}, u32[]{:S(2)}, u32[]{:S(2)}) collective-permute-start(bf16[2,64,128]{2,1,0:T(8,128)(2,1)S(1)} %pad_maximum_fusion.3.after.refs_0_), channel_id=1, source_target_pairs={{0,1},{1,0},{2,3},{3,2},{4,5},{5,4},{6,7},{7,6},{8,9},{9,8},{10,11... | collective-permute-start | bytes 98312 | tf_op jit(solution)/shard_map/ppermute | solution.py:544
  12.1 1.8 %collective-permute-start.3 = (bf16[4,64,128]{2,1,0:T(8,128)(2,1)S(1)}, bf16[4,64,128]{2,1,0:T(8,128)(2,1)S(1)}, u32[]{:S(2)}, u32[]{:S(2)}) collective-permute-start(bf16[4,64,128]{2,1,0:T(8,128)(2,1)S(1)} %pad_maximum_fusion.2.after), channel_id=1, source_target_pairs={{0,4},{4,0},{1,5},{5,1},{2,6},{6,2},{3,7},{7,3},{8,12},{12,8},{9,1... | collective-permute-start | bytes 196616 | tf_op jit(solution)/shard_map/ppermute | solution.py:544
  19.4 2.2 %collective-permute-start.4 = (f32[21,64,128]{2,1,0:T(8,128)S(1)}, f32[21,64,128]{2,1,0:T(8,128)S(1)}, u32[]{:S(2)}, u32[]{:S(2)}) collective-permute-start(f32[21,64,128]{2,1,0:T(8,128)S(1)} %get-tuple-element.60), channel_id=1, source_target_pairs={{0,4},{4,0},{1,5},{5,1},{2,6},{6,2},{3,7},{7,3},{8,12},{12,8},{9,1... | collective-permute-start | bytes 2064392 | tf_op jit(solution)/shard_map/ppermute | solution.py:544
  22.0 5.6 %collective-permute-start.7 = (f16[336,128]{1,0:T(8,128)(2,1)S(1)}, f16[336,128]{1,0:T(8,128)(2,1)S(1)}, u32[]{:S(2)}, u32[]{:S(2)}) collective-permute-start(f16[336,128]{1,0:T(8,128)(2,1)S(1)} %convert_element_type.67), channel_id=1, source_target_pairs={{0,24},{8,16},{16,8},{24,0},{1,25},{9,17},{17,9},{25,1},{2,26},{10... | collective-permute-start | bytes 258056 | tf_op jit(solution)/shard_map/ppermute | solution.py:544
  23.0 6.3 %collective-permute-start.6 = (f16[336,128]{1,0:T(8,128)(2,1)S(1)}, f16[336,128]{1,0:T(8,128)(2,1)S(1)}, u32[]{:S(2)}, u32[]{:S(2)}) collective-permute-start(f16[336,128]{1,0:T(8,128)(2,1)S(1)} %convert_element_type.65), channel_id=1, source_target_pairs={{0,16},{8,24},{16,0},{24,8},{1,17},{9,25},{17,1},{25,9},{2,18},{10... | collective-permute-start | bytes 258056 | tf_op jit(solution)/shard_map/ppermute | solution.py:544
  25.3 4.6 %collective-permute-start.5 = (f16[336,128]{1,0:T(8,128)(2,1)S(1)}, f16[336,128]{1,0:T(8,128)(2,1)S(1)}, u32[]{:S(2)}, u32[]{:S(2)}) collective-permute-start(f16[336,128]{1,0:T(8,128)(2,1)S(1)} %convert_element_type.63), channel_id=1, source_target_pairs={{0,8},{8,0},{16,24},{24,16},{1,9},{9,1},{17,25},{25,17},{2,10},{10... | collective-permute-start | bytes 258056 | tf_op jit(solution)/shard_map/ppermute | solution.py:544
  30.9 11.1 %collective-permute-start.10 = (f16[400,128]{1,0:T(8,128)(2,1)S(1)}, f16[400,128]{1,0:T(8,128)(2,1)S(1)}, u32[]{:S(2)}, u32[]{:S(2)}) collective-permute-start(f16[400,128]{1,0:T(8,128)(2,1)S(1)} %convert_element_type.73), channel_id=1, source_target_pairs={{0,3},{1,2},{2,1},{3,0},{4,7},{5,6},{6,5},{7,4},{8,11},{9,10},{10,... | collective-permute-start | bytes 307208 | tf_op jit(solution)/shard_map/ppermute | solution.py:544
  38.6 8.4 %collective-permute-start.9 = (f16[400,128]{1,0:T(8,128)(2,1)S(1)}, f16[400,128]{1,0:T(8,128)(2,1)S(1)}, u32[]{:S(2)}, u32[]{:S(2)}) collective-permute-start(f16[400,128]{1,0:T(8,128)(2,1)S(1)} %convert_element_type.71), channel_id=1, source_target_pairs={{0,2},{1,3},{2,0},{3,1},{4,6},{5,7},{6,4},{7,5},{8,10},{9,11},{10,... | collective-permute-start | bytes 307208 | tf_op jit(solution)/shard_map/ppermute | solution.py:544
  38.6 8.4 %collective-permute-start.8 = (f16[400,128]{1,0:T(8,128)(2,1)S(1)}, f16[400,128]{1,0:T(8,128)(2,1)S(1)}, u32[]{:S(2)}, u32[]{:S(2)}) collective-permute-start(f16[400,128]{1,0:T(8,128)(2,1)S(1)} %convert_element_type.69), channel_id=1, source_target_pairs={{0,1},{1,0},{2,3},{3,2},{4,5},{5,4},{6,7},{7,6},{8,9},{9,8},{10,11... | collective-permute-start | bytes 307208 | tf_op jit(solution)/shard_map/ppermute | solution.py:544
  47.9 6.2 %collective-permute-start.13 = (f16[336,128]{1,0:T(8,128)(2,1)S(1)}, f16[336,128]{1,0:T(8,128)(2,1)S(1)}, u32[]{:S(2)}, u32[]{:S(2)}) collective-permute-start(f16[336,128]{1,0:T(8,128)(2,1)S(1)} %get-tuple-element.55), channel_id=1, source_target_pairs={{0,24},{8,16},{16,8},{24,0},{1,25},{9,17},{17,9},{25,1},{2,26},{10... | collective-permute-start | bytes 258056 | tf_op jit(solution)/shard_map/ppermute | solution.py:544
  49.5 5.0 %collective-permute-start.12 = (f16[336,128]{1,0:T(8,128)(2,1)S(1)}, f16[336,128]{1,0:T(8,128)(2,1)S(1)}, u32[]{:S(2)}, u32[]{:S(2)}) collective-permute-start(f16[336,128]{1,0:T(8,128)(2,1)S(1)} %get-tuple-element.55), channel_id=1, source_target_pairs={{0,16},{8,24},{16,0},{24,8},{1,17},{9,25},{17,1},{25,9},{2,18},{10... | collective-permute-start | bytes 258056 | tf_op jit(solution)/shard_map/ppermute | solution.py:544
  50.6 4.5 %collective-permute-start.11 = (f16[336,128]{1,0:T(8,128)(2,1)S(1)}, f16[336,128]{1,0:T(8,128)(2,1)S(1)}, u32[]{:S(2)}, u32[]{:S(2)}) collective-permute-start(f16[336,128]{1,0:T(8,128)(2,1)S(1)} %get-tuple-element.55), channel_id=1, source_target_pairs={{0,8},{8,0},{16,24},{24,16},{1,9},{9,1},{17,25},{25,17},{2,10},{10... | collective-permute-start | bytes 258056 | tf_op jit(solution)/shard_map/ppermute | solution.py:544
  51.4 3.7 %collective-permute-start.14 = (f16[336,128]{1,0:T(8,128)(2,1)S(1)}, f16[336,128]{1,0:T(8,128)(2,1)S(1)}, u32[]{:S(2)}, u32[]{:S(2)}) collective-permute-start(f16[336,128]{1,0:T(8,128)(2,1)S(1)} %get-tuple-element.55), channel_id=1, source_target_pairs={{0,4},{4,0},{1,5},{5,1},{2,6},{6,2},{3,7},{7,3},{8,12},{12,8},{9,1... | collective-permute-start | bytes 258056 | tf_op jit(solution)/shard_map/ppermute | solution.py:544
  54.0 2.9 %collective-permute-start.17 = (f16[336,128]{1,0:T(8,128)(2,1)S(1)}, f16[336,128]{1,0:T(8,128)(2,1)S(1)}, u32[]{:S(2)}, u32[]{:S(2)}) collective-permute-start(f16[336,128]{1,0:T(8,128)(2,1)S(1)} %collective-permute-done.13), channel_id=1, source_target_pairs={{0,4},{4,0},{1,5},{5,1},{2,6},{6,2},{3,7},{7,3},{8,12},{12,8},{9,1... | collective-permute-start | bytes 258056 | tf_op jit(solution)/shard_map/ppermute | solution.py:544
  54.5 2.5 %collective-permute-start.16 = (f16[336,128]{1,0:T(8,128)(2,1)S(1)}, f16[336,128]{1,0:T(8,128)(2,1)S(1)}, u32[]{:S(2)}, u32[]{:S(2)}) collective-permute-start(f16[336,128]{1,0:T(8,128)(2,1)S(1)} %collective-permute-done.12), channel_id=1, source_target_pairs={{0,4},{4,0},{1,5},{5,1},{2,6},{6,2},{3,7},{7,3},{8,12},{12,8},{9,1... | collective-permute-start | bytes 258056 | tf_op jit(solution)/shard_map/ppermute | solution.py:544
  55.1 1.9 %collective-permute-start.15 = (f16[336,128]{1,0:T(8,128)(2,1)S(1)}, f16[336,128]{1,0:T(8,128)(2,1)S(1)}, u32[]{:S(2)}, u32[]{:S(2)}) collective-permute-start(f16[336,128]{1,0:T(8,128)(2,1)S(1)} %collective-permute-done.11), channel_id=1, source_target_pairs={{0,4},{4,0},{1,5},{5,1},{2,6},{6,2},{3,7},{7,3},{8,12},{12,8},{9,1... | collective-permute-start | bytes 258056 | tf_op jit(solution)/shard_map/ppermute | solution.py:544

commit v7 on v5

--- a/solution.py
+++ b/solution.py
@@ -23,56 +23,69 @@
         target[i * (slab + 1) : i * (slab + 1) + slab, :] = source[i].astype(f32)
 
 
-def cube_kernel(
-    depth_blocks,
-    slab,
-    after,
-    factor_depth,
-    core,
-    data,
-    weight,
-    cube_out,
-    cube_turned_out,
-    core_out,
-    depth_out,
-    spread,
-    depth_here,
-    core_here,
-    fetched,
-    cube_wide,
-    sems,
-):
-    rank = core.shape[0]
-    half = slab // 2
-    pairs = rank // 2
-    width = depth_blocks * slab
+def bring_kernel(factor_depth, core, coords, core_out, depth_out, coords_out, depth_here, core_here, sems):
+    width = depth_here.shape[1]
+    pairs = core_out.shape[0]
     start = pl.multiple_of(lax.axis_index("ka") * width, width)
     copies = [
-        pltpu.make_async_copy(source.at[0], fetched.at[at], sems.at[2 + at]) for at, source in enumerate((data, weight))
+        pltpu.make_async_copy(factor_depth.at[:, pl.ds(start, width)], depth_here, sems.at[0]),
+        pltpu.make_async_copy(core, core_here, sems.at[1]),
+        pltpu.make_async_copy(coords, coords_out, sems.at[2]),
     ]
-    core_copy = pltpu.make_async_copy(core, core_here, sems.at[0])
-    core_copy.start()
-    depth_copy = pltpu.make_async_copy(factor_depth.at[:, pl.ds(start, width)], depth_here, sems.at[1])
-    depth_copy.start()
     for copy in copies:
         copy.start()
-    depth_copy.wait()
-    depth = depth_here[...].astype(f32).T
-    depth_out[...] = depth.astype(bf16)
-    order = [depth[t * slab + h * half : t * slab + (h + 1) * half] for h in range(2) for t in range(depth_blocks)]
-    depth = jnp.concatenate(order, axis=0).astype(bf16)
-    count = depth_blocks * half
-    core_copy.wait()
-
-    def one_rank(r1, carry):
-        piece = dot(depth, core_here[r1], ((1,), (1,)))
-        wide = jnp.concatenate([piece[:count], piece[count:]], axis=1)
-        cube_wide[pl.ds(r1, count, stride=rank + 1), :] = wide
-        return carry
-
-    lax.fori_loop(0, rank, one_rank, 0, unroll=16)
+    copies[0].wait()
+    depth_out[...] = depth_here[...].astype(f32).T.astype(bf16)
+    copies[1].wait()
     for pair in range(pairs):
         core_out[pair] = jnp.concatenate([core_here[pair], core_here[pairs + pair]], axis=0)
+    copies[2].wait()
+
+
+def bring(factor_depth, core, coords, width):
+    rank = core.shape[0]
+    return pl.pallas_call(
+        bring_kernel,
+        out_shape=(
+            jax.ShapeDtypeStruct((rank // 2, 2 * rank, rank), bf16),
+            jax.ShapeDtypeStruct((width, rank), bf16),
+            jax.ShapeDtypeStruct(coords.shape, coords.dtype),
+        ),
+        in_specs=[pl.BlockSpec(memory_space=pltpu.HBM)] * 3,
+        out_specs=[pl.BlockSpec(memory_space=pltpu.VMEM)] * 2 + [pl.BlockSpec(memory_space=pltpu.SMEM)],
+        scratch_shapes=[
+            pltpu.VMEM((rank, width), bf16),
+            pltpu.VMEM(core.shape, bf16),
+            pltpu.SemaphoreType.DMA((3,)),
+        ],
+        compiler_params=pltpu.CompilerParams(vmem_limit_bytes=16 * 2**20),
+        cost_estimate=pl.CostEstimate(flops=10**6, bytes_accessed=4 * 2**20, transcendentals=0),
+        name="bring",
+    )(factor_depth, core, coords)
+
+
+def cube_kernel(slab, after, core, depth, data, weight, cube_out, cube_turned_out, spread, fetched, cube_wide, sems):
+    pairs, _, rank = core.shape
+    half = slab // 2
+    depth_blocks = cube_out.shape[0]
+    copies = [
+        pltpu.make_async_copy(source.at[0], fetched.at[at], sems.at[at]) for at, source in enumerate((data, weight))
+    ]
+    for copy in copies:
+        copy.start()
+    order = [depth[t * slab + h * half : t * slab + (h + 1) * half] for h in range(2) for t in range(depth_blocks)]
+    ordered = jnp.concatenate(order, axis=0)
+    count = depth_blocks * half
+
+    def one_pair(pair, carry):
+        piece = dot(ordered, core[pair], ((1,), (1,)))
+        for which in range(2):
+            here = piece[:, which * rank : (which + 1) * rank]
+            wide = jnp.concatenate([here[:count], here[count:]], axis=1)
+            cube_wide[pl.ds(which * pairs + pair, count, stride=rank + 1), :] = wide
+        return carry
+
+    lax.fori_loop(0, pairs, one_pair, 0, unroll=8)
     for t in range(depth_blocks):
         for kp in range(half):
             at = (t * half + kp) * (rank + 1)
@@ -84,33 +97,31 @@
         spread_out(fetched.at[at], spread.at[at])
 
 
-def first_cubes(after, factor_depth, core, data, weight, depth_blocks):
-    rank = core.shape[0]
+def first_cubes(after, core, depth, data, weight):
+    pairs, _, rank = core.shape
     _, rows, slab, cols = data.shape
     half = slab // 2
-    width = depth_blocks * slab
+    depth_blocks = depth.shape[0] // slab
     return pl.pallas_call(
-        functools.partial(cube_kernel, depth_blocks, slab),
+        functools.partial(cube_kernel, slab),
         out_shape=(
             jax.ShapeDtypeStruct((depth_blocks, half * rank, 2 * rank), bf16),
             jax.ShapeDtypeStruct((depth_blocks, 2 * rank, half * rank), bf16),
-            jax.ShapeDtypeStruct((rank // 2, 2 * rank, rank), bf16),
-            jax.ShapeDtypeStruct((width, rank), bf16),
             jax.ShapeDtypeStruct((2, rows * (slab + 1), cols), f32),
         ),
-        in_specs=[pl.BlockSpec(memory_space=pl.ANY)] + [pl.BlockSpec(memory_space=pltpu.HBM)] * 4,
-        out_specs=[pl.BlockSpec(memory_space=pltpu.VMEM)] * 5,
+        in_specs=[pl.BlockSpec(memory_space=pl.ANY)]
+        + [pl.BlockSpec(memory_space=pltpu.VMEM)] * 2
+        + [pl.BlockSpec(memory_space=pltpu.HBM)] * 2,
+        out_specs=[pl.BlockSpec(memory_space=pltpu.VMEM)] * 3,
         scratch_shapes=[
-            pltpu.VMEM((rank, width), bf16),
-            pltpu.VMEM(core.shape, bf16),
             pltpu.VMEM((2, rows, slab, cols), bf16),
             pltpu.VMEM((depth_blocks * half * (rank + 1), 2 * rank), f32),
-            pltpu.SemaphoreType.DMA((4,)),
+            pltpu.SemaphoreType.DMA((2,)),
         ],
         compiler_params=pltpu.CompilerParams(vmem_limit_bytes=40 * 2**20),
         cost_estimate=pl.CostEstimate(flops=10**9, bytes_accessed=4 * 2**20, transcendentals=0),
         name="first_cubes",
-    )(after, factor_depth, core, data, weight)
+    )(after, core, depth, data, weight)
 
 
 def masks_of(relative, sizes):
@@ -126,11 +137,10 @@
         core,
         depth_turned,
         _,
-        core_out,
+        *outs,
+        cols_out,
+        spread,
         rows_out,
-        cols_out,
-        depth_out,
-        spread,
         row_table,
         col_table,
         wide_col,
@@ -170,8 +180,14 @@
         for copy in fetches(slot):
             copy.wait()
 
-    second_all[...] = jnp.zeros_like(second_all)
-    depth_all[...] = jnp.zeros_like(depth_all)
+    for s in range(slots):
+
+        @pl.when(s >= count)
+        def _():
+            lines = slice(s * slab, (s + 1) * slab)
+            second_all[:, lines, :] = jnp.zeros((pairs, slab, 2 * rank), bf16)
+            depth_all[lines, :] = jnp.zeros((slab, rank), bf16)
+
     depth_sum[...] = jnp.zeros_like(depth_sum)
     rows_out[...] = jnp.zeros_like(rows_out)
     cols_out[...] = jnp.zeros_like(cols_out)
@@ -189,9 +205,9 @@
             for which in range(2):
                 spread_out(fetched.at[lax.rem(slot, 2), which], spread.at[which])
 
-        row_at = (coords[0, 0, slot, 0] - row_base) ^ row_mask
-        col_at = (coords[0, 0, slot, 1] - col_base) ^ col_mask
-        depth_at = coords[0, 0, slot, 2] - depth_base
+        row_at = (coords[0, 0, 0, slot] - row_base) ^ row_mask
+        col_at = (coords[0, 1, 0, slot] - col_base) ^ col_mask
+        depth_at = coords[0, 2, 0, slot] - depth_base
         row_factor = row_table[row_at]
         row_turned = row_factor.astype(f32).T.astype(bf16)
         col_factor = col_table[col_at]
@@ -200,7 +216,7 @@
         own_depth = depth_turned[pl.ds(pl.multiple_of(depth_at * slab, slab), slab), :]
         depth_all[pl.ds(pl.multiple_of(slot * slab, slab), slab), :] = own_depth
 
-        step = 4
+        step = 8
         groups = half // step
         wide_factor = wide_col[...]
         def second_of(g):
@@ -230,7 +246,7 @@
                     lines = pl.ds(h * half + g * step + kp, rank, stride=slab + 1)
                     by_rank[lines, :] = wider[:, h * cols : (h + 1) * cols]
 
-        row_sum = jnp.zeros((rank, rows), f32)
+        row_sum = jnp.zeros((rows, rank), f32)
         seconds = [second_of(g) for g in range(groups)]
         models = [None] * groups
         models[0] = dot(row_turned, seconds[0])
@@ -239,8 +255,8 @@
                 models[g + 1] = dot(row_turned, seconds[g + 1])
             residual = residual_of(g, models[g])
             keep_back(g, dot(row_factor, residual))
-            row_sum = row_sum + dot(seconds[g], residual, ((1,), (1,)))
-        rows_out[row_at] += row_sum
+            row_sum = row_sum + dot(residual, seconds[g], ((1,), (1,)))
+        rows_out[row_at] += row_sum.T
         wide = dot(cube_turned[depth_at], backward[...])
         cols_out[col_at] += wide[:rank, :cols] + wide[rank:, cols:]
         lines = pl.ds(pl.multiple_of(slot * slab, slab), slab)
@@ -257,24 +273,38 @@
 
     lax.fori_loop(0, count, one_slot, 0)
 
-    def one_chunk(at, total):
+    if relative:
+        sides = [(outs[0], 0), (outs[1], 0)]
+        core_spots = [sides[at // (pairs // 2)] + (at % (pairs // 2),) for at in range(pairs)]
+        row_count = len(row_spots) // 2
+        row_places = [sides[at // row_count] + (pairs // 2 + at % row_count,) for at in range(2 * row_count)]
+    else:
+        core_spots = [(outs[0], 0, at) for at in range(pairs)]
+        row_places = [(outs[1], 0, at) for at in range(len(row_spots))]
+    total = jnp.zeros((second_all.shape[1], rank), f32)
+    for at in range(pairs):
         pair = at ^ core_mask
         second = second_all[pair]
         total = total + dot(second, core[pair])
         piece = dot(second, depth_all[...], ((0,), (0,)))
-        core_out[at] = jnp.concatenate([piece[:rank], piece[rank:]], axis=1)
-        return total
-
-    total = lax.fori_loop(0, pairs, one_chunk, jnp.zeros((second_all.shape[1], rank), f32), unroll=16)
+        out, _, line = core_spots[at]
+        out[line] = jnp.concatenate([piece[:rank], piece[rank:]], axis=1)
+    for at, (out, _, line) in enumerate(row_places):
+        out[line] = rows_out[at]
     for s in range(slots):
 
         @pl.when(s < count)
         def _():
-            at = coords[0, 0, s, 2] - depth_base
+            at = coords[0, 2, 0, s] - depth_base
             lines = pl.ds(pl.multiple_of(at * slab, slab), slab)
             depth_sum[lines, :] += total[s * slab : (s + 1) * slab]
 
-    depth_out[...] = depth_sum[...].T
+    depth = depth_sum[...].T
+    if relative:
+        for out in outs:
+            out[pairs // 2 + row_count] = depth
+    else:
+        outs[2][...] = depth
 
 
 def terms(relative, sizes, row_spots, col_spots, counts, coords, data, weight, cube, cube_turned, pieces, core, depth, spread):
@@ -283,23 +313,32 @@
     half = slab // 2
     depth_blocks = cube.shape[0]
 
-    outs = (
-        jax.ShapeDtypeStruct((rank // 2, rank, 2 * rank), f32),
-        jax.ShapeDtypeStruct((len(row_spots), rank, rows), f32),
+    width = depth_blocks * slab
+    if relative:
+        chunks = (rank // 2 + len(row_spots)) // 2 + 1
+        outs = (jax.ShapeDtypeStruct((chunks, rank, rows), f32),) * 2
+    else:
+        outs = (
+            jax.ShapeDtypeStruct((rank // 2, rank, 2 * rank), f32),
+            jax.ShapeDtypeStruct((len(row_spots), rank, rows), f32),
+            jax.ShapeDtypeStruct((rank, width), f32),
+        )
+    outs += (
         jax.ShapeDtypeStruct((len(col_spots), rank, cols), f32),
-        jax.ShapeDtypeStruct((rank, depth_blocks * slab), f32),
         jax.ShapeDtypeStruct(spread.shape, f32),
     )
     return pl.pallas_call(
         functools.partial(terms_kernel, relative, sizes, row_spots, col_spots),
         out_shape=outs,
         grid_spec=pltpu.PrefetchScalarGridSpec(
-            num_scalar_prefetch=2,
+            num_scalar_prefetch=0,
             grid=(),
-            in_specs=[pl.BlockSpec(memory_space=pl.ANY)] * 2
+            in_specs=[pl.BlockSpec(memory_space=pltpu.SMEM)] * 2
+            + [pl.BlockSpec(memory_space=pltpu.HBM)] * 2
             + [pl.BlockSpec(memory_space=pltpu.VMEM)] * (5 + len(pieces)),
-            out_specs=[pl.BlockSpec(memory_space=pltpu.VMEM)] * 5,
+            out_specs=[pl.BlockSpec(memory_space=pltpu.VMEM)] * len(outs),
             scratch_shapes=[
+                pltpu.VMEM((len(row_spots), rank, rows), f32),
                 pltpu.VMEM((len(row_spots), rank, rows), bf16),
                 pltpu.VMEM((len(col_spots), rank, cols), bf16),
                 pltpu.VMEM((2 * rank, 2 * cols), bf16),
@@ -312,7 +351,7 @@
                 pltpu.SemaphoreType.DMA((2, 2)),
             ],
         ),
-        input_output_aliases={8 + len(pieces): 4},
+        input_output_aliases={8 + len(pieces): len(outs) - 1},
         compiler_params=pltpu.CompilerParams(vmem_limit_bytes=40 * 2**20),
         cost_estimate=pl.CostEstimate(flops=10**9, bytes_accessed=16 * 2**20, transcendentals=0),
         name="terms",
@@ -364,12 +403,10 @@
 def fill_message(out, *parts):
     at = 0
     mark = None
-    for which, part in enumerate(parts):
-        lanes = part.shape[-1]
-        flat, exponent = scaled(part.reshape(-1, lanes))
+    for which, (flat, exponent) in enumerate(parts):
         out[at : at + flat.shape[0], :] = flat
         at += flat.shape[0]
-        exponent = jnp.broadcast_to(exponent[:1], (mark_rows, lanes))
+        exponent = jnp.broadcast_to(exponent[:1], (mark_rows, flat.shape[1]))
         line = lax.broadcasted_iota(jnp.int32, exponent.shape, 0)
         mark = exponent if mark is None else jnp.where(line >= which, exponent, mark)
     out[at : at + mark_rows, :] = mark
@@ -400,7 +437,8 @@
     own_rows[...] = keep[half : half + n_ka] + got[half : half + n_ka]
     for mask in range(1, n_ia):
         lines = slice(mask * n_ka, (mask + 1) * n_ka)
-        fill_message(messages[mask - 1], keep[lines] + got[lines], depth)
+        core = (keep[lines] + got[lines]).reshape(-1, depth.shape[1])
+        fill_message(messages[mask - 1], scaled(core), (flat, exponent))
 
 
 def after_cores(n_ia, n_ka, keep, got):
@@ -420,8 +458,9 @@
         core = core + message_part(message, 0, count * rank, 0)
         depths.append(message_part(message, count * rank, rank, 1))
     depth_out[...] = tree_sum(depths)
+    flat, exponent = scaled(core)
     for mask in range(n_ka):
-        fill_message(outs[mask], core, own_rows[mask], cols_sum[mask])
+        fill_message(outs[mask], (flat, exponent), scaled(own_rows[mask]), scaled(cols_sum[mask]))
 
 
 def after_rows(n_ia, n_ka, own_core, own_depth, own_rows, cols_sum, messages):
@@ -448,7 +487,7 @@
         cores.append(jnp.concatenate([part[(at ^ mask) * rank : ((at ^ mask) + 1) * rank] for at in range(n_ka)]))
     rows_out[...] = tree_sum(message_part(message, n_ka * rank, rank, 1) for message in messages)
     cols = tree_sum(message_part(message, (n_ka + 1) * rank, rank, 2) for message in messages)
-    fill_message(out, tree_sum(cores), cols)
+    fill_message(out, scaled(tree_sum(cores)), scaled(cols))
 
 
 def after_depths(n_ka, rank, messages):
@@ -534,10 +573,19 @@
         and rank // 2 == devices
         and factor_rows.shape[1] == rows
         and factor_cols.shape[1] == cols
+        and rows == cols == 2 * rank == depth_blocks * slab
     )
 
+    core_pairs, own_depth, coords = bring(
+        depth_here,
+        core_here,
+        pltpu.with_memory_space_constraint(coords.transpose(0, 3, 1, 2), pltpu.HBM),
+        depth_blocks * slab,
+    )
     if by_swaps:
-        own = jnp.stack([factor_rows, swap(factor_rows, "ja", n_ja, 1), factor_cols])
+        other_rows = swap(factor_rows, "ja", n_ja, 1)
+        other_rows, core_pairs = lax.optimization_barrier((other_rows, core_pairs))
+        own = jnp.stack([factor_rows, other_rows, factor_cols])
         pieces = [own] + [swap(own, "ka", n_ka, mask) for mask in range(1, n_ka)]
         row_spots = [(mask, line) for line in range(n_ja) for mask in range(n_ka)]
         col_spots = [(mask, n_ja) for mask in range(n_ka)]
@@ -548,12 +596,11 @@
         col_table = col_table.reshape(rank, col_chunks, cols).transpose(1, 0, 2)
         pieces = [row_table, col_table]
         row_spots = [(0, line) for line in range(row_chunks)]
+        own = row_table
         col_spots = [(1, line) for line in range(col_chunks)]
 
-    cube, cube_turned, core_pairs, own_depth, spread = first_cubes(
-        pieces[0], depth_here, core_here, data, weight, depth_blocks
-    )
-    core_sum, rows_sum, cols_sum, depth_sum, _ = terms(
+    cube, cube_turned, spread = first_cubes(own, core_pairs, own_depth, data, weight)
+    *sums, cols_sum, _ = terms(
         by_swaps,
         sizes,
         row_spots,
@@ -571,6 +618,7 @@
     )
 
     if not by_swaps:
+        core_sum, rows_sum, depth_sum = sums
         rows_whole = rows_sum.transpose(1, 0, 2).reshape(rank, row_chunks * rows)
         cols_whole = cols_sum.transpose(1, 0, 2).reshape(rank, col_chunks * cols)
         core_whole = core_sum.reshape(rank // 2, rank, 2, rank).transpose(2, 0, 1, 3).reshape(rank, rank, rank)
@@ -581,9 +629,7 @@
             lax.psum(core_whole, ("ia", "ja", "ka")),
         )
 
-    half = devices // 2
-    keep = jnp.concatenate([core_sum[:half], rows_sum[:n_ka], depth_sum[None]])
-    send = jnp.concatenate([core_sum[half:], rows_sum[n_ka:], depth_sum[None]])
+    keep, send = sums
     got = swap(send, "ja", n_ja, 1)
     own_core, own_depth, own_rows, messages = after_cores(n_ia, n_ka, keep, got)
     messages = [swap(message.astype(wire), "ia", n_ia, at + 1).astype(f32) for at, message in enumerate(messages)]

time: 56.7 us -> 57.3 us (1.011); the launches traced: 57.5 us -> 56.4 us
  Pallas kernels: 18.8 us -> 12.7 us
  starting transfers between devices: 17.6 us -> 23.2 us
  local copies, waits for them, and re-layouts: 0.86 us -> 0 us
    pallas_call x1, Pallas kernels: 10.4 us -> 3.49 us  [terms(): pl.pallas_call(functools.partial(terms_kernel, relative, sizes, row_spots...]
    ppermute x18, starting transfers between devices: 17.6 us -> 23.2 us  [swap(): return lax.ppermute(value, axis, [(at, at ^ mask) for at in range(size)])]
    pallas_call x1 -> x2, Pallas kernels: 3.44 us -> 4.3 us  [the longest x1 2.22 us: first_cubes(): pl.pallas_call(functools.partial(cube_kernel, slab), out_shape=(jax.Shape...]
    unnamed x1 -> x0, local copies, waits for them, and re-layouts: 0.77 us -> none
  transfers between devices with their start and end apart: 18 -> 18, of which waited for: 10 -> 9; matrix products, arithmetic and copies ran while one was open for 2% -> 0% of each run, Pallas kernels for 9% -> 11%
where the time goes in v7:
time: 57.3 us; the launch traced here: 56.4 us
  starting transfers between devices  23.2 us (40%)
  waiting for transfers between devices  17.9 us (31%)
  Pallas kernels  12.7 us (22%)
  between operations  1.54 us (3%)
  other arithmetic  1.05 us (2%)
    ppermute x18, starting transfers between devices, swap(): return lax.ppermute(value, axis, [(at, at ^ mask) for at in range(size)])  23.2 us
    ppermute x18, waiting for transfers between devices, swap(): return lax.ppermute(value, axis, [(at, at ^ mask) for at in range(size)])  17.9 us
    pallas_call x1, Pallas kernels, terms(): pl.pallas_call(functools.partial(terms_kernel, relative, sizes, row_spots...  3.49 us
    pallas_call x2, Pallas kernels, unpack(): pl.pallas_call(functools.partial(unpack_kernel, sizes, rank, 0 if near el...  2.92 us
    pallas_call x1, Pallas kernels, first_cubes(): pl.pallas_call(functools.partial(cube_kernel, slab), out_shape=(jax.Shape...  2.22 us
    pallas_call x1, Pallas kernels, bring(): pl.pallas_call(bring_kernel, out_shape=(jax.ShapeDtypeStruct((rank // 2,...  2.07 us
    pallas_call x3, Pallas kernels, vmem_call(): pl.pallas_call(kernel, out_shape=out_shape, in_specs=[pl.BlockSpec(memory...  1.96 us
  transfers between devices with their start and end apart: 18, of which 9 were waited for; matrix products, arithmetic and copies ran while one was open for 0% of the time, Pallas kernels for 11%

profile of v7, /device:TPU:0, one launch (start us, length us, event | category | flops | bytes accessed | tf_op | source)
XLA Modules:
  0.0 56.4 jit_solution(10576379867092372821)
XLA Ops:
  0.6 0.5 collective-permute-start
  1.8 2.1 %bring.1 = (bf16[32,128,64]{2,1,0:T(8,128)(2,1)S(1)}, bf16[128,64]{1,0:T(8,128)(2,1)S(1)}, s32[1,3,1,5]{3,2,1,0:T(1,128)S(1)}) custom-call(bf16[64,512]{1,0:T(8,128)(2,1)} %factor_depth.1, bf16[64,64,64]{2,1,0:T(8,128)(2,1)} %core.1, s32[1,3,1,5]{3,2,1,0:T(1,128)} %bitcast.13), custom_call_target="tpu_custom_call" | custom-call | flops 1000000 | bytes 4194304 | tf_op jit(solution)/shard_map/bring/pallas_call | solution.py:47
  3.9 0.0 collective-permute-done
  3.9 0.7 %pad_maximum_fusion.after.refs_0_ = bf16[3,64,128]{2,1,0:T(8,128)(2,1)S(1)} fusion(bf16[1,64,128]{2,1,0:T(8,128)(2,1)} %bitcast.10, bf16[1,64,128]{2,1,0:T(8,128)(2,1)S(1)} %bitcast.12, bf16[1,64,128]{2,1,0:T(8,128)(2,1)} %bitcast.11), kind=kLoop, calls=%fused_computation | loop fusion | flops 49152 | bytes 98304 | tf_op jit(solution)/shard_map/stack | solution.py:588
  4.6 4.7 %collective-permute-start.3 = (bf16[3,64,128]{2,1,0:T(8,128)(2,1)S(1)}, bf16[3,64,128]{2,1,0:T(8,128)(2,1)S(1)}, u32[]{:S(2)}, u32[]{:S(2)}) collective-permute-start(bf16[3,64,128]{2,1,0:T(8,128)(2,1)S(1)} %pad_maximum_fusion.after.refs_0_), channel_id=1, source_target_pairs={{0,3},{1,2},{2,1},{3,0},{4,7},{5,6},{6,5},{7,4},{8,11},{9,10},{10,... | collective-permute-start | bytes 147464 | tf_op jit(solution)/shard_map/ppermute | solution.py:553
  9.3 0.0 collective-permute-start.2
  9.3 0.6 %collective-permute-start.1 = (bf16[3,64,128]{2,1,0:T(8,128)(2,1)S(1)}, bf16[3,64,128]{2,1,0:T(8,128)(2,1)S(1)}, u32[]{:S(2)}, u32[]{:S(2)}) collective-permute-start(bf16[3,64,128]{2,1,0:T(8,128)(2,1)S(1)} %pad_maximum_fusion.after.refs_0_), channel_id=1, source_target_pairs={{0,1},{1,0},{2,3},{3,2},{4,5},{5,4},{6,7},{7,6},{8,9},{9,8},{10,11... | collective-permute-start | bytes 147464 | tf_op jit(solution)/shard_map/ppermute | solution.py:553
  9.9 2.2 %first_cubes.1 = (bf16[4,1024,128]{2,1,0:T(8,128)(2,1)S(1)}, bf16[4,128,1024]{2,1,0:T(8,128)(2,1)S(1)}, f32[2,4224,128]{2,1,0:T(8,128)S(1)}) custom-call(bf16[3,64,128]{2,1,0:T(8,128)(2,1)S(1)} %pad_maximum_fusion.after.refs_0_, bf16[32,128,64]{2,1,0:T(8,128)(2,1)S(1)} %get-tuple-element.33.core.refs_4_, ...), custom_call_target="tpu_custom_call" | custom-call | flops 1000000000 | bytes 4194304 | tf_op jit(solution)/shard_map/first_cubes/pallas_call | solution.py:105
  12.2 0.0 collective-permute-done.3.refs_3_
  12.2 2.3 %collective-permute-done.2.refs_2_ = bf16[3,64,128]{2,1,0:T(8,128)(2,1)S(1)} collective-permute-done((bf16[3,64,128]{2,1,0:T(8,128)(2,1)S(1)}, bf16[3,64,128]{2,1,0:T(8,128)(2,1)S(1)}, u32[]{:S(2)}, u32[]{:S(2)}) %collective-permute-start.2) | collective-permute-done | bytes 49184 | tf_op jit(solution)/shard_map/ppermute | solution.py:553
  14.4 0.0 collective-permute-done.1.refs_1_
  14.4 3.5 %terms.1 = (f32[21,64,128]{2,1,0:T(8,128)S(1)}, f32[21,64,128]{2,1,0:T(8,128)S(1)}, f32[4,64,128]{2,1,0:T(8,128)S(1)}, f32[2,4224,128]{2,1,0:T(8,128)S(1)}) custom-call(s32[1,1,1]{2,1,0:T(1,128)S(6)} %copy.16.counts, s32[1,3,1,5]{3,2,1,0:T(1,128)S(1)} %get-tuple-element.30.coords, ...), custom_call_target="tpu_custom_call", output_to_operand_aliasing={{3}: (12, {})} | custom-call | flops 1000000000 | bytes 16777216 | tf_op jit(solution)/shard_map/terms/pallas_call | solution.py:330
  17.9 0.1 collective-permute-start.4
  18.0 2.1 %collective-permute-done.4.got = f32[21,64,128]{2,1,0:T(8,128)S(1)} collective-permute-done((f32[21,64,128]{2,1,0:T(8,128)S(1)}, f32[21,64,128]{2,1,0:T(8,128)S(1)}, u32[]{:S(2)}, u32[]{:S(2)}) %collective-permute-start.4) | collective-permute-done | bytes 688160 | tf_op jit(solution)/shard_map/ppermute | solution.py:553
  20.1 0.3 after_cores.1
  20.5 4.3 %collective-permute-start.7 = (f16[336,128]{1,0:T(8,128)(2,1)S(1)}, f16[336,128]{1,0:T(8,128)(2,1)S(1)}, u32[]{:S(2)}, u32[]{:S(2)}) collective-permute-start(f16[336,128]{1,0:T(8,128)(2,1)S(1)} %convert_element_type.67), channel_id=1, source_target_pairs={{0,24},{8,16},{16,8},{24,0},{1,25},{9,17},{17,9},{25,1},{2,26},{10... | collective-permute-start | bytes 258056 | tf_op jit(solution)/shard_map/ppermute | solution.py:553
  24.8 4.6 %collective-permute-start.6 = (f16[336,128]{1,0:T(8,128)(2,1)S(1)}, f16[336,128]{1,0:T(8,128)(2,1)S(1)}, u32[]{:S(2)}, u32[]{:S(2)}) collective-permute-start(f16[336,128]{1,0:T(8,128)(2,1)S(1)} %convert_element_type.65), channel_id=1, source_target_pairs={{0,16},{8,24},{16,0},{24,8},{1,17},{9,25},{17,1},{25,9},{2,18},{10... | collective-permute-start | bytes 258056 | tf_op jit(solution)/shard_map/ppermute | solution.py:553
  29.3 0.1 collective-permute-start.5
  29.4 0.0 collective-permute-done.7
  29.5 2.6 %collective-permute-done.6 = f16[336,128]{1,0:T(8,128)(2,1)S(1)} collective-permute-done((f16[336,128]{1,0:T(8,128)(2,1)S(1)}, f16[336,128]{1,0:T(8,128)(2,1)S(1)}, u32[]{:S(2)}, u32[]{:S(2)}) %collective-permute-start.6) | collective-permute-done | bytes 86048 | tf_op jit(solution)/shard_map/ppermute | solution.py:553
  32.1 1.8 %collective-permute-done.5 = f16[336,128]{1,0:T(8,128)(2,1)S(1)} collective-permute-done((f16[336,128]{1,0:T(8,128)(2,1)S(1)}, f16[336,128]{1,0:T(8,128)(2,1)S(1)}, u32[]{:S(2)}, u32[]{:S(2)}) %collective-permute-start.5) | collective-permute-done | bytes 86048 | tf_op jit(solution)/shard_map/ppermute | solution.py:553
  33.9 0.9 %after_rows.1 = (f32[64,128]{1,0:T(8,128)}, f32[400,128]{1,0:T(8,128)S(1)}, f32[400,128]{1,0:T(8,128)S(1)}, f32[400,128]{1,0:T(8,128)S(1)}, f32[400,128]{1,0:T(8,128)S(1)}) custom-call(f32[4,64,128]{2,1,0:T(8,128)S(1)} %get-tuple-element.40.own_core, f32[64,128]{1,0:T(8,128)S(1)} %get-tuple-element.41.own_depth, ...), custom_call_target="tpu_custom_call" | custom-call | tf_op jit(solution)/shard_map/after_rows/pallas_call | solution.py:366
  34.9 3.0 %collective-permute-start.10 = (f16[400,128]{1,0:T(8,128)(2,1)S(1)}, f16[400,128]{1,0:T(8,128)(2,1)S(1)}, u32[]{:S(2)}, u32[]{:S(2)}) collective-permute-start(f16[400,128]{1,0:T(8,128)(2,1)S(1)} %convert_element_type.73), channel_id=1, source_target_pairs={{0,3},{1,2},{2,1},{3,0},{4,7},{5,6},{6,5},{7,4},{8,11},{9,10},{10,... | collective-permute-start | bytes 307208 | tf_op jit(solution)/shard_map/ppermute | solution.py:553
  37.9 0.0 collective-permute-start.9
  37.9 1.5 %collective-permute-start.8 = (f16[400,128]{1,0:T(8,128)(2,1)S(1)}, f16[400,128]{1,0:T(8,128)(2,1)S(1)}, u32[]{:S(2)}, u32[]{:S(2)}) collective-permute-start(f16[400,128]{1,0:T(8,128)(2,1)S(1)} %convert_element_type.69), channel_id=1, source_target_pairs={{0,1},{1,0},{2,3},{3,2},{4,5},{5,4},{6,7},{7,6},{8,9},{9,8},{10,11... | collective-permute-start | bytes 307208 | tf_op jit(solution)/shard_map/ppermute | solution.py:553
  39.4 2.7 %collective-permute-done.10 = f16[400,128]{1,0:T(8,128)(2,1)S(1)} collective-permute-done((f16[400,128]{1,0:T(8,128)(2,1)S(1)}, f16[400,128]{1,0:T(8,128)(2,1)S(1)}, u32[]{:S(2)}, u32[]{:S(2)}) %collective-permute-start.10) | collective-permute-done | bytes 102432 | tf_op jit(solution)/shard_map/ppermute | solution.py:553
  42.1 2.4 %collective-permute-done.9 = f16[400,128]{1,0:T(8,128)(2,1)S(1)} collective-permute-done((f16[400,128]{1,0:T(8,128)(2,1)S(1)}, f16[400,128]{1,0:T(8,128)(2,1)S(1)}, u32[]{:S(2)}, u32[]{:S(2)}) %collective-permute-start.9) | collective-permute-done | bytes 102432 | tf_op jit(solution)/shard_map/ppermute | solution.py:553
  44.6 0.0 collective-permute-done.8
  44.6 0.8 %after_depths.1 = (f32[336,128]{1,0:T(8,128)S(1)}, f32[64,128]{1,0:T(8,128)}) custom-call(f32[400,128]{1,0:T(8,128)S(1)} %get-tuple-element.47.refs_0_, f32[400,128]{1,0:T(8,128)S(1)} %convert_element_type.70.refs_1_, f32[400,128]{1,0:T(8,128)S(1)} %convert_element_type.72.refs_2_, f32[400,128]{1,0:T(8,128)S(1)} %convert_element_type.74.refs_3_), custom_call_target="tpu_custom_call" | custom-call | tf_op jit(solution)/shard_map/after_depths/pallas_call | solution.py:366
  45.4 2.5 %collective-permute-start.13 = (f16[336,128]{1,0:T(8,128)(2,1)S(1)}, f16[336,128]{1,0:T(8,128)(2,1)S(1)}, u32[]{:S(2)}, u32[]{:S(2)}) collective-permute-start(f16[336,128]{1,0:T(8,128)(2,1)S(1)} %get-tuple-element.57), channel_id=1, source_target_pairs={{0,24},{8,16},{16,8},{24,0},{1,25},{9,17},{17,9},{25,1},{2,26},{10... | collective-permute-start | bytes 258056 | tf_op jit(solution)/shard_map/ppermute | solution.py:553
  48.0 0.5 collective-permute-start.12
  48.4 0.5 collective-permute-start.11
  49.0 0.0 collective-permute-start.14
  49.0 2.0 %collective-permute-done.13 = f16[336,128]{1,0:T(8,128)(2,1)S(1)} collective-permute-done((f16[336,128]{1,0:T(8,128)(2,1)S(1)}, f16[336,128]{1,0:T(8,128)(2,1)S(1)}, u32[]{:S(2)}, u32[]{:S(2)}) %collective-permute-start.13) | collective-permute-done | bytes 86048 | tf_op jit(solution)/shard_map/ppermute | solution.py:553
  50.9 0.0 collective-permute-start.17
  51.0 1.8 %collective-permute-done.12 = f16[336,128]{1,0:T(8,128)(2,1)S(1)} collective-permute-done((f16[336,128]{1,0:T(8,128)(2,1)S(1)}, f16[336,128]{1,0:T(8,128)(2,1)S(1)}, u32[]{:S(2)}, u32[]{:S(2)}) %collective-permute-start.12) | collective-permute-done | bytes 86048 | tf_op jit(solution)/shard_map/ppermute | solution.py:553
  52.7 0.0 collective-permute-start.16
  52.7 0.2 collective-permute-done.11
  52.9 0.3 collective-permute-start.15
  53.3 0.0 collective-permute-done.14
  53.3 1.8 %unpack_near.1 = (f32[64,64,64]{2,1,0:T(8,128)}, f32[64,128]{1,0:T(8,128)}) custom-call(f32[336,128]{1,0:T(8,128)S(1)} %get-tuple-element.56.refs_0_, f32[336,128]{1,0:T(8,128)S(1)} %convert_element_type.77.refs_1_, f32[336,128]{1,0:T(8,128)S(1)} %convert_element_type.78.refs_2_, f32[336,128]{1,0:T(8,128)S(1)} %convert_element_type.79.refs_3_), custom_call_target="tpu_custom_call" | custom-call | flops 1000000 | bytes 4194304 | tf_op jit(solution)/shard_map/unpack_near/pallas_call | solution.py:531
  55.1 0.0 collective-permute-done.17
  55.1 0.0 collective-permute-done.16
  55.2 0.0 collective-permute-done.15
  55.2 1.1 %unpack_far.1 = f32[64,64,64]{2,1,0:T(8,128)} custom-call(f32[336,128]{1,0:T(8,128)S(1)} %convert_element_type.80.refs_0_, f32[336,128]{1,0:T(8,128)S(1)} %convert_element_type.81.refs_1_, f32[336,128]{1,0:T(8,128)S(1)} %convert_element_type.82.refs_2_, f32[336,128]{1,0:T(8,128)S(1)} %convert_element_type.83.refs_3_, ...), custom_call_target="tpu_custom_call", output_to_operand_aliasing={{}: (4, {})} | custom-call | flops 1000000 | bytes 4194304 | tf_op jit(solution)/shard_map/unpack_far/pallas_call | solution.py:531
  (20 shorter events, 0.3 us)
Async XLA Ops:
  0.6 3.3 %collective-permute-start = (bf16[64,128]{1,0:T(8,128)(2,1)}, bf16[64,128]{1,0:T(8,128)(2,1)S(1)}, u32[]{:S(2)}, u32[]{:S(2)}) collective-permute-start(bf16[64,128]{1,0:T(8,128)(2,1)} %param.12), channel_id=1, source_target_pairs={{0,4},{4,0},{1,5},{5,1},{2,6},{6,2},{3,7},{7,3},{8,12},{12,8},{9,1... | collective-permute-start | bytes 49160 | tf_op jit(solution)/shard_map/ppermute | solution.py:553
  4.6 7.5 %collective-permute-start.3 = (bf16[3,64,128]{2,1,0:T(8,128)(2,1)S(1)}, bf16[3,64,128]{2,1,0:T(8,128)(2,1)S(1)}, u32[]{:S(2)}, u32[]{:S(2)}) collective-permute-start(bf16[3,64,128]{2,1,0:T(8,128)(2,1)S(1)} %pad_maximum_fusion.after.refs_0_), channel_id=1, source_target_pairs={{0,3},{1,2},{2,1},{3,0},{4,7},{5,6},{6,5},{7,4},{8,11},{9,10},{10,... | collective-permute-start | bytes 147464 | tf_op jit(solution)/shard_map/ppermute | solution.py:553
  9.3 5.1 %collective-permute-start.2 = (bf16[3,64,128]{2,1,0:T(8,128)(2,1)S(1)}, bf16[3,64,128]{2,1,0:T(8,128)(2,1)S(1)}, u32[]{:S(2)}, u32[]{:S(2)}) collective-permute-start(bf16[3,64,128]{2,1,0:T(8,128)(2,1)S(1)} %pad_maximum_fusion.after.refs_0_), channel_id=1, source_target_pairs={{0,2},{1,3},{2,0},{3,1},{4,6},{5,7},{6,4},{7,5},{8,10},{9,11},{10,... | collective-permute-start | bytes 147464 | tf_op jit(solution)/shard_map/ppermute | solution.py:553
  9.3 5.1 %collective-permute-start.1 = (bf16[3,64,128]{2,1,0:T(8,128)(2,1)S(1)}, bf16[3,64,128]{2,1,0:T(8,128)(2,1)S(1)}, u32[]{:S(2)}, u32[]{:S(2)}) collective-permute-start(bf16[3,64,128]{2,1,0:T(8,128)(2,1)S(1)} %pad_maximum_fusion.after.refs_0_), channel_id=1, source_target_pairs={{0,1},{1,0},{2,3},{3,2},{4,5},{5,4},{6,7},{7,6},{8,9},{9,8},{10,11... | collective-permute-start | bytes 147464 | tf_op jit(solution)/shard_map/ppermute | solution.py:553
  17.9 2.2 %collective-permute-start.4 = (f32[21,64,128]{2,1,0:T(8,128)S(1)}, f32[21,64,128]{2,1,0:T(8,128)S(1)}, u32[]{:S(2)}, u32[]{:S(2)}) collective-permute-start(f32[21,64,128]{2,1,0:T(8,128)S(1)} %get-tuple-element.39), channel_id=1, source_target_pairs={{0,4},{4,0},{1,5},{5,1},{2,6},{6,2},{3,7},{7,3},{8,12},{12,8},{9,1... | collective-permute-start | bytes 2064392 | tf_op jit(solution)/shard_map/ppermute | solution.py:553
  20.5 9.0 %collective-permute-start.7 = (f16[336,128]{1,0:T(8,128)(2,1)S(1)}, f16[336,128]{1,0:T(8,128)(2,1)S(1)}, u32[]{:S(2)}, u32[]{:S(2)}) collective-permute-start(f16[336,128]{1,0:T(8,128)(2,1)S(1)} %convert_element_type.67), channel_id=1, source_target_pairs={{0,24},{8,16},{16,8},{24,0},{1,25},{9,17},{17,9},{25,1},{2,26},{10... | collective-permute-start | bytes 258056 | tf_op jit(solution)/shard_map/ppermute | solution.py:553
  24.8 7.3 %collective-permute-start.6 = (f16[336,128]{1,0:T(8,128)(2,1)S(1)}, f16[336,128]{1,0:T(8,128)(2,1)S(1)}, u32[]{:S(2)}, u32[]{:S(2)}) collective-permute-start(f16[336,128]{1,0:T(8,128)(2,1)S(1)} %convert_element_type.65), channel_id=1, source_target_pairs={{0,16},{8,24},{16,0},{24,8},{1,17},{9,25},{17,1},{25,9},{2,18},{10... | collective-permute-start | bytes 258056 | tf_op jit(solution)/shard_map/ppermute | solution.py:553
  29.3 4.6 %collective-permute-start.5 = (f16[336,128]{1,0:T(8,128)(2,1)S(1)}, f16[336,128]{1,0:T(8,128)(2,1)S(1)}, u32[]{:S(2)}, u32[]{:S(2)}) collective-permute-start(f16[336,128]{1,0:T(8,128)(2,1)S(1)} %convert_element_type.63), channel_id=1, source_target_pairs={{0,8},{8,0},{16,24},{24,16},{1,9},{9,1},{17,25},{25,17},{2,10},{10... | collective-permute-start | bytes 258056 | tf_op jit(solution)/shard_map/ppermute | solution.py:553
  34.9 7.2 %collective-permute-start.10 = (f16[400,128]{1,0:T(8,128)(2,1)S(1)}, f16[400,128]{1,0:T(8,128)(2,1)S(1)}, u32[]{:S(2)}, u32[]{:S(2)}) collective-permute-start(f16[400,128]{1,0:T(8,128)(2,1)S(1)} %convert_element_type.73), channel_id=1, source_target_pairs={{0,3},{1,2},{2,1},{3,0},{4,7},{5,6},{6,5},{7,4},{8,11},{9,10},{10,... | collective-permute-start | bytes 307208 | tf_op jit(solution)/shard_map/ppermute | solution.py:553
  37.9 6.7 %collective-permute-start.9 = (f16[400,128]{1,0:T(8,128)(2,1)S(1)}, f16[400,128]{1,0:T(8,128)(2,1)S(1)}, u32[]{:S(2)}, u32[]{:S(2)}) collective-permute-start(f16[400,128]{1,0:T(8,128)(2,1)S(1)} %convert_element_type.71), channel_id=1, source_target_pairs={{0,2},{1,3},{2,0},{3,1},{4,6},{5,7},{6,4},{7,5},{8,10},{9,11},{10,... | collective-permute-start | bytes 307208 | tf_op jit(solution)/shard_map/ppermute | solution.py:553
  37.9 6.7 %collective-permute-start.8 = (f16[400,128]{1,0:T(8,128)(2,1)S(1)}, f16[400,128]{1,0:T(8,128)(2,1)S(1)}, u32[]{:S(2)}, u32[]{:S(2)}) collective-permute-start(f16[400,128]{1,0:T(8,128)(2,1)S(1)} %convert_element_type.69), channel_id=1, source_target_pairs={{0,1},{1,0},{2,3},{3,2},{4,5},{5,4},{6,7},{7,6},{8,9},{9,8},{10,11... | collective-permute-start | bytes 307208 | tf_op jit(solution)/shard_map/ppermute | solution.py:553
  45.4 5.5 %collective-permute-start.13 = (f16[336,128]{1,0:T(8,128)(2,1)S(1)}, f16[336,128]{1,0:T(8,128)(2,1)S(1)}, u32[]{:S(2)}, u32[]{:S(2)}) collective-permute-start(f16[336,128]{1,0:T(8,128)(2,1)S(1)} %get-tuple-element.57), channel_id=1, source_target_pairs={{0,24},{8,16},{16,8},{24,0},{1,25},{9,17},{17,9},{25,1},{2,26},{10... | collective-permute-start | bytes 258056 | tf_op jit(solution)/shard_map/ppermute | solution.py:553
  48.0 4.8 %collective-permute-start.12 = (f16[336,128]{1,0:T(8,128)(2,1)S(1)}, f16[336,128]{1,0:T(8,128)(2,1)S(1)}, u32[]{:S(2)}, u32[]{:S(2)}) collective-permute-start(f16[336,128]{1,0:T(8,128)(2,1)S(1)} %get-tuple-element.57), channel_id=1, source_target_pairs={{0,16},{8,24},{16,0},{24,8},{1,17},{9,25},{17,1},{25,9},{2,18},{10... | collective-permute-start | bytes 258056 | tf_op jit(solution)/shard_map/ppermute | solution.py:553
  48.4 4.5 %collective-permute-start.11 = (f16[336,128]{1,0:T(8,128)(2,1)S(1)}, f16[336,128]{1,0:T(8,128)(2,1)S(1)}, u32[]{:S(2)}, u32[]{:S(2)}) collective-permute-start(f16[336,128]{1,0:T(8,128)(2,1)S(1)} %get-tuple-element.57), channel_id=1, source_target_pairs={{0,8},{8,0},{16,24},{24,16},{1,9},{9,1},{17,25},{25,17},{2,10},{10... | collective-permute-start | bytes 258056 | tf_op jit(solution)/shard_map/ppermute | solution.py:553
  49.0 4.3 %collective-permute-start.14 = (f16[336,128]{1,0:T(8,128)(2,1)S(1)}, f16[336,128]{1,0:T(8,128)(2,1)S(1)}, u32[]{:S(2)}, u32[]{:S(2)}) collective-permute-start(f16[336,128]{1,0:T(8,128)(2,1)S(1)} %get-tuple-element.57), channel_id=1, source_target_pairs={{0,4},{4,0},{1,5},{5,1},{2,6},{6,2},{3,7},{7,3},{8,12},{12,8},{9,1... | collective-permute-start | bytes 258056 | tf_op jit(solution)/shard_map/ppermute | solution.py:553
  50.9 4.2 %collective-permute-start.17 = (f16[336,128]{1,0:T(8,128)(2,1)S(1)}, f16[336,128]{1,0:T(8,128)(2,1)S(1)}, u32[]{:S(2)}, u32[]{:S(2)}) collective-permute-start(f16[336,128]{1,0:T(8,128)(2,1)S(1)} %collective-permute-done.13), channel_id=1, source_target_pairs={{0,4},{4,0},{1,5},{5,1},{2,6},{6,2},{3,7},{7,3},{8,12},{12,8},{9,1... | collective-permute-start | bytes 258056 | tf_op jit(solution)/shard_map/ppermute | solution.py:553
  52.7 2.4 %collective-permute-start.16 = (f16[336,128]{1,0:T(8,128)(2,1)S(1)}, f16[336,128]{1,0:T(8,128)(2,1)S(1)}, u32[]{:S(2)}, u32[]{:S(2)}) collective-permute-start(f16[336,128]{1,0:T(8,128)(2,1)S(1)} %collective-permute-done.12), channel_id=1, source_target_pairs={{0,4},{4,0},{1,5},{5,1},{2,6},{6,2},{3,7},{7,3},{8,12},{12,8},{9,1... | collective-permute-start | bytes 258056 | tf_op jit(solution)/shard_map/ppermute | solution.py:553
  52.9 2.3 %collective-permute-start.15 = (f16[336,128]{1,0:T(8,128)(2,1)S(1)}, f16[336,128]{1,0:T(8,128)(2,1)S(1)}, u32[]{:S(2)}, u32[]{:S(2)}) collective-permute-start(f16[336,128]{1,0:T(8,128)(2,1)S(1)} %collective-permute-done.11), channel_id=1, source_target_pairs={{0,4},{4,0},{1,5},{5,1},{2,6},{6,2},{3,7},{7,3},{8,12},{12,8},{9,1... | collective-permute-start | bytes 258056 | tf_op jit(solution)/shard_map/ppermute | solution.py:553

commit v8 on v7

--- a/solution.py
+++ b/solution.py
@@ -23,62 +23,52 @@
         target[i * (slab + 1) : i * (slab + 1) + slab, :] = source[i].astype(f32)
 
 
-def bring_kernel(factor_depth, core, coords, core_out, depth_out, coords_out, depth_here, core_here, sems):
+def cube_kernel(
+    slab,
+    after,
+    factor_depth,
+    core,
+    coords,
+    data,
+    weight,
+    cube_out,
+    cube_turned_out,
+    core_out,
+    depth_out,
+    coords_out,
+    spread,
+    depth_here,
+    core_here,
+    fetched,
+    cube_wide,
+    sems,
+):
+    pairs, _, rank = core_out.shape
+    half = slab // 2
+    depth_blocks = cube_out.shape[0]
     width = depth_here.shape[1]
-    pairs = core_out.shape[0]
     start = pl.multiple_of(lax.axis_index("ka") * width, width)
     copies = [
         pltpu.make_async_copy(factor_depth.at[:, pl.ds(start, width)], depth_here, sems.at[0]),
         pltpu.make_async_copy(core, core_here, sems.at[1]),
         pltpu.make_async_copy(coords, coords_out, sems.at[2]),
+        pltpu.make_async_copy(data.at[0], fetched.at[0], sems.at[3]),
+        pltpu.make_async_copy(weight.at[0], fetched.at[1], sems.at[4]),
     ]
     for copy in copies:
         copy.start()
     copies[0].wait()
-    depth_out[...] = depth_here[...].astype(f32).T.astype(bf16)
+    depth = depth_here[...].astype(f32).T.astype(bf16)
+    depth_out[...] = depth
+    order = [depth[t * slab + h * half : t * slab + (h + 1) * half] for h in range(2) for t in range(depth_blocks)]
+    ordered = jnp.concatenate(order, axis=0)
+    count = depth_blocks * half
     copies[1].wait()
     for pair in range(pairs):
         core_out[pair] = jnp.concatenate([core_here[pair], core_here[pairs + pair]], axis=0)
-    copies[2].wait()
-
-
-def bring(factor_depth, core, coords, width):
-    rank = core.shape[0]
-    return pl.pallas_call(
-        bring_kernel,
-        out_shape=(
-            jax.ShapeDtypeStruct((rank // 2, 2 * rank, rank), bf16),
-            jax.ShapeDtypeStruct((width, rank), bf16),
-            jax.ShapeDtypeStruct(coords.shape, coords.dtype),
-        ),
-        in_specs=[pl.BlockSpec(memory_space=pltpu.HBM)] * 3,
-        out_specs=[pl.BlockSpec(memory_space=pltpu.VMEM)] * 2 + [pl.BlockSpec(memory_space=pltpu.SMEM)],
-        scratch_shapes=[
-            pltpu.VMEM((rank, width), bf16),
-            pltpu.VMEM(core.shape, bf16),
-            pltpu.SemaphoreType.DMA((3,)),
-        ],
-        compiler_params=pltpu.CompilerParams(vmem_limit_bytes=16 * 2**20),
-        cost_estimate=pl.CostEstimate(flops=10**6, bytes_accessed=4 * 2**20, transcendentals=0),
-        name="bring",
-    )(factor_depth, core, coords)
-
-
-def cube_kernel(slab, after, core, depth, data, weight, cube_out, cube_turned_out, spread, fetched, cube_wide, sems):
-    pairs, _, rank = core.shape
-    half = slab // 2
-    depth_blocks = cube_out.shape[0]
-    copies = [
-        pltpu.make_async_copy(source.at[0], fetched.at[at], sems.at[at]) for at, source in enumerate((data, weight))
-    ]
-    for copy in copies:
-        copy.start()
-    order = [depth[t * slab + h * half : t * slab + (h + 1) * half] for h in range(2) for t in range(depth_blocks)]
-    ordered = jnp.concatenate(order, axis=0)
-    count = depth_blocks * half
 
     def one_pair(pair, carry):
-        piece = dot(ordered, core[pair], ((1,), (1,)))
+        piece = dot(ordered, core_out[pair], ((1,), (1,)))
         for which in range(2):
             here = piece[:, which * rank : (which + 1) * rank]
             wide = jnp.concatenate([here[:count], here[count:]], axis=1)
@@ -92,36 +82,41 @@
             block = cube_wide[at : at + rank, :]
             cube_out[t, kp * rank : (kp + 1) * rank, :] = block.astype(bf16)
         cube_turned_out[t] = cube_out[t].astype(f32).T.astype(bf16)
-    for at, copy in enumerate(copies):
+    for copy in copies[2:]:
         copy.wait()
+    for at in range(2):
         spread_out(fetched.at[at], spread.at[at])
 
 
-def first_cubes(after, core, depth, data, weight):
-    pairs, _, rank = core.shape
+def first_cubes(after, factor_depth, core, coords, data, weight, depth_blocks):
+    rank = core.shape[0]
     _, rows, slab, cols = data.shape
     half = slab // 2
-    depth_blocks = depth.shape[0] // slab
+    width = depth_blocks * slab
     return pl.pallas_call(
         functools.partial(cube_kernel, slab),
         out_shape=(
             jax.ShapeDtypeStruct((depth_blocks, half * rank, 2 * rank), bf16),
             jax.ShapeDtypeStruct((depth_blocks, 2 * rank, half * rank), bf16),
+            jax.ShapeDtypeStruct((rank // 2, 2 * rank, rank), bf16),
+            jax.ShapeDtypeStruct((width, rank), bf16),
+            jax.ShapeDtypeStruct(coords.shape, coords.dtype),
             jax.ShapeDtypeStruct((2, rows * (slab + 1), cols), f32),
         ),
-        in_specs=[pl.BlockSpec(memory_space=pl.ANY)]
-        + [pl.BlockSpec(memory_space=pltpu.VMEM)] * 2
-        + [pl.BlockSpec(memory_space=pltpu.HBM)] * 2,
-        out_specs=[pl.BlockSpec(memory_space=pltpu.VMEM)] * 3,
+        in_specs=[pl.BlockSpec(memory_space=pl.ANY)] + [pl.BlockSpec(memory_space=pltpu.HBM)] * 5,
+        out_specs=[pl.BlockSpec(memory_space=pltpu.VMEM)] * 4
+        + [pl.BlockSpec(memory_space=pltpu.SMEM), pl.BlockSpec(memory_space=pltpu.VMEM)],
         scratch_shapes=[
+            pltpu.VMEM((rank, width), bf16),
+            pltpu.VMEM(core.shape, bf16),
             pltpu.VMEM((2, rows, slab, cols), bf16),
             pltpu.VMEM((depth_blocks * half * (rank + 1), 2 * rank), f32),
-            pltpu.SemaphoreType.DMA((2,)),
+            pltpu.SemaphoreType.DMA((5,)),
         ],
         compiler_params=pltpu.CompilerParams(vmem_limit_bytes=40 * 2**20),
         cost_estimate=pl.CostEstimate(flops=10**9, bytes_accessed=4 * 2**20, transcendentals=0),
         name="first_cubes",
-    )(after, core, depth, data, weight)
+    )(after, factor_depth, core, coords, data, weight)
 
 
 def masks_of(relative, sizes):
@@ -576,16 +571,8 @@
         and rows == cols == 2 * rank == depth_blocks * slab
     )
 
-    core_pairs, own_depth, coords = bring(
-        depth_here,
-        core_here,
-        pltpu.with_memory_space_constraint(coords.transpose(0, 3, 1, 2), pltpu.HBM),
-        depth_blocks * slab,
-    )
     if by_swaps:
-        other_rows = swap(factor_rows, "ja", n_ja, 1)
-        other_rows, core_pairs = lax.optimization_barrier((other_rows, core_pairs))
-        own = jnp.stack([factor_rows, other_rows, factor_cols])
+        own = jnp.stack([factor_rows, swap(factor_rows, "ja", n_ja, 1), factor_cols])
         pieces = [own] + [swap(own, "ka", n_ka, mask) for mask in range(1, n_ka)]
         row_spots = [(mask, line) for line in range(n_ja) for mask in range(n_ka)]
         col_spots = [(mask, n_ja) for mask in range(n_ka)]
@@ -599,7 +586,15 @@
         own = row_table
         col_spots = [(1, line) for line in range(col_chunks)]
 
-    cube, cube_turned, spread = first_cubes(own, core_pairs, own_depth, data, weight)
+    cube, cube_turned, core_pairs, own_depth, coords, spread = first_cubes(
+        own,
+        depth_here,
+        core_here,
+        pltpu.with_memory_space_constraint(coords.transpose(0, 3, 1, 2), pltpu.HBM),
+        data,
+        weight,
+        depth_blocks,
+    )
     *sums, cols_sum, _ = terms(
         by_swaps,
         sizes,

time: 57.3 us -> 56.4 us (0.984)
  starting transfers between devices: 23.2 us -> 21.3 us
  Pallas kernels: 12.7 us -> 14.1 us
    pallas_call x1 -> x0, Pallas kernels: 2.07 us -> none  [bring(): pl.pallas_call(bring_kernel, out_shape=(jax.ShapeDtypeStruct((rank // 2,...]
    ppermute x18, starting transfers between devices: 23.2 us -> 21.3 us  [swap(): return lax.ppermute(value, axis, [(at, at ^ mask) for at in range(size)])]
    pallas_call x1, Pallas kernels: 2.22 us -> 4.01 us  [first_cubes(): pl.pallas_call(functools.partial(cube_kernel, slab), out_shape=(jax.Shape...]
    pallas_call x1, Pallas kernels: 3.49 us -> 5.24 us  [terms(): pl.pallas_call(functools.partial(terms_kernel, relative, sizes, row_spots...]
  transfers between devices with their start and end apart: 18 -> 18, of which waited for: 9 -> 10; matrix products, arithmetic and copies ran while one was open for 0% -> 0% of each run, Pallas kernels for 11% -> 10%
where the time goes in v8:
time: 56.4 us; the launch traced here: 55.6 us
  starting transfers between devices  21.3 us (38%)
  waiting for transfers between devices  17.5 us (31%)
  Pallas kernels  14.1 us (25%)
  between operations  1.52 us (3%)
  other arithmetic  1.05 us (2%)
    ppermute x18, starting transfers between devices, swap(): return lax.ppermute(value, axis, [(at, at ^ mask) for at in range(size)])  21.3 us
    ppermute x18, waiting for transfers between devices, swap(): return lax.ppermute(value, axis, [(at, at ^ mask) for at in range(size)])  17.5 us
    pallas_call x1, Pallas kernels, terms(): pl.pallas_call(functools.partial(terms_kernel, relative, sizes, row_spots...  5.24 us
    pallas_call x1, Pallas kernels, first_cubes(): pl.pallas_call(functools.partial(cube_kernel, slab), out_shape=(jax.Shape...  4.01 us
    pallas_call x2, Pallas kernels, unpack(): pl.pallas_call(functools.partial(unpack_kernel, sizes, rank, 0 if near el...  2.92 us
    pallas_call x3, Pallas kernels, vmem_call(): pl.pallas_call(kernel, out_shape=out_shape, in_specs=[pl.BlockSpec(memory...  1.96 us
  transfers between devices with their start and end apart: 18, of which 10 were waited for; matrix products, arithmetic and copies ran while one was open for 0% of the time, Pallas kernels for 10%

profile of v8, /device:TPU:0, one launch (start us, length us, event | category | flops | bytes accessed | tf_op | source)
XLA Modules:
  0.0 55.6 jit_solution(11356721215074163119)
XLA Ops:
  0.6 0.5 collective-permute-start
  1.8 0.4 collective-permute-done
  2.2 0.7 %pad_maximum_fusion.after.refs_0_ = bf16[3,64,128]{2,1,0:T(8,128)(2,1)S(1)} fusion(bf16[1,64,128]{2,1,0:T(8,128)(2,1)} %bitcast.10, bf16[1,64,128]{2,1,0:T(8,128)(2,1)S(1)} %bitcast.12, bf16[1,64,128]{2,1,0:T(8,128)(2,1)} %bitcast.11), kind=kLoop, calls=%fused_computation | loop fusion | flops 49152 | bytes 98304 | tf_op jit(solution)/shard_map/stack | solution.py:575
  2.9 5.0 %collective-permute-start.3 = (bf16[3,64,128]{2,1,0:T(8,128)(2,1)S(1)}, bf16[3,64,128]{2,1,0:T(8,128)(2,1)S(1)}, u32[]{:S(2)}, u32[]{:S(2)}) collective-permute-start(bf16[3,64,128]{2,1,0:T(8,128)(2,1)S(1)} %pad_maximum_fusion.after.refs_0_), channel_id=1, source_target_pairs={{0,3},{1,2},{2,1},{3,0},{4,7},{5,6},{6,5},{7,4},{8,11},{9,10},{10,... | collective-permute-start | bytes 147464 | tf_op jit(solution)/shard_map/ppermute | solution.py:548
  7.9 0.0 collective-permute-start.2
  7.9 0.6 %collective-permute-start.1 = (bf16[3,64,128]{2,1,0:T(8,128)(2,1)S(1)}, bf16[3,64,128]{2,1,0:T(8,128)(2,1)S(1)}, u32[]{:S(2)}, u32[]{:S(2)}) collective-permute-start(bf16[3,64,128]{2,1,0:T(8,128)(2,1)S(1)} %pad_maximum_fusion.after.refs_0_), channel_id=1, source_target_pairs={{0,1},{1,0},{2,3},{3,2},{4,5},{5,4},{6,7},{7,6},{8,9},{9,8},{10,11... | collective-permute-start | bytes 147464 | tf_op jit(solution)/shard_map/ppermute | solution.py:548
  8.6 4.0 %first_cubes.1 = (bf16[4,1024,128]{2,1,0:T(8,128)(2,1)S(1)}, bf16[4,128,1024]{2,1,0:T(8,128)(2,1)S(1)}, bf16[32,128,64]{2,1,0:T(8,128)(2,1)S(1)}, bf16[128,64]{1...) custom-call(bf16[3,64,128]{2,1,0:T(8,128)(2,1)S(1)} %pad_maximum_fusion.after.refs_0_, ...), custom_call_target="tpu_custom_call" | custom-call | flops 1000000000 | bytes 4194304 | tf_op jit(solution)/shard_map/first_cubes/pallas_call | solution.py:96
  12.6 0.0 collective-permute-done.3.refs_3_
  12.6 0.3 collective-permute-done.2.refs_2_
  12.9 0.0 collective-permute-done.1.refs_1_
  12.9 5.2 %terms.1 = (f32[21,64,128]{2,1,0:T(8,128)S(1)}, f32[21,64,128]{2,1,0:T(8,128)S(1)}, f32[4,64,128]{2,1,0:T(8,128)S(1)}, f32[2,4224,128]{2,1,0:T(8,128)S(1)}) custom-call(s32[1,1,1]{2,1,0:T(1,128)S(6)} %copy.16.counts, s32[1,3,1,5]{3,2,1,0:T(1,128)S(1)} %get-tuple-element.28.coords, ...), custom_call_target="tpu_custom_call", output_to_operand_aliasing={{3}: (12, {})} | custom-call | flops 1000000000 | bytes 16777216 | tf_op jit(solution)/shard_map/terms/pallas_call | solution.py:325
  18.2 0.1 collective-permute-start.4
  18.3 2.1 %collective-permute-done.4.got = f32[21,64,128]{2,1,0:T(8,128)S(1)} collective-permute-done((f32[21,64,128]{2,1,0:T(8,128)S(1)}, f32[21,64,128]{2,1,0:T(8,128)S(1)}, u32[]{:S(2)}, u32[]{:S(2)}) %collective-permute-start.4) | collective-permute-done | bytes 688160 | tf_op jit(solution)/shard_map/ppermute | solution.py:548
  20.4 0.3 after_cores.1
  20.7 6.3 %collective-permute-start.7 = (f16[336,128]{1,0:T(8,128)(2,1)S(1)}, f16[336,128]{1,0:T(8,128)(2,1)S(1)}, u32[]{:S(2)}, u32[]{:S(2)}) collective-permute-start(f16[336,128]{1,0:T(8,128)(2,1)S(1)} %convert_element_type.67), channel_id=1, source_target_pairs={{0,24},{8,16},{16,8},{24,0},{1,25},{9,17},{17,9},{25,1},{2,26},{10... | collective-permute-start | bytes 258056 | tf_op jit(solution)/shard_map/ppermute | solution.py:548
  27.0 0.0 collective-permute-start.6
  27.0 0.7 %collective-permute-start.5 = (f16[336,128]{1,0:T(8,128)(2,1)S(1)}, f16[336,128]{1,0:T(8,128)(2,1)S(1)}, u32[]{:S(2)}, u32[]{:S(2)}) collective-permute-start(f16[336,128]{1,0:T(8,128)(2,1)S(1)} %convert_element_type.63), channel_id=1, source_target_pairs={{0,8},{8,0},{16,24},{24,16},{1,9},{9,1},{17,25},{25,17},{2,10},{10... | collective-permute-start | bytes 258056 | tf_op jit(solution)/shard_map/ppermute | solution.py:548
  27.7 2.4 %collective-permute-done.7 = f16[336,128]{1,0:T(8,128)(2,1)S(1)} collective-permute-done((f16[336,128]{1,0:T(8,128)(2,1)S(1)}, f16[336,128]{1,0:T(8,128)(2,1)S(1)}, u32[]{:S(2)}, u32[]{:S(2)}) %collective-permute-start.7) | collective-permute-done | bytes 86048 | tf_op jit(solution)/shard_map/ppermute | solution.py:548
  30.1 1.8 %collective-permute-done.6 = f16[336,128]{1,0:T(8,128)(2,1)S(1)} collective-permute-done((f16[336,128]{1,0:T(8,128)(2,1)S(1)}, f16[336,128]{1,0:T(8,128)(2,1)S(1)}, u32[]{:S(2)}, u32[]{:S(2)}) %collective-permute-start.6) | collective-permute-done | bytes 86048 | tf_op jit(solution)/shard_map/ppermute | solution.py:548
  31.9 0.0 collective-permute-done.5
  32.0 0.9 %after_rows.1 = (f32[64,128]{1,0:T(8,128)}, f32[400,128]{1,0:T(8,128)S(1)}, f32[400,128]{1,0:T(8,128)S(1)}, f32[400,128]{1,0:T(8,128)S(1)}, f32[400,128]{1,0:T(8,128)S(1)}) custom-call(f32[4,64,128]{2,1,0:T(8,128)S(1)} %get-tuple-element.36.own_core, f32[64,128]{1,0:T(8,128)S(1)} %get-tuple-element.37.own_depth, ...), custom_call_target="tpu_custom_call" | custom-call | tf_op jit(solution)/shard_map/after_rows/pallas_call | solution.py:361
  32.9 0.1 collective-permute-start.10
  33.0 3.0 %collective-permute-start.9 = (f16[400,128]{1,0:T(8,128)(2,1)S(1)}, f16[400,128]{1,0:T(8,128)(2,1)S(1)}, u32[]{:S(2)}, u32[]{:S(2)}) collective-permute-start(f16[400,128]{1,0:T(8,128)(2,1)S(1)} %convert_element_type.71), channel_id=1, source_target_pairs={{0,2},{1,3},{2,0},{3,1},{4,6},{5,7},{6,4},{7,5},{8,10},{9,11},{10,... | collective-permute-start | bytes 307208 | tf_op jit(solution)/shard_map/ppermute | solution.py:548
  36.0 1.5 %collective-permute-start.8 = (f16[400,128]{1,0:T(8,128)(2,1)S(1)}, f16[400,128]{1,0:T(8,128)(2,1)S(1)}, u32[]{:S(2)}, u32[]{:S(2)}) collective-permute-start(f16[400,128]{1,0:T(8,128)(2,1)S(1)} %convert_element_type.69), channel_id=1, source_target_pairs={{0,1},{1,0},{2,3},{3,2},{4,5},{5,4},{6,7},{7,6},{8,9},{9,8},{10,11... | collective-permute-start | bytes 307208 | tf_op jit(solution)/shard_map/ppermute | solution.py:548
  37.5 3.1 %collective-permute-done.10 = f16[400,128]{1,0:T(8,128)(2,1)S(1)} collective-permute-done((f16[400,128]{1,0:T(8,128)(2,1)S(1)}, f16[400,128]{1,0:T(8,128)(2,1)S(1)}, u32[]{:S(2)}, u32[]{:S(2)}) %collective-permute-start.10) | collective-permute-done | bytes 102432 | tf_op jit(solution)/shard_map/ppermute | solution.py:548
  40.6 3.4 %collective-permute-done.9 = f16[400,128]{1,0:T(8,128)(2,1)S(1)} collective-permute-done((f16[400,128]{1,0:T(8,128)(2,1)S(1)}, f16[400,128]{1,0:T(8,128)(2,1)S(1)}, u32[]{:S(2)}, u32[]{:S(2)}) %collective-permute-start.9) | collective-permute-done | bytes 102432 | tf_op jit(solution)/shard_map/ppermute | solution.py:548
  44.0 0.0 collective-permute-done.8
  44.0 0.8 %after_depths.1 = (f32[336,128]{1,0:T(8,128)S(1)}, f32[64,128]{1,0:T(8,128)}) custom-call(f32[400,128]{1,0:T(8,128)S(1)} %get-tuple-element.43.refs_0_, f32[400,128]{1,0:T(8,128)S(1)} %convert_element_type.70.refs_1_, f32[400,128]{1,0:T(8,128)S(1)} %convert_element_type.72.refs_2_, f32[400,128]{1,0:T(8,128)S(1)} %convert_element_type.74.refs_3_), custom_call_target="tpu_custom_call" | custom-call | tf_op jit(solution)/shard_map/after_depths/pallas_call | solution.py:361
  44.8 2.5 %collective-permute-start.13 = (f16[336,128]{1,0:T(8,128)(2,1)S(1)}, f16[336,128]{1,0:T(8,128)(2,1)S(1)}, u32[]{:S(2)}, u32[]{:S(2)}) collective-permute-start(f16[336,128]{1,0:T(8,128)(2,1)S(1)} %get-tuple-element.53), channel_id=1, source_target_pairs={{0,24},{8,16},{16,8},{24,0},{1,25},{9,17},{17,9},{25,1},{2,26},{10... | collective-permute-start | bytes 258056 | tf_op jit(solution)/shard_map/ppermute | solution.py:548
  47.4 0.6 %collective-permute-start.12 = (f16[336,128]{1,0:T(8,128)(2,1)S(1)}, f16[336,128]{1,0:T(8,128)(2,1)S(1)}, u32[]{:S(2)}, u32[]{:S(2)}) collective-permute-start(f16[336,128]{1,0:T(8,128)(2,1)S(1)} %get-tuple-element.53), channel_id=1, source_target_pairs={{0,16},{8,24},{16,0},{24,8},{1,17},{9,25},{17,1},{25,9},{2,18},{10... | collective-permute-start | bytes 258056 | tf_op jit(solution)/shard_map/ppermute | solution.py:548
  47.9 0.5 collective-permute-start.11
  48.4 0.0 collective-permute-start.14
  48.4 2.6 %collective-permute-done.13 = f16[336,128]{1,0:T(8,128)(2,1)S(1)} collective-permute-done((f16[336,128]{1,0:T(8,128)(2,1)S(1)}, f16[336,128]{1,0:T(8,128)(2,1)S(1)}, u32[]{:S(2)}, u32[]{:S(2)}) %collective-permute-start.13) | collective-permute-done | bytes 86048 | tf_op jit(solution)/shard_map/ppermute | solution.py:548
  51.0 0.0 collective-permute-start.17
  51.0 0.9 %collective-permute-done.12 = f16[336,128]{1,0:T(8,128)(2,1)S(1)} collective-permute-done((f16[336,128]{1,0:T(8,128)(2,1)S(1)}, f16[336,128]{1,0:T(8,128)(2,1)S(1)}, u32[]{:S(2)}, u32[]{:S(2)}) %collective-permute-start.12) | collective-permute-done | bytes 86048 | tf_op jit(solution)/shard_map/ppermute | solution.py:548
  51.9 0.0 collective-permute-start.16
  51.9 0.5 collective-permute-done.11
  52.4 0.0 collective-permute-start.15
  52.5 0.0 collective-permute-done.14
  52.5 1.8 %unpack_near.1 = (f32[64,64,64]{2,1,0:T(8,128)}, f32[64,128]{1,0:T(8,128)}) custom-call(f32[336,128]{1,0:T(8,128)S(1)} %get-tuple-element.52.refs_0_, f32[336,128]{1,0:T(8,128)S(1)} %convert_element_type.77.refs_1_, f32[336,128]{1,0:T(8,128)S(1)} %convert_element_type.78.refs_2_, f32[336,128]{1,0:T(8,128)S(1)} %convert_element_type.79.refs_3_), custom_call_target="tpu_custom_call" | custom-call | flops 1000000 | bytes 4194304 | tf_op jit(solution)/shard_map/unpack_near/pallas_call | solution.py:526
  54.3 0.0 collective-permute-done.17
  54.3 0.0 collective-permute-done.16
  54.4 0.0 collective-permute-done.15
  54.4 1.1 %unpack_far.1 = f32[64,64,64]{2,1,0:T(8,128)} custom-call(f32[336,128]{1,0:T(8,128)S(1)} %convert_element_type.80.refs_0_, f32[336,128]{1,0:T(8,128)S(1)} %convert_element_type.81.refs_1_, f32[336,128]{1,0:T(8,128)S(1)} %convert_element_type.82.refs_2_, f32[336,128]{1,0:T(8,128)S(1)} %convert_element_type.83.refs_3_, ...), custom_call_target="tpu_custom_call", output_to_operand_aliasing={{}: (4, {})} | custom-call | flops 1000000 | bytes 4194304 | tf_op jit(solution)/shard_map/unpack_far/pallas_call | solution.py:526
  (20 shorter events, 0.3 us)
Async XLA Ops:
  0.6 1.6 %collective-permute-start = (bf16[64,128]{1,0:T(8,128)(2,1)}, bf16[64,128]{1,0:T(8,128)(2,1)S(1)}, u32[]{:S(2)}, u32[]{:S(2)}) collective-permute-start(bf16[64,128]{1,0:T(8,128)(2,1)} %param.12), channel_id=1, source_target_pairs={{0,4},{4,0},{1,5},{5,1},{2,6},{6,2},{3,7},{7,3},{8,12},{12,8},{9,1... | collective-permute-start | bytes 49160 | tf_op jit(solution)/shard_map/ppermute | solution.py:548
  2.9 9.7 %collective-permute-start.3 = (bf16[3,64,128]{2,1,0:T(8,128)(2,1)S(1)}, bf16[3,64,128]{2,1,0:T(8,128)(2,1)S(1)}, u32[]{:S(2)}, u32[]{:S(2)}) collective-permute-start(bf16[3,64,128]{2,1,0:T(8,128)(2,1)S(1)} %pad_maximum_fusion.after.refs_0_), channel_id=1, source_target_pairs={{0,3},{1,2},{2,1},{3,0},{4,7},{5,6},{6,5},{7,4},{8,11},{9,10},{10,... | collective-permute-start | bytes 147464 | tf_op jit(solution)/shard_map/ppermute | solution.py:548
  7.9 5.0 %collective-permute-start.2 = (bf16[3,64,128]{2,1,0:T(8,128)(2,1)S(1)}, bf16[3,64,128]{2,1,0:T(8,128)(2,1)S(1)}, u32[]{:S(2)}, u32[]{:S(2)}) collective-permute-start(bf16[3,64,128]{2,1,0:T(8,128)(2,1)S(1)} %pad_maximum_fusion.after.refs_0_), channel_id=1, source_target_pairs={{0,2},{1,3},{2,0},{3,1},{4,6},{5,7},{6,4},{7,5},{8,10},{9,11},{10,... | collective-permute-start | bytes 147464 | tf_op jit(solution)/shard_map/ppermute | solution.py:548
  7.9 5.0 %collective-permute-start.1 = (bf16[3,64,128]{2,1,0:T(8,128)(2,1)S(1)}, bf16[3,64,128]{2,1,0:T(8,128)(2,1)S(1)}, u32[]{:S(2)}, u32[]{:S(2)}) collective-permute-start(bf16[3,64,128]{2,1,0:T(8,128)(2,1)S(1)} %pad_maximum_fusion.after.refs_0_), channel_id=1, source_target_pairs={{0,1},{1,0},{2,3},{3,2},{4,5},{5,4},{6,7},{7,6},{8,9},{9,8},{10,11... | collective-permute-start | bytes 147464 | tf_op jit(solution)/shard_map/ppermute | solution.py:548
  18.2 2.2 %collective-permute-start.4 = (f32[21,64,128]{2,1,0:T(8,128)S(1)}, f32[21,64,128]{2,1,0:T(8,128)S(1)}, u32[]{:S(2)}, u32[]{:S(2)}) collective-permute-start(f32[21,64,128]{2,1,0:T(8,128)S(1)} %get-tuple-element.35), channel_id=1, source_target_pairs={{0,4},{4,0},{1,5},{5,1},{2,6},{6,2},{3,7},{7,3},{8,12},{12,8},{9,1... | collective-permute-start | bytes 2064392 | tf_op jit(solution)/shard_map/ppermute | solution.py:548
  20.7 9.4 %collective-permute-start.7 = (f16[336,128]{1,0:T(8,128)(2,1)S(1)}, f16[336,128]{1,0:T(8,128)(2,1)S(1)}, u32[]{:S(2)}, u32[]{:S(2)}) collective-permute-start(f16[336,128]{1,0:T(8,128)(2,1)S(1)} %convert_element_type.67), channel_id=1, source_target_pairs={{0,24},{8,16},{16,8},{24,0},{1,25},{9,17},{17,9},{25,1},{2,26},{10... | collective-permute-start | bytes 258056 | tf_op jit(solution)/shard_map/ppermute | solution.py:548
  27.0 4.9 %collective-permute-start.6 = (f16[336,128]{1,0:T(8,128)(2,1)S(1)}, f16[336,128]{1,0:T(8,128)(2,1)S(1)}, u32[]{:S(2)}, u32[]{:S(2)}) collective-permute-start(f16[336,128]{1,0:T(8,128)(2,1)S(1)} %convert_element_type.65), channel_id=1, source_target_pairs={{0,16},{8,24},{16,0},{24,8},{1,17},{9,25},{17,1},{25,9},{2,18},{10... | collective-permute-start | bytes 258056 | tf_op jit(solution)/shard_map/ppermute | solution.py:548
  27.0 4.9 %collective-permute-start.5 = (f16[336,128]{1,0:T(8,128)(2,1)S(1)}, f16[336,128]{1,0:T(8,128)(2,1)S(1)}, u32[]{:S(2)}, u32[]{:S(2)}) collective-permute-start(f16[336,128]{1,0:T(8,128)(2,1)S(1)} %convert_element_type.63), channel_id=1, source_target_pairs={{0,8},{8,0},{16,24},{24,16},{1,9},{9,1},{17,25},{25,17},{2,10},{10... | collective-permute-start | bytes 258056 | tf_op jit(solution)/shard_map/ppermute | solution.py:548
  32.9 7.7 %collective-permute-start.10 = (f16[400,128]{1,0:T(8,128)(2,1)S(1)}, f16[400,128]{1,0:T(8,128)(2,1)S(1)}, u32[]{:S(2)}, u32[]{:S(2)}) collective-permute-start(f16[400,128]{1,0:T(8,128)(2,1)S(1)} %convert_element_type.73), channel_id=1, source_target_pairs={{0,3},{1,2},{2,1},{3,0},{4,7},{5,6},{6,5},{7,4},{8,11},{9,10},{10,... | collective-permute-start | bytes 307208 | tf_op jit(solution)/shard_map/ppermute | solution.py:548
  33.0 11.0 %collective-permute-start.9 = (f16[400,128]{1,0:T(8,128)(2,1)S(1)}, f16[400,128]{1,0:T(8,128)(2,1)S(1)}, u32[]{:S(2)}, u32[]{:S(2)}) collective-permute-start(f16[400,128]{1,0:T(8,128)(2,1)S(1)} %convert_element_type.71), channel_id=1, source_target_pairs={{0,2},{1,3},{2,0},{3,1},{4,6},{5,7},{6,4},{7,5},{8,10},{9,11},{10,... | collective-permute-start | bytes 307208 | tf_op jit(solution)/shard_map/ppermute | solution.py:548
  36.0 8.0 %collective-permute-start.8 = (f16[400,128]{1,0:T(8,128)(2,1)S(1)}, f16[400,128]{1,0:T(8,128)(2,1)S(1)}, u32[]{:S(2)}, u32[]{:S(2)}) collective-permute-start(f16[400,128]{1,0:T(8,128)(2,1)S(1)} %convert_element_type.69), channel_id=1, source_target_pairs={{0,1},{1,0},{2,3},{3,2},{4,5},{5,4},{6,7},{7,6},{8,9},{9,8},{10,11... | collective-permute-start | bytes 307208 | tf_op jit(solution)/shard_map/ppermute | solution.py:548
  44.8 6.2 %collective-permute-start.13 = (f16[336,128]{1,0:T(8,128)(2,1)S(1)}, f16[336,128]{1,0:T(8,128)(2,1)S(1)}, u32[]{:S(2)}, u32[]{:S(2)}) collective-permute-start(f16[336,128]{1,0:T(8,128)(2,1)S(1)} %get-tuple-element.53), channel_id=1, source_target_pairs={{0,24},{8,16},{16,8},{24,0},{1,25},{9,17},{17,9},{25,1},{2,26},{10... | collective-permute-start | bytes 258056 | tf_op jit(solution)/shard_map/ppermute | solution.py:548
  47.4 4.5 %collective-permute-start.12 = (f16[336,128]{1,0:T(8,128)(2,1)S(1)}, f16[336,128]{1,0:T(8,128)(2,1)S(1)}, u32[]{:S(2)}, u32[]{:S(2)}) collective-permute-start(f16[336,128]{1,0:T(8,128)(2,1)S(1)} %get-tuple-element.53), channel_id=1, source_target_pairs={{0,16},{8,24},{16,0},{24,8},{1,17},{9,25},{17,1},{25,9},{2,18},{10... | collective-permute-start | bytes 258056 | tf_op jit(solution)/shard_map/ppermute | solution.py:548
  47.9 4.5 %collective-permute-start.11 = (f16[336,128]{1,0:T(8,128)(2,1)S(1)}, f16[336,128]{1,0:T(8,128)(2,1)S(1)}, u32[]{:S(2)}, u32[]{:S(2)}) collective-permute-start(f16[336,128]{1,0:T(8,128)(2,1)S(1)} %get-tuple-element.53), channel_id=1, source_target_pairs={{0,8},{8,0},{16,24},{24,16},{1,9},{9,1},{17,25},{25,17},{2,10},{10... | collective-permute-start | bytes 258056 | tf_op jit(solution)/shard_map/ppermute | solution.py:548
  48.4 4.1 %collective-permute-start.14 = (f16[336,128]{1,0:T(8,128)(2,1)S(1)}, f16[336,128]{1,0:T(8,128)(2,1)S(1)}, u32[]{:S(2)}, u32[]{:S(2)}) collective-permute-start(f16[336,128]{1,0:T(8,128)(2,1)S(1)} %get-tuple-element.53), channel_id=1, source_target_pairs={{0,4},{4,0},{1,5},{5,1},{2,6},{6,2},{3,7},{7,3},{8,12},{12,8},{9,1... | collective-permute-start | bytes 258056 | tf_op jit(solution)/shard_map/ppermute | solution.py:548
  51.0 3.3 %collective-permute-start.17 = (f16[336,128]{1,0:T(8,128)(2,1)S(1)}, f16[336,128]{1,0:T(8,128)(2,1)S(1)}, u32[]{:S(2)}, u32[]{:S(2)}) collective-permute-start(f16[336,128]{1,0:T(8,128)(2,1)S(1)} %collective-permute-done.13), channel_id=1, source_target_pairs={{0,4},{4,0},{1,5},{5,1},{2,6},{6,2},{3,7},{7,3},{8,12},{12,8},{9,1... | collective-permute-start | bytes 258056 | tf_op jit(solution)/shard_map/ppermute | solution.py:548
  51.9 2.5 %collective-permute-start.16 = (f16[336,128]{1,0:T(8,128)(2,1)S(1)}, f16[336,128]{1,0:T(8,128)(2,1)S(1)}, u32[]{:S(2)}, u32[]{:S(2)}) collective-permute-start(f16[336,128]{1,0:T(8,128)(2,1)S(1)} %collective-permute-done.12), channel_id=1, source_target_pairs={{0,4},{4,0},{1,5},{5,1},{2,6},{6,2},{3,7},{7,3},{8,12},{12,8},{9,1... | collective-permute-start | bytes 258056 | tf_op jit(solution)/shard_map/ppermute | solution.py:548
  52.4 1.9 %collective-permute-start.15 = (f16[336,128]{1,0:T(8,128)(2,1)S(1)}, f16[336,128]{1,0:T(8,128)(2,1)S(1)}, u32[]{:S(2)}, u32[]{:S(2)}) collective-permute-start(f16[336,128]{1,0:T(8,128)(2,1)S(1)} %collective-permute-done.11), channel_id=1, source_target_pairs={{0,4},{4,0},{1,5},{5,1},{2,6},{6,2},{3,7},{7,3},{8,12},{12,8},{9,1... | collective-permute-start | bytes 258056 | tf_op jit(solution)/shard_map/ppermute | solution.py:548

commit v9 on v8

--- a/solution.py
+++ b/solution.py
@@ -276,11 +276,11 @@
     else:
         core_spots = [(outs[0], 0, at) for at in range(pairs)]
         row_places = [(outs[1], 0, at) for at in range(len(row_spots))]
-    total = jnp.zeros((second_all.shape[1], rank), f32)
+    deep = jnp.concatenate([second_all[pair] for pair in range(pairs)], axis=1)
+    total = dot(deep, core[...].reshape(pairs * 2 * rank, rank))
     for at in range(pairs):
         pair = at ^ core_mask
         second = second_all[pair]
-        total = total + dot(second, core[pair])
         piece = dot(second, depth_all[...], ((0,), (0,)))
         out, _, line = core_spots[at]
         out[line] = jnp.concatenate([piece[:rank], piece[rank:]], axis=1)
@@ -491,14 +491,15 @@
     return vmem_call(functools.partial(after_depths_kernel, n_ka, rank), outs, *messages, name="after_depths")
 
 
-def unpack_kernel(sizes, rank, first_message, *refs):
-    n_ia, n_ka = sizes["ia"], sizes["ka"]
-    messages = refs[:n_ia]
-    core_out, *cols_out, whole, sems = refs[n_ia if first_message == 0 else n_ia + 1 :]
+def unpack_kernel(sizes, rank, first_message, count, with_cols, *refs):
+    n_ka = sizes["ka"]
+    messages, refs = refs[:count], refs[count:]
+    cols_from, refs = refs[:with_cols], refs[with_cols:]
+    core_out, *cols_out, whole, sems = refs[0 if first_message == 0 else 1 :]
     pairs = rank // 2
     own = masks_of(True, sizes)[2]
     copies = []
-    for at in range(n_ia):
+    for at in range(count):
         first = pl.multiple_of(((own // n_ka) ^ (first_message + at)) * n_ka, n_ka)
         for mask in range(n_ka):
             piece = message_part(messages[at], mask * rank, rank, 0)
@@ -509,35 +510,36 @@
             lines = pl.ds(h * pairs + first, n_ka)
             copies.append(pltpu.make_async_copy(whole.at[at, h], core_out.at[lines], sems.at[2 * at + h]))
             copies[-1].start()
-    for out in cols_out:
-        out[...] = tree_sum(message_part(message, n_ka * rank, rank, 1) for message in messages)
+    if with_cols:
+        cols_out[0][...] = tree_sum(message_part(message, n_ka * rank, rank, 1) for message in cols_from)
     for copy in copies:
         copy.wait()
 
 
-def unpack(sizes, rank, messages, core=None):
+def unpack(sizes, rank, first_message, messages, core=None, cols_from=()):
     lanes = messages[0].shape[1]
-    near = core is None
+    count = len(messages)
+    given = [] if core is None else [core]
     out_shape = [jax.ShapeDtypeStruct((rank, rank, rank), f32)]
     out_specs = [pl.BlockSpec(memory_space=pltpu.HBM)]
-    if near:
+    if cols_from:
         out_shape.append(jax.ShapeDtypeStruct((rank, lanes), f32))
         out_specs.append(pl.BlockSpec(memory_space=pltpu.VMEM))
     return pl.pallas_call(
-        functools.partial(unpack_kernel, sizes, rank, 0 if near else sizes["ia"]),
+        functools.partial(unpack_kernel, sizes, rank, first_message, count, len(cols_from)),
         out_shape=tuple(out_shape),
-        in_specs=[pl.BlockSpec(memory_space=pltpu.VMEM)] * len(messages)
-        + ([] if near else [pl.BlockSpec(memory_space=pltpu.HBM)]),
+        in_specs=[pl.BlockSpec(memory_space=pltpu.VMEM)] * (count + len(cols_from))
+        + [pl.BlockSpec(memory_space=pltpu.HBM)] * len(given),
         out_specs=tuple(out_specs),
         scratch_shapes=[
-            pltpu.VMEM((len(messages), 2, sizes["ka"], rank, rank), f32),
-            pltpu.SemaphoreType.DMA((2 * len(messages),)),
+            pltpu.VMEM((count, 2, sizes["ka"], rank, rank), f32),
+            pltpu.SemaphoreType.DMA((2 * count,)),
         ],
-        input_output_aliases={} if near else {len(messages): 0},
+        input_output_aliases={count + len(cols_from): 0} if given else {},
         compiler_params=pltpu.CompilerParams(vmem_limit_bytes=24 * 2**20),
         cost_estimate=pl.CostEstimate(flops=10**6, bytes_accessed=4 * 2**20, transcendentals=0),
-        name="unpack_near" if near else "unpack_far",
-    )(*messages, *([] if near else [core]))
+        name=f"unpack_{first_message}",
+    )(*messages, *cols_from, *given)
 
 
 def power_of_two(n):
@@ -636,8 +638,10 @@
     sent = message.astype(wire)
     sent = [sent] + [swap(sent, "ia", n_ia, mask) for mask in range(1, n_ia)]
     other = [swap(each, "ja", n_ja, 1) for each in sent]
-    core_near, cols_total = unpack(sizes, rank, [each.astype(f32) for each in sent])
-    (core_total,) = unpack(sizes, rank, [each.astype(f32) for each in other], core_near)
+    near = [message] + [each.astype(f32) for each in sent[1:]]
+    (core_own,) = unpack(sizes, rank, 0, near[:1])
+    core_near, cols_total = unpack(sizes, rank, 1, near[1:], core_own, near)
+    (core_total,) = unpack(sizes, rank, n_ia, [each.astype(f32) for each in other], core_near)
     return (rows_total, cols_total, depth_total, core_total)
 
 

time: 56.4 us -> 57.5 us (1.020); the launches traced: 55.6 us -> 57.6 us
  starting transfers between devices: 21.3 us -> 22.7 us
  Pallas kernels: 14.1 us -> 14.9 us
    ppermute x18, starting transfers between devices: 21.3 us -> 22.7 us  [swap(): return lax.ppermute(value, axis, [(at, at ^ mask) for at in range(size)])]
    pallas_call x2 -> x3, Pallas kernels: 2.92 us -> 3.65 us  [unpack(): pl.pallas_call(functools.partial(unpack_kernel, sizes, rank, first_messag...]
  transfers between devices with their start and end apart: 18 -> 18, of which waited for: 10 -> 10; matrix products, arithmetic and copies ran while one was open for 0% -> 0% of each run, Pallas kernels for 10% -> 11%
where the time goes in v9:
time: 57.5 us; the launch traced here: 57.6 us
  starting transfers between devices  22.7 us (39%)
  waiting for transfers between devices  17.4 us (30%)
  Pallas kernels  14.9 us (26%)
  between operations  1.53 us (3%)
  other arithmetic  1.04 us (2%)
    ppermute x18, starting transfers between devices, swap(): return lax.ppermute(value, axis, [(at, at ^ mask) for at in range(size)])  22.7 us
    ppermute x18, waiting for transfers between devices, swap(): return lax.ppermute(value, axis, [(at, at ^ mask) for at in range(size)])  17.4 us
    pallas_call x1, Pallas kernels, terms(): pl.pallas_call(functools.partial(terms_kernel, relative, sizes, row_spots...  5.28 us
    pallas_call x1, Pallas kernels, first_cubes(): pl.pallas_call(functools.partial(cube_kernel, slab), out_shape=(jax.Shape...  4.01 us
    pallas_call x3, Pallas kernels, unpack(): pl.pallas_call(functools.partial(unpack_kernel, sizes, rank, first_messag...  3.65 us
    pallas_call x3, Pallas kernels, vmem_call(): pl.pallas_call(kernel, out_shape=out_shape, in_specs=[pl.BlockSpec(memory...  1.96 us
  transfers between devices with their start and end apart: 18, of which 10 were waited for; matrix products, arithmetic and copies ran while one was open for 0% of the time, Pallas kernels for 11%

profile of v9, /device:TPU:0, one launch (start us, length us, event | category | flops | bytes accessed | tf_op | source)
XLA Modules:
  0.0 57.6 jit_solution(9346631690101341421)
XLA Ops:
  0.6 0.5 collective-permute-start
  1.8 0.4 collective-permute-done
  2.2 0.7 %pad_maximum_fusion.after.refs_0_ = bf16[3,64,128]{2,1,0:T(8,128)(2,1)S(1)} fusion(bf16[1,64,128]{2,1,0:T(8,128)(2,1)} %bitcast.10, bf16[1,64,128]{2,1,0:T(8,128)(2,1)S(1)} %bitcast.12, bf16[1,64,128]{2,1,0:T(8,128)(2,1)} %bitcast.11), kind=kLoop, calls=%fused_computation | loop fusion | flops 49152 | bytes 98304 | tf_op jit(solution)/shard_map/stack | solution.py:577
  2.9 5.0 %collective-permute-start.3 = (bf16[3,64,128]{2,1,0:T(8,128)(2,1)S(1)}, bf16[3,64,128]{2,1,0:T(8,128)(2,1)S(1)}, u32[]{:S(2)}, u32[]{:S(2)}) collective-permute-start(bf16[3,64,128]{2,1,0:T(8,128)(2,1)S(1)} %pad_maximum_fusion.after.refs_0_), channel_id=1, source_target_pairs={{0,3},{1,2},{2,1},{3,0},{4,7},{5,6},{6,5},{7,4},{8,11},{9,10},{10,... | collective-permute-start | bytes 147464 | tf_op jit(solution)/shard_map/ppermute | solution.py:550
  7.9 0.0 collective-permute-start.2
  7.9 0.6 %collective-permute-start.1 = (bf16[3,64,128]{2,1,0:T(8,128)(2,1)S(1)}, bf16[3,64,128]{2,1,0:T(8,128)(2,1)S(1)}, u32[]{:S(2)}, u32[]{:S(2)}) collective-permute-start(bf16[3,64,128]{2,1,0:T(8,128)(2,1)S(1)} %pad_maximum_fusion.after.refs_0_), channel_id=1, source_target_pairs={{0,1},{1,0},{2,3},{3,2},{4,5},{5,4},{6,7},{7,6},{8,9},{9,8},{10,11... | collective-permute-start | bytes 147464 | tf_op jit(solution)/shard_map/ppermute | solution.py:550
  8.6 4.0 %first_cubes.1 = (bf16[4,1024,128]{2,1,0:T(8,128)(2,1)S(1)}, bf16[4,128,1024]{2,1,0:T(8,128)(2,1)S(1)}, bf16[32,128,64]{2,1,0:T(8,128)(2,1)S(1)}, bf16[128,64]{1...) custom-call(bf16[3,64,128]{2,1,0:T(8,128)(2,1)S(1)} %pad_maximum_fusion.after.refs_0_, ...), custom_call_target="tpu_custom_call" | custom-call | flops 1000000000 | bytes 4194304 | tf_op jit(solution)/shard_map/first_cubes/pallas_call | solution.py:96
  12.6 0.0 collective-permute-done.3.refs_3_
  12.6 0.3 collective-permute-done.2.refs_2_
  12.9 0.0 collective-permute-done.1.refs_1_
  12.9 5.3 %terms.1 = (f32[21,64,128]{2,1,0:T(8,128)S(1)}, f32[21,64,128]{2,1,0:T(8,128)S(1)}, f32[4,64,128]{2,1,0:T(8,128)S(1)}, f32[2,4224,128]{2,1,0:T(8,128)S(1)}) custom-call(s32[1,1,1]{2,1,0:T(1,128)S(6)} %copy.18.counts, s32[1,3,1,5]{3,2,1,0:T(1,128)S(1)} %get-tuple-element.28.coords, ...), custom_call_target="tpu_custom_call", output_to_operand_aliasing={{3}: (12, {})} | custom-call | flops 1000000000 | bytes 16777216 | tf_op jit(solution)/shard_map/terms/pallas_call | solution.py:325
  18.2 0.1 collective-permute-start.4
  18.3 2.1 %collective-permute-done.4.got = f32[21,64,128]{2,1,0:T(8,128)S(1)} collective-permute-done((f32[21,64,128]{2,1,0:T(8,128)S(1)}, f32[21,64,128]{2,1,0:T(8,128)S(1)}, u32[]{:S(2)}, u32[]{:S(2)}) %collective-permute-start.4) | collective-permute-done | bytes 688160 | tf_op jit(solution)/shard_map/ppermute | solution.py:550
  20.4 0.3 after_cores.1
  20.7 7.4 %collective-permute-start.7 = (f16[336,128]{1,0:T(8,128)(2,1)S(1)}, f16[336,128]{1,0:T(8,128)(2,1)S(1)}, u32[]{:S(2)}, u32[]{:S(2)}) collective-permute-start(f16[336,128]{1,0:T(8,128)(2,1)S(1)} %convert_element_type.64), channel_id=1, source_target_pairs={{0,24},{8,16},{16,8},{24,0},{1,25},{9,17},{17,9},{25,1},{2,26},{10... | collective-permute-start | bytes 258056 | tf_op jit(solution)/shard_map/ppermute | solution.py:550
  28.1 0.0 collective-permute-start.6
  28.1 0.7 %collective-permute-start.5 = (f16[336,128]{1,0:T(8,128)(2,1)S(1)}, f16[336,128]{1,0:T(8,128)(2,1)S(1)}, u32[]{:S(2)}, u32[]{:S(2)}) collective-permute-start(f16[336,128]{1,0:T(8,128)(2,1)S(1)} %convert_element_type.60), channel_id=1, source_target_pairs={{0,8},{8,0},{16,24},{24,16},{1,9},{9,1},{17,25},{25,17},{2,10},{10... | collective-permute-start | bytes 258056 | tf_op jit(solution)/shard_map/ppermute | solution.py:550
  28.8 2.2 %collective-permute-done.7 = f16[336,128]{1,0:T(8,128)(2,1)S(1)} collective-permute-done((f16[336,128]{1,0:T(8,128)(2,1)S(1)}, f16[336,128]{1,0:T(8,128)(2,1)S(1)}, u32[]{:S(2)}, u32[]{:S(2)}) %collective-permute-start.7) | collective-permute-done | bytes 86048 | tf_op jit(solution)/shard_map/ppermute | solution.py:550
  31.1 1.7 %collective-permute-done.6 = f16[336,128]{1,0:T(8,128)(2,1)S(1)} collective-permute-done((f16[336,128]{1,0:T(8,128)(2,1)S(1)}, f16[336,128]{1,0:T(8,128)(2,1)S(1)}, u32[]{:S(2)}, u32[]{:S(2)}) %collective-permute-start.6) | collective-permute-done | bytes 86048 | tf_op jit(solution)/shard_map/ppermute | solution.py:550
  32.8 0.0 collective-permute-done.5
  32.8 0.9 %after_rows.1 = (f32[64,128]{1,0:T(8,128)}, f32[400,128]{1,0:T(8,128)S(1)}, f32[400,128]{1,0:T(8,128)S(1)}, f32[400,128]{1,0:T(8,128)S(1)}, f32[400,128]{1,0:T(8,128)S(1)}) custom-call(f32[4,64,128]{2,1,0:T(8,128)S(1)} %get-tuple-element.36.own_core, f32[64,128]{1,0:T(8,128)S(1)} %get-tuple-element.37.own_depth, ...), custom_call_target="tpu_custom_call" | custom-call | tf_op jit(solution)/shard_map/after_rows/pallas_call | solution.py:361
  33.8 0.1 collective-permute-start.10
  33.8 2.5 %collective-permute-start.9 = (f16[400,128]{1,0:T(8,128)(2,1)S(1)}, f16[400,128]{1,0:T(8,128)(2,1)S(1)}, u32[]{:S(2)}, u32[]{:S(2)}) collective-permute-start(f16[400,128]{1,0:T(8,128)(2,1)S(1)} %convert_element_type.68), channel_id=1, source_target_pairs={{0,2},{1,3},{2,0},{3,1},{4,6},{5,7},{6,4},{7,5},{8,10},{9,11},{10,... | collective-permute-start | bytes 307208 | tf_op jit(solution)/shard_map/ppermute | solution.py:550
  36.4 1.9 %collective-permute-start.8 = (f16[400,128]{1,0:T(8,128)(2,1)S(1)}, f16[400,128]{1,0:T(8,128)(2,1)S(1)}, u32[]{:S(2)}, u32[]{:S(2)}) collective-permute-start(f16[400,128]{1,0:T(8,128)(2,1)S(1)} %convert_element_type.66), channel_id=1, source_target_pairs={{0,1},{1,0},{2,3},{3,2},{4,5},{5,4},{6,7},{7,6},{8,9},{9,8},{10,11... | collective-permute-start | bytes 307208 | tf_op jit(solution)/shard_map/ppermute | solution.py:550
  38.3 3.1 %collective-permute-done.10 = f16[400,128]{1,0:T(8,128)(2,1)S(1)} collective-permute-done((f16[400,128]{1,0:T(8,128)(2,1)S(1)}, f16[400,128]{1,0:T(8,128)(2,1)S(1)}, u32[]{:S(2)}, u32[]{:S(2)}) %collective-permute-start.10) | collective-permute-done | bytes 102432 | tf_op jit(solution)/shard_map/ppermute | solution.py:550
  41.5 3.6 %collective-permute-done.9 = f16[400,128]{1,0:T(8,128)(2,1)S(1)} collective-permute-done((f16[400,128]{1,0:T(8,128)(2,1)S(1)}, f16[400,128]{1,0:T(8,128)(2,1)S(1)}, u32[]{:S(2)}, u32[]{:S(2)}) %collective-permute-start.9) | collective-permute-done | bytes 102432 | tf_op jit(solution)/shard_map/ppermute | solution.py:550
  45.1 0.0 collective-permute-done.8
  45.2 0.8 %after_depths.1 = (f32[336,128]{1,0:T(8,128)S(1)}, f32[64,128]{1,0:T(8,128)}) custom-call(f32[400,128]{1,0:T(8,128)S(1)} %get-tuple-element.43.refs_0_, f32[400,128]{1,0:T(8,128)S(1)} %convert_element_type.67.refs_1_, f32[400,128]{1,0:T(8,128)S(1)} %convert_element_type.69.refs_2_, f32[400,128]{1,0:T(8,128)S(1)} %convert_element_type.71.refs_3_), custom_call_target="tpu_custom_call" | custom-call | tf_op jit(solution)/shard_map/after_depths/pallas_call | solution.py:361
  46.0 1.2 %collective-permute-start.13 = (f16[336,128]{1,0:T(8,128)(2,1)S(1)}, f16[336,128]{1,0:T(8,128)(2,1)S(1)}, u32[]{:S(2)}, u32[]{:S(2)}) collective-permute-start(f16[336,128]{1,0:T(8,128)(2,1)S(1)} %convert_element_type.72), channel_id=1, source_target_pairs={{0,24},{8,16},{16,8},{24,0},{1,25},{9,17},{17,9},{25,1},{2,26},{10... | collective-permute-start | bytes 258056 | tf_op jit(solution)/shard_map/ppermute | solution.py:550
  47.2 2.0 %collective-permute-start.12 = (f16[336,128]{1,0:T(8,128)(2,1)S(1)}, f16[336,128]{1,0:T(8,128)(2,1)S(1)}, u32[]{:S(2)}, u32[]{:S(2)}) collective-permute-start(f16[336,128]{1,0:T(8,128)(2,1)S(1)} %convert_element_type.72), channel_id=1, source_target_pairs={{0,16},{8,24},{16,0},{24,8},{1,17},{9,25},{17,1},{25,9},{2,18},{10... | collective-permute-start | bytes 258056 | tf_op jit(solution)/shard_map/ppermute | solution.py:550
  49.2 0.3 collective-permute-start.11
  49.5 0.0 collective-permute-start.14
  49.5 2.6 %collective-permute-done.13 = f16[336,128]{1,0:T(8,128)(2,1)S(1)} collective-permute-done((f16[336,128]{1,0:T(8,128)(2,1)S(1)}, f16[336,128]{1,0:T(8,128)(2,1)S(1)}, u32[]{:S(2)}, u32[]{:S(2)}) %collective-permute-start.13) | collective-permute-done | bytes 86048 | tf_op jit(solution)/shard_map/ppermute | solution.py:550
  52.2 0.0 collective-permute-start.17
  52.2 0.2 collective-permute-done.12
  52.4 0.3 collective-permute-start.16
  52.7 1.0 %collective-permute-done.11 = f16[336,128]{1,0:T(8,128)(2,1)S(1)} collective-permute-done((f16[336,128]{1,0:T(8,128)(2,1)S(1)}, f16[336,128]{1,0:T(8,128)(2,1)S(1)}, u32[]{:S(2)}, u32[]{:S(2)}) %collective-permute-start.11) | collective-permute-done | bytes 86048 | tf_op jit(solution)/shard_map/ppermute | solution.py:550
  53.7 0.0 collective-permute-start.15
  53.7 0.8 %unpack_0.1.refs_7_ = f32[64,64,64]{2,1,0:T(8,128)} custom-call(f32[336,128]{1,0:T(8,128)S(1)} %get-tuple-element.48.refs_0_.refs_3_), custom_call_target="tpu_custom_call" | custom-call | flops 1000000 | bytes 4194304 | tf_op jit(solution)/shard_map/unpack_0/pallas_call | solution.py:528
  54.6 0.0 collective-permute-done.14
  54.6 1.7 %unpack_1.1 = (f32[64,64,64]{2,1,0:T(8,128)}, f32[64,128]{1,0:T(8,128)}) custom-call(f32[336,128]{1,0:T(8,128)S(1)} %convert_element_type.73.refs_0_.refs_4_, f32[336,128]{1,0:T(8,128)S(1)} %convert_element_type.74.refs_1_.refs_5_, f32[336,128]{1,0:T(8,128)S(1)} %convert_element_type.75.refs_2_.refs_6_, ...), custom_call_target="tpu_custom_call", output_to_operand_aliasing={{0}: (7, {})} | custom-call | flops 1000000 | bytes 4194304 | tf_op jit(solution)/shard_map/unpack_1/pallas_call | solution.py:528
  56.3 0.0 collective-permute-done.17
  56.3 0.0 collective-permute-done.16
  56.4 0.0 collective-permute-done.15
  56.4 1.1 %unpack_4.1 = f32[64,64,64]{2,1,0:T(8,128)} custom-call(f32[336,128]{1,0:T(8,128)S(1)} %convert_element_type.76.refs_0_, f32[336,128]{1,0:T(8,128)S(1)} %convert_element_type.77.refs_1_, f32[336,128]{1,0:T(8,128)S(1)} %convert_element_type.78.refs_2_, f32[336,128]{1,0:T(8,128)S(1)} %convert_element_type.79.refs_3_, ...), custom_call_target="tpu_custom_call", output_to_operand_aliasing={{}: (4, {})} | custom-call | flops 1000000 | bytes 4194304 | tf_op jit(solution)/shard_map/unpack_4/pallas_call | solution.py:528
  (20 shorter events, 0.3 us)
Async XLA Ops:
  0.6 1.6 %collective-permute-start = (bf16[64,128]{1,0:T(8,128)(2,1)}, bf16[64,128]{1,0:T(8,128)(2,1)S(1)}, u32[]{:S(2)}, u32[]{:S(2)}) collective-permute-start(bf16[64,128]{1,0:T(8,128)(2,1)} %param.12), channel_id=1, source_target_pairs={{0,4},{4,0},{1,5},{5,1},{2,6},{6,2},{3,7},{7,3},{8,12},{12,8},{9,1... | collective-permute-start | bytes 49160 | tf_op jit(solution)/shard_map/ppermute | solution.py:550
  2.9 9.7 %collective-permute-start.3 = (bf16[3,64,128]{2,1,0:T(8,128)(2,1)S(1)}, bf16[3,64,128]{2,1,0:T(8,128)(2,1)S(1)}, u32[]{:S(2)}, u32[]{:S(2)}) collective-permute-start(bf16[3,64,128]{2,1,0:T(8,128)(2,1)S(1)} %pad_maximum_fusion.after.refs_0_), channel_id=1, source_target_pairs={{0,3},{1,2},{2,1},{3,0},{4,7},{5,6},{6,5},{7,4},{8,11},{9,10},{10,... | collective-permute-start | bytes 147464 | tf_op jit(solution)/shard_map/ppermute | solution.py:550
  7.9 5.0 %collective-permute-start.2 = (bf16[3,64,128]{2,1,0:T(8,128)(2,1)S(1)}, bf16[3,64,128]{2,1,0:T(8,128)(2,1)S(1)}, u32[]{:S(2)}, u32[]{:S(2)}) collective-permute-start(bf16[3,64,128]{2,1,0:T(8,128)(2,1)S(1)} %pad_maximum_fusion.after.refs_0_), channel_id=1, source_target_pairs={{0,2},{1,3},{2,0},{3,1},{4,6},{5,7},{6,4},{7,5},{8,10},{9,11},{10,... | collective-permute-start | bytes 147464 | tf_op jit(solution)/shard_map/ppermute | solution.py:550
  7.9 5.0 %collective-permute-start.1 = (bf16[3,64,128]{2,1,0:T(8,128)(2,1)S(1)}, bf16[3,64,128]{2,1,0:T(8,128)(2,1)S(1)}, u32[]{:S(2)}, u32[]{:S(2)}) collective-permute-start(bf16[3,64,128]{2,1,0:T(8,128)(2,1)S(1)} %pad_maximum_fusion.after.refs_0_), channel_id=1, source_target_pairs={{0,1},{1,0},{2,3},{3,2},{4,5},{5,4},{6,7},{7,6},{8,9},{9,8},{10,11... | collective-permute-start | bytes 147464 | tf_op jit(solution)/shard_map/ppermute | solution.py:550
  18.2 2.2 %collective-permute-start.4 = (f32[21,64,128]{2,1,0:T(8,128)S(1)}, f32[21,64,128]{2,1,0:T(8,128)S(1)}, u32[]{:S(2)}, u32[]{:S(2)}) collective-permute-start(f32[21,64,128]{2,1,0:T(8,128)S(1)} %get-tuple-element.35), channel_id=1, source_target_pairs={{0,4},{4,0},{1,5},{5,1},{2,6},{6,2},{3,7},{7,3},{8,12},{12,8},{9,1... | collective-permute-start | bytes 2064392 | tf_op jit(solution)/shard_map/ppermute | solution.py:550
  20.7 10.3 %collective-permute-start.7 = (f16[336,128]{1,0:T(8,128)(2,1)S(1)}, f16[336,128]{1,0:T(8,128)(2,1)S(1)}, u32[]{:S(2)}, u32[]{:S(2)}) collective-permute-start(f16[336,128]{1,0:T(8,128)(2,1)S(1)} %convert_element_type.64), channel_id=1, source_target_pairs={{0,24},{8,16},{16,8},{24,0},{1,25},{9,17},{17,9},{25,1},{2,26},{10... | collective-permute-start | bytes 258056 | tf_op jit(solution)/shard_map/ppermute | solution.py:550
  28.1 4.7 %collective-permute-start.6 = (f16[336,128]{1,0:T(8,128)(2,1)S(1)}, f16[336,128]{1,0:T(8,128)(2,1)S(1)}, u32[]{:S(2)}, u32[]{:S(2)}) collective-permute-start(f16[336,128]{1,0:T(8,128)(2,1)S(1)} %convert_element_type.62), channel_id=1, source_target_pairs={{0,16},{8,24},{16,0},{24,8},{1,17},{9,25},{17,1},{25,9},{2,18},{10... | collective-permute-start | bytes 258056 | tf_op jit(solution)/shard_map/ppermute | solution.py:550
  28.1 4.7 %collective-permute-start.5 = (f16[336,128]{1,0:T(8,128)(2,1)S(1)}, f16[336,128]{1,0:T(8,128)(2,1)S(1)}, u32[]{:S(2)}, u32[]{:S(2)}) collective-permute-start(f16[336,128]{1,0:T(8,128)(2,1)S(1)} %convert_element_type.60), channel_id=1, source_target_pairs={{0,8},{8,0},{16,24},{24,16},{1,9},{9,1},{17,25},{25,17},{2,10},{10... | collective-permute-start | bytes 258056 | tf_op jit(solution)/shard_map/ppermute | solution.py:550
  33.8 7.7 %collective-permute-start.10 = (f16[400,128]{1,0:T(8,128)(2,1)S(1)}, f16[400,128]{1,0:T(8,128)(2,1)S(1)}, u32[]{:S(2)}, u32[]{:S(2)}) collective-permute-start(f16[400,128]{1,0:T(8,128)(2,1)S(1)} %convert_element_type.70), channel_id=1, source_target_pairs={{0,3},{1,2},{2,1},{3,0},{4,7},{5,6},{6,5},{7,4},{8,11},{9,10},{10,... | collective-permute-start | bytes 307208 | tf_op jit(solution)/shard_map/ppermute | solution.py:550
  33.8 11.3 %collective-permute-start.9 = (f16[400,128]{1,0:T(8,128)(2,1)S(1)}, f16[400,128]{1,0:T(8,128)(2,1)S(1)}, u32[]{:S(2)}, u32[]{:S(2)}) collective-permute-start(f16[400,128]{1,0:T(8,128)(2,1)S(1)} %convert_element_type.68), channel_id=1, source_target_pairs={{0,2},{1,3},{2,0},{3,1},{4,6},{5,7},{6,4},{7,5},{8,10},{9,11},{10,... | collective-permute-start | bytes 307208 | tf_op jit(solution)/shard_map/ppermute | solution.py:550
  36.4 8.7 %collective-permute-start.8 = (f16[400,128]{1,0:T(8,128)(2,1)S(1)}, f16[400,128]{1,0:T(8,128)(2,1)S(1)}, u32[]{:S(2)}, u32[]{:S(2)}) collective-permute-start(f16[400,128]{1,0:T(8,128)(2,1)S(1)} %convert_element_type.66), channel_id=1, source_target_pairs={{0,1},{1,0},{2,3},{3,2},{4,5},{5,4},{6,7},{7,6},{8,9},{9,8},{10,11... | collective-permute-start | bytes 307208 | tf_op jit(solution)/shard_map/ppermute | solution.py:550
  46.0 6.2 %collective-permute-start.13 = (f16[336,128]{1,0:T(8,128)(2,1)S(1)}, f16[336,128]{1,0:T(8,128)(2,1)S(1)}, u32[]{:S(2)}, u32[]{:S(2)}) collective-permute-start(f16[336,128]{1,0:T(8,128)(2,1)S(1)} %convert_element_type.72), channel_id=1, source_target_pairs={{0,24},{8,16},{16,8},{24,0},{1,25},{9,17},{17,9},{25,1},{2,26},{10... | collective-permute-start | bytes 258056 | tf_op jit(solution)/shard_map/ppermute | solution.py:550
  47.2 5.2 %collective-permute-start.12 = (f16[336,128]{1,0:T(8,128)(2,1)S(1)}, f16[336,128]{1,0:T(8,128)(2,1)S(1)}, u32[]{:S(2)}, u32[]{:S(2)}) collective-permute-start(f16[336,128]{1,0:T(8,128)(2,1)S(1)} %convert_element_type.72), channel_id=1, source_target_pairs={{0,16},{8,24},{16,0},{24,8},{1,17},{9,25},{17,1},{25,9},{2,18},{10... | collective-permute-start | bytes 258056 | tf_op jit(solution)/shard_map/ppermute | solution.py:550
  49.2 4.5 %collective-permute-start.11 = (f16[336,128]{1,0:T(8,128)(2,1)S(1)}, f16[336,128]{1,0:T(8,128)(2,1)S(1)}, u32[]{:S(2)}, u32[]{:S(2)}) collective-permute-start(f16[336,128]{1,0:T(8,128)(2,1)S(1)} %convert_element_type.72), channel_id=1, source_target_pairs={{0,8},{8,0},{16,24},{24,16},{1,9},{9,1},{17,25},{25,17},{2,10},{10... | collective-permute-start | bytes 258056 | tf_op jit(solution)/shard_map/ppermute | solution.py:550
  49.5 5.1 %collective-permute-start.14 = (f16[336,128]{1,0:T(8,128)(2,1)S(1)}, f16[336,128]{1,0:T(8,128)(2,1)S(1)}, u32[]{:S(2)}, u32[]{:S(2)}) collective-permute-start(f16[336,128]{1,0:T(8,128)(2,1)S(1)} %convert_element_type.72), channel_id=1, source_target_pairs={{0,4},{4,0},{1,5},{5,1},{2,6},{6,2},{3,7},{7,3},{8,12},{12,8},{9,1... | collective-permute-start | bytes 258056 | tf_op jit(solution)/shard_map/ppermute | solution.py:550
  52.2 4.1 %collective-permute-start.17 = (f16[336,128]{1,0:T(8,128)(2,1)S(1)}, f16[336,128]{1,0:T(8,128)(2,1)S(1)}, u32[]{:S(2)}, u32[]{:S(2)}) collective-permute-start(f16[336,128]{1,0:T(8,128)(2,1)S(1)} %collective-permute-done.13), channel_id=1, source_target_pairs={{0,4},{4,0},{1,5},{5,1},{2,6},{6,2},{3,7},{7,3},{8,12},{12,8},{9,1... | collective-permute-start | bytes 258056 | tf_op jit(solution)/shard_map/ppermute | solution.py:550
  52.4 4.0 %collective-permute-start.16 = (f16[336,128]{1,0:T(8,128)(2,1)S(1)}, f16[336,128]{1,0:T(8,128)(2,1)S(1)}, u32[]{:S(2)}, u32[]{:S(2)}) collective-permute-start(f16[336,128]{1,0:T(8,128)(2,1)S(1)} %collective-permute-done.12), channel_id=1, source_target_pairs={{0,4},{4,0},{1,5},{5,1},{2,6},{6,2},{3,7},{7,3},{8,12},{12,8},{9,1... | collective-permute-start | bytes 258056 | tf_op jit(solution)/shard_map/ppermute | solution.py:550
  53.7 2.7 %collective-permute-start.15 = (f16[336,128]{1,0:T(8,128)(2,1)S(1)}, f16[336,128]{1,0:T(8,128)(2,1)S(1)}, u32[]{:S(2)}, u32[]{:S(2)}) collective-permute-start(f16[336,128]{1,0:T(8,128)(2,1)S(1)} %collective-permute-done.11), channel_id=1, source_target_pairs={{0,4},{4,0},{1,5},{5,1},{2,6},{6,2},{3,7},{7,3},{8,12},{12,8},{9,1... | collective-permute-start | bytes 258056 | tf_op jit(solution)/shard_map/ppermute | solution.py:550

commit v10 on v8

--- a/solution.py
+++ b/solution.py
@@ -362,7 +362,7 @@
         kernel,
         out_shape=out_shape,
         in_specs=[pl.BlockSpec(memory_space=pltpu.VMEM)] * len(operands),
-        out_specs=jax.tree.map(lambda _: pl.BlockSpec(memory_space=pltpu.VMEM), out_shape),
+        out_specs=tuple(pl.BlockSpec(memory_space=pltpu.VMEM) for _ in out_shape),
         compiler_params=pltpu.CompilerParams(vmem_limit_bytes=24 * 2**20),
         name=name,
     )(*operands)
@@ -445,14 +445,14 @@
 
 
 def after_rows_kernel(n_ia, n_ka, own_core, own_depth, own_rows, cols_sum, *refs):
-    messages, depth_out, outs = refs[: n_ia - 1], refs[n_ia - 1], refs[n_ia:]
+    messages, refs = refs[: n_ia - 1], refs[n_ia - 1 :]
+    depth_out, *outs = refs
     count, rank, lanes = own_core.shape
+    depths = [own_depth[...]] + [message_part(message, count * rank, rank, 1) for message in messages]
+    depth_out[...] = tree_sum(depths)
     core = own_core[...].reshape(count * rank, lanes)
-    depths = [own_depth[...]]
     for message in messages:
         core = core + message_part(message, 0, count * rank, 0)
-        depths.append(message_part(message, count * rank, rank, 1))
-    depth_out[...] = tree_sum(depths)
     flat, exponent = scaled(core)
     for mask in range(n_ka):
         fill_message(outs[mask], (flat, exponent), scaled(own_rows[mask]), scaled(cols_sum[mask]))
@@ -475,12 +475,12 @@
 
 
 def after_depths_kernel(n_ka, rank, *refs):
-    messages, out, rows_out = refs[:n_ka], refs[-2], refs[-1]
+    messages, (out, rows_out) = refs[:n_ka], refs[n_ka:]
+    rows_out[...] = tree_sum(message_part(message, n_ka * rank, rank, 1) for message in messages)
     cores = []
     for mask, message in enumerate(messages):
         part = message_part(message, 0, n_ka * rank, 0)
         cores.append(jnp.concatenate([part[(at ^ mask) * rank : ((at ^ mask) + 1) * rank] for at in range(n_ka)]))
-    rows_out[...] = tree_sum(message_part(message, n_ka * rank, rank, 1) for message in messages)
     cols = tree_sum(message_part(message, (n_ka + 1) * rank, rank, 2) for message in messages)
     fill_message(out, scaled(tree_sum(cores)), scaled(cols))
 
@@ -494,50 +494,57 @@
 def unpack_kernel(sizes, rank, first_message, *refs):
     n_ia, n_ka = sizes["ia"], sizes["ka"]
     messages = refs[:n_ia]
-    core_out, *cols_out, whole, sems = refs[n_ia if first_message == 0 else n_ia + 1 :]
+    near = first_message == 0
     pairs = rank // 2
-    own = masks_of(True, sizes)[2]
+    ia, ja, ka = lax.axis_index("ia"), lax.axis_index("ja"), lax.axis_index("ka")
     copies = []
+    if near:
+        rows_total, depth_total, core_out, rows_out, depth_out, cols_out, cols_here, whole, sems = refs[n_ia:]
+        cols_here[...] = tree_sum(message_part(message, n_ka * rank, rank, 1) for message in messages)
+        for source, out in ((rows_total, rows_out), (depth_total, depth_out), (cols_here, cols_out)):
+            copies.append(pltpu.make_async_copy(source, out, sems.at[2 * n_ia + len(copies)]))
+            copies[-1].start()
+    else:
+        core_out, whole, sems = refs[n_ia + 1 :]
     for at in range(n_ia):
-        first = pl.multiple_of(((own // n_ka) ^ (first_message + at)) * n_ka, n_ka)
+        first = pl.multiple_of(((ja * n_ia + ia) ^ (first_message + at)) * n_ka, n_ka)
         for mask in range(n_ka):
             piece = message_part(messages[at], mask * rank, rank, 0)
-            line = lax.rem(own, n_ka) ^ mask
-            whole[at, 0, line] = piece[:, :rank]
-            whole[at, 1, line] = piece[:, rank:]
+            whole[at, 0, ka ^ mask] = piece[:, :rank]
+            whole[at, 1, ka ^ mask] = piece[:, rank:]
         for h in range(2):
             lines = pl.ds(h * pairs + first, n_ka)
             copies.append(pltpu.make_async_copy(whole.at[at, h], core_out.at[lines], sems.at[2 * at + h]))
             copies[-1].start()
-    for out in cols_out:
-        out[...] = tree_sum(message_part(message, n_ka * rank, rank, 1) for message in messages)
     for copy in copies:
         copy.wait()
 
 
-def unpack(sizes, rank, messages, core=None):
+def unpack(sizes, rank, messages, core=None, *totals):
     lanes = messages[0].shape[1]
     near = core is None
+    given = list(totals) if near else [core]
+    scratch = [pltpu.VMEM((rank, lanes), f32)] if near else []
     out_shape = [jax.ShapeDtypeStruct((rank, rank, rank), f32)]
-    out_specs = [pl.BlockSpec(memory_space=pltpu.HBM)]
     if near:
-        out_shape.append(jax.ShapeDtypeStruct((rank, lanes), f32))
-        out_specs.append(pl.BlockSpec(memory_space=pltpu.VMEM))
+        out_shape += [jax.ShapeDtypeStruct(total.shape, f32) for total in totals]
+        out_shape += [jax.ShapeDtypeStruct((rank, lanes), f32)]
     return pl.pallas_call(
         functools.partial(unpack_kernel, sizes, rank, 0 if near else sizes["ia"]),
         out_shape=tuple(out_shape),
         in_specs=[pl.BlockSpec(memory_space=pltpu.VMEM)] * len(messages)
-        + ([] if near else [pl.BlockSpec(memory_space=pltpu.HBM)]),
-        out_specs=tuple(out_specs),
+        + [pl.BlockSpec(memory_space=pltpu.VMEM if near else pltpu.HBM)] * len(given),
+        out_specs=tuple(pl.BlockSpec(memory_space=pltpu.HBM) for _ in out_shape),
         scratch_shapes=[
+            *scratch,
             pltpu.VMEM((len(messages), 2, sizes["ka"], rank, rank), f32),
-            pltpu.SemaphoreType.DMA((2 * len(messages),)),
+            pltpu.SemaphoreType.DMA((2 * len(messages) + 3,)),
         ],
         input_output_aliases={} if near else {len(messages): 0},
         compiler_params=pltpu.CompilerParams(vmem_limit_bytes=24 * 2**20),
         cost_estimate=pl.CostEstimate(flops=10**6, bytes_accessed=4 * 2**20, transcendentals=0),
         name="unpack_near" if near else "unpack_far",
-    )(*messages, *([] if near else [core]))
+    )(*messages, *given)
 
 
 def power_of_two(n):
@@ -636,7 +643,9 @@
     sent = message.astype(wire)
     sent = [sent] + [swap(sent, "ia", n_ia, mask) for mask in range(1, n_ia)]
     other = [swap(each, "ja", n_ja, 1) for each in sent]
-    core_near, cols_total = unpack(sizes, rank, [each.astype(f32) for each in sent])
+    core_near, rows_total, depth_total, cols_total = unpack(
+        sizes, rank, [each.astype(f32) for each in sent], None, rows_total, depth_total
+    )
     (core_total,) = unpack(sizes, rank, [each.astype(f32) for each in other], core_near)
     return (rows_total, cols_total, depth_total, core_total)
 

time: 56.4 us -> 55.2 us (0.979)
  Pallas kernels: 14.1 us -> 12.4 us
  starting transfers between devices: 21.3 us -> 22.6 us
    ppermute x18, starting transfers between devices: 21.3 us -> 22.6 us  [swap(): return lax.ppermute(value, axis, [(at, at ^ mask) for at in range(size)])]
    pallas_call x3, Pallas kernels: 1.96 us -> 0.79 us  [vmem_call(): pl.pallas_call(kernel, out_shape=out_shape, in_specs=[pl.BlockSpec(memory...]
    pallas_call x2, Pallas kernels: 2.92 us -> 2.34 us  [unpack(): pl.pallas_call(functools.partial(unpack_kernel, sizes, rank, 0 if near el...]
  transfers between devices with their start and end apart: 18 -> 18, of which waited for: 10 -> 10; matrix products, arithmetic and copies ran while one was open for 0% -> 0% of each run, Pallas kernels for 10% -> 9%
where the time goes in v10:
time: 55.2 us; the launch traced here: 54.8 us
  starting transfers between devices  22.6 us (41%)
  waiting for transfers between devices  17.2 us (31%)
  Pallas kernels  12.4 us (22%)
  between operations  1.54 us (3%)
  other arithmetic  1.05 us (2%)
    ppermute x18, starting transfers between devices, swap(): return lax.ppermute(value, axis, [(at, at ^ mask) for at in range(size)])  22.6 us
    ppermute x18, waiting for transfers between devices, swap(): return lax.ppermute(value, axis, [(at, at ^ mask) for at in range(size)])  17.2 us
    pallas_call x1, Pallas kernels, terms(): pl.pallas_call(functools.partial(terms_kernel, relative, sizes, row_spots...  5.24 us
    pallas_call x1, Pallas kernels, first_cubes(): pl.pallas_call(functools.partial(cube_kernel, slab), out_shape=(jax.Shape...  4.01 us
    pallas_call x2, Pallas kernels, unpack(): pl.pallas_call(functools.partial(unpack_kernel, sizes, rank, 0 if near el...  2.34 us
  transfers between devices with their start and end apart: 18, of which 10 were waited for; matrix products, arithmetic and copies ran while one was open for 0% of the time, Pallas kernels for 9%

profile of v10, /device:TPU:0, one launch (start us, length us, event | category | flops | bytes accessed | tf_op | source)
XLA Modules:
  0.0 54.8 jit_solution(10358848113173028205)
XLA Ops:
  0.6 0.5 collective-permute-start
  1.8 0.4 collective-permute-done
  2.2 0.7 %pad_maximum_fusion.after.refs_0_ = bf16[3,64,128]{2,1,0:T(8,128)(2,1)S(1)} fusion(bf16[1,64,128]{2,1,0:T(8,128)(2,1)} %bitcast.10, bf16[1,64,128]{2,1,0:T(8,128)(2,1)S(1)} %bitcast.12, bf16[1,64,128]{2,1,0:T(8,128)(2,1)} %bitcast.11), kind=kLoop, calls=%fused_computation | loop fusion | flops 49152 | bytes 98304 | tf_op jit(solution)/shard_map/stack | solution.py:582
  2.9 5.0 %collective-permute-start.3 = (bf16[3,64,128]{2,1,0:T(8,128)(2,1)S(1)}, bf16[3,64,128]{2,1,0:T(8,128)(2,1)S(1)}, u32[]{:S(2)}, u32[]{:S(2)}) collective-permute-start(bf16[3,64,128]{2,1,0:T(8,128)(2,1)S(1)} %pad_maximum_fusion.after.refs_0_), channel_id=1, source_target_pairs={{0,3},{1,2},{2,1},{3,0},{4,7},{5,6},{6,5},{7,4},{8,11},{9,10},{10,... | collective-permute-start | bytes 147464 | tf_op jit(solution)/shard_map/ppermute | solution.py:555
  7.9 0.0 collective-permute-start.2
  7.9 0.6 %collective-permute-start.1 = (bf16[3,64,128]{2,1,0:T(8,128)(2,1)S(1)}, bf16[3,64,128]{2,1,0:T(8,128)(2,1)S(1)}, u32[]{:S(2)}, u32[]{:S(2)}) collective-permute-start(bf16[3,64,128]{2,1,0:T(8,128)(2,1)S(1)} %pad_maximum_fusion.after.refs_0_), channel_id=1, source_target_pairs={{0,1},{1,0},{2,3},{3,2},{4,5},{5,4},{6,7},{7,6},{8,9},{9,8},{10,11... | collective-permute-start | bytes 147464 | tf_op jit(solution)/shard_map/ppermute | solution.py:555
  8.6 4.0 %first_cubes.1 = (bf16[4,1024,128]{2,1,0:T(8,128)(2,1)S(1)}, bf16[4,128,1024]{2,1,0:T(8,128)(2,1)S(1)}, bf16[32,128,64]{2,1,0:T(8,128)(2,1)S(1)}, bf16[128,64]{1...) custom-call(bf16[3,64,128]{2,1,0:T(8,128)(2,1)S(1)} %pad_maximum_fusion.after.refs_0_, ...), custom_call_target="tpu_custom_call" | custom-call | flops 1000000000 | bytes 4194304 | tf_op jit(solution)/shard_map/first_cubes/pallas_call | solution.py:96
  12.6 0.0 collective-permute-done.3.refs_3_
  12.6 0.3 collective-permute-done.2.refs_2_
  12.9 0.0 collective-permute-done.1.refs_1_
  12.9 5.2 %terms.1 = (f32[21,64,128]{2,1,0:T(8,128)S(1)}, f32[21,64,128]{2,1,0:T(8,128)S(1)}, f32[4,64,128]{2,1,0:T(8,128)S(1)}, f32[2,4224,128]{2,1,0:T(8,128)S(1)}) custom-call(s32[1,1,1]{2,1,0:T(1,128)S(6)} %copy.16.counts, s32[1,3,1,5]{3,2,1,0:T(1,128)S(1)} %get-tuple-element.30.coords, ...), custom_call_target="tpu_custom_call", output_to_operand_aliasing={{3}: (12, {})} | custom-call | flops 1000000000 | bytes 16777216 | tf_op jit(solution)/shard_map/terms/pallas_call | solution.py:325
  18.2 0.1 collective-permute-start.4
  18.3 2.1 %collective-permute-done.4.got = f32[21,64,128]{2,1,0:T(8,128)S(1)} collective-permute-done((f32[21,64,128]{2,1,0:T(8,128)S(1)}, f32[21,64,128]{2,1,0:T(8,128)S(1)}, u32[]{:S(2)}, u32[]{:S(2)}) %collective-permute-start.4) | collective-permute-done | bytes 688160 | tf_op jit(solution)/shard_map/ppermute | solution.py:555
  20.4 0.3 after_cores.1
  20.7 0.1 collective-permute-start.7
  20.8 6.4 %collective-permute-start.6 = (f16[336,128]{1,0:T(8,128)(2,1)S(1)}, f16[336,128]{1,0:T(8,128)(2,1)S(1)}, u32[]{:S(2)}, u32[]{:S(2)}) collective-permute-start(f16[336,128]{1,0:T(8,128)(2,1)S(1)} %convert_element_type.65), channel_id=1, source_target_pairs={{0,16},{8,24},{16,0},{24,8},{1,17},{9,25},{17,1},{25,9},{2,18},{10... | collective-permute-start | bytes 258056 | tf_op jit(solution)/shard_map/ppermute | solution.py:555
  27.2 1.5 %collective-permute-start.5 = (f16[336,128]{1,0:T(8,128)(2,1)S(1)}, f16[336,128]{1,0:T(8,128)(2,1)S(1)}, u32[]{:S(2)}, u32[]{:S(2)}) collective-permute-start(f16[336,128]{1,0:T(8,128)(2,1)S(1)} %convert_element_type.63), channel_id=1, source_target_pairs={{0,8},{8,0},{16,24},{24,16},{1,9},{9,1},{17,25},{25,17},{2,10},{10... | collective-permute-start | bytes 258056 | tf_op jit(solution)/shard_map/ppermute | solution.py:555
  28.7 0.0 collective-permute-done.7
  28.7 2.5 %collective-permute-done.6 = f16[336,128]{1,0:T(8,128)(2,1)S(1)} collective-permute-done((f16[336,128]{1,0:T(8,128)(2,1)S(1)}, f16[336,128]{1,0:T(8,128)(2,1)S(1)}, u32[]{:S(2)}, u32[]{:S(2)}) %collective-permute-start.6) | collective-permute-done | bytes 86048 | tf_op jit(solution)/shard_map/ppermute | solution.py:555
  31.2 1.8 %collective-permute-done.5 = f16[336,128]{1,0:T(8,128)(2,1)S(1)} collective-permute-done((f16[336,128]{1,0:T(8,128)(2,1)S(1)}, f16[336,128]{1,0:T(8,128)(2,1)S(1)}, u32[]{:S(2)}, u32[]{:S(2)}) %collective-permute-start.5) | collective-permute-done | bytes 86048 | tf_op jit(solution)/shard_map/ppermute | solution.py:555
  33.0 0.3 after_rows.1
  33.4 0.1 collective-permute-start.10
  33.4 1.8 %collective-permute-start.9 = (f16[400,128]{1,0:T(8,128)(2,1)S(1)}, f16[400,128]{1,0:T(8,128)(2,1)S(1)}, u32[]{:S(2)}, u32[]{:S(2)}) collective-permute-start(f16[400,128]{1,0:T(8,128)(2,1)S(1)} %convert_element_type.71), channel_id=1, source_target_pairs={{0,2},{1,3},{2,0},{3,1},{4,6},{5,7},{6,4},{7,5},{8,10},{9,11},{10,... | collective-permute-start | bytes 307208 | tf_op jit(solution)/shard_map/ppermute | solution.py:555
  35.3 2.6 %collective-permute-start.8 = (f16[400,128]{1,0:T(8,128)(2,1)S(1)}, f16[400,128]{1,0:T(8,128)(2,1)S(1)}, u32[]{:S(2)}, u32[]{:S(2)}) collective-permute-start(f16[400,128]{1,0:T(8,128)(2,1)S(1)} %convert_element_type.69), channel_id=1, source_target_pairs={{0,1},{1,0},{2,3},{3,2},{4,5},{5,4},{6,7},{7,6},{8,9},{9,8},{10,11... | collective-permute-start | bytes 307208 | tf_op jit(solution)/shard_map/ppermute | solution.py:555
  37.9 3.1 %collective-permute-done.10 = f16[400,128]{1,0:T(8,128)(2,1)S(1)} collective-permute-done((f16[400,128]{1,0:T(8,128)(2,1)S(1)}, f16[400,128]{1,0:T(8,128)(2,1)S(1)}, u32[]{:S(2)}, u32[]{:S(2)}) %collective-permute-start.10) | collective-permute-done | bytes 102432 | tf_op jit(solution)/shard_map/ppermute | solution.py:555
  41.1 3.1 %collective-permute-done.9 = f16[400,128]{1,0:T(8,128)(2,1)S(1)} collective-permute-done((f16[400,128]{1,0:T(8,128)(2,1)S(1)}, f16[400,128]{1,0:T(8,128)(2,1)S(1)}, u32[]{:S(2)}, u32[]{:S(2)}) %collective-permute-start.9) | collective-permute-done | bytes 102432 | tf_op jit(solution)/shard_map/ppermute | solution.py:555
  44.2 0.0 collective-permute-done.8
  44.2 0.3 after_depths.1
  44.5 1.2 %collective-permute-start.13 = (f16[336,128]{1,0:T(8,128)(2,1)S(1)}, f16[336,128]{1,0:T(8,128)(2,1)S(1)}, u32[]{:S(2)}, u32[]{:S(2)}) collective-permute-start(f16[336,128]{1,0:T(8,128)(2,1)S(1)} %get-tuple-element.57), channel_id=1, source_target_pairs={{0,24},{8,16},{16,8},{24,0},{1,25},{9,17},{17,9},{25,1},{2,26},{10... | collective-permute-start | bytes 258056 | tf_op jit(solution)/shard_map/ppermute | solution.py:555
  45.8 2.0 %collective-permute-start.12 = (f16[336,128]{1,0:T(8,128)(2,1)S(1)}, f16[336,128]{1,0:T(8,128)(2,1)S(1)}, u32[]{:S(2)}, u32[]{:S(2)}) collective-permute-start(f16[336,128]{1,0:T(8,128)(2,1)S(1)} %get-tuple-element.57), channel_id=1, source_target_pairs={{0,16},{8,24},{16,0},{24,8},{1,17},{9,25},{17,1},{25,9},{2,18},{10... | collective-permute-start | bytes 258056 | tf_op jit(solution)/shard_map/ppermute | solution.py:555
  47.8 0.3 collective-permute-start.11
  48.1 0.0 collective-permute-start.14
  48.1 2.8 %collective-permute-done.13 = f16[336,128]{1,0:T(8,128)(2,1)S(1)} collective-permute-done((f16[336,128]{1,0:T(8,128)(2,1)S(1)}, f16[336,128]{1,0:T(8,128)(2,1)S(1)}, u32[]{:S(2)}, u32[]{:S(2)}) %collective-permute-start.13) | collective-permute-done | bytes 86048 | tf_op jit(solution)/shard_map/ppermute | solution.py:555
  50.9 0.0 collective-permute-start.17
  50.9 0.1 collective-permute-done.12
  51.0 0.4 collective-permute-start.16
  51.4 0.9 %collective-permute-done.11 = f16[336,128]{1,0:T(8,128)(2,1)S(1)} collective-permute-done((f16[336,128]{1,0:T(8,128)(2,1)S(1)}, f16[336,128]{1,0:T(8,128)(2,1)S(1)}, u32[]{:S(2)}, u32[]{:S(2)}) %collective-permute-start.11) | collective-permute-done | bytes 86048 | tf_op jit(solution)/shard_map/ppermute | solution.py:555
  52.3 0.0 collective-permute-start.15
  52.3 0.0 collective-permute-done.14
  52.4 1.2 %unpack_near.1 = (f32[64,64,64]{2,1,0:T(8,128)}, f32[64,128]{1,0:T(8,128)}, f32[64,128]{1,0:T(8,128)}, f32[64,128]{1,0:T(8,128)}) custom-call(f32[336,128]{1,0:T(8,128)S(1)} %get-tuple-element.56.refs_0_, f32[336,128]{1,0:T(8,128)S(1)} %convert_element_type.77.refs_1_, f32[336,128]{1,0:T(8,128)S(1)} %convert_element_type.78.refs_2_, ...), custom_call_target="tpu_custom_call" | custom-call | flops 1000000 | bytes 4194304 | tf_op jit(solution)/shard_map/unpack_near/pallas_call | solution.py:532
  53.5 0.0 collective-permute-done.17
  53.6 0.0 collective-permute-done.16
  53.6 0.0 collective-permute-done.15
  53.6 1.2 %unpack_far.1 = f32[64,64,64]{2,1,0:T(8,128)} custom-call(f32[336,128]{1,0:T(8,128)S(1)} %convert_element_type.80.refs_0_, f32[336,128]{1,0:T(8,128)S(1)} %convert_element_type.81.refs_1_, f32[336,128]{1,0:T(8,128)S(1)} %convert_element_type.82.refs_2_, f32[336,128]{1,0:T(8,128)S(1)} %convert_element_type.83.refs_3_, ...), custom_call_target="tpu_custom_call", output_to_operand_aliasing={{}: (4, {})} | custom-call | flops 1000000 | bytes 4194304 | tf_op jit(solution)/shard_map/unpack_far/pallas_call | solution.py:532
  (20 shorter events, 0.3 us)
Async XLA Ops:
  0.6 1.6 %collective-permute-start = (bf16[64,128]{1,0:T(8,128)(2,1)}, bf16[64,128]{1,0:T(8,128)(2,1)S(1)}, u32[]{:S(2)}, u32[]{:S(2)}) collective-permute-start(bf16[64,128]{1,0:T(8,128)(2,1)} %param.12), channel_id=1, source_target_pairs={{0,4},{4,0},{1,5},{5,1},{2,6},{6,2},{3,7},{7,3},{8,12},{12,8},{9,1... | collective-permute-start | bytes 49160 | tf_op jit(solution)/shard_map/ppermute | solution.py:555
  2.9 9.7 %collective-permute-start.3 = (bf16[3,64,128]{2,1,0:T(8,128)(2,1)S(1)}, bf16[3,64,128]{2,1,0:T(8,128)(2,1)S(1)}, u32[]{:S(2)}, u32[]{:S(2)}) collective-permute-start(bf16[3,64,128]{2,1,0:T(8,128)(2,1)S(1)} %pad_maximum_fusion.after.refs_0_), channel_id=1, source_target_pairs={{0,3},{1,2},{2,1},{3,0},{4,7},{5,6},{6,5},{7,4},{8,11},{9,10},{10,... | collective-permute-start | bytes 147464 | tf_op jit(solution)/shard_map/ppermute | solution.py:555
  7.9 5.0 %collective-permute-start.2 = (bf16[3,64,128]{2,1,0:T(8,128)(2,1)S(1)}, bf16[3,64,128]{2,1,0:T(8,128)(2,1)S(1)}, u32[]{:S(2)}, u32[]{:S(2)}) collective-permute-start(bf16[3,64,128]{2,1,0:T(8,128)(2,1)S(1)} %pad_maximum_fusion.after.refs_0_), channel_id=1, source_target_pairs={{0,2},{1,3},{2,0},{3,1},{4,6},{5,7},{6,4},{7,5},{8,10},{9,11},{10,... | collective-permute-start | bytes 147464 | tf_op jit(solution)/shard_map/ppermute | solution.py:555
  7.9 5.0 %collective-permute-start.1 = (bf16[3,64,128]{2,1,0:T(8,128)(2,1)S(1)}, bf16[3,64,128]{2,1,0:T(8,128)(2,1)S(1)}, u32[]{:S(2)}, u32[]{:S(2)}) collective-permute-start(bf16[3,64,128]{2,1,0:T(8,128)(2,1)S(1)} %pad_maximum_fusion.after.refs_0_), channel_id=1, source_target_pairs={{0,1},{1,0},{2,3},{3,2},{4,5},{5,4},{6,7},{7,6},{8,9},{9,8},{10,11... | collective-permute-start | bytes 147464 | tf_op jit(solution)/shard_map/ppermute | solution.py:555
  18.2 2.2 %collective-permute-start.4 = (f32[21,64,128]{2,1,0:T(8,128)S(1)}, f32[21,64,128]{2,1,0:T(8,128)S(1)}, u32[]{:S(2)}, u32[]{:S(2)}) collective-permute-start(f32[21,64,128]{2,1,0:T(8,128)S(1)} %get-tuple-element.37), channel_id=1, source_target_pairs={{0,4},{4,0},{1,5},{5,1},{2,6},{6,2},{3,7},{7,3},{8,12},{12,8},{9,1... | collective-permute-start | bytes 2064392 | tf_op jit(solution)/shard_map/ppermute | solution.py:555
  20.7 8.0 %collective-permute-start.7 = (f16[336,128]{1,0:T(8,128)(2,1)S(1)}, f16[336,128]{1,0:T(8,128)(2,1)S(1)}, u32[]{:S(2)}, u32[]{:S(2)}) collective-permute-start(f16[336,128]{1,0:T(8,128)(2,1)S(1)} %convert_element_type.67), channel_id=1, source_target_pairs={{0,24},{8,16},{16,8},{24,0},{1,25},{9,17},{17,9},{25,1},{2,26},{10... | collective-permute-start | bytes 258056 | tf_op jit(solution)/shard_map/ppermute | solution.py:555
  20.8 10.4 %collective-permute-start.6 = (f16[336,128]{1,0:T(8,128)(2,1)S(1)}, f16[336,128]{1,0:T(8,128)(2,1)S(1)}, u32[]{:S(2)}, u32[]{:S(2)}) collective-permute-start(f16[336,128]{1,0:T(8,128)(2,1)S(1)} %convert_element_type.65), channel_id=1, source_target_pairs={{0,16},{8,24},{16,0},{24,8},{1,17},{9,25},{17,1},{25,9},{2,18},{10... | collective-permute-start | bytes 258056 | tf_op jit(solution)/shard_map/ppermute | solution.py:555
  27.2 5.8 %collective-permute-start.5 = (f16[336,128]{1,0:T(8,128)(2,1)S(1)}, f16[336,128]{1,0:T(8,128)(2,1)S(1)}, u32[]{:S(2)}, u32[]{:S(2)}) collective-permute-start(f16[336,128]{1,0:T(8,128)(2,1)S(1)} %convert_element_type.63), channel_id=1, source_target_pairs={{0,8},{8,0},{16,24},{24,16},{1,9},{9,1},{17,25},{25,17},{2,10},{10... | collective-permute-start | bytes 258056 | tf_op jit(solution)/shard_map/ppermute | solution.py:555
  33.4 7.7 %collective-permute-start.10 = (f16[400,128]{1,0:T(8,128)(2,1)S(1)}, f16[400,128]{1,0:T(8,128)(2,1)S(1)}, u32[]{:S(2)}, u32[]{:S(2)}) collective-permute-start(f16[400,128]{1,0:T(8,128)(2,1)S(1)} %convert_element_type.73), channel_id=1, source_target_pairs={{0,3},{1,2},{2,1},{3,0},{4,7},{5,6},{6,5},{7,4},{8,11},{9,10},{10,... | collective-permute-start | bytes 307208 | tf_op jit(solution)/shard_map/ppermute | solution.py:555
  33.4 10.7 %collective-permute-start.9 = (f16[400,128]{1,0:T(8,128)(2,1)S(1)}, f16[400,128]{1,0:T(8,128)(2,1)S(1)}, u32[]{:S(2)}, u32[]{:S(2)}) collective-permute-start(f16[400,128]{1,0:T(8,128)(2,1)S(1)} %convert_element_type.71), channel_id=1, source_target_pairs={{0,2},{1,3},{2,0},{3,1},{4,6},{5,7},{6,4},{7,5},{8,10},{9,11},{10,... | collective-permute-start | bytes 307208 | tf_op jit(solution)/shard_map/ppermute | solution.py:555
  35.3 8.9 %collective-permute-start.8 = (f16[400,128]{1,0:T(8,128)(2,1)S(1)}, f16[400,128]{1,0:T(8,128)(2,1)S(1)}, u32[]{:S(2)}, u32[]{:S(2)}) collective-permute-start(f16[400,128]{1,0:T(8,128)(2,1)S(1)} %convert_element_type.69), channel_id=1, source_target_pairs={{0,1},{1,0},{2,3},{3,2},{4,5},{5,4},{6,7},{7,6},{8,9},{9,8},{10,11... | collective-permute-start | bytes 307208 | tf_op jit(solution)/shard_map/ppermute | solution.py:555
  44.5 6.3 %collective-permute-start.13 = (f16[336,128]{1,0:T(8,128)(2,1)S(1)}, f16[336,128]{1,0:T(8,128)(2,1)S(1)}, u32[]{:S(2)}, u32[]{:S(2)}) collective-permute-start(f16[336,128]{1,0:T(8,128)(2,1)S(1)} %get-tuple-element.57), channel_id=1, source_target_pairs={{0,24},{8,16},{16,8},{24,0},{1,25},{9,17},{17,9},{25,1},{2,26},{10... | collective-permute-start | bytes 258056 | tf_op jit(solution)/shard_map/ppermute | solution.py:555
  45.8 5.3 %collective-permute-start.12 = (f16[336,128]{1,0:T(8,128)(2,1)S(1)}, f16[336,128]{1,0:T(8,128)(2,1)S(1)}, u32[]{:S(2)}, u32[]{:S(2)}) collective-permute-start(f16[336,128]{1,0:T(8,128)(2,1)S(1)} %get-tuple-element.57), channel_id=1, source_target_pairs={{0,16},{8,24},{16,0},{24,8},{1,17},{9,25},{17,1},{25,9},{2,18},{10... | collective-permute-start | bytes 258056 | tf_op jit(solution)/shard_map/ppermute | solution.py:555
  47.8 4.5 %collective-permute-start.11 = (f16[336,128]{1,0:T(8,128)(2,1)S(1)}, f16[336,128]{1,0:T(8,128)(2,1)S(1)}, u32[]{:S(2)}, u32[]{:S(2)}) collective-permute-start(f16[336,128]{1,0:T(8,128)(2,1)S(1)} %get-tuple-element.57), channel_id=1, source_target_pairs={{0,8},{8,0},{16,24},{24,16},{1,9},{9,1},{17,25},{25,17},{2,10},{10... | collective-permute-start | bytes 258056 | tf_op jit(solution)/shard_map/ppermute | solution.py:555
  48.1 4.2 %collective-permute-start.14 = (f16[336,128]{1,0:T(8,128)(2,1)S(1)}, f16[336,128]{1,0:T(8,128)(2,1)S(1)}, u32[]{:S(2)}, u32[]{:S(2)}) collective-permute-start(f16[336,128]{1,0:T(8,128)(2,1)S(1)} %get-tuple-element.57), channel_id=1, source_target_pairs={{0,4},{4,0},{1,5},{5,1},{2,6},{6,2},{3,7},{7,3},{8,12},{12,8},{9,1... | collective-permute-start | bytes 258056 | tf_op jit(solution)/shard_map/ppermute | solution.py:555
  50.9 2.7 %collective-permute-start.17 = (f16[336,128]{1,0:T(8,128)(2,1)S(1)}, f16[336,128]{1,0:T(8,128)(2,1)S(1)}, u32[]{:S(2)}, u32[]{:S(2)}) collective-permute-start(f16[336,128]{1,0:T(8,128)(2,1)S(1)} %collective-permute-done.13), channel_id=1, source_target_pairs={{0,4},{4,0},{1,5},{5,1},{2,6},{6,2},{3,7},{7,3},{8,12},{12,8},{9,1... | collective-permute-start | bytes 258056 | tf_op jit(solution)/shard_map/ppermute | solution.py:555
  51.0 2.5 %collective-permute-start.16 = (f16[336,128]{1,0:T(8,128)(2,1)S(1)}, f16[336,128]{1,0:T(8,128)(2,1)S(1)}, u32[]{:S(2)}, u32[]{:S(2)}) collective-permute-start(f16[336,128]{1,0:T(8,128)(2,1)S(1)} %collective-permute-done.12), channel_id=1, source_target_pairs={{0,4},{4,0},{1,5},{5,1},{2,6},{6,2},{3,7},{7,3},{8,12},{12,8},{9,1... | collective-permute-start | bytes 258056 | tf_op jit(solution)/shard_map/ppermute | solution.py:555
  52.3 1.3 %collective-permute-start.15 = (f16[336,128]{1,0:T(8,128)(2,1)S(1)}, f16[336,128]{1,0:T(8,128)(2,1)S(1)}, u32[]{:S(2)}, u32[]{:S(2)}) collective-permute-start(f16[336,128]{1,0:T(8,128)(2,1)S(1)} %collective-permute-done.11), channel_id=1, source_target_pairs={{0,4},{4,0},{1,5},{5,1},{2,6},{6,2},{3,7},{7,3},{8,12},{12,8},{9,1... | collective-permute-start | bytes 258056 | tf_op jit(solution)/shard_map/ppermute | solution.py:555

commit v11 on v10

--- a/solution.py
+++ b/solution.py
@@ -126,6 +126,31 @@
     return ja * sizes["ka"] + ka, ka, (ja * sizes["ia"] + ia) * sizes["ka"] + ka
 
 
+def core_chunk(second, depth):
+    rank = depth.shape[1]
+    piece = dot(second, depth, ((0,), (0,)))
+    return jnp.concatenate([piece[:rank], piece[rank:]], axis=1)
+
+
+def keep_kernel(sizes, second_all, depth_all, out):
+    core_mask = masks_of(True, sizes)[2]
+    for at in range(out.shape[0]):
+        out[at] = core_chunk(second_all[at ^ core_mask], depth_all[...])
+
+
+def keep_terms(sizes, second_all, depth_all):
+    pairs, _, lanes = second_all.shape
+    return pl.pallas_call(
+        functools.partial(keep_kernel, sizes),
+        out_shape=jax.ShapeDtypeStruct((pairs // 2, depth_all.shape[1], lanes), f32),
+        in_specs=[pl.BlockSpec(memory_space=pltpu.VMEM)] * 2,
+        out_specs=pl.BlockSpec(memory_space=pltpu.VMEM),
+        compiler_params=pltpu.CompilerParams(vmem_limit_bytes=24 * 2**20),
+        cost_estimate=pl.CostEstimate(flops=10**9, bytes_accessed=4 * 2**20, transcendentals=0),
+        name="keep_terms",
+    )(second_all, depth_all)
+
+
 def terms_kernel(relative, sizes, row_spots, col_spots, counts, coords, data, weight, cube, cube_turned, *refs):
     pieces = refs[: 1 + max(at for at, _ in row_spots + col_spots)]
     (
@@ -134,6 +159,8 @@
         _,
         *outs,
         cols_out,
+        second_all,
+        depth_all,
         spread,
         rows_out,
         row_table,
@@ -141,8 +168,6 @@
         wide_col,
         backward,
         by_rank,
-        second_all,
-        depth_all,
         depth_sum,
         fetched,
         sems,
@@ -269,22 +294,20 @@
     lax.fori_loop(0, count, one_slot, 0)
 
     if relative:
-        sides = [(outs[0], 0), (outs[1], 0)]
-        core_spots = [sides[at // (pairs // 2)] + (at % (pairs // 2),) for at in range(pairs)]
-        row_count = len(row_spots) // 2
-        row_places = [sides[at // row_count] + (pairs // 2 + at % row_count,) for at in range(2 * row_count)]
+        start, row_count = pairs // 2, len(row_spots) // 2
+        core_spots = [None] * start + [(outs[1], at) for at in range(start)]
+        row_places = [(outs[0], at) for at in range(row_count)] + [(outs[1], start + at) for at in range(row_count)]
     else:
-        core_spots = [(outs[0], 0, at) for at in range(pairs)]
-        row_places = [(outs[1], 0, at) for at in range(len(row_spots))]
+        core_spots = [(outs[0], at) for at in range(pairs)]
+        row_places = [(outs[1], at) for at in range(len(row_spots))]
     total = jnp.zeros((second_all.shape[1], rank), f32)
-    for at in range(pairs):
-        pair = at ^ core_mask
-        second = second_all[pair]
-        total = total + dot(second, core[pair])
-        piece = dot(second, depth_all[...], ((0,), (0,)))
-        out, _, line = core_spots[at]
-        out[line] = jnp.concatenate([piece[:rank], piece[rank:]], axis=1)
-    for at, (out, _, line) in enumerate(row_places):
+    for pair in range(pairs):
+        total = total + dot(second_all[pair], core[pair])
+    for at, spot in enumerate(core_spots):
+        if spot is not None:
+            out, line = spot
+            out[line] = core_chunk(second_all[at ^ core_mask], depth_all[...])
+    for at, (out, line) in enumerate(row_places):
         out[line] = rows_out[at]
     for s in range(slots):
 
@@ -296,8 +319,8 @@
 
     depth = depth_sum[...].T
     if relative:
-        for out in outs:
-            out[pairs // 2 + row_count] = depth
+        outs[0][row_count] = depth
+        outs[1][start + row_count] = depth
     else:
         outs[2][...] = depth
 
@@ -310,8 +333,8 @@
 
     width = depth_blocks * slab
     if relative:
-        chunks = (rank // 2 + len(row_spots)) // 2 + 1
-        outs = (jax.ShapeDtypeStruct((chunks, rank, rows), f32),) * 2
+        chunks = len(row_spots) // 2 + 1
+        outs = tuple(jax.ShapeDtypeStruct((at, rank, rows), f32) for at in (chunks, rank // 4 + chunks))
     else:
         outs = (
             jax.ShapeDtypeStruct((rank // 2, rank, 2 * rank), f32),
@@ -320,6 +343,8 @@
         )
     outs += (
         jax.ShapeDtypeStruct((len(col_spots), rank, cols), f32),
+        jax.ShapeDtypeStruct((rank // 2, slots * slab, 2 * rank), bf16),
+        jax.ShapeDtypeStruct((slots * slab, rank), bf16),
         jax.ShapeDtypeStruct(spread.shape, f32),
     )
     return pl.pallas_call(
@@ -339,8 +364,6 @@
                 pltpu.VMEM((2 * rank, 2 * cols), bf16),
                 pltpu.VMEM((half * rank, 2 * cols), bf16),
                 pltpu.VMEM((rank * (slab + 1), cols), f32),
-                pltpu.VMEM((rank // 2, slots * slab, 2 * rank), bf16),
-                pltpu.VMEM((slots * slab, rank), bf16),
                 pltpu.VMEM((depth_blocks * slab, rank), f32),
                 pltpu.VMEM((2, 2, rows, slab, cols), bf16),
                 pltpu.SemaphoreType.DMA((2, 2)),
@@ -423,24 +446,24 @@
     return values[0]
 
 
-def after_cores_kernel(n_ia, n_ka, keep, got, own_core, own_depth, own_rows, *messages):
+def after_cores_kernel(n_ia, n_ka, core_keep, keep, got, own_core, own_depth, own_rows, *messages):
     half = n_ia * n_ka
-    depth = keep[half + n_ka] + got[half + n_ka]
+    depth = keep[n_ka] + got[half + n_ka]
     flat, exponent = scaled(depth)
     own_depth[...] = flat * power_of(exponent)[:1]
-    own_core[...] = keep[:n_ka] + got[:n_ka]
-    own_rows[...] = keep[half : half + n_ka] + got[half : half + n_ka]
+    own_core[...] = core_keep[:n_ka] + got[:n_ka]
+    own_rows[...] = keep[:n_ka] + got[half : half + n_ka]
     for mask in range(1, n_ia):
         lines = slice(mask * n_ka, (mask + 1) * n_ka)
-        core = (keep[lines] + got[lines]).reshape(-1, depth.shape[1])
+        core = (core_keep[lines] + got[lines]).reshape(-1, depth.shape[1])
         fill_message(messages[mask - 1], scaled(core), (flat, exponent))
 
 
-def after_cores(n_ia, n_ka, keep, got):
+def after_cores(n_ia, n_ka, core_keep, keep, got):
     _, rank, lanes = keep.shape
     outs = [jax.ShapeDtypeStruct(shape, f32) for shape in ((n_ka, rank, lanes), (rank, lanes), (n_ka, rank, lanes))]
     outs += [message_shape(n_ka + 1, rank, lanes)] * (n_ia - 1)
-    outs = vmem_call(functools.partial(after_cores_kernel, n_ia, n_ka), tuple(outs), keep, got, name="after_cores")
+    outs = vmem_call(functools.partial(after_cores_kernel, n_ia, n_ka), tuple(outs), core_keep, keep, got, name="after_cores")
     return outs[0], outs[1], outs[2], outs[3:]
 
 
@@ -602,7 +625,7 @@
         weight,
         depth_blocks,
     )
-    *sums, cols_sum, _ = terms(
+    *sums, cols_sum, second_all, depth_all, _ = terms(
         by_swaps,
         sizes,
         row_spots,
@@ -633,7 +656,8 @@
 
     keep, send = sums
     got = swap(send, "ja", n_ja, 1)
-    own_core, own_depth, own_rows, messages = after_cores(n_ia, n_ka, keep, got)
+    core_keep = keep_terms(sizes, second_all, depth_all)
+    own_core, own_depth, own_rows, messages = after_cores(n_ia, n_ka, core_keep, keep, got)
     messages = [swap(message.astype(wire), "ia", n_ia, at + 1).astype(f32) for at, message in enumerate(messages)]
     depth_total, messages = after_rows(n_ia, n_ka, own_core, own_depth, own_rows, cols_sum, messages)
     messages = [messages[0]] + [

time: 55.2 us -> 54.2 us (0.982); the launches traced: 54.8 us -> 54.5 us
  Pallas kernels: 12.4 us -> 9.54 us
  starting transfers between devices: 22.6 us -> 24.8 us
    pallas_call x1, Pallas kernels: 5.24 us -> 1.82 us  [terms(): pl.pallas_call(functools.partial(terms_kernel, relative, sizes, row_spots...]
    ppermute x18, starting transfers between devices: 22.6 us -> 24.8 us  [swap(): return lax.ppermute(value, axis, [(at, at ^ mask) for at in range(size)])]
    pallas_call x0 -> x1, Pallas kernels: none -> 0.58 us  [keep_terms(): pl.pallas_call(functools.partial(keep_kernel, sizes), out_shape=jax.Shape...]
  transfers between devices with their start and end apart: 18 -> 18, of which waited for: 10 -> 10; matrix products, arithmetic and copies ran while one was open for 0% -> 0% of each run, Pallas kernels for 9% -> 11%
where the time goes in v11:
time: 54.2 us; the launch traced here: 54.5 us
  starting transfers between devices  24.8 us (46%)
  waiting for transfers between devices  17.5 us (32%)
  Pallas kernels  9.54 us (18%)
  between operations  1.54 us (3%)
  other arithmetic  1.05 us (2%)
    ppermute x18, starting transfers between devices, swap(): return lax.ppermute(value, axis, [(at, at ^ mask) for at in range(size)])  24.8 us
    ppermute x18, waiting for transfers between devices, swap(): return lax.ppermute(value, axis, [(at, at ^ mask) for at in range(size)])  17.5 us
    pallas_call x1, Pallas kernels, first_cubes(): pl.pallas_call(functools.partial(cube_kernel, slab), out_shape=(jax.Shape...  4.01 us
    pallas_call x2, Pallas kernels, unpack(): pl.pallas_call(functools.partial(unpack_kernel, sizes, rank, 0 if near el...  2.34 us
    pallas_call x1, Pallas kernels, terms(): pl.pallas_call(functools.partial(terms_kernel, relative, sizes, row_spots...  1.82 us
  transfers between devices with their start and end apart: 18, of which 10 were waited for; matrix products, arithmetic and copies ran while one was open for 0% of the time, Pallas kernels for 11%

profile of v11, /device:TPU:0, one launch (start us, length us, event | category | flops | bytes accessed | tf_op | source)
XLA Modules:
  0.0 54.5 jit_solution(18088998921824748530)
XLA Ops:
  0.6 0.5 collective-permute-start
  1.8 0.4 collective-permute-done
  2.2 0.7 %pad_maximum_fusion.after.refs_0_ = bf16[3,64,128]{2,1,0:T(8,128)(2,1)S(1)} fusion(bf16[1,64,128]{2,1,0:T(8,128)(2,1)} %bitcast.10, bf16[1,64,128]{2,1,0:T(8,128)(2,1)S(1)} %bitcast.12, bf16[1,64,128]{2,1,0:T(8,128)(2,1)} %bitcast.11), kind=kLoop, calls=%fused_computation | loop fusion | flops 49152 | bytes 98304 | tf_op jit(solution)/shard_map/stack | solution.py:605
  2.9 5.0 %collective-permute-start.3 = (bf16[3,64,128]{2,1,0:T(8,128)(2,1)S(1)}, bf16[3,64,128]{2,1,0:T(8,128)(2,1)S(1)}, u32[]{:S(2)}, u32[]{:S(2)}) collective-permute-start(bf16[3,64,128]{2,1,0:T(8,128)(2,1)S(1)} %pad_maximum_fusion.after.refs_0_), channel_id=1, source_target_pairs={{0,3},{1,2},{2,1},{3,0},{4,7},{5,6},{6,5},{7,4},{8,11},{9,10},{10,... | collective-permute-start | bytes 147464 | tf_op jit(solution)/shard_map/ppermute | solution.py:578
  7.9 0.0 collective-permute-start.2
  7.9 0.6 %collective-permute-start.1 = (bf16[3,64,128]{2,1,0:T(8,128)(2,1)S(1)}, bf16[3,64,128]{2,1,0:T(8,128)(2,1)S(1)}, u32[]{:S(2)}, u32[]{:S(2)}) collective-permute-start(bf16[3,64,128]{2,1,0:T(8,128)(2,1)S(1)} %pad_maximum_fusion.after.refs_0_), channel_id=1, source_target_pairs={{0,1},{1,0},{2,3},{3,2},{4,5},{5,4},{6,7},{7,6},{8,9},{9,8},{10,11... | collective-permute-start | bytes 147464 | tf_op jit(solution)/shard_map/ppermute | solution.py:578
  8.6 4.0 %first_cubes.1 = (bf16[4,1024,128]{2,1,0:T(8,128)(2,1)S(1)}, bf16[4,128,1024]{2,1,0:T(8,128)(2,1)S(1)}, bf16[32,128,64]{2,1,0:T(8,128)(2,1)S(1)}, bf16[128,64]{1...) custom-call(bf16[3,64,128]{2,1,0:T(8,128)(2,1)S(1)} %pad_maximum_fusion.after.refs_0_, ...), custom_call_target="tpu_custom_call" | custom-call | flops 1000000000 | bytes 4194304 | tf_op jit(solution)/shard_map/first_cubes/pallas_call | solution.py:96
  12.6 0.0 collective-permute-done.3.refs_3_
  12.6 0.3 collective-permute-done.2.refs_2_
  12.9 0.0 collective-permute-done.1.refs_1_
  12.9 1.8 %terms.1 = (f32[5,64,128]{2,1,0:T(8,128)S(1)}, f32[21,64,128]{2,1,0:T(8,128)S(1)}, f32[4,64,128]{2,1,0:T(8,128)S(1)}, bf16[32,160,128]{2,1,0:T(8,128)(2,1)S(1)},...) custom-call(s32[1,1,1]{2,1,0:T(1,128)S(6)} %copy.16.counts, ...), custom_call_target="tpu_custom_call", output_to_operand_aliasing={{5}: (12, {})} | custom-call | flops 1000000000 | bytes 16777216 | tf_op jit(solution)/shard_map/terms/pallas_call | solution.py:350
  14.8 0.7 %collective-permute-start.4 = (f32[21,64,128]{2,1,0:T(8,128)S(1)}, f32[21,64,128]{2,1,0:T(8,128)S(1)}, u32[]{:S(2)}, u32[]{:S(2)}) collective-permute-start(f32[21,64,128]{2,1,0:T(8,128)S(1)} %get-tuple-element.41), channel_id=1, source_target_pairs={{0,4},{4,0},{1,5},{5,1},{2,6},{6,2},{3,7},{7,3},{8,12},{12,8},{9,1... | collective-permute-start | bytes 2064392 | tf_op jit(solution)/shard_map/ppermute | solution.py:578
  15.5 0.6 %keep_terms.1.core_keep = f32[16,64,128]{2,1,0:T(8,128)S(1)} custom-call(bf16[32,160,128]{2,1,0:T(8,128)(2,1)S(1)} %get-tuple-element.38.second_all, bf16[160,64]{1,0:T(8,128)(2,1)S(1)} %get-tuple-element.39.depth_all), custom_call_target="tpu_custom_call" | custom-call | flops 1000000000 | bytes 4194304 | tf_op jit(solution)/shard_map/keep_terms/pallas_call | solution.py:143
  16.1 1.2 %collective-permute-done.4.got = f32[21,64,128]{2,1,0:T(8,128)S(1)} collective-permute-done((f32[21,64,128]{2,1,0:T(8,128)S(1)}, f32[21,64,128]{2,1,0:T(8,128)S(1)}, u32[]{:S(2)}, u32[]{:S(2)}) %collective-permute-start.4) | collective-permute-done | bytes 688160 | tf_op jit(solution)/shard_map/ppermute | solution.py:578
  17.3 0.3 after_cores.1
  17.6 9.1 %collective-permute-start.7 = (f16[336,128]{1,0:T(8,128)(2,1)S(1)}, f16[336,128]{1,0:T(8,128)(2,1)S(1)}, u32[]{:S(2)}, u32[]{:S(2)}) collective-permute-start(f16[336,128]{1,0:T(8,128)(2,1)S(1)} %convert_element_type.67), channel_id=1, source_target_pairs={{0,24},{8,16},{16,8},{24,0},{1,25},{9,17},{17,9},{25,1},{2,26},{10... | collective-permute-start | bytes 258056 | tf_op jit(solution)/shard_map/ppermute | solution.py:578
  26.7 0.0 collective-permute-start.6
  26.7 0.7 %collective-permute-start.5 = (f16[336,128]{1,0:T(8,128)(2,1)S(1)}, f16[336,128]{1,0:T(8,128)(2,1)S(1)}, u32[]{:S(2)}, u32[]{:S(2)}) collective-permute-start(f16[336,128]{1,0:T(8,128)(2,1)S(1)} %convert_element_type.63), channel_id=1, source_target_pairs={{0,8},{8,0},{16,24},{24,16},{1,9},{9,1},{17,25},{25,17},{2,10},{10... | collective-permute-start | bytes 258056 | tf_op jit(solution)/shard_map/ppermute | solution.py:578
  27.4 2.4 %collective-permute-done.7 = f16[336,128]{1,0:T(8,128)(2,1)S(1)} collective-permute-done((f16[336,128]{1,0:T(8,128)(2,1)S(1)}, f16[336,128]{1,0:T(8,128)(2,1)S(1)}, u32[]{:S(2)}, u32[]{:S(2)}) %collective-permute-start.7) | collective-permute-done | bytes 86048 | tf_op jit(solution)/shard_map/ppermute | solution.py:578
  29.8 1.8 %collective-permute-done.6 = f16[336,128]{1,0:T(8,128)(2,1)S(1)} collective-permute-done((f16[336,128]{1,0:T(8,128)(2,1)S(1)}, f16[336,128]{1,0:T(8,128)(2,1)S(1)}, u32[]{:S(2)}, u32[]{:S(2)}) %collective-permute-start.6) | collective-permute-done | bytes 86048 | tf_op jit(solution)/shard_map/ppermute | solution.py:578
  31.6 0.0 collective-permute-done.5
  31.7 0.3 after_rows.1
  32.0 0.1 collective-permute-start.10
  32.1 2.8 %collective-permute-start.9 = (f16[400,128]{1,0:T(8,128)(2,1)S(1)}, f16[400,128]{1,0:T(8,128)(2,1)S(1)}, u32[]{:S(2)}, u32[]{:S(2)}) collective-permute-start(f16[400,128]{1,0:T(8,128)(2,1)S(1)} %convert_element_type.71), channel_id=1, source_target_pairs={{0,2},{1,3},{2,0},{3,1},{4,6},{5,7},{6,4},{7,5},{8,10},{9,11},{10,... | collective-permute-start | bytes 307208 | tf_op jit(solution)/shard_map/ppermute | solution.py:578
  34.9 1.6 %collective-permute-start.8 = (f16[400,128]{1,0:T(8,128)(2,1)S(1)}, f16[400,128]{1,0:T(8,128)(2,1)S(1)}, u32[]{:S(2)}, u32[]{:S(2)}) collective-permute-start(f16[400,128]{1,0:T(8,128)(2,1)S(1)} %convert_element_type.69), channel_id=1, source_target_pairs={{0,1},{1,0},{2,3},{3,2},{4,5},{5,4},{6,7},{7,6},{8,9},{9,8},{10,11... | collective-permute-start | bytes 307208 | tf_op jit(solution)/shard_map/ppermute | solution.py:578
  36.5 3.1 %collective-permute-done.10 = f16[400,128]{1,0:T(8,128)(2,1)S(1)} collective-permute-done((f16[400,128]{1,0:T(8,128)(2,1)S(1)}, f16[400,128]{1,0:T(8,128)(2,1)S(1)}, u32[]{:S(2)}, u32[]{:S(2)}) %collective-permute-start.10) | collective-permute-done | bytes 102432 | tf_op jit(solution)/shard_map/ppermute | solution.py:578
  39.7 4.2 %collective-permute-done.9 = f16[400,128]{1,0:T(8,128)(2,1)S(1)} collective-permute-done((f16[400,128]{1,0:T(8,128)(2,1)S(1)}, f16[400,128]{1,0:T(8,128)(2,1)S(1)}, u32[]{:S(2)}, u32[]{:S(2)}) %collective-permute-start.9) | collective-permute-done | bytes 102432 | tf_op jit(solution)/shard_map/ppermute | solution.py:578
  43.9 0.0 collective-permute-done.8
  43.9 0.3 after_depths.1
  44.2 1.7 %collective-permute-start.13 = (f16[336,128]{1,0:T(8,128)(2,1)S(1)}, f16[336,128]{1,0:T(8,128)(2,1)S(1)}, u32[]{:S(2)}, u32[]{:S(2)}) collective-permute-start(f16[336,128]{1,0:T(8,128)(2,1)S(1)} %get-tuple-element.61), channel_id=1, source_target_pairs={{0,24},{8,16},{16,8},{24,0},{1,25},{9,17},{17,9},{25,1},{2,26},{10... | collective-permute-start | bytes 258056 | tf_op jit(solution)/shard_map/ppermute | solution.py:578
  45.9 1.5 %collective-permute-start.12 = (f16[336,128]{1,0:T(8,128)(2,1)S(1)}, f16[336,128]{1,0:T(8,128)(2,1)S(1)}, u32[]{:S(2)}, u32[]{:S(2)}) collective-permute-start(f16[336,128]{1,0:T(8,128)(2,1)S(1)} %get-tuple-element.61), channel_id=1, source_target_pairs={{0,16},{8,24},{16,0},{24,8},{1,17},{9,25},{17,1},{25,9},{2,18},{10... | collective-permute-start | bytes 258056 | tf_op jit(solution)/shard_map/ppermute | solution.py:578
  47.4 0.3 collective-permute-start.11
  47.8 0.0 collective-permute-start.14
  47.8 2.2 %collective-permute-done.13 = f16[336,128]{1,0:T(8,128)(2,1)S(1)} collective-permute-done((f16[336,128]{1,0:T(8,128)(2,1)S(1)}, f16[336,128]{1,0:T(8,128)(2,1)S(1)}, u32[]{:S(2)}, u32[]{:S(2)}) %collective-permute-start.13) | collective-permute-done | bytes 86048 | tf_op jit(solution)/shard_map/ppermute | solution.py:578
  50.0 0.0 collective-permute-start.17
  50.0 0.9 %collective-permute-done.12 = f16[336,128]{1,0:T(8,128)(2,1)S(1)} collective-permute-done((f16[336,128]{1,0:T(8,128)(2,1)S(1)}, f16[336,128]{1,0:T(8,128)(2,1)S(1)}, u32[]{:S(2)}, u32[]{:S(2)}) %collective-permute-start.12) | collective-permute-done | bytes 86048 | tf_op jit(solution)/shard_map/ppermute | solution.py:578
  50.8 0.0 collective-permute-start.16
  50.8 1.1 %collective-permute-done.11 = f16[336,128]{1,0:T(8,128)(2,1)S(1)} collective-permute-done((f16[336,128]{1,0:T(8,128)(2,1)S(1)}, f16[336,128]{1,0:T(8,128)(2,1)S(1)}, u32[]{:S(2)}, u32[]{:S(2)}) %collective-permute-start.11) | collective-permute-done | bytes 86048 | tf_op jit(solution)/shard_map/ppermute | solution.py:578
  51.9 0.0 collective-permute-start.15
  52.0 0.0 collective-permute-done.14
  52.0 1.2 %unpack_near.1 = (f32[64,64,64]{2,1,0:T(8,128)}, f32[64,128]{1,0:T(8,128)}, f32[64,128]{1,0:T(8,128)}, f32[64,128]{1,0:T(8,128)}) custom-call(f32[336,128]{1,0:T(8,128)S(1)} %get-tuple-element.60.refs_0_, f32[336,128]{1,0:T(8,128)S(1)} %convert_element_type.77.refs_1_, f32[336,128]{1,0:T(8,128)S(1)} %convert_element_type.78.refs_2_, ...), custom_call_target="tpu_custom_call" | custom-call | flops 1000000 | bytes 4194304 | tf_op jit(solution)/shard_map/unpack_near/pallas_call | solution.py:555
  53.2 0.0 collective-permute-done.17
  53.2 0.0 collective-permute-done.16
  53.3 0.0 collective-permute-done.15
  53.3 1.2 %unpack_far.1 = f32[64,64,64]{2,1,0:T(8,128)} custom-call(f32[336,128]{1,0:T(8,128)S(1)} %convert_element_type.80.refs_0_, f32[336,128]{1,0:T(8,128)S(1)} %convert_element_type.81.refs_1_, f32[336,128]{1,0:T(8,128)S(1)} %convert_element_type.82.refs_2_, f32[336,128]{1,0:T(8,128)S(1)} %convert_element_type.83.refs_3_, ...), custom_call_target="tpu_custom_call", output_to_operand_aliasing={{}: (4, {})} | custom-call | flops 1000000 | bytes 4194304 | tf_op jit(solution)/shard_map/unpack_far/pallas_call | solution.py:555
  (20 shorter events, 0.3 us)
Async XLA Ops:
  0.6 1.6 %collective-permute-start = (bf16[64,128]{1,0:T(8,128)(2,1)}, bf16[64,128]{1,0:T(8,128)(2,1)S(1)}, u32[]{:S(2)}, u32[]{:S(2)}) collective-permute-start(bf16[64,128]{1,0:T(8,128)(2,1)} %param.12), channel_id=1, source_target_pairs={{0,4},{4,0},{1,5},{5,1},{2,6},{6,2},{3,7},{7,3},{8,12},{12,8},{9,1... | collective-permute-start | bytes 49160 | tf_op jit(solution)/shard_map/ppermute | solution.py:578
  2.9 9.7 %collective-permute-start.3 = (bf16[3,64,128]{2,1,0:T(8,128)(2,1)S(1)}, bf16[3,64,128]{2,1,0:T(8,128)(2,1)S(1)}, u32[]{:S(2)}, u32[]{:S(2)}) collective-permute-start(bf16[3,64,128]{2,1,0:T(8,128)(2,1)S(1)} %pad_maximum_fusion.after.refs_0_), channel_id=1, source_target_pairs={{0,3},{1,2},{2,1},{3,0},{4,7},{5,6},{6,5},{7,4},{8,11},{9,10},{10,... | collective-permute-start | bytes 147464 | tf_op jit(solution)/shard_map/ppermute | solution.py:578
  7.9 5.0 %collective-permute-start.2 = (bf16[3,64,128]{2,1,0:T(8,128)(2,1)S(1)}, bf16[3,64,128]{2,1,0:T(8,128)(2,1)S(1)}, u32[]{:S(2)}, u32[]{:S(2)}) collective-permute-start(bf16[3,64,128]{2,1,0:T(8,128)(2,1)S(1)} %pad_maximum_fusion.after.refs_0_), channel_id=1, source_target_pairs={{0,2},{1,3},{2,0},{3,1},{4,6},{5,7},{6,4},{7,5},{8,10},{9,11},{10,... | collective-permute-start | bytes 147464 | tf_op jit(solution)/shard_map/ppermute | solution.py:578
  7.9 5.0 %collective-permute-start.1 = (bf16[3,64,128]{2,1,0:T(8,128)(2,1)S(1)}, bf16[3,64,128]{2,1,0:T(8,128)(2,1)S(1)}, u32[]{:S(2)}, u32[]{:S(2)}) collective-permute-start(bf16[3,64,128]{2,1,0:T(8,128)(2,1)S(1)} %pad_maximum_fusion.after.refs_0_), channel_id=1, source_target_pairs={{0,1},{1,0},{2,3},{3,2},{4,5},{5,4},{6,7},{7,6},{8,9},{9,8},{10,11... | collective-permute-start | bytes 147464 | tf_op jit(solution)/shard_map/ppermute | solution.py:578
  14.8 2.5 %collective-permute-start.4 = (f32[21,64,128]{2,1,0:T(8,128)S(1)}, f32[21,64,128]{2,1,0:T(8,128)S(1)}, u32[]{:S(2)}, u32[]{:S(2)}) collective-permute-start(f32[21,64,128]{2,1,0:T(8,128)S(1)} %get-tuple-element.41), channel_id=1, source_target_pairs={{0,4},{4,0},{1,5},{5,1},{2,6},{6,2},{3,7},{7,3},{8,12},{12,8},{9,1... | collective-permute-start | bytes 2064392 | tf_op jit(solution)/shard_map/ppermute | solution.py:578
  17.6 12.2 %collective-permute-start.7 = (f16[336,128]{1,0:T(8,128)(2,1)S(1)}, f16[336,128]{1,0:T(8,128)(2,1)S(1)}, u32[]{:S(2)}, u32[]{:S(2)}) collective-permute-start(f16[336,128]{1,0:T(8,128)(2,1)S(1)} %convert_element_type.67), channel_id=1, source_target_pairs={{0,24},{8,16},{16,8},{24,0},{1,25},{9,17},{17,9},{25,1},{2,26},{10... | collective-permute-start | bytes 258056 | tf_op jit(solution)/shard_map/ppermute | solution.py:578
  26.7 4.9 %collective-permute-start.6 = (f16[336,128]{1,0:T(8,128)(2,1)S(1)}, f16[336,128]{1,0:T(8,128)(2,1)S(1)}, u32[]{:S(2)}, u32[]{:S(2)}) collective-permute-start(f16[336,128]{1,0:T(8,128)(2,1)S(1)} %convert_element_type.65), channel_id=1, source_target_pairs={{0,16},{8,24},{16,0},{24,8},{1,17},{9,25},{17,1},{25,9},{2,18},{10... | collective-permute-start | bytes 258056 | tf_op jit(solution)/shard_map/ppermute | solution.py:578
  26.7 4.9 %collective-permute-start.5 = (f16[336,128]{1,0:T(8,128)(2,1)S(1)}, f16[336,128]{1,0:T(8,128)(2,1)S(1)}, u32[]{:S(2)}, u32[]{:S(2)}) collective-permute-start(f16[336,128]{1,0:T(8,128)(2,1)S(1)} %convert_element_type.63), channel_id=1, source_target_pairs={{0,8},{8,0},{16,24},{24,16},{1,9},{9,1},{17,25},{25,17},{2,10},{10... | collective-permute-start | bytes 258056 | tf_op jit(solution)/shard_map/ppermute | solution.py:578
  32.0 7.7 %collective-permute-start.10 = (f16[400,128]{1,0:T(8,128)(2,1)S(1)}, f16[400,128]{1,0:T(8,128)(2,1)S(1)}, u32[]{:S(2)}, u32[]{:S(2)}) collective-permute-start(f16[400,128]{1,0:T(8,128)(2,1)S(1)} %convert_element_type.73), channel_id=1, source_target_pairs={{0,3},{1,2},{2,1},{3,0},{4,7},{5,6},{6,5},{7,4},{8,11},{9,10},{10,... | collective-permute-start | bytes 307208 | tf_op jit(solution)/shard_map/ppermute | solution.py:578
  32.1 11.8 %collective-permute-start.9 = (f16[400,128]{1,0:T(8,128)(2,1)S(1)}, f16[400,128]{1,0:T(8,128)(2,1)S(1)}, u32[]{:S(2)}, u32[]{:S(2)}) collective-permute-start(f16[400,128]{1,0:T(8,128)(2,1)S(1)} %convert_element_type.71), channel_id=1, source_target_pairs={{0,2},{1,3},{2,0},{3,1},{4,6},{5,7},{6,4},{7,5},{8,10},{9,11},{10,... | collective-permute-start | bytes 307208 | tf_op jit(solution)/shard_map/ppermute | solution.py:578
  34.9 9.0 %collective-permute-start.8 = (f16[400,128]{1,0:T(8,128)(2,1)S(1)}, f16[400,128]{1,0:T(8,128)(2,1)S(1)}, u32[]{:S(2)}, u32[]{:S(2)}) collective-permute-start(f16[400,128]{1,0:T(8,128)(2,1)S(1)} %convert_element_type.69), channel_id=1, source_target_pairs={{0,1},{1,0},{2,3},{3,2},{4,5},{5,4},{6,7},{7,6},{8,9},{9,8},{10,11... | collective-permute-start | bytes 307208 | tf_op jit(solution)/shard_map/ppermute | solution.py:578
  44.2 5.8 %collective-permute-start.13 = (f16[336,128]{1,0:T(8,128)(2,1)S(1)}, f16[336,128]{1,0:T(8,128)(2,1)S(1)}, u32[]{:S(2)}, u32[]{:S(2)}) collective-permute-start(f16[336,128]{1,0:T(8,128)(2,1)S(1)} %get-tuple-element.61), channel_id=1, source_target_pairs={{0,24},{8,16},{16,8},{24,0},{1,25},{9,17},{17,9},{25,1},{2,26},{10... | collective-permute-start | bytes 258056 | tf_op jit(solution)/shard_map/ppermute | solution.py:578
  45.9 4.9 %collective-permute-start.12 = (f16[336,128]{1,0:T(8,128)(2,1)S(1)}, f16[336,128]{1,0:T(8,128)(2,1)S(1)}, u32[]{:S(2)}, u32[]{:S(2)}) collective-permute-start(f16[336,128]{1,0:T(8,128)(2,1)S(1)} %get-tuple-element.61), channel_id=1, source_target_pairs={{0,16},{8,24},{16,0},{24,8},{1,17},{9,25},{17,1},{25,9},{2,18},{10... | collective-permute-start | bytes 258056 | tf_op jit(solution)/shard_map/ppermute | solution.py:578
  47.4 4.5 %collective-permute-start.11 = (f16[336,128]{1,0:T(8,128)(2,1)S(1)}, f16[336,128]{1,0:T(8,128)(2,1)S(1)}, u32[]{:S(2)}, u32[]{:S(2)}) collective-permute-start(f16[336,128]{1,0:T(8,128)(2,1)S(1)} %get-tuple-element.61), channel_id=1, source_target_pairs={{0,8},{8,0},{16,24},{24,16},{1,9},{9,1},{17,25},{25,17},{2,10},{10... | collective-permute-start | bytes 258056 | tf_op jit(solution)/shard_map/ppermute | solution.py:578
  47.8 4.2 %collective-permute-start.14 = (f16[336,128]{1,0:T(8,128)(2,1)S(1)}, f16[336,128]{1,0:T(8,128)(2,1)S(1)}, u32[]{:S(2)}, u32[]{:S(2)}) collective-permute-start(f16[336,128]{1,0:T(8,128)(2,1)S(1)} %get-tuple-element.61), channel_id=1, source_target_pairs={{0,4},{4,0},{1,5},{5,1},{2,6},{6,2},{3,7},{7,3},{8,12},{12,8},{9,1... | collective-permute-start | bytes 258056 | tf_op jit(solution)/shard_map/ppermute | solution.py:578
  50.0 3.2 %collective-permute-start.17 = (f16[336,128]{1,0:T(8,128)(2,1)S(1)}, f16[336,128]{1,0:T(8,128)(2,1)S(1)}, u32[]{:S(2)}, u32[]{:S(2)}) collective-permute-start(f16[336,128]{1,0:T(8,128)(2,1)S(1)} %collective-permute-done.13), channel_id=1, source_target_pairs={{0,4},{4,0},{1,5},{5,1},{2,6},{6,2},{3,7},{7,3},{8,12},{12,8},{9,1... | collective-permute-start | bytes 258056 | tf_op jit(solution)/shard_map/ppermute | solution.py:578
  50.8 2.4 %collective-permute-start.16 = (f16[336,128]{1,0:T(8,128)(2,1)S(1)}, f16[336,128]{1,0:T(8,128)(2,1)S(1)}, u32[]{:S(2)}, u32[]{:S(2)}) collective-permute-start(f16[336,128]{1,0:T(8,128)(2,1)S(1)} %collective-permute-done.12), channel_id=1, source_target_pairs={{0,4},{4,0},{1,5},{5,1},{2,6},{6,2},{3,7},{7,3},{8,12},{12,8},{9,1... | collective-permute-start | bytes 258056 | tf_op jit(solution)/shard_map/ppermute | solution.py:578
  51.9 1.3 %collective-permute-start.15 = (f16[336,128]{1,0:T(8,128)(2,1)S(1)}, f16[336,128]{1,0:T(8,128)(2,1)S(1)}, u32[]{:S(2)}, u32[]{:S(2)}) collective-permute-start(f16[336,128]{1,0:T(8,128)(2,1)S(1)} %collective-permute-done.11), channel_id=1, source_target_pairs={{0,4},{4,0},{1,5},{5,1},{2,6},{6,2},{3,7},{7,3},{8,12},{12,8},{9,1... | collective-permute-start | bytes 258056 | tf_op jit(solution)/shard_map/ppermute | solution.py:578
